TPU v7x, 128 devices: a whole 4x4x4 slice. The times are simulated.
128 devices in a mesh: pat: 16 (over z_hi, y, core), code: 8 (over z_lo, x).
Axes of the slice: x: 4, y: 4, z: 4 (z_hi: 2, z_lo: 2; z = z_hi * 2 + z_lo), core: 2. Of those that a mesh axis runs over, the one named last changes fastest.
Arguments:
- tile_data: bfloat16 [16, 8, 16, 128, 512], P('pat', 'code'), may hold values from 0 to 7, as said below
- tile_list: int32 [16, 8, 3, 16], P('pat', 'code'), may hold values from 0 to 31, as said below
- tile_count: int32 [16, 8], P('pat', 'code'), may hold values from 8 to 16, as said below
- visit_counts: int32 [512], P('pat'), may hold values from 1 to 256, as said below
- code_factor_t: float32 [64, 65536], P(None, 'code'), may hold values from 0.004 to 0.33, as said below
- visit_mix: float32 [64, 64], replicated, may hold values from -0.15 to 1.2
- patient_weight: float32 [512, 64], P('pat'), may hold values from 0.5 to 30, as said below
Outputs:
- code_factor_new: float32 [64, 65536], P(None, 'code')
- mix_new: float32 [64, 64], replicated
- patient_weight_new: float32 [512, 64], P(('pat', 'code'))
Inputs may be any that keep to these rules, and one draw needn't show every extreme that they name: `tile_list`: for device (p, c) and slot t: entry 0 is a patient of pat index p (0 to 31), entry 1 a visit block below that patient's visits divided by 128 and rounded up, entry 2 a code block of code index c (0 to 15). A triple may repeat; such tiles add. `tile_count`: slots at or past a device's count are not in use; some device uses all slots. `visit_counts`: some patient has 256 visits. `tile_data`: Whole-number counts. Rows past the patient's visit count and slots not in use hold left-over values that are not part of the data. `code_factor_t`: Positive. `patient_weight`: Positive.
All inputs are finite; a program needn't handle non-finite values.
Results may differ from a plain program's by a relative error of at most 0.0073.
Values may be sent and summed in bfloat16 or wider, within the bound.
No kernel may reach another device: no remote copies, remote signals or barrier semaphores. Data moves between devices by JAX's collectives and lax.ppermute only.
A program may use at most 64 MiB of HBM per device.

v0:
```python
import jax
import jax.numpy as jnp
from jax import lax
from jax.sharding import PartitionSpec as P

VBLOCKS = 2
NS_STEPS = 8


highest = lax.Precision.HIGHEST
damping = 0.1
epsilon = 1e-06


def damped_solve(gram, right):
    eye_mat = jnp.eye(gram.shape[0], dtype=gram.dtype)
    shifted = gram + damping * jnp.mean(jnp.diagonal(gram)) * eye_mat
    lower_factor = jnp.linalg.cholesky(shifted)
    halfway = lax.linalg.triangular_solve(lower_factor, right, left_side=True, lower=True)
    return lax.linalg.triangular_solve(
        lower_factor, halfway, left_side=True, lower=True, transpose_a=True
    )


def newton_schulz(target):
    norm_sq = jnp.sum(target * target, axis=(1, 2, 3), keepdims=True)
    iterate = target / jnp.sqrt(norm_sq + epsilon)
    for step_number in range(NS_STEPS):
        inner_gram = jnp.einsum("kbrv,kbsv->krs", iterate, iterate, precision=highest)
        iterate = 1.5 * iterate - 0.5 * jnp.einsum(
            "krs,kbsv->kbrv", inner_gram, iterate, precision=highest
        )
    return iterate


def keep_rows(owners, visit_block, live_count, visits_row, slot_total, tile_rows):
    match = owners[:, None] == jnp.arange(visits_row.shape[0], dtype=jnp.int32)[None, :]
    own_visits = jnp.sum(jnp.where(match, visits_row[None, :], 0), axis=1)
    row_index = visit_block[:, None] * tile_rows + jnp.arange(tile_rows, dtype=jnp.int32)[None, :]
    in_use = jnp.arange(slot_total, dtype=jnp.int32) < live_count
    return (row_index < own_visits[:, None]) & in_use[:, None]


def body(tile_data, tile_list, tile_count, visit_counts, code_factor_t, visit_mix, patient_weight):
    tile_slab = tile_data[0, 0]
    owners = tile_list[0, 0, 0]
    visit_block = tile_list[0, 0, 1]
    code_block = tile_list[0, 0, 2]
    live_count = tile_count[0, 0]
    factor_rank = visit_mix.shape[0]
    pat_row = visit_counts.shape[0]
    slot_total, tile_rows, tile_cols = tile_slab.shape
    block_count = code_factor_t.shape[1] // tile_cols
    pat_own = pat_row // lax.axis_size("code")
    segment_total = pat_row * VBLOCKS
    group_size = min(16, slot_total)
    live_turns = (live_count + group_size - 1) // group_size
    keep_mask = keep_rows(owners, visit_block, live_count, visit_counts, slot_total, tile_rows)
    segment = owners * VBLOCKS + visit_block
    code_blocks = code_factor_t.astype(jnp.bfloat16).reshape(factor_rank, block_count, tile_cols)

    def masked_group():
        return jnp.where(keep_mask[:, :, None], tile_slab, jnp.zeros((), jnp.bfloat16))

    def product_step(counter, running):
        masked = masked_group()
        picked = jnp.take(code_blocks, code_block, axis=1)
        contrib = jnp.einsum("rtc,tvc->trv", picked, masked, preferred_element_type=jnp.float32)
        return running.at[segment].add(contrib)

    code_partial = lax.fori_loop(
        0, live_turns, product_step, jnp.zeros((segment_total, factor_rank, tile_rows), jnp.float32)
    )
    code_partial = code_partial.reshape(pat_row, VBLOCKS, factor_rank, tile_rows)
    gram_partial = jnp.dot(code_factor_t, code_factor_t.T, precision=highest)
    code_index = lax.axis_index("code")
    own_products = lax.psum_scatter(code_partial, "code", scatter_dimension=0, tiled=True)
    code_gram = lax.psum(gram_partial, "code")
    weight_mine = lax.dynamic_slice_in_dim(patient_weight, code_index * pat_own, pat_own, 0)
    target = jnp.einsum("rs,ks,kbsv->kbrv", visit_mix, weight_mine, own_products, precision=highest)
    polar_factor = newton_schulz(target)
    projected = jnp.einsum("kbrv,kbsv->krs", polar_factor, own_products, precision=highest)
    numer_partial = jnp.einsum("kis,ks->is", projected, weight_mine, precision=highest)
    weight_partial = jnp.dot(weight_mine.T, weight_mine, precision=highest)
    mix_numer, weight_gram = lax.psum((numer_partial, weight_partial), ("pat", "code"))
    mix_new = damped_solve(code_gram * weight_gram, mix_numer.T).T
    mix_gram = jnp.dot(mix_new.T, mix_new, precision=highest)
    diag_terms = jnp.einsum("is,kis->ks", mix_new, projected, precision=highest)
    weight_new = jnp.maximum(damped_solve(mix_gram * code_gram, diag_terms.T).T, 0.0)
    spread = (
        jnp.einsum("is,kbiv->kbsv", mix_new, polar_factor, precision=highest)
        * weight_new[:, None, :, None]
    ).astype(jnp.bfloat16)
    new_partial = jnp.dot(weight_new.T, weight_new, precision=highest)
    weight_gram_new = lax.psum(new_partial, ("pat", "code"))
    spread_all = lax.all_gather(spread, "code", axis=0, tiled=True)
    spread_flat = spread_all.reshape(segment_total, factor_rank, tile_rows)

    def numer_step(counter, running):
        masked = masked_group()
        picked = jnp.take(spread_flat, segment, axis=0)
        contrib = jnp.einsum("trv,tvc->trc", picked, masked, preferred_element_type=jnp.float32)
        return running.at[code_block].add(contrib)

    numer_blocks = lax.fori_loop(
        0, live_turns, numer_step, jnp.zeros((block_count, factor_rank, tile_cols), jnp.float32)
    )
    numer_local = jnp.transpose(numer_blocks, (1, 0, 2))
    code_system = mix_gram * weight_gram_new
    numer_sums = lax.psum(numer_local, "pat")
    code_new = jnp.maximum(
        damped_solve(code_system, numer_sums.reshape(factor_rank, block_count * tile_cols)), 0.0
    )
    return (code_new, mix_new, weight_new)


def solution(mesh):
    placed = (
        P("pat", "code", None, None, None),
        P("pat", "code", None, None),
        P("pat", "code"),
        P("pat"),
        P(None, "code"),
        P(),
        P("pat", None),
    )
    return jax.shard_map(
        body,
        mesh=mesh,
        in_specs=placed,
        out_specs=(P(None, "code"), P(), P(("pat", "code"), None)),
        check_vma=False,
    )
```

profile of v0, /device:TPU:3, one launch (start us, length us, event | category | flops | bytes accessed | tf_op | source)
XLA Modules:
  0.0 369.9 jit_solution(10287543827223742106)
XLA Ops:
  7.9 0.7 bitcast_multiply_fusion.2
  8.5 0.7 slice_bitcast_fusion.1
  9.2 0.7 fusion.68
  9.9 0.7 compare_and_fusion
  10.6 1.7 convert_element_type.12
  12.7 0.6 gather_fusion.1
  13.4 2.4 fusion.3
  16.0 1.4 while.24
  16.0 1.3 scatter_fusion
  17.4 1.3 copy-done.1
  18.8 4.0 %fusion.74 = f32[64,64]{1,0:T(8,128)S(1)} fusion(f32[64,8192]{1,0:T(8,128)} %param.16), kind=kOutput, calls=%fused_computation.131 | convolution fusion | flops 402653184 | bytes 2113536 | tf_op jit(solution)/shard_map/dot_general | solution.py:75
  22.8 25.5 %psum.35 = f32[64,64]{1,0:T(8,128)S(1)} all-reduce(f32[64,64]{1,0:T(8,128)S(1)} %fusion.74), channel_id=1, replica_groups=mesh['pat'=16,'code'=8] {'code'}, use_global_device_ids=true, to_apply=%region_0.1 | all-reduce | flops 4096 | bytes 32768 | tf_op jit(solution)/shard_map/psum | solution.py:78
  48.3 0.7 constant_dynamic-slice_fusion
  49.0 0.7 fusion.133
  49.9 7.7 %reduce-scatter.2.cloned.1.call-done = f32[4,2,64,128]{3,2,1,0:T(8,128)} async-done(((f32[32,2,64,128]{3,2,1,0:T(8,128)}), f32[4,2,64,128]{3,2,1,0:T(8,128)}) %reduce-scatter.2.cloned.1.call-update) | async-done | bytes 262160 | tf_op jit(solution)/shard_map/reduce_scatter | solution.py:77
  57.6 1.5 multiply_reduce_fusion
  66.0 69.4 %all-reduce = (f32[64,64]{0,1:T(8,128)S(1)}, f32[64,64]{1,0:T(8,128)S(1)}) all-reduce(f32[64,64]{0,1:T(8,128)S(1)} %bitcast.258, f32[64,64]{1,0:T(8,128)S(1)} %fusion.75), channel_id=1, replica_groups=mesh['pat'=16,'code'=8] {'pat','code'}, use_global_device_ids=true, to_apply=%region_11.13 | all-reduce | flops 8192 | bytes 65536 | tf_op jit(solution)/shard_map/psum | solution.py:85
  135.4 0.8 gather_fusion
  136.2 0.6 reduce_sum.45
  137.6 5.9 %cholesky.59 = f32[64,64]{1,0:T(8,128)S(1)} custom-call(f32[64,64]{1,0:T(8,128)S(1)} %copy.44), custom_call_target="Cholesky" | custom-call | tf_op jit(solution)/shard_map/jit(cholesky)/cholesky | solution.py:18
  143.5 0.6 compare_reduce_fusion.2
  144.2 0.7 fusion.38
  144.8 4.9 %custom-call.17 = f32[1,64,64]{1,2,0:T(8,128)S(1)} custom-call(f32[1,64,64]{2,1,0:T(8,128)S(1)} %fusion.38), custom_call_target="InvertDiagBlocksLowerTriangular" | custom-call | tf_op jit(solution)/shard_map/triangular_solve | solution.py:20
  150.4 0.8 gather_fusion.2
  151.2 0.6 reduce_sum.48
  152.6 5.9 %cholesky.70 = f32[64,64]{1,0:T(8,128)S(1)} custom-call(f32[64,64]{1,0:T(8,128)S(1)} %copy.47), custom_call_target="Cholesky" | custom-call | tf_op jit(solution)/shard_map/jit(cholesky)/cholesky | solution.py:18
  158.5 0.6 compare_reduce_fusion.1
  159.2 0.7 fusion.39
  159.8 4.9 %custom-call.18 = f32[1,64,64]{1,2,0:T(8,128)S(1)} custom-call(f32[1,64,64]{2,1,0:T(8,128)S(1)} %fusion.39), custom_call_target="InvertDiagBlocksLowerTriangular" | custom-call | tf_op jit(solution)/shard_map/triangular_solve | solution.py:20
  164.7 0.6 fusion.83
  165.7 1.1 fusion.21
  166.8 30.6 %all-gather.2.cloned.1.call-done = bf16[32,2,64,128]{3,2,1,0:T(8,128)(2,1)} async-done(((bf16[4,2,64,128]{3,2,1,0:T(8,128)(2,1)}), bf16[32,2,64,128]{3,2,1,0:T(8,128)(2,1)}) %all-gather.2.cloned.1.call-update) | async-done | bytes 1048592 | tf_op jit(solution)/shard_map/all_gather | solution.py:96
  197.4 1.8 gather_fusion.4
  199.3 1.8 fusion.2
  201.3 3.6 while.25
  201.3 3.5 scatter_fusion.1
  204.9 1.6 copy.83
  206.5 0.7 copy.51
  207.4 70.3 %psum.38 = f32[64,64]{1,0:T(8,128)S(1)} all-reduce(f32[64,64]{1,0:T(8,128)S(1)} %fusion.84), channel_id=1, replica_groups=mesh['pat'=16,'code'=8] {'pat','code'}, use_global_device_ids=true, to_apply=%region_13.15 | all-reduce | flops 4096 | bytes 32768 | tf_op jit(solution)/shard_map/psum | solution.py:95
  277.7 0.8 gather_fusion.3
  278.5 0.6 reduce_sum.49
  279.9 5.9 %cholesky.81 = f32[64,64]{1,0:T(8,128)S(1)} custom-call(f32[64,64]{1,0:T(8,128)S(1)} %copy.49), custom_call_target="Cholesky" | custom-call | tf_op jit(solution)/shard_map/jit(cholesky)/cholesky | solution.py:18
  285.8 0.7 compare_reduce_fusion
  286.5 0.6 fusion.40
  287.1 4.9 %custom-call.19 = f32[1,64,64]{1,2,0:T(8,128)S(1)} custom-call(f32[1,64,64]{2,1,0:T(8,128)S(1)} %fusion.40), custom_call_target="InvertDiagBlocksLowerTriangular" | custom-call | tf_op jit(solution)/shard_map/triangular_solve | solution.py:20
  292.0 64.7 %all-reduce.3.cloned.1.call-done = f32[64,8192]{1,0:T(8,128)} async-done(((f32[64,8192]{1,0:T(8,128)}), f32[64,8192]{1,0:T(8,128)}) %all-reduce.3.cloned.1.call-update) | async-done | bytes 2097168 | tf_op jit(solution)/shard_map/psum | solution.py:110
  356.7 3.5 fusion.44
  360.1 3.3 convolution_maximum_fusion
  (72 shorter events, 9.8 us)
Async XLA Ops:
  7.2 50.5 %copy-start = (f32[64,64]{1,0:T(8,128)S(1)}, f32[64,64]{1,0:T(8,128)}, u32[]{:S(2)}) copy-start(f32[64,64]{1,0:T(8,128)} %param.17) | copy-start | bytes 49156
  7.2 50.4 %reduce-scatter.2.cloned.1.call-start = ((), (), s32[]{:S(2)}) async-start(), calls=%async_computation.1 | async-start | bytes 2359296 | tf_op jit(solution)/shard_map/reduce_scatter | solution.py:77
  10.6 1.8 copy-start.5
  17.4 1.3 copy-start.1
  18.7 178.7 %all-gather.2.cloned.1.call-start = ((), (), s32[]{:S(2)}) async-start(), calls=%async_computation.2 | async-start | bytes 1179648 | tf_op jit(solution)/shard_map/all_gather | solution.py:96
  63.1 2.3 copy-start.3
  65.9 133.4 %copy-start.2 = (bf16[1,1,16,128,512]{4,3,2,1,0:T(8,128)(2,1)S(1)}, bf16[1,1,16,128,512]{4,3,2,1,0:T(8,128)(2,1)}, u32[]{:S(2)}) copy-start(bf16[1,1,16,128,512]{4,3,2,1,0:T(8,128)(2,1)} %param.12) | copy-start | bytes 6291460
  165.7 41.5 %copy-start.4 = (f32[4,64]{1,0:T(4,128)}, f32[4,64]{1,0:T(4,128)S(1)}, u32[]{:S(2)}) copy-start(f32[4,64]{1,0:T(4,128)S(1)} %convolution_maximum_fusion.1) | copy-start | bytes 3076
  166.7 189.9 %all-reduce.3.cloned.1.call-start = ((), (), s32[]{:S(2)}) async-start(), calls=%async_computation.3 | async-start | bytes 4194304 | tf_op jit(solution)/shard_map/psum | solution.py:110
Sparse Core Ops, SparseCore 0:
  18.9 38.7 reduce-scatter.1
  166.9 30.5 all-gather.1
  206.6 150.0 all-reduce.2
where the time goes:
time: 371 us; the launch traced here: 370 us
  blocking collectives  165 us (44%)
  waiting for transfers between devices  103 us (28%)
  other arithmetic  47 us (13%)
  matrix products  26 us (7%)
  between operations  16.8 us (5%)
  local copies, waits for them, and re-layouts  11.7 us (3%)
    psum x1, blocking collectives, body(): weight_gram_new = lax.psum(new_partial, ('pat', 'code'))  70.3 us
    psum x1, blocking collectives, body(): lax.psum((numer_partial, weight_partial), ('pat', 'code'))  69.4 us
    psum x1, waiting for transfers between devices, body(): numer_sums = lax.psum(numer_local, 'pat')  64.7 us
    all_gather x1, waiting for transfers between devices, body(): spread_all = lax.all_gather(spread, 'code', axis=0, tiled=True)  30.6 us
    psum x1, blocking collectives, body(): code_gram = lax.psum(gram_partial, 'code')  25.5 us
    another operation x9, other arithmetic, damped_solve(): lower_factor = jnp.linalg.cholesky(shifted)  19.6 us
    another operation x6, other arithmetic, damped_solve(): lax.linalg.triangular_solve(lower_factor, halfway, left_side=True, lower=...  16.6 us
    reduce_scatter x1, waiting for transfers between devices, body(): lax.psum_scatter(code_partial, 'code', scatter_dimension=0, tiled=True)  7.7 us
  transfers between devices with their start and end apart: 3, of which 3 were waited for; matrix products, arithmetic and copies ran while one was open for 5% of the time, Pallas kernels for 0%

commit v1 on v0

v1 whole, which is shorter than its diff:
```python
import jax
import jax.numpy as jnp
from jax import lax
from jax.experimental import pallas as pl
from jax.experimental.pallas import tpu as pltpu
from jax.sharding import PartitionSpec as P

VBLOCKS = 2
NS_STEPS = 8
damping = 0.1
epsilon = 1e-06
F32, BF16, F16 = jnp.float32, jnp.bfloat16, jnp.float16
VM = pl.BlockSpec(memory_space=pltpu.VMEM)
SM = pl.BlockSpec(memory_space=pltpu.SMEM)
PARAMS = pltpu.CompilerParams(vmem_limit_bytes=48 * 1024 * 1024)


def mm(a, b, dims=((1,), (0,))):
    return lax.dot_general(
        a, b, (dims, ((), ())), precision=lax.Precision.HIGHEST, preferred_element_type=F32
    )


def mm16(a, b, dims=((1,), (0,))):
    return lax.dot_general(a, b, (dims, ((), ())), preferred_element_type=F32)


NT = ((1,), (1,))
TN = ((0,), (0,))


def split(x):
    high = x.astype(BF16)
    return high, (x - high.astype(F32)).astype(BF16)


def fold(x):
    half = x.shape[1] // 2
    return x[:, :half] + x[:, half:]


def damped_inverse(gram):
    size = gram.shape[0]
    eye = lax.broadcasted_iota(jnp.int32, (size, size), 0) == lax.broadcasted_iota(
        jnp.int32, (size, size), 1
    )
    mean = jnp.sum(jnp.where(eye, gram, 0.0), keepdims=True) / size
    work = jnp.concatenate(
        [gram + jnp.where(eye, damping * mean, 0.0), eye.astype(F32)], axis=1
    )
    row_at = lax.broadcasted_iota(jnp.int32, work.shape, 0)
    for j in range(size):
        row = work[j : j + 1, :]
        row = row / row[:, j : j + 1]
        work = jnp.where(row_at == j, row, work - work[:, j : j + 1] * row)
    return work[:, size:]


def live_rows(t, list_ref, count_ref, visits_ref, tile_rows):
    k, b, g = list_ref[0, t], list_ref[1, t], list_ref[2, t]
    kept = jnp.where(t < count_ref[0, 0], visits_ref[k] - tile_rows * b, 0)
    return k, b, g, kept


def products_kernel(list_ref, count_ref, visits_ref, tile_ref, code_ref, out_ref):
    slots, rows, cols = tile_ref.shape
    rank = code_ref.shape[0]
    out_ref[...] = jnp.zeros(out_ref.shape, F32)
    lane = lax.broadcasted_iota(jnp.int32, (rank, rows), 1)
    for t in range(slots):
        k, b, g, kept = live_rows(t, list_ref, count_ref, visits_ref, rows)
        codes = code_ref[:, pl.ds(pl.multiple_of(g * cols, cols), cols)].astype(BF16)
        part = mm16(codes, tile_ref[t], NT)
        out_ref[k * VBLOCKS + b] += jnp.where(lane < kept, part, 0.0)


def gram_kernel(code_ref, out_ref):
    high, low = split(code_ref[...])
    cross = mm16(high, low, NT)
    high, low = split(mm16(high, high, NT) + cross + cross.T)
    out_ref[...] = jnp.concatenate([high, low], axis=1)


def polar_kernel(at_ref, prod_ref, mix_ref, weight_ref, gram_ref, out_ref):
    dests = out_ref.shape[0]
    segs, rank, rows = prod_ref.shape
    own = segs // VBLOCKS
    prods = [
        jnp.concatenate([prod_ref[VBLOCKS * j + b] for b in range(VBLOCKS)], axis=1)
        for j in range(own)
    ]
    zs = []
    for j in range(own):
        weight = weight_ref[pl.ds(at_ref[0] * own + j, 1), :]
        target = mm(mix_ref[...] * weight, prods[j])
        zs.append(target / jnp.sqrt(jnp.sum(target * target, keepdims=True) + epsilon))
    for _ in range(NS_STEPS):
        grams = [mm(z, z, NT) for z in zs]
        zs = [1.5 * z - 0.5 * mm(g, z) for g, z in zip(grams, zs)]
    pieces = []
    for z in zs:
        z = z.astype(BF16)
        pieces += [z[:, b * rows : (b + 1) * rows] for b in range(VBLOCKS)]
    for z, p in zip(zs, prods):
        pieces.append(jnp.concatenate(split(mm(z, p, NT)), axis=1))
    pieces.append(gram_ref[...])
    for d in range(dests):
        for i, piece in enumerate(pieces):
            out_ref[d, i * rank : (i + 1) * rank, :] = piece


def numer_kernel(got_ref, weight_ref, out_ref):
    sources = got_ref.shape[0]
    rank = out_ref.shape[0]
    own = weight_ref.shape[0] // sources
    first = own * VBLOCKS * rank
    weight = weight_ref[...]
    twice = jnp.concatenate([weight, weight], axis=1)
    total = jnp.zeros(out_ref.shape, F32)
    for d in range(sources):
        for j in range(own):
            at = first + j * rank
            k = d * own + j
            total += got_ref[d, at : at + rank, :].astype(F32) * twice[k : k + 1, :]
    out_ref[...] = jnp.concatenate([fold(total), mm(weight, weight, TN)], axis=1)


def update_kernel(
    place_ref, list_ref, count_ref, visits_ref, sum_a, sum_b, got_ref, tile_ref,
    keep_ref, send_ref, wgram_ref, mix_ref, mgram_ref, own_ref, acc_ref, all_ref,
):
    sources = got_ref.shape[0]
    slots, rows, cols = tile_ref.shape
    rank = mix_ref.shape[0]
    patients = all_ref.shape[0]
    own = patients // sources
    first = own * VBLOCKS * rank
    last = first + own * rank
    sums = sum_a[...] + sum_b[...]
    code_gram = got_ref[0, last : last + rank, :].astype(F32)
    for d in range(1, sources):
        code_gram += got_ref[d, last : last + rank, :].astype(F32)
    code_gram = fold(code_gram)
    mix = mm(sums[:, :rank], damped_inverse(code_gram * sums[:, rank:]))
    mix_ref[...] = mix
    mix_gram = mm(mix, mix, TN)
    mgram_ref[...] = mix_gram
    inverse = damped_inverse(mix_gram * code_gram)
    twice = jnp.concatenate([mix, mix], axis=1)
    terms = []
    for d in range(sources):
        for j in range(own):
            at = first + j * rank
            terms.append(
                jnp.sum(got_ref[d, at : at + rank, :].astype(F32) * twice, axis=0, keepdims=True)
            )
    weight = jnp.maximum(mm(fold(jnp.concatenate(terms, axis=0)), inverse), 0.0)
    all_ref[...] = weight
    for j in range(own):
        own_ref[j : j + 1, :] = all_ref[pl.ds(place_ref[0] * own + j, 1), :]
    gram = mm(weight, weight, TN)
    wgram_ref[...] = jnp.concatenate([gram, jnp.zeros_like(gram)], axis=1)
    acc_ref[...] = jnp.zeros(acc_ref.shape, F32)
    lane = lax.broadcasted_iota(jnp.int32, (rank, rows), 1)
    for t in range(slots):
        k, b, g, kept = live_rows(t, list_ref, count_ref, visits_ref, rows)
        high, low = split(mix * all_ref[pl.ds(k, 1), :])
        at = pl.multiple_of((lax.rem(k, own) * VBLOCKS + b) * rank, rank)
        polar = got_ref[lax.div(k, own), pl.ds(at, rank), :]
        spread = mm16(high, polar, TN) + mm16(low, polar, TN)
        spread = jnp.where(lane < kept, spread, 0.0).astype(BF16)
        acc_ref[g] += mm16(spread, tile_ref[t])
    parity = place_ref[1]
    for j in range(keep_ref.shape[0]):
        keep_ref[j] = acc_ref[2 * j + parity]
        send_ref[j] = acc_ref[2 * j + 1 - parity]


def pair_kernel(keep_ref, came_ref, gram_a, gram_b, out_ref):
    lanes = gram_a.shape[1]
    slabs = keep_ref.shape[2] // lanes
    rank = gram_a.shape[0]
    high, low = split(gram_a[...] + gram_b[...])
    piece = jnp.concatenate([high[:, :rank], low[:, :rank]], axis=1)
    for j in range(keep_ref.shape[0]):
        both = (keep_ref[j] + came_ref[j]).astype(BF16)
        for i in range(slabs):
            out_ref[j, i] = both[:, i * lanes : (i + 1) * lanes]
        out_ref[j, slabs] = piece


def factor_kernel(got_ref, mgram_ref, out_ref):
    sources, slabs = got_ref.shape[0], got_ref.shape[1] - 1
    sums = []
    for i in range(slabs + 1):
        total = got_ref[0, i].astype(F32)
        for d in range(1, sources):
            total += got_ref[d, i].astype(F32)
        sums.append(total)
    inverse = damped_inverse(mgram_ref[...] * fold(sums[slabs]))
    code = jnp.maximum(mm(inverse, jnp.concatenate(sums[:slabs], axis=1)), 0.0).astype(BF16)
    for d in range(sources):
        out_ref[d] = code


def place_kernel(place_ref, mine_ref, came_ref, out_ref):
    parity = place_ref[1]
    cols = mine_ref.shape[2]
    for j in range(mine_ref.shape[0]):
        at = pl.multiple_of((2 * j + parity) * cols, cols)
        out_ref[:, pl.ds(at, cols)] = mine_ref[j].astype(F32)
        at = pl.multiple_of((2 * j + 1 - parity) * cols, cols)
        out_ref[:, pl.ds(at, cols)] = came_ref[j].astype(F32)


def call(kernel, outs, specs, args, scratch=()):
    many = isinstance(outs, tuple)
    return pl.pallas_call(
        kernel,
        out_shape=outs,
        in_specs=specs,
        out_specs=(VM,) * len(outs) if many else VM,
        scratch_shapes=scratch,
        compiler_params=PARAMS,
    )(*args)


def body(tile_data, tile_list, tile_count, visit_counts, code_factor_t, visit_mix, patient_weight):
    tiles = tile_data[0, 0]
    listing = tile_list[0, 0]
    slots, rows, cols = tiles.shape
    rank = visit_mix.shape[0]
    patients = visit_counts.shape[0]
    n_code, n_pat = lax.axis_size("code"), lax.axis_size("pat")
    half = n_pat // 2
    own = patients // n_code
    code_at, pat_at = lax.axis_index("code"), lax.axis_index("pat")
    place = jnp.stack([code_at, lax.rem(pat_at, 2)]).astype(jnp.int32)
    shape = jax.ShapeDtypeStruct

    partial = call(
        products_kernel, shape((patients * VBLOCKS, rank, rows), F32),
        [SM, SM, SM, VM, VM], (listing, tile_count, visit_counts, tiles, code_factor_t),
    )
    sent = partial.astype(F16).reshape(n_code, own * VBLOCKS * rank, rows)
    got = lax.all_to_all(sent, "code", 0, 0, tiled=True)
    gram = call(gram_kernel, shape((rank, 2 * rank), BF16), [VM], (code_factor_t,))
    products = jnp.sum(got.astype(F32), axis=0).reshape(own * VBLOCKS, rank, rows)

    length = (own * VBLOCKS + own + 1) * rank
    message = call(
        polar_kernel, shape((n_code, length, rows), BF16),
        [SM, VM, VM, VM, VM], (place, products, visit_mix, patient_weight, gram),
    )
    shared = lax.all_to_all(message, "code", 0, 0, tiled=True)
    sums = call(numer_kernel, shape((rank, 2 * rank), F32), [VM, VM], (shared, patient_weight))

    def swap(x, bit):
        return lax.ppermute(x, "pat", [(i, i ^ bit) for i in range(n_pat)])

    around = [swap(sums, bit) for bit in (2, 4, 6)]
    sums = sums + around[0] + around[1] + around[2]
    sums = sums + swap(sums, 8)
    other = swap(sums, 1)
    keep, send, wgram, mix_new, mix_gram, weight_new = call(
        update_kernel,
        (
            shape((half, rank, cols), F32), shape((half, rank, cols), F32),
            shape((rank, 2 * rank), F32), shape((rank, rank), F32),
            shape((rank, rank), F32), shape((own, rank), F32),
        ),
        [SM, SM, SM, SM, VM, VM, VM, VM],
        (place, listing, tile_count, visit_counts, sums, other, shared, tiles),
        [pltpu.VMEM((n_pat, rank, cols), F32), pltpu.VMEM((patients, rank), F32)],
    )
    came, wgram_came = swap(send, 1), swap(wgram, 1)
    lanes = 2 * rank
    packed = call(
        pair_kernel, shape((half, cols // lanes + 1, rank, lanes), BF16),
        [VM] * 4, (keep, came, wgram, wgram_came),
    )
    groups = [[core + 2 * i for i in range(half)] for core in (0, 1)]

    def exchange(x):
        return lax.all_to_all(x, "pat", 0, 0, axis_index_groups=groups, tiled=True)

    code = call(
        factor_kernel, shape((half, rank, cols), BF16), [VM, VM], (exchange(packed), mix_gram)
    )
    mine = exchange(code)
    code_new = call(
        place_kernel, shape((rank, n_pat * cols), F32), [SM, VM, VM], (place, mine, swap(mine, 1))
    )
    return (code_new, mix_new, weight_new)


def solution(mesh):
    placed = (
        P("pat", "code", None, None, None),
        P("pat", "code", None, None),
        P("pat", "code"),
        P("pat"),
        P(None, "code"),
        P(),
        P("pat", None),
    )
    return jax.shard_map(
        body,
        mesh=mesh,
        in_specs=placed,
        out_specs=(P(None, "code"), P(), P(("pat", "code"), None)),
        check_vma=False,
    )
```

time: 371 us -> 139 us (0.37)
  blocking collectives: 165 us -> 56.8 us
  waiting for transfers between devices: 103 us -> 22.2 us
  other arithmetic: 47 us -> 1.46 us
  Pallas kernels: 0 us -> 32.9 us
  matrix products: 26 us -> 0 us
  starting transfers between devices: 0.12 us -> 19.8 us
  between operations: 16.8 us -> 1.37 us
  local copies, waits for them, and re-layouts: 11.7 us -> 2.95 us
    psum x3 -> x0, blocking collectives: 165 us -> none  [the longest x1 70.3 us: body(): weight_gram_new = lax.psum(new_partial, ('pat', 'code'))]
    psum x1 -> x0, waiting for transfers between devices: 64.7 us -> none  [body(): numer_sums = lax.psum(numer_local, 'pat')]
    all_to_all x0 -> x3, blocking collectives: none -> 56.8 us  [the longest x2 31.2 us: exchange(): return lax.all_to_all(x, 'pat', 0, 0, axis_index_groups=groups, tiled=True)]
    another operation x15 -> x1, other arithmetic: 36.2 us -> 0.07 us  [body(): place = jnp.stack([code_at, lax.rem(pat_at, 2)]).astype(jnp.int32)]
    pallas_call x0 -> x8, Pallas kernels: none -> 32.9 us  [call(): pl.pallas_call(kernel, out_shape=outs, in_specs=specs, out_specs=(VM,) *...]
    all_gather x1 -> x0, waiting for transfers between devices: 30.6 us -> none  [body(): spread_all = lax.all_gather(spread, 'code', axis=0, tiled=True)]
    dot_general x26 -> x0, matrix products: 18.5 us -> none  [the longest x1 4.03 us: body(): gram_partial = jnp.dot(code_factor_t, code_factor_t.T, precision=highest)]
    ppermute x0 -> x8, starting transfers between devices: none -> 14.2 us  [swap(): return lax.ppermute(x, 'pat', [(i, i ^ bit) for i in range(n_pat)])]
  transfers between devices with their start and end apart: 3 -> 9, of which waited for: 3 -> 7; matrix products, arithmetic and copies ran while one was open for 5% -> 0% of each run, Pallas kernels for 0% -> 1%
where the time goes in v1:
time: 139 us; the launch traced here: 137 us
  blocking collectives  56.8 us (41%)
  Pallas kernels  32.9 us (24%)
  waiting for transfers between devices  22.2 us (16%)
  starting transfers between devices  19.8 us (14%)
  local copies, waits for them, and re-layouts  2.95 us (2%)
  other arithmetic  1.46 us (1%)
    pallas_call x8, Pallas kernels, call(): pl.pallas_call(kernel, out_shape=outs, in_specs=specs, out_specs=(VM,) *...  32.9 us
    all_to_all x2, blocking collectives, exchange(): return lax.all_to_all(x, 'pat', 0, 0, axis_index_groups=groups, tiled=True)  31.2 us
    all_to_all x1, blocking collectives, body(): shared = lax.all_to_all(message, 'code', 0, 0, tiled=True)  25.6 us
    ppermute x8, starting transfers between devices, swap(): return lax.ppermute(x, 'pat', [(i, i ^ bit) for i in range(n_pat)])  14.2 us
    all_to_all x1, waiting for transfers between devices, body(): got = lax.all_to_all(sent, 'code', 0, 0, tiled=True)  12.7 us
    ppermute x8, waiting for transfers between devices, swap(): return lax.ppermute(x, 'pat', [(i, i ^ bit) for i in range(n_pat)])  9.5 us
    all_to_all x1, starting transfers between devices, body(): got = lax.all_to_all(sent, 'code', 0, 0, tiled=True)  5.62 us
    unnamed x15, local copies, waits for them, and re-layouts  2.95 us
  transfers between devices with their start and end apart: 9, of which 7 were waited for; matrix products, arithmetic and copies ran while one was open for 0% of the time, Pallas kernels for 1%

profile of v1, /device:TPU:3, one launch (start us, length us, event | category | flops | bytes accessed | tf_op | source)
XLA Modules:
  0.0 137.4 jit_solution(6854970218015404864)
XLA Ops:
  1.3 0.7 copy.12
  2.0 0.0 copy-start.1
  2.0 1.6 %copy-done.1 = bf16[1,1,16,128,512]{4,3,2,1,0:T(8,128)(2,1)S(1)} copy-done((bf16[1,1,16,128,512]{4,3,2,1,0:T(8,128)(2,1)S(1)}, bf16[1,1,16,128,512]{4,3,2,1,0:T(8,128)(2,1)}, u32[]{:S(2)}) %copy-start.1) | copy-done | bytes 2097176
  3.6 0.0 copy-start.5
  3.6 0.7 copy-done.5
  4.2 2.5 %shard_map.94 = f32[64,64,128]{2,1,0:T(8,128)S(1)} custom-call(s32[3,16]{1,0:T(4,128)S(1)} %bitcast.11, s32[1,1]{1,0:T(1,128)S(6)} %copy.13.count_ref, s32[32]{0:T(128)S(1)} %copy-done.5, bf16[16,128,512]{2,1,0:T(8,128)(2,1)S(1)} %bitcast.8, f32[64,8192]{1,0:T(8,128)} %code_ref.3), custom_call_target="tpu_custom_call" | custom-call | tf_op jit(solution)/shard_map/pallas_call | solution.py:218
  6.7 0.0 copy-start
  6.7 1.2 convert_element_type.6
  7.9 5.6 %all-to-all-start = ((f16[8,512,128]{2,1,0:T(8,128)(2,1)}), f16[8,512,128]{2,1,0:T(8,128)(2,1)S(1)}, u32[]{:S(2)}, u32[]{:S(2)}) async-start(f16[8,512,128]{2,1,0:T(8,128)(2,1)} %bitcast.3), calls=%async_computation | async-start | bytes 2097152 | tf_op jit(solution)/shard_map/all_to_all | solution.py:246
  13.5 0.0 copy-start.3
  13.5 0.0 copy-start.4
  13.5 0.0 copy-done
  13.5 0.8 shard_map.95.gram_ref
  14.4 0.1 pad_add_fusion.at_ref.place_ref
  14.5 12.7 %all-to-all-done = f16[8,512,128]{2,1,0:T(8,128)(2,1)S(1)} async-done(((f16[8,512,128]{2,1,0:T(8,128)(2,1)}), f16[8,512,128]{2,1,0:T(8,128)(2,1)S(1)}, u32[]{:S(2)}, u32[]{:S(2)}) %all-to-all-start) | async-done | bytes 1048608 | tf_op jit(solution)/shard_map/all_to_all | solution.py:246
  27.1 0.1 convert_reduce_fusion
  27.3 0.0 copy-done.3
  27.3 0.0 copy-done.4
  27.3 5.1 %shard_map.96 = bf16[8,832,128]{2,1,0:T(8,128)(2,1)S(1)} custom-call(s32[2]{0:T(128)S(1)} %pad_add_fusion.at_ref.place_ref, f32[8,64,128]{2,1,0:T(8,128)S(1)} %bitcast.10, f32[64,64]{1,0:T(8,128)S(1)} %copy-done.4, f32[32,64]{1,0:T(8,128)S(1)} %copy-done.3, bf16[64,128]{1,0:T(8,128)(2,1)S(1)} %shard_map.95.gram_ref), custom_call_target="tpu_custom_call" | custom-call | tf_op jit(solution)/shard_map/pallas_call | solution.py:218
  32.5 0.0 copy-start.2
  32.5 0.0 copy-start.6
  32.5 25.6 %all_to_all.20.got_ref = bf16[8,832,128]{2,1,0:T(8,128)(2,1)S(1)} all-to-all(bf16[8,832,128]{2,1,0:T(8,128)(2,1)S(1)} %shard_map.96), channel_id=1, replica_groups=mesh['pat'=16,'code'=8] {'code'}, dimensions={0} | all-to-all | bytes 3407872 | tf_op jit(solution)/shard_map/all_to_all | solution.py:255
  58.1 0.3 shard_map.97
  58.4 2.8 %collective-permute-start.2 = (f32[64,128]{1,0:T(8,128)S(1)}, f32[64,128]{1,0:T(8,128)S(1)}, u32[]{:S(2)}, u32[]{:S(2)}) collective-permute-start(f32[64,128]{1,0:T(8,128)S(1)} %shard_map.97), channel_id=1, source_target_pairs={{0,48},{8,56},{16,32},{24,40},{32,16},{40,24},{48,0},{56,8},{64,11... | collective-permute-start | bytes 98312 | tf_op jit(solution)/shard_map/ppermute | solution.py:259
  61.2 0.4 collective-permute-start.1
  61.6 0.3 collective-permute-start
  61.9 0.6 collective-permute-done.2
  62.5 3.0 %collective-permute-done.1 = f32[64,128]{1,0:T(8,128)S(1)} collective-permute-done((f32[64,128]{1,0:T(8,128)S(1)}, f32[64,128]{1,0:T(8,128)S(1)}, u32[]{:S(2)}, u32[]{:S(2)}) %collective-permute-start.1) | collective-permute-done | bytes 32800 | tf_op jit(solution)/shard_map/ppermute | solution.py:259
  65.5 0.0 collective-permute-done
  65.5 3.4 %collective-permute-start.3 = (f32[64,128]{1,0:T(8,128)S(1)}, f32[64,128]{1,0:T(8,128)S(1)}, u32[]{:S(2)}, u32[]{:S(2)}) collective-permute-start(f32[64,128]{1,0:T(8,128)S(1)} %add_add_fusion), channel_id=1, source_target_pairs={{0,64},{8,72},{16,80},{24,88},{32,96},{40,104},{48,112},{56,120},{... | collective-permute-start | bytes 98312 | tf_op jit(solution)/shard_map/ppermute | solution.py:259
  68.9 1.3 collective-permute-done.3
  70.2 4.5 %collective-permute-start.4 = (f32[64,128]{1,0:T(8,128)S(1)}, f32[64,128]{1,0:T(8,128)S(1)}, u32[]{:S(2)}, u32[]{:S(2)}) collective-permute-start(f32[64,128]{1,0:T(8,128)S(1)} %add.15.sum_a), channel_id=1, source_target_pairs={{0,8},{8,0},{16,24},{24,16},{32,40},{40,32},{48,56},{56,48},{64,72... | collective-permute-start | bytes 98312 | tf_op jit(solution)/shard_map/ppermute | solution.py:259
  74.7 0.9 collective-permute-done.4.sum_b
  75.5 0.0 copy-done.2
  75.5 0.0 copy-done.6
  75.5 16.0 %shard_map.98 = (f32[8,64,512]{2,1,0:T(8,128)S(1)}, f32[8,64,512]{2,1,0:T(8,128)S(1)}, f32[64,128]{1,0:T(8,128)S(1)}, f32[64,64]{1,0:T(8,128)}, f32[64,64]{1,0:T(8,128)S(1)}, /*index=5*/f32[4,64]{1,0:T(4,128)}) custom-call(s32[2]{0:T(128)S(1)} %pad_add_fusion.at_ref.place_ref, s32[3,16]{1,0:T(4,128)S(1)} %bitcast.12, s32[1,1]{1,0:T(1,128)S(6)} %copy.13.count_ref, ...), custom_call_target="tpu_custom_call" | custom-call | tf_op jit(solution)/shard_map/pallas_call | solution.py:218
  91.5 0.3 collective-permute-start.5
  91.9 0.2 collective-permute-start.6
  92.0 2.2 %collective-permute-done.6.gram_b = f32[64,128]{1,0:T(8,128)S(1)} collective-permute-done((f32[64,128]{1,0:T(8,128)S(1)}, f32[64,128]{1,0:T(8,128)S(1)}, u32[]{:S(2)}, u32[]{:S(2)}) %collective-permute-start.6) | collective-permute-done | bytes 32800 | tf_op jit(solution)/shard_map/ppermute | solution.py:259
  94.2 0.0 collective-permute-done.5.came_ref
  94.2 0.1 shard_map.99
  94.4 18.6 %all_to_all.21.got_ref = bf16[8,5,64,128]{3,2,1,0:T(8,128)(2,1)S(1)} all-to-all(bf16[8,5,64,128]{3,2,1,0:T(8,128)(2,1)S(1)} %shard_map.99), channel_id=1, replica_groups={{0,16,32,48,64,80,96,112},{8,24,40,56,72,88,104,120},{1,17,33,49,65,81,..., dimensions={0} | all-to-all | bytes 1310720 | tf_op jit(solution)/shard_map/all_to_all | solution.py:285
  112.9 6.0 %shard_map.100 = bf16[8,64,512]{2,1,0:T(8,128)(2,1)S(1)} custom-call(bf16[8,5,64,128]{3,2,1,0:T(8,128)(2,1)S(1)} %all_to_all.21.got_ref, f32[64,64]{1,0:T(8,128)S(1)} %get-tuple-element.12.mgram_ref), custom_call_target="tpu_custom_call" | custom-call | tf_op jit(solution)/shard_map/pallas_call | solution.py:218
  118.9 12.6 %all_to_all.22.mine_ref = bf16[8,64,512]{2,1,0:T(8,128)(2,1)S(1)} all-to-all(bf16[8,64,512]{2,1,0:T(8,128)(2,1)S(1)} %shard_map.100), channel_id=1, replica_groups={{0,16,32,48,64,80,96,112},{8,24,40,56,72,88,104,120},{1,17,33,49,65,81,..., dimensions={0} | all-to-all | bytes 1048576 | tf_op jit(solution)/shard_map/all_to_all | solution.py:285
  131.6 2.3 %collective-permute-start.7 = (bf16[8,64,512]{2,1,0:T(8,128)(2,1)S(1)}, bf16[8,64,512]{2,1,0:T(8,128)(2,1)S(1)}, u32[]{:S(2)}, u32[]{:S(2)}) collective-permute-start(bf16[8,64,512]{2,1,0:T(8,128)(2,1)S(1)} %all_to_all.22.mine_ref), channel_id=1, source_target_pairs={{0,8},{8,0},{16,24},{24,16},{32,40},{40,32},{48,56},{56,48},{64,72... | collective-permute-start | bytes 1572872 | tf_op jit(solution)/shard_map/ppermute | solution.py:259
  133.9 1.5 %collective-permute-done.7.came_ref = bf16[8,64,512]{2,1,0:T(8,128)(2,1)S(1)} collective-permute-done((bf16[8,64,512]{2,1,0:T(8,128)(2,1)S(1)}, bf16[8,64,512]{2,1,0:T(8,128)(2,1)S(1)}, u32[]{:S(2)}, u32[]{:S(2)}) %collective-permute-start.7) | collective-permute-done | bytes 524320 | tf_op jit(solution)/shard_map/ppermute | solution.py:259
  135.4 2.0 %shard_map.101 = f32[64,8192]{1,0:T(8,128)} custom-call(s32[2]{0:T(128)S(1)} %pad_add_fusion.at_ref.place_ref, bf16[8,64,512]{2,1,0:T(8,128)(2,1)S(1)} %all_to_all.22.mine_ref, bf16[8,64,512]{2,1,0:T(8,128)(2,1)S(1)} %collective-permute-done.7.came_ref), custom_call_target="tpu_custom_call" | custom-call | tf_op jit(solution)/shard_map/pallas_call | solution.py:218
  (2 shorter events, 0.0 us)
Async XLA Ops:
  2.0 1.6 %copy-start.1 = (bf16[1,1,16,128,512]{4,3,2,1,0:T(8,128)(2,1)S(1)}, bf16[1,1,16,128,512]{4,3,2,1,0:T(8,128)(2,1)}, u32[]{:S(2)}) copy-start(bf16[1,1,16,128,512]{4,3,2,1,0:T(8,128)(2,1)} %param.7) | copy-start | bytes 6291460
  3.6 0.7 copy-start.5
  6.7 6.9 %copy-start = (f32[64,8192]{1,0:T(8,128)S(1)}, f32[64,8192]{1,0:T(8,128)}, u32[]{:S(2)}) copy-start(f32[64,8192]{1,0:T(8,128)} %code_ref.3) | copy-start | bytes 6291460
  7.9 19.2 %all-to-all-start = ((f16[8,512,128]{2,1,0:T(8,128)(2,1)}), f16[8,512,128]{2,1,0:T(8,128)(2,1)S(1)}, u32[]{:S(2)}, u32[]{:S(2)}) async-start(f16[8,512,128]{2,1,0:T(8,128)(2,1)} %bitcast.3), calls=%async_computation | async-start | bytes 2097152 | tf_op jit(solution)/shard_map/all_to_all | solution.py:246
  13.5 13.8 %copy-start.3 = (f32[32,64]{1,0:T(8,128)S(1)}, f32[32,64]{1,0:T(8,128)}, u32[]{:S(2)}) copy-start(f32[32,64]{1,0:T(8,128)} %weight_ref.3) | copy-start | bytes 24580
  13.5 13.8 %copy-start.4 = (f32[64,64]{1,0:T(8,128)S(1)}, f32[64,64]{1,0:T(8,128)}, u32[]{:S(2)}) copy-start(f32[64,64]{1,0:T(8,128)} %mix_ref.1) | copy-start | bytes 49156
  32.5 43.1 %copy-start.2 = (bf16[1,1,16,128,512]{4,3,2,1,0:T(8,128)(2,1)S(1)}, bf16[1,1,16,128,512]{4,3,2,1,0:T(8,128)(2,1)}, u32[]{:S(2)}) copy-start(bf16[1,1,16,128,512]{4,3,2,1,0:T(8,128)(2,1)} %param.7) | copy-start | bytes 6291460
  32.5 43.1 %copy-start.6 = (s32[32]{0:T(128)S(1)}, s32[32]{0:T(128)}, u32[]{:S(2)}) copy-start(s32[32]{0:T(128)} %visits_ref.3) | copy-start | bytes 388
  58.4 4.1 %collective-permute-start.2 = (f32[64,128]{1,0:T(8,128)S(1)}, f32[64,128]{1,0:T(8,128)S(1)}, u32[]{:S(2)}, u32[]{:S(2)}) collective-permute-start(f32[64,128]{1,0:T(8,128)S(1)} %shard_map.97), channel_id=1, source_target_pairs={{0,48},{8,56},{16,32},{24,40},{32,16},{40,24},{48,0},{56,8},{64,11... | collective-permute-start | bytes 98312 | tf_op jit(solution)/shard_map/ppermute | solution.py:259
  61.2 4.3 %collective-permute-start.1 = (f32[64,128]{1,0:T(8,128)S(1)}, f32[64,128]{1,0:T(8,128)S(1)}, u32[]{:S(2)}, u32[]{:S(2)}) collective-permute-start(f32[64,128]{1,0:T(8,128)S(1)} %shard_map.97), channel_id=1, source_target_pairs={{0,32},{8,40},{16,48},{24,56},{32,0},{40,8},{48,16},{56,24},{64,96... | collective-permute-start | bytes 98312 | tf_op jit(solution)/shard_map/ppermute | solution.py:259
  61.6 3.9 %collective-permute-start = (f32[64,128]{1,0:T(8,128)S(1)}, f32[64,128]{1,0:T(8,128)S(1)}, u32[]{:S(2)}, u32[]{:S(2)}) collective-permute-start(f32[64,128]{1,0:T(8,128)S(1)} %shard_map.97), channel_id=1, source_target_pairs={{0,16},{8,24},{16,0},{24,8},{32,48},{40,56},{48,32},{56,40},{64,80... | collective-permute-start | bytes 98312 | tf_op jit(solution)/shard_map/ppermute | solution.py:259
  65.5 4.7 %collective-permute-start.3 = (f32[64,128]{1,0:T(8,128)S(1)}, f32[64,128]{1,0:T(8,128)S(1)}, u32[]{:S(2)}, u32[]{:S(2)}) collective-permute-start(f32[64,128]{1,0:T(8,128)S(1)} %add_add_fusion), channel_id=1, source_target_pairs={{0,64},{8,72},{16,80},{24,88},{32,96},{40,104},{48,112},{56,120},{... | collective-permute-start | bytes 98312 | tf_op jit(solution)/shard_map/ppermute | solution.py:259
  70.2 5.3 %collective-permute-start.4 = (f32[64,128]{1,0:T(8,128)S(1)}, f32[64,128]{1,0:T(8,128)S(1)}, u32[]{:S(2)}, u32[]{:S(2)}) collective-permute-start(f32[64,128]{1,0:T(8,128)S(1)} %add.15.sum_a), channel_id=1, source_target_pairs={{0,8},{8,0},{16,24},{24,16},{32,40},{40,32},{48,56},{56,48},{64,72... | collective-permute-start | bytes 98312 | tf_op jit(solution)/shard_map/ppermute | solution.py:259
  91.5 2.7 %collective-permute-start.5 = (f32[8,64,512]{2,1,0:T(8,128)S(1)}, f32[8,64,512]{2,1,0:T(8,128)S(1)}, u32[]{:S(2)}, u32[]{:S(2)}) collective-permute-start(f32[8,64,512]{2,1,0:T(8,128)S(1)} %get-tuple-element.10), channel_id=1, source_target_pairs={{0,8},{8,0},{16,24},{24,16},{32,40},{40,32},{48,56},{56,48},{64,72... | collective-permute-start | bytes 3145736 | tf_op jit(solution)/shard_map/ppermute | solution.py:259
  91.9 2.4 %collective-permute-start.6 = (f32[64,128]{1,0:T(8,128)S(1)}, f32[64,128]{1,0:T(8,128)S(1)}, u32[]{:S(2)}, u32[]{:S(2)}) collective-permute-start(f32[64,128]{1,0:T(8,128)S(1)} %get-tuple-element.11.gram_a), channel_id=1, source_target_pairs={{0,8},{8,0},{16,24},{24,16},{32,40},{40,32},{48,56},{56,48},{64,72... | collective-permute-start | bytes 98312 | tf_op jit(solution)/shard_map/ppermute | solution.py:259
  131.6 3.9 %collective-permute-start.7 = (bf16[8,64,512]{2,1,0:T(8,128)(2,1)S(1)}, bf16[8,64,512]{2,1,0:T(8,128)(2,1)S(1)}, u32[]{:S(2)}, u32[]{:S(2)}) collective-permute-start(bf16[8,64,512]{2,1,0:T(8,128)(2,1)S(1)} %all_to_all.22.mine_ref), channel_id=1, source_target_pairs={{0,8},{8,0},{16,24},{24,16},{32,40},{40,32},{48,56},{56,48},{64,72... | collective-permute-start | bytes 1572872 | tf_op jit(solution)/shard_map/ppermute | solution.py:259

commit v2 on v1

v2 whole, which is shorter than its diff:
```python
import jax
import jax.numpy as jnp
from jax import lax
from jax.experimental import pallas as pl
from jax.experimental.pallas import tpu as pltpu
from jax.sharding import PartitionSpec as P

VBLOCKS = 2
NS_STEPS = 8
damping = 0.1
epsilon = 1e-06
F32, BF16, F16 = jnp.float32, jnp.bfloat16, jnp.float16
VM = pl.BlockSpec(memory_space=pltpu.VMEM)
SM = pl.BlockSpec(memory_space=pltpu.SMEM)
PARAMS = pltpu.CompilerParams(vmem_limit_bytes=48 * 1024 * 1024)


def mm(a, b, dims=((1,), (0,))):
    return lax.dot_general(
        a, b, (dims, ((), ())), precision=lax.Precision.HIGHEST, preferred_element_type=F32
    )


def mm16(a, b, dims=((1,), (0,))):
    return lax.dot_general(a, b, (dims, ((), ())), preferred_element_type=F32)


NT = ((1,), (1,))
TN = ((0,), (0,))


def split(x):
    high = x.astype(BF16)
    return high, (x - high.astype(F32)).astype(BF16)


def fold(x):
    half = x.shape[1] // 2
    return x[:, :half] + x[:, half:]


def times2(x, y):
    return [[x[i][0] * y[0][j] + x[i][1] * y[1][j] for j in (0, 1)] for i in (0, 1)]


def flip2(x):
    return [[x[0][0], x[1][0]], [x[0][1], x[1][1]]]


def inverse2(x):
    r = 1.0 / (x[0][0] * x[1][1] - x[0][1] * x[1][0])
    return [[x[1][1] * r, -x[0][1] * r], [-x[1][0] * r, x[0][0] * r]]


def inverse4(p):
    a = [[p[0][0], p[0][1]], [p[0][1], p[1][1]]]
    b = [[p[0][2], p[0][3]], [p[1][2], p[1][3]]]
    ai = inverse2(a)
    t = times2(ai, b)
    bt = times2(flip2(b), t)
    si = inverse2([[p[2][2] - bt[0][0], p[2][3] - bt[0][1]], [p[2][3] - bt[1][0], p[3][3] - bt[1][1]]])
    r = times2(t, si)
    u = times2(r, flip2(t))
    return [
        [ai[0][0] + u[0][0], ai[0][1] + u[0][1], -r[0][0], -r[0][1]],
        [ai[1][0] + u[1][0], ai[1][1] + u[1][1], -r[1][0], -r[1][1]],
        [-r[0][0], -r[1][0], si[0][0], si[0][1]],
        [-r[0][1], -r[1][1], si[1][0], si[1][1]],
    ]


def damped_inverse(gram):
    size = gram.shape[0]
    eye = lax.broadcasted_iota(jnp.int32, (size, size), 0) == lax.broadcasted_iota(
        jnp.int32, (size, size), 1
    )
    mean = jnp.sum(jnp.where(eye, gram, 0.0), keepdims=True) / size
    work = jnp.concatenate(
        [gram + jnp.where(eye, damping * mean, 0.0), eye.astype(F32)], axis=1
    )
    lanes = 2 * size
    blocks = [work[i : i + 8] for i in range(0, size, 8)]
    row_at = lax.broadcasted_iota(jnp.int32, (8, lanes), 0)
    for j in range(0, size, 4):
        owner, at = j // 8, j % 8
        rows = [blocks[owner][at + i : at + i + 1] for i in range(4)]
        pivot = [
            [jnp.broadcast_to(row[:, j + k : j + k + 1], (1, lanes)) for k in range(4)]
            for row in rows
        ]
        inverse = inverse4(pivot)
        fresh = []
        for i in range(4):
            total = inverse[i][0] * rows[0]
            for k in range(1, 4):
                total = total + inverse[i][k] * rows[k]
            fresh.append(total)
        after = []
        for m, block in enumerate(blocks):
            value = block
            for k in range(4):
                value = value - block[:, j + k : j + k + 1] * fresh[k]
            if m == owner:
                for k in range(4):
                    value = jnp.where(row_at == at + k, fresh[k], value)
            after.append(value)
        blocks = after
    return jnp.concatenate(blocks, axis=0)[:, size:]


def live_rows(t, list_ref, count_ref, visits_ref, tile_rows):
    k, b, g = list_ref[0, t], list_ref[1, t], list_ref[2, t]
    kept = jnp.where(t < count_ref[0, 0], visits_ref[k] - tile_rows * b, 0)
    return k, b, g, kept


def products_kernel(list_ref, count_ref, visits_ref, tile_ref, code_ref, out_ref):
    slots, rows, cols = tile_ref.shape
    rank = code_ref.shape[0]
    out_ref[...] = jnp.zeros(out_ref.shape, F32)
    lane = lax.broadcasted_iota(jnp.int32, (rank, rows), 1)
    for t in range(slots):
        k, b, g, kept = live_rows(t, list_ref, count_ref, visits_ref, rows)
        codes = code_ref[:, pl.ds(pl.multiple_of(g * cols, cols), cols)].astype(BF16)
        part = mm16(codes, tile_ref[t], NT)
        out_ref[k * VBLOCKS + b] += jnp.where(lane < kept, part, 0.0)


def gram_kernel(code_ref, weight_ref, code_gram_ref, weight_gram_ref):
    high, low = split(code_ref[...])
    cross = mm16(high, low, NT)
    code_gram_ref[...] = mm16(high, high, NT) + cross + cross.T
    weight = weight_ref[...]
    weight_gram_ref[...] = mm(weight, weight, TN)


def inverse_kernel(a_ref, b_ref, out_ref):
    out_ref[...] = damped_inverse(a_ref[...] * b_ref[...])


def polar_kernel(at_ref, prod_ref, mix_ref, weight_ref, numer_ref, out_ref):
    dests = out_ref.shape[0]
    segs, rank, rows = prod_ref.shape
    own = segs // VBLOCKS
    prods = [
        jnp.concatenate([prod_ref[VBLOCKS * j + b] for b in range(VBLOCKS)], axis=1)
        for j in range(own)
    ]
    weights = [weight_ref[pl.ds(at_ref[0] * own + j, 1), :] for j in range(own)]
    zs = []
    for j in range(own):
        target = mm(mix_ref[...] * weights[j], prods[j])
        zs.append(target / jnp.sqrt(jnp.sum(target * target, keepdims=True) + epsilon))
    for _ in range(NS_STEPS):
        grams = [mm(z, z, NT) for z in zs]
        zs = [1.5 * z - 0.5 * mm(g, z) for g, z in zip(grams, zs)]
    pieces = []
    for z in zs:
        z = z.astype(BF16)
        pieces += [z[:, b * rows : (b + 1) * rows] for b in range(VBLOCKS)]
    numer = jnp.zeros((rank, rank), F32)
    for z, p, weight in zip(zs, prods, weights):
        projected = mm(z, p, NT)
        numer += projected * weight
        pieces.append(jnp.concatenate(split(projected), axis=1))
    numer_ref[...] = jnp.concatenate([numer[: rank // 2], numer[rank // 2 :]], axis=1)
    for d in range(dests):
        for i, piece in enumerate(pieces):
            out_ref[d, i * rank : (i + 1) * rank, :] = piece


def mix_kernel(sum_a, sum_b, inverse_ref, code_gram_ref, mix_ref, mgram_ref, out_ref):
    sums = sum_a[...] + sum_b[...]
    rank = mix_ref.shape[0]
    numer = jnp.concatenate([sums[:, :rank], sums[:, rank:]], axis=0)
    mix = mm(numer, inverse_ref[...])
    mix_ref[...] = mix
    mix_gram = mm(mix, mix, TN)
    mgram_ref[...] = mix_gram
    out_ref[...] = damped_inverse(mix_gram * code_gram_ref[...])


def weight_kernel(place_ref, got_ref, mix_ref, inverse_ref, weight_ref, wgram_ref, own_ref):
    sources = got_ref.shape[0]
    rank = mix_ref.shape[0]
    own = own_ref.shape[0]
    first = own * VBLOCKS * rank
    mix = mix_ref[...]
    twice = jnp.concatenate([mix, mix], axis=1)
    terms = []
    for d in range(sources):
        for j in range(own):
            at = first + j * rank
            terms.append(
                jnp.sum(got_ref[d, at : at + rank, :].astype(F32) * twice, axis=0, keepdims=True)
            )
    weight = jnp.maximum(mm(fold(jnp.concatenate(terms, axis=0)), inverse_ref[...]), 0.0)
    weight_ref[...] = weight
    for j in range(own):
        own_ref[j : j + 1, :] = weight_ref[pl.ds(place_ref[0] * own + j, 1), :]
    wgram_ref[...] = mm(weight, weight, TN)


def numer_kernel(
    place_ref, list_ref, count_ref, visits_ref, got_ref, mix_ref, weight_ref, tile_ref,
    keep_ref, send_ref, acc_ref,
):
    slots, rows, cols = tile_ref.shape
    rank = mix_ref.shape[0]
    own = weight_ref.shape[0] // got_ref.shape[0]
    mix = mix_ref[...]
    acc_ref[...] = jnp.zeros(acc_ref.shape, F32)
    lane = lax.broadcasted_iota(jnp.int32, (rank, rows), 1)
    for t in range(slots):
        k, b, g, kept = live_rows(t, list_ref, count_ref, visits_ref, rows)
        high, low = split(mix * weight_ref[pl.ds(k, 1), :])
        at = pl.multiple_of((lax.rem(k, own) * VBLOCKS + b) * rank, rank)
        polar = got_ref[lax.div(k, own), pl.ds(at, rank), :]
        spread = mm16(high, polar, TN) + mm16(low, polar, TN)
        spread = jnp.where(lane < kept, spread, 0.0).astype(BF16)
        acc_ref[g] += mm16(spread, tile_ref[t])
    parity = place_ref[1]
    for j in range(keep_ref.shape[0]):
        keep_ref[j] = acc_ref[2 * j + parity]
        send_ref[j] = acc_ref[2 * j + 1 - parity]


def factor_kernel(got_ref, inverse_ref, out_ref):
    sources = got_ref.shape[0]
    total = got_ref[0].astype(F32)
    for d in range(1, sources):
        total += got_ref[d].astype(F32)
    code = jnp.maximum(mm(inverse_ref[...], total), 0.0).astype(BF16)
    for d in range(sources):
        out_ref[d] = code


def place_kernel(place_ref, mine_ref, came_ref, out_ref):
    parity = place_ref[1]
    cols = mine_ref.shape[2]
    for j in range(mine_ref.shape[0]):
        at = pl.multiple_of((2 * j + parity) * cols, cols)
        out_ref[:, pl.ds(at, cols)] = mine_ref[j].astype(F32)
        at = pl.multiple_of((2 * j + 1 - parity) * cols, cols)
        out_ref[:, pl.ds(at, cols)] = came_ref[j].astype(F32)


def call(kernel, outs, specs, args, scratch=(), flops=1e9):
    many = isinstance(outs, tuple)
    return pl.pallas_call(
        kernel,
        out_shape=outs,
        in_specs=specs,
        out_specs=(VM,) * len(outs) if many else VM,
        scratch_shapes=scratch,
        compiler_params=PARAMS,
        cost_estimate=pl.CostEstimate(flops=int(flops), bytes_accessed=65536, transcendentals=0),
    )(*args)


def swap(x, axis, bit):
    size = lax.axis_size(axis)
    return lax.ppermute(x, axis, [(i, i ^ bit) for i in range(size)])


def swap_z(x, high, low):
    n_pat, n_code = lax.axis_size("pat"), lax.axis_size("code")
    pairs = [
        (p * n_code + c, (p ^ (high * n_pat // 2)) * n_code + (c ^ (low * n_code // 2)))
        for p in range(n_pat)
        for c in range(n_code)
    ]
    return lax.ppermute(x, ("pat", "code"), pairs)


def plus(x, parts):
    for part in parts:
        x = x + part
    return x


def sum_pat(x):
    x = plus(x, [swap(x, "pat", bit) for bit in (2, 4, 6)])
    x = x + swap(x, "pat", 8)
    return x + swap(x, "pat", 1)


def body(tile_data, tile_list, tile_count, visit_counts, code_factor_t, visit_mix, patient_weight):
    tiles = tile_data[0, 0]
    listing = tile_list[0, 0]
    slots, rows, cols = tiles.shape
    rank = visit_mix.shape[0]
    patients = visit_counts.shape[0]
    n_code, n_pat = lax.axis_size("code"), lax.axis_size("pat")
    half = n_pat // 2
    own = patients // n_code
    code_at, pat_at = lax.axis_index("code"), lax.axis_index("pat")
    place = jnp.stack([code_at, lax.rem(pat_at, 2)]).astype(jnp.int32)
    shape = jax.ShapeDtypeStruct
    square = shape((rank, rank), F32)

    partial = call(
        products_kernel, shape((patients * VBLOCKS, rank, rows), F32),
        [SM, SM, SM, VM, VM], (listing, tile_count, visit_counts, tiles, code_factor_t),
    )
    sent = partial.astype(F16).reshape(n_code, own * VBLOCKS * rank, rows)
    got = lax.all_to_all(sent, "code", 0, 0, tiled=True)
    code_gram, weight_gram = call(
        gram_kernel, (square, square), [VM, VM], (code_factor_t, patient_weight)
    )
    code_gram = plus(code_gram, [swap(code_gram, "code", bit) for bit in (1, 2, 3)])
    code_gram = code_gram + swap(code_gram, "code", 4)
    inverse_mix = call(
        inverse_kernel, square, [VM, VM], (code_gram, sum_pat(weight_gram)), flops=4e9
    )
    products = jnp.sum(got.astype(F32), axis=0).reshape(own * VBLOCKS, rank, rows)

    length = (own * VBLOCKS + own) * rank
    sums, message = call(
        polar_kernel,
        (shape((rank // 2, 2 * rank), F32), shape((n_code, length, rows), BF16)),
        [SM, VM, VM, VM], (place, products, visit_mix, patient_weight), flops=5e9,
    )
    shared = lax.all_to_all(message, "code", 0, 0, tiled=True)
    sums = plus(sums, [swap(sums, "code", bit) for bit in (1, 2, 3)])
    sums = plus(sums, [swap_z(sums, high, low) for high, low in ((0, 1), (1, 0), (1, 1))])
    sums = plus(sums, [swap(sums, "pat", bit) for bit in (2, 4, 6)])
    mix_new, mix_gram, inverse_weight = call(
        mix_kernel, (square,) * 3, [VM] * 4,
        (sums, swap(sums, "pat", 1), inverse_mix, code_gram), flops=4e9,
    )
    weights, wgram, weight_new = call(
        weight_kernel, (shape((patients, rank), F32), square, shape((own, rank), F32)),
        [SM, VM, VM, VM], (place, shared, mix_new, inverse_weight),
    )
    block = shape((half, rank, cols), F32)
    keep, send = call(
        numer_kernel, (block, block), [SM, SM, SM, SM, VM, VM, VM, VM],
        (place, listing, tile_count, visit_counts, shared, mix_new, weights, tiles),
        [pltpu.VMEM((n_pat, rank, cols), F32)], flops=4e9,
    )
    groups = [[core + 2 * i for i in range(half)] for core in (0, 1)]

    def exchange(x):
        return lax.all_to_all(x, "pat", 0, 0, axis_index_groups=groups, tiled=True)

    summed = exchange((keep + swap(send, "pat", 1)).astype(BF16))
    inverse_code = call(inverse_kernel, square, [VM, VM], (mix_gram, sum_pat(wgram)), flops=4e9)
    code = call(
        factor_kernel, shape((half, rank, cols), BF16), [VM, VM], (summed, inverse_code)
    )
    mine = exchange(code)
    code_new = call(
        place_kernel, shape((rank, n_pat * cols), F32),
        [SM, VM, VM], (place, mine, swap(mine, "pat", 1)),
    )
    return (code_new, mix_new, weight_new)


def solution(mesh):
    placed = (
        P("pat", "code", None, None, None),
        P("pat", "code", None, None),
        P("pat", "code"),
        P("pat"),
        P(None, "code"),
        P(),
        P("pat", None),
    )
    return jax.shard_map(
        body,
        mesh=mesh,
        in_specs=placed,
        out_specs=(P(None, "code"), P(), P(("pat", "code"), None)),
        check_vma=False,
    )
```

time: 139 us -> 135 us (0.971)
  blocking collectives: 56.8 us -> 17.4 us
  starting transfers between devices: 19.8 us -> 54.4 us
  Pallas kernels: 32.9 us -> 27.3 us
  waiting for transfers between devices: 22.2 us -> 25.7 us
    all_to_all x1 -> x0, blocking collectives: 25.6 us -> none  [body(): shared = lax.all_to_all(message, 'code', 0, 0, tiled=True)]
    ppermute x8 -> x26, starting transfers between devices: 14.2 us -> 37.3 us  [the longest x23 34 us: swap(): return lax.ppermute(x, axis, [(i, i ^ bit) for i in range(size)])]
    all_to_all x2 -> x1, blocking collectives: 31.2 us -> 17.4 us  [exchange(): return lax.all_to_all(x, 'pat', 0, 0, axis_index_groups=groups, tiled=True)]
    all_to_all x0 -> x2, starting transfers between devices: none -> 11.4 us  [the longest x1 5.79 us: exchange(): return lax.all_to_all(x, 'pat', 0, 0, axis_index_groups=groups, tiled=True)]
    ppermute x8 -> x26, waiting for transfers between devices: 9.5 us -> 18.1 us  [the longest x23 18.1 us: swap(): return lax.ppermute(x, axis, [(i, i ^ bit) for i in range(size)])]
    pallas_call x8 -> x10, Pallas kernels: 32.9 us -> 27.3 us  [call(): pl.pallas_call(kernel, out_shape=outs, in_specs=specs, out_specs=(VM,) *...]
    all_to_all x1, waiting for transfers between devices: 12.7 us -> 7.58 us  [body(): got = lax.all_to_all(sent, 'code', 0, 0, tiled=True)]
    unnamed x15 -> x19, local copies, waits for them, and re-layouts: 2.95 us -> 3.86 us
  transfers between devices with their start and end apart: 9 -> 29, of which waited for: 7 -> 7; matrix products, arithmetic and copies ran while one was open for 0% -> 1% of each run, Pallas kernels for 1% -> 12%
where the time goes in v2:
time: 135 us; the launch traced here: 132 us
  starting transfers between devices  54.4 us (40%)
  Pallas kernels  27.3 us (20%)
  waiting for transfers between devices  25.7 us (19%)
  blocking collectives  17.4 us (13%)
  local copies, waits for them, and re-layouts  3.86 us (3%)
  other arithmetic  2.49 us (2%)
  between operations  1.47 us (1%)
    ppermute x23, starting transfers between devices, swap(): return lax.ppermute(x, axis, [(i, i ^ bit) for i in range(size)])  34 us
    pallas_call x10, Pallas kernels, call(): pl.pallas_call(kernel, out_shape=outs, in_specs=specs, out_specs=(VM,) *...  27.3 us
    ppermute x23, waiting for transfers between devices, swap(): return lax.ppermute(x, axis, [(i, i ^ bit) for i in range(size)])  18.1 us
    all_to_all x1, blocking collectives, exchange(): return lax.all_to_all(x, 'pat', 0, 0, axis_index_groups=groups, tiled=True)  17.4 us
    all_to_all x1, waiting for transfers between devices, body(): got = lax.all_to_all(sent, 'code', 0, 0, tiled=True)  7.58 us
    all_to_all x1, starting transfers between devices, exchange(): return lax.all_to_all(x, 'pat', 0, 0, axis_index_groups=groups, tiled=True)  5.79 us
    all_to_all x1, starting transfers between devices, body(): shared = lax.all_to_all(message, 'code', 0, 0, tiled=True)  5.64 us
    all_to_all x1, starting transfers between devices, body(): got = lax.all_to_all(sent, 'code', 0, 0, tiled=True)  5.62 us
  transfers between devices with their start and end apart: 29, of which 7 were waited for; matrix products, arithmetic and copies ran while one was open for 1% of the time, Pallas kernels for 12%

profile of v2, /device:TPU:3, one launch (start us, length us, event | category | flops | bytes accessed | tf_op | source)
XLA Modules:
  0.0 132.5 jit_solution(4326990268539002167)
XLA Ops:
  1.3 0.7 copy.12
  2.0 1.6 %copy-done.1 = bf16[1,1,16,128,512]{4,3,2,1,0:T(8,128)(2,1)S(1)} copy-done((bf16[1,1,16,128,512]{4,3,2,1,0:T(8,128)(2,1)S(1)}, bf16[1,1,16,128,512]{4,3,2,1,0:T(8,128)(2,1)}, u32[]{:S(2)}) %copy-start.1) | copy-done | bytes 2097176
  3.6 0.7 copy-done.3
  4.2 2.5 %shard_map.94 = f32[64,64,128]{2,1,0:T(8,128)S(1)} custom-call(s32[3,16]{1,0:T(4,128)S(1)} %bitcast.11, s32[1,1]{1,0:T(1,128)S(6)} %copy.13.count_ref, s32[32]{0:T(128)S(1)} %copy-done.3, bf16[16,128,512]{2,1,0:T(8,128)(2,1)S(1)} %bitcast.8, f32[64,8192]{1,0:T(8,128)} %code_ref.3), custom_call_target="tpu_custom_call" | custom-call | flops 1000000000 | bytes 65536 | tf_op jit(solution)/shard_map/pallas_call | solution.py:250
  6.7 1.2 convert_element_type.9
  7.9 5.6 %all-to-all-start = ((f16[8,512,128]{2,1,0:T(8,128)(2,1)}), f16[8,512,128]{2,1,0:T(8,128)(2,1)S(1)}, u32[]{:S(2)}, u32[]{:S(2)}) async-start(f16[8,512,128]{2,1,0:T(8,128)(2,1)} %bitcast.3), calls=%async_computation | async-start | bytes 2097152 | tf_op jit(solution)/shard_map/all_to_all | solution.py:307
  13.6 0.8 shard_map.96
  14.3 1.3 collective-permute-start.12
  15.6 0.7 collective-permute-start.11
  16.3 2.7 %collective-permute-start.16 = (f32[64,64]{1,0:T(8,128)S(1)}, f32[64,64]{1,0:T(8,128)S(1)}, u32[]{:S(2)}, u32[]{:S(2)}) collective-permute-start(f32[64,64]{1,0:T(8,128)S(1)} %get-tuple-element.18), channel_id=1, source_target_pairs={{0,48},{8,56},{16,32},{24,40},{32,16},{40,24},{48,0},{56,8},{64,11... | collective-permute-start | bytes 49160 | tf_op jit(solution)/shard_map/ppermute | solution.py:263
  19.0 0.4 collective-permute-start.15
  19.7 7.6 %all-to-all-done = f16[8,512,128]{2,1,0:T(8,128)(2,1)S(1)} async-done(((f16[8,512,128]{2,1,0:T(8,128)(2,1)}), f16[8,512,128]{2,1,0:T(8,128)(2,1)S(1)}, u32[]{:S(2)}, u32[]{:S(2)}) %all-to-all-start) | async-done | bytes 1048608 | tf_op jit(solution)/shard_map/all_to_all | solution.py:307
  27.4 6.3 %shard_map.95 = (f32[32,128]{1,0:T(8,128)S(1)}, bf16[8,768,128]{2,1,0:T(8,128)(2,1)}) custom-call(s32[2]{0:T(128)S(1)} %pad_add_fusion.at_ref.place_ref, f32[8,64,128]{2,1,0:T(8,128)S(1)} %bitcast.10, f32[64,64]{1,0:T(8,128)S(1)} %copy-done.5, f32[32,64]{1,0:T(8,128)S(1)} %copy-done.6), custom_call_target="tpu_custom_call" | custom-call | flops 5000000000 | bytes 65536 | tf_op jit(solution)/shard_map/pallas_call | solution.py:250
  33.7 1.3 collective-permute-start.2
  34.9 3.0 %collective-permute-start.1 = (f32[32,128]{1,0:T(8,128)S(1)}, f32[32,128]{1,0:T(8,128)S(1)}, u32[]{:S(2)}, u32[]{:S(2)}) collective-permute-start(f32[32,128]{1,0:T(8,128)S(1)} %get-tuple-element.16), channel_id=1, source_target_pairs={{0,2},{1,3},{2,0},{3,1},{4,6},{5,7},{6,4},{7,5},{8,10},{9,11},{10,... | collective-permute-start | bytes 49160 | tf_op jit(solution)/shard_map/ppermute | solution.py:263
  38.0 5.6 %all-to-all-start.1 = ((bf16[8,768,128]{2,1,0:T(8,128)(2,1)}), bf16[8,768,128]{2,1,0:T(8,128)(2,1)}, u32[]{:S(2)}, u32[]{:S(2)}) async-start(bf16[8,768,128]{2,1,0:T(8,128)(2,1)} %get-tuple-element.15), calls=%async_computation.1 | async-start | bytes 3145728 | tf_op jit(solution)/shard_map/all_to_all | solution.py:324
  43.8 3.3 %collective-permute-start.17 = (f32[64,64]{1,0:T(8,128)S(1)}, f32[64,64]{1,0:T(8,128)S(1)}, u32[]{:S(2)}, u32[]{:S(2)}) collective-permute-start(f32[64,64]{1,0:T(8,128)S(1)} %add_add_fusion.1), channel_id=1, source_target_pairs={{0,64},{8,72},{16,80},{24,88},{32,96},{40,104},{48,112},{56,120},{... | collective-permute-start | bytes 49160 | tf_op jit(solution)/shard_map/ppermute | solution.py:263
  47.1 0.4 collective-permute-start.5
  47.6 2.1 %collective-permute-start.4 = (f32[32,128]{1,0:T(8,128)S(1)}, f32[32,128]{1,0:T(8,128)S(1)}, u32[]{:S(2)}, u32[]{:S(2)}) collective-permute-start(f32[32,128]{1,0:T(8,128)S(1)} %add_add_fusion.5), channel_id=1, source_target_pairs={{0,64},{1,65},{2,66},{3,67},{4,68},{5,69},{6,70},{7,71},{8,72},{9,... | collective-permute-start | bytes 49160 | tf_op jit(solution)/shard_map/ppermute | solution.py:273
  49.7 0.8 collective-permute-start.3
  50.5 10.2 %collective-permute-done.10 = f32[64,64]{1,0:T(8,128)S(1)} collective-permute-done((f32[64,64]{1,0:T(8,128)S(1)}, f32[64,64]{1,0:T(8,128)S(1)}, u32[]{:S(2)}, u32[]{:S(2)}) %collective-permute-start.10) | collective-permute-done | bytes 16416 | tf_op jit(solution)/shard_map/ppermute | solution.py:263
  60.7 1.2 collective-permute-start.13
  61.9 3.2 %collective-permute-start.18 = (f32[64,64]{1,0:T(8,128)S(1)}, f32[64,64]{1,0:T(8,128)S(1)}, u32[]{:S(2)}, u32[]{:S(2)}) collective-permute-start(f32[64,64]{1,0:T(8,128)S(1)} %add.88), channel_id=1, source_target_pairs={{0,8},{8,0},{16,24},{24,16},{32,40},{40,32},{48,56},{56,48},{64,72... | collective-permute-start | bytes 49160 | tf_op jit(solution)/shard_map/ppermute | solution.py:263
  65.1 2.8 %collective-permute-start.8 = (f32[32,128]{1,0:T(8,128)S(1)}, f32[32,128]{1,0:T(8,128)S(1)}, u32[]{:S(2)}, u32[]{:S(2)}) collective-permute-start(f32[32,128]{1,0:T(8,128)S(1)} %add_add_fusion.4), channel_id=1, source_target_pairs={{0,48},{8,56},{16,32},{24,40},{32,16},{40,24},{48,0},{56,8},{64,11... | collective-permute-start | bytes 49160 | tf_op jit(solution)/shard_map/ppermute | solution.py:263
  67.9 0.4 collective-permute-start.7
  68.6 0.4 collective-permute-done.8
  69.0 3.0 %collective-permute-done.7 = f32[32,128]{1,0:T(8,128)S(1)} collective-permute-done((f32[32,128]{1,0:T(8,128)S(1)}, f32[32,128]{1,0:T(8,128)S(1)}, u32[]{:S(2)}, u32[]{:S(2)}) %collective-permute-start.7) | collective-permute-done | bytes 16416 | tf_op jit(solution)/shard_map/ppermute | solution.py:263
  72.0 1.7 %collective-permute-start.9 = (f32[32,128]{1,0:T(8,128)S(1)}, f32[32,128]{1,0:T(8,128)S(1)}, u32[]{:S(2)}, u32[]{:S(2)}) collective-permute-start(f32[32,128]{1,0:T(8,128)S(1)} %add_add_fusion.3.sum_a), channel_id=1, source_target_pairs={{0,8},{8,0},{16,24},{24,16},{32,40},{40,32},{48,56},{56,48},{64,72... | collective-permute-start | bytes 49160 | tf_op jit(solution)/shard_map/ppermute | solution.py:263
  73.7 2.8 %shard_map.97.inverse_ref = f32[64,64]{1,0:T(8,128)S(1)} custom-call(f32[64,64]{1,0:T(8,128)S(1)} %add.84.a_ref.code_gram_ref, f32[64,64]{1,0:T(8,128)S(1)} %add.89.b_ref), custom_call_target="tpu_custom_call" | custom-call | flops 4000000000 | bytes 65536 | tf_op jit(solution)/shard_map/pallas_call | solution.py:250
  76.5 3.2 %shard_map.98 = (f32[64,64]{1,0:T(8,128)}, f32[64,64]{1,0:T(8,128)S(1)}, f32[64,64]{1,0:T(8,128)S(1)}) custom-call(f32[32,128]{1,0:T(8,128)S(1)} %add_add_fusion.3.sum_a, f32[32,128]{1,0:T(8,128)S(1)} %collective-permute-done.9.sum_b, f32[64,64]{1,0:T(8,128)S(1)} %shard_map.97.inverse_ref, f32[64,64]{1,0:T(8,128)S(1)} %add.84.a_ref.code_gram_ref), custom_call_target="tpu_custom_call" | custom-call | flops 4000000000 | bytes 65536 | tf_op jit(solution)/shard_map/pallas_call | solution.py:250
  79.8 0.9 copy-done.7
  80.7 2.4 %shard_map.99 = (f32[32,64]{1,0:T(8,128)S(1)}, f32[64,64]{1,0:T(8,128)S(1)}, f32[4,64]{1,0:T(4,128)}) custom-call(s32[2]{0:T(128)S(1)} %pad_add_fusion.at_ref.place_ref, bf16[8,768,128]{2,1,0:T(8,128)(2,1)} %all-to-all-done.1.got_ref, f32[64,64]{1,0:T(8,128)S(1)} %copy-done.7, f32[64,64]{1,0:T(8,128)S(1)} %get-tuple-element.20.inverse_ref), custom_call_target="tpu_custom_call" | custom-call | flops 1000000000 | bytes 65536 | tf_op jit(solution)/shard_map/pallas_call | solution.py:250
  83.1 4.2 %shard_map.100 = (f32[8,64,512]{2,1,0:T(8,128)S(1)}, f32[8,64,512]{2,1,0:T(8,128)S(1)}) custom-call(s32[2]{0:T(128)S(1)} %pad_add_fusion.at_ref.place_ref, s32[3,16]{1,0:T(4,128)S(1)} %bitcast.12, s32[1,1]{1,0:T(1,128)S(6)} %copy.13.count_ref, s32[32]{0:T(128)S(1)} %copy-done.4, bf16[8,768,128]{2,1,0:T(8,128)(2,1)} %all-to-all-done.1.got_ref, ...), custom_call_target="tpu_custom_call" | custom-call | flops 4000000000 | bytes 65536 | tf_op jit(solution)/shard_map/pallas_call | solution.py:250
  87.4 0.8 collective-permute-start.22
  88.2 0.9 collective-permute-start.21
  89.1 1.6 %collective-permute-start.20 = (f32[64,64]{1,0:T(8,128)S(1)}, f32[64,64]{1,0:T(8,128)S(1)}, u32[]{:S(2)}, u32[]{:S(2)}) collective-permute-start(f32[64,64]{1,0:T(8,128)S(1)} %get-tuple-element.25), channel_id=1, source_target_pairs={{0,16},{8,24},{16,0},{24,8},{32,48},{40,56},{48,32},{56,40},{64,80... | collective-permute-start | bytes 49160 | tf_op jit(solution)/shard_map/ppermute | solution.py:263
  90.7 1.0 add_convert_fusion
  91.7 5.8 %all-to-all-start.2 = ((bf16[8,64,512]{2,1,0:T(8,128)(2,1)}), bf16[8,64,512]{2,1,0:T(8,128)(2,1)S(1)}, u32[]{:S(2)}, u32[]{:S(2)}) async-start(bf16[8,64,512]{2,1,0:T(8,128)(2,1)} %add_convert_fusion), calls=%async_computation.2 | async-start | bytes 1048576 | tf_op jit(solution)/shard_map/all_to_all | solution.py:345
  97.5 3.0 %collective-permute-start.23 = (f32[64,64]{1,0:T(8,128)S(1)}, f32[64,64]{1,0:T(8,128)S(1)}, u32[]{:S(2)}, u32[]{:S(2)}) collective-permute-start(f32[64,64]{1,0:T(8,128)S(1)} %add_add_fusion), channel_id=1, source_target_pairs={{0,64},{8,72},{16,80},{24,88},{32,96},{40,104},{48,112},{56,120},{... | collective-permute-start | bytes 49160 | tf_op jit(solution)/shard_map/ppermute | solution.py:263
  100.6 2.1 %collective-permute-done.23 = f32[64,64]{1,0:T(8,128)S(1)} collective-permute-done((f32[64,64]{1,0:T(8,128)S(1)}, f32[64,64]{1,0:T(8,128)S(1)}, u32[]{:S(2)}, u32[]{:S(2)}) %collective-permute-start.23) | collective-permute-done | bytes 16416 | tf_op jit(solution)/shard_map/ppermute | solution.py:263
  102.7 3.7 %collective-permute-start.24 = (f32[64,64]{1,0:T(8,128)S(1)}, f32[64,64]{1,0:T(8,128)S(1)}, u32[]{:S(2)}, u32[]{:S(2)}) collective-permute-start(f32[64,64]{1,0:T(8,128)S(1)} %add.94), channel_id=1, source_target_pairs={{0,8},{8,0},{16,24},{24,16},{32,40},{40,32},{48,56},{56,48},{64,72... | collective-permute-start | bytes 49160 | tf_op jit(solution)/shard_map/ppermute | solution.py:263
  106.4 0.9 collective-permute-done.24
  107.2 2.8 %shard_map.101.inverse_ref = f32[64,64]{1,0:T(8,128)S(1)} custom-call(f32[64,64]{1,0:T(8,128)S(1)} %get-tuple-element.24.a_ref, f32[64,64]{1,0:T(8,128)S(1)} %add.95.b_ref), custom_call_target="tpu_custom_call" | custom-call | flops 4000000000 | bytes 65536 | tf_op jit(solution)/shard_map/pallas_call | solution.py:250
  110.0 0.4 shard_map.102
  110.4 17.4 %all_to_all.20.mine_ref = bf16[8,64,512]{2,1,0:T(8,128)(2,1)S(1)} all-to-all(bf16[8,64,512]{2,1,0:T(8,128)(2,1)S(1)} %shard_map.102), channel_id=1, replica_groups={{0,16,32,48,64,80,96,112},{8,24,40,56,72,88,104,120},{1,17,33,49,65,81,..., dimensions={0} | all-to-all | bytes 1048576 | tf_op jit(solution)/shard_map/all_to_all | solution.py:345
  127.7 1.2 collective-permute-start.25
  128.9 1.5 %collective-permute-done.25.came_ref = bf16[8,64,512]{2,1,0:T(8,128)(2,1)S(1)} collective-permute-done((bf16[8,64,512]{2,1,0:T(8,128)(2,1)S(1)}, bf16[8,64,512]{2,1,0:T(8,128)(2,1)S(1)}, u32[]{:S(2)}, u32[]{:S(2)}) %collective-permute-start.25) | collective-permute-done | bytes 524320 | tf_op jit(solution)/shard_map/ppermute | solution.py:263
  130.5 2.0 %shard_map.103 = f32[64,8192]{1,0:T(8,128)} custom-call(s32[2]{0:T(128)S(1)} %pad_add_fusion.at_ref.place_ref, bf16[8,64,512]{2,1,0:T(8,128)(2,1)S(1)} %all_to_all.20.mine_ref, bf16[8,64,512]{2,1,0:T(8,128)(2,1)S(1)} %collective-permute-done.25.came_ref), custom_call_target="tpu_custom_call" | custom-call | flops 1000000000 | bytes 65536 | tf_op jit(solution)/shard_map/pallas_call | solution.py:250
  (55 shorter events, 1.2 us)
Async XLA Ops:
  2.0 1.6 %copy-start.1 = (bf16[1,1,16,128,512]{4,3,2,1,0:T(8,128)(2,1)S(1)}, bf16[1,1,16,128,512]{4,3,2,1,0:T(8,128)(2,1)}, u32[]{:S(2)}) copy-start(bf16[1,1,16,128,512]{4,3,2,1,0:T(8,128)(2,1)} %param.7) | copy-start | bytes 6291460
  3.6 0.7 copy-start.3
  6.7 6.9 %copy-start = (f32[64,8192]{1,0:T(8,128)S(1)}, f32[64,8192]{1,0:T(8,128)}, u32[]{:S(2)}) copy-start(f32[64,8192]{1,0:T(8,128)} %code_ref.3) | copy-start | bytes 6291460
  6.7 6.9 %copy-start.6 = (f32[32,64]{1,0:T(8,128)S(1)}, f32[32,64]{1,0:T(8,128)}, u32[]{:S(2)}) copy-start(f32[32,64]{1,0:T(8,128)} %weight_ref.3) | copy-start | bytes 24580
  7.9 19.3 %all-to-all-start = ((f16[8,512,128]{2,1,0:T(8,128)(2,1)}), f16[8,512,128]{2,1,0:T(8,128)(2,1)S(1)}, u32[]{:S(2)}, u32[]{:S(2)}) async-start(f16[8,512,128]{2,1,0:T(8,128)(2,1)} %bitcast.3), calls=%async_computation | async-start | bytes 2097152 | tf_op jit(solution)/shard_map/all_to_all | solution.py:307
  13.6 13.8 %copy-start.5 = (f32[64,64]{1,0:T(8,128)S(1)}, f32[64,64]{1,0:T(8,128)}, u32[]{:S(2)}) copy-start(f32[64,64]{1,0:T(8,128)} %mix_ref.1) | copy-start | bytes 49156
  14.3 33.3 %collective-permute-start.12 = (f32[64,64]{1,0:T(8,128)S(1)}, f32[64,64]{1,0:T(8,128)S(1)}, u32[]{:S(2)}, u32[]{:S(2)}) collective-permute-start(f32[64,64]{1,0:T(8,128)S(1)} %get-tuple-element.17), channel_id=1, source_target_pairs={{0,3},{1,2},{2,1},{3,0},{4,7},{5,6},{6,5},{7,4},{8,11},{9,10},{10,... | collective-permute-start | bytes 49160 | tf_op jit(solution)/shard_map/ppermute | solution.py:263
  15.6 34.1 %collective-permute-start.11 = (f32[64,64]{1,0:T(8,128)S(1)}, f32[64,64]{1,0:T(8,128)S(1)}, u32[]{:S(2)}, u32[]{:S(2)}) collective-permute-start(f32[64,64]{1,0:T(8,128)S(1)} %get-tuple-element.17), channel_id=1, source_target_pairs={{0,2},{1,3},{2,0},{3,1},{4,6},{5,7},{6,4},{7,5},{8,10},{9,11},{10,... | collective-permute-start | bytes 49160 | tf_op jit(solution)/shard_map/ppermute | solution.py:263
  16.3 17.4 %collective-permute-start.16 = (f32[64,64]{1,0:T(8,128)S(1)}, f32[64,64]{1,0:T(8,128)S(1)}, u32[]{:S(2)}, u32[]{:S(2)}) collective-permute-start(f32[64,64]{1,0:T(8,128)S(1)} %get-tuple-element.18), channel_id=1, source_target_pairs={{0,48},{8,56},{16,32},{24,40},{32,16},{40,24},{48,0},{56,8},{64,11... | collective-permute-start | bytes 49160 | tf_op jit(solution)/shard_map/ppermute | solution.py:263
  19.0 15.9 %collective-permute-start.15 = (f32[64,64]{1,0:T(8,128)S(1)}, f32[64,64]{1,0:T(8,128)S(1)}, u32[]{:S(2)}, u32[]{:S(2)}) collective-permute-start(f32[64,64]{1,0:T(8,128)S(1)} %get-tuple-element.18), channel_id=1, source_target_pairs={{0,32},{8,40},{16,48},{24,56},{32,0},{40,8},{48,16},{56,24},{64,96... | collective-permute-start | bytes 49160 | tf_op jit(solution)/shard_map/ppermute | solution.py:263
  19.4 18.6 %collective-permute-start.14 = (f32[64,64]{1,0:T(8,128)S(1)}, f32[64,64]{1,0:T(8,128)S(1)}, u32[]{:S(2)}, u32[]{:S(2)}) collective-permute-start(f32[64,64]{1,0:T(8,128)S(1)} %get-tuple-element.18), channel_id=1, source_target_pairs={{0,16},{8,24},{16,0},{24,8},{32,48},{40,56},{48,32},{56,40},{64,80... | collective-permute-start | bytes 49160 | tf_op jit(solution)/shard_map/ppermute | solution.py:263
  33.7 9.9 %collective-permute-start.2 = (f32[32,128]{1,0:T(8,128)S(1)}, f32[32,128]{1,0:T(8,128)S(1)}, u32[]{:S(2)}, u32[]{:S(2)}) collective-permute-start(f32[32,128]{1,0:T(8,128)S(1)} %get-tuple-element.16), channel_id=1, source_target_pairs={{0,3},{1,2},{2,1},{3,0},{4,7},{5,6},{6,5},{7,4},{8,11},{9,10},{10,... | collective-permute-start | bytes 49160 | tf_op jit(solution)/shard_map/ppermute | solution.py:263
  34.9 8.9 %collective-permute-start.1 = (f32[32,128]{1,0:T(8,128)S(1)}, f32[32,128]{1,0:T(8,128)S(1)}, u32[]{:S(2)}, u32[]{:S(2)}) collective-permute-start(f32[32,128]{1,0:T(8,128)S(1)} %get-tuple-element.16), channel_id=1, source_target_pairs={{0,2},{1,3},{2,0},{3,1},{4,6},{5,7},{6,4},{7,5},{8,10},{9,11},{10,... | collective-permute-start | bytes 49160 | tf_op jit(solution)/shard_map/ppermute | solution.py:263
  38.0 9.2 %collective-permute-start = (f32[32,128]{1,0:T(8,128)S(1)}, f32[32,128]{1,0:T(8,128)S(1)}, u32[]{:S(2)}, u32[]{:S(2)}) collective-permute-start(f32[32,128]{1,0:T(8,128)S(1)} %get-tuple-element.16), channel_id=1, source_target_pairs={{0,1},{1,0},{2,3},{3,2},{4,5},{5,4},{6,7},{7,6},{8,9},{9,8},{10,11... | collective-permute-start | bytes 49160 | tf_op jit(solution)/shard_map/ppermute | solution.py:263
  38.0 41.8 %all-to-all-start.1 = ((bf16[8,768,128]{2,1,0:T(8,128)(2,1)}), bf16[8,768,128]{2,1,0:T(8,128)(2,1)}, u32[]{:S(2)}, u32[]{:S(2)}) async-start(bf16[8,768,128]{2,1,0:T(8,128)(2,1)} %get-tuple-element.15), calls=%async_computation.1 | async-start | bytes 3145728 | tf_op jit(solution)/shard_map/all_to_all | solution.py:324
  43.6 17.0 %collective-permute-start.10 = (f32[64,64]{1,0:T(8,128)S(1)}, f32[64,64]{1,0:T(8,128)S(1)}, u32[]{:S(2)}, u32[]{:S(2)}) collective-permute-start(f32[64,64]{1,0:T(8,128)S(1)} %get-tuple-element.17), channel_id=1, source_target_pairs={{0,1},{1,0},{2,3},{3,2},{4,5},{5,4},{6,7},{7,6},{8,9},{9,8},{10,11... | collective-permute-start | bytes 49160 | tf_op jit(solution)/shard_map/ppermute | solution.py:263
  43.8 18.0 %collective-permute-start.17 = (f32[64,64]{1,0:T(8,128)S(1)}, f32[64,64]{1,0:T(8,128)S(1)}, u32[]{:S(2)}, u32[]{:S(2)}) collective-permute-start(f32[64,64]{1,0:T(8,128)S(1)} %add_add_fusion.1), channel_id=1, source_target_pairs={{0,64},{8,72},{16,80},{24,88},{32,96},{40,104},{48,112},{56,120},{... | collective-permute-start | bytes 49160 | tf_op jit(solution)/shard_map/ppermute | solution.py:263
  47.1 17.9 %collective-permute-start.5 = (f32[32,128]{1,0:T(8,128)S(1)}, f32[32,128]{1,0:T(8,128)S(1)}, u32[]{:S(2)}, u32[]{:S(2)}) collective-permute-start(f32[32,128]{1,0:T(8,128)S(1)} %add_add_fusion.5), channel_id=1, source_target_pairs={{0,68},{1,69},{2,70},{3,71},{4,64},{5,65},{6,66},{7,67},{8,76},{9,... | collective-permute-start | bytes 49160 | tf_op jit(solution)/shard_map/ppermute | solution.py:273
  47.6 17.5 %collective-permute-start.4 = (f32[32,128]{1,0:T(8,128)S(1)}, f32[32,128]{1,0:T(8,128)S(1)}, u32[]{:S(2)}, u32[]{:S(2)}) collective-permute-start(f32[32,128]{1,0:T(8,128)S(1)} %add_add_fusion.5), channel_id=1, source_target_pairs={{0,64},{1,65},{2,66},{3,67},{4,68},{5,69},{6,70},{7,71},{8,72},{9,... | collective-permute-start | bytes 49160 | tf_op jit(solution)/shard_map/ppermute | solution.py:273
  49.7 15.4 %collective-permute-start.3 = (f32[32,128]{1,0:T(8,128)S(1)}, f32[32,128]{1,0:T(8,128)S(1)}, u32[]{:S(2)}, u32[]{:S(2)}) collective-permute-start(f32[32,128]{1,0:T(8,128)S(1)} %add_add_fusion.5), channel_id=1, source_target_pairs={{0,4},{1,5},{2,6},{3,7},{4,0},{5,1},{6,2},{7,3},{8,12},{9,13},{10,... | collective-permute-start | bytes 49160 | tf_op jit(solution)/shard_map/ppermute | solution.py:273
  60.7 7.9 %collective-permute-start.13 = (f32[64,64]{1,0:T(8,128)S(1)}, f32[64,64]{1,0:T(8,128)S(1)}, u32[]{:S(2)}, u32[]{:S(2)}) collective-permute-start(f32[64,64]{1,0:T(8,128)S(1)} %add_add_fusion.2), channel_id=1, source_target_pairs={{0,4},{1,5},{2,6},{3,7},{4,0},{5,1},{6,2},{7,3},{8,12},{9,13},{10,... | collective-permute-start | bytes 49160 | tf_op jit(solution)/shard_map/ppermute | solution.py:263
  61.9 6.7 %collective-permute-start.18 = (f32[64,64]{1,0:T(8,128)S(1)}, f32[64,64]{1,0:T(8,128)S(1)}, u32[]{:S(2)}, u32[]{:S(2)}) collective-permute-start(f32[64,64]{1,0:T(8,128)S(1)} %add.88), channel_id=1, source_target_pairs={{0,8},{8,0},{16,24},{24,16},{32,40},{40,32},{48,56},{56,48},{64,72... | collective-permute-start | bytes 49160 | tf_op jit(solution)/shard_map/ppermute | solution.py:263
  65.1 3.9 %collective-permute-start.8 = (f32[32,128]{1,0:T(8,128)S(1)}, f32[32,128]{1,0:T(8,128)S(1)}, u32[]{:S(2)}, u32[]{:S(2)}) collective-permute-start(f32[32,128]{1,0:T(8,128)S(1)} %add_add_fusion.4), channel_id=1, source_target_pairs={{0,48},{8,56},{16,32},{24,40},{32,16},{40,24},{48,0},{56,8},{64,11... | collective-permute-start | bytes 49160 | tf_op jit(solution)/shard_map/ppermute | solution.py:263
  67.9 4.1 %collective-permute-start.7 = (f32[32,128]{1,0:T(8,128)S(1)}, f32[32,128]{1,0:T(8,128)S(1)}, u32[]{:S(2)}, u32[]{:S(2)}) collective-permute-start(f32[32,128]{1,0:T(8,128)S(1)} %add_add_fusion.4), channel_id=1, source_target_pairs={{0,32},{8,40},{16,48},{24,56},{32,0},{40,8},{48,16},{56,24},{64,96... | collective-permute-start | bytes 49160 | tf_op jit(solution)/shard_map/ppermute | solution.py:263
  68.2 3.7 %collective-permute-start.6 = (f32[32,128]{1,0:T(8,128)S(1)}, f32[32,128]{1,0:T(8,128)S(1)}, u32[]{:S(2)}, u32[]{:S(2)}) collective-permute-start(f32[32,128]{1,0:T(8,128)S(1)} %add_add_fusion.4), channel_id=1, source_target_pairs={{0,16},{8,24},{16,0},{24,8},{32,48},{40,56},{48,32},{56,40},{64,80... | collective-permute-start | bytes 49160 | tf_op jit(solution)/shard_map/ppermute | solution.py:263
  72.0 4.5 %collective-permute-start.9 = (f32[32,128]{1,0:T(8,128)S(1)}, f32[32,128]{1,0:T(8,128)S(1)}, u32[]{:S(2)}, u32[]{:S(2)}) collective-permute-start(f32[32,128]{1,0:T(8,128)S(1)} %add_add_fusion.3.sum_a), channel_id=1, source_target_pairs={{0,8},{8,0},{16,24},{24,16},{32,40},{40,32},{48,56},{56,48},{64,72... | collective-permute-start | bytes 49160 | tf_op jit(solution)/shard_map/ppermute | solution.py:263
  79.7 3.4 %copy-start.2 = (bf16[1,1,16,128,512]{4,3,2,1,0:T(8,128)(2,1)S(1)}, bf16[1,1,16,128,512]{4,3,2,1,0:T(8,128)(2,1)}, u32[]{:S(2)}) copy-start(bf16[1,1,16,128,512]{4,3,2,1,0:T(8,128)(2,1)} %param.7) | copy-start | bytes 6291460
  79.7 3.4 %copy-start.4 = (s32[32]{0:T(128)S(1)}, s32[32]{0:T(128)}, u32[]{:S(2)}) copy-start(s32[32]{0:T(128)} %visits_ref.3) | copy-start | bytes 388
  79.8 0.9 copy-start.7
  80.7 2.4 %copy-start.8 = (f32[64,64]{1,0:T(8,128)S(1)}, f32[64,64]{1,0:T(8,128)}, u32[]{:S(2)}) copy-start(f32[64,64]{1,0:T(8,128)} %get-tuple-element.13.mix_ref) | copy-start | bytes 49156
  87.3 3.4 %collective-permute-start.19 = (f32[8,64,512]{2,1,0:T(8,128)S(1)}, f32[8,64,512]{2,1,0:T(8,128)S(1)}, u32[]{:S(2)}, u32[]{:S(2)}) collective-permute-start(f32[8,64,512]{2,1,0:T(8,128)S(1)} %get-tuple-element.23), channel_id=1, source_target_pairs={{0,8},{8,0},{16,24},{24,16},{32,40},{40,32},{48,56},{56,48},{64,72... | collective-permute-start | bytes 3145736 | tf_op jit(solution)/shard_map/ppermute | solution.py:263
  87.4 10.1 %collective-permute-start.22 = (f32[64,64]{1,0:T(8,128)S(1)}, f32[64,64]{1,0:T(8,128)S(1)}, u32[]{:S(2)}, u32[]{:S(2)}) collective-permute-start(f32[64,64]{1,0:T(8,128)S(1)} %get-tuple-element.25), channel_id=1, source_target_pairs={{0,48},{8,56},{16,32},{24,40},{32,16},{40,24},{48,0},{56,8},{64,11... | collective-permute-start | bytes 49160 | tf_op jit(solution)/shard_map/ppermute | solution.py:263
  88.2 9.3 %collective-permute-start.21 = (f32[64,64]{1,0:T(8,128)S(1)}, f32[64,64]{1,0:T(8,128)S(1)}, u32[]{:S(2)}, u32[]{:S(2)}) collective-permute-start(f32[64,64]{1,0:T(8,128)S(1)} %get-tuple-element.25), channel_id=1, source_target_pairs={{0,32},{8,40},{16,48},{24,56},{32,0},{40,8},{48,16},{56,24},{64,96... | collective-permute-start | bytes 49160 | tf_op jit(solution)/shard_map/ppermute | solution.py:263
  89.1 8.4 %collective-permute-start.20 = (f32[64,64]{1,0:T(8,128)S(1)}, f32[64,64]{1,0:T(8,128)S(1)}, u32[]{:S(2)}, u32[]{:S(2)}) collective-permute-start(f32[64,64]{1,0:T(8,128)S(1)} %get-tuple-element.25), channel_id=1, source_target_pairs={{0,16},{8,24},{16,0},{24,8},{32,48},{40,56},{48,32},{56,40},{64,80... | collective-permute-start | bytes 49160 | tf_op jit(solution)/shard_map/ppermute | solution.py:263
  91.7 18.3 %all-to-all-start.2 = ((bf16[8,64,512]{2,1,0:T(8,128)(2,1)}), bf16[8,64,512]{2,1,0:T(8,128)(2,1)S(1)}, u32[]{:S(2)}, u32[]{:S(2)}) async-start(bf16[8,64,512]{2,1,0:T(8,128)(2,1)} %add_convert_fusion), calls=%async_computation.2 | async-start | bytes 1048576 | tf_op jit(solution)/shard_map/all_to_all | solution.py:345
  97.5 5.1 %collective-permute-start.23 = (f32[64,64]{1,0:T(8,128)S(1)}, f32[64,64]{1,0:T(8,128)S(1)}, u32[]{:S(2)}, u32[]{:S(2)}) collective-permute-start(f32[64,64]{1,0:T(8,128)S(1)} %add_add_fusion), channel_id=1, source_target_pairs={{0,64},{8,72},{16,80},{24,88},{32,96},{40,104},{48,112},{56,120},{... | collective-permute-start | bytes 49160 | tf_op jit(solution)/shard_map/ppermute | solution.py:263
  102.7 4.6 %collective-permute-start.24 = (f32[64,64]{1,0:T(8,128)S(1)}, f32[64,64]{1,0:T(8,128)S(1)}, u32[]{:S(2)}, u32[]{:S(2)}) collective-permute-start(f32[64,64]{1,0:T(8,128)S(1)} %add.94), channel_id=1, source_target_pairs={{0,8},{8,0},{16,24},{24,16},{32,40},{40,32},{48,56},{56,48},{64,72... | collective-permute-start | bytes 49160 | tf_op jit(solution)/shard_map/ppermute | solution.py:263
  127.7 2.7 %collective-permute-start.25 = (bf16[8,64,512]{2,1,0:T(8,128)(2,1)S(1)}, bf16[8,64,512]{2,1,0:T(8,128)(2,1)S(1)}, u32[]{:S(2)}, u32[]{:S(2)}) collective-permute-start(bf16[8,64,512]{2,1,0:T(8,128)(2,1)S(1)} %all_to_all.20.mine_ref), channel_id=1, source_target_pairs={{0,8},{8,0},{16,24},{24,16},{32,40},{40,32},{48,56},{56,48},{64,72... | collective-permute-start | bytes 1572872 | tf_op jit(solution)/shard_map/ppermute | solution.py:263

commit v3 on v2

--- a/solution.py
+++ b/solution.py
@@ -67,6 +67,11 @@
         [-r[0][0], -r[1][0], si[0][0], si[0][1]],
         [-r[0][1], -r[1][1], si[1][0], si[1][1]],
     ]
+
+
+def halves(x):
+    low = x.shape[0] // 2
+    return jnp.concatenate([x[:low], x[low:]], axis=1)
 
 
 def damped_inverse(gram):
@@ -138,67 +143,73 @@
     out_ref[...] = damped_inverse(a_ref[...] * b_ref[...])
 
 
-def polar_kernel(at_ref, prod_ref, mix_ref, weight_ref, numer_ref, out_ref):
-    dests = out_ref.shape[0]
+def polar_kernel(at_ref, prod_ref, mix_ref, weight_ref, proj_ref, polar_ref):
+    dests = polar_ref.shape[0]
     segs, rank, rows = prod_ref.shape
     own = segs // VBLOCKS
     prods = [
         jnp.concatenate([prod_ref[VBLOCKS * j + b] for b in range(VBLOCKS)], axis=1)
         for j in range(own)
     ]
-    weights = [weight_ref[pl.ds(at_ref[0] * own + j, 1), :] for j in range(own)]
     zs = []
     for j in range(own):
-        target = mm(mix_ref[...] * weights[j], prods[j])
+        weight = weight_ref[pl.ds(at_ref[0] * own + j, 1), :]
+        target = mm(mix_ref[...] * weight, prods[j])
         zs.append(target / jnp.sqrt(jnp.sum(target * target, keepdims=True) + epsilon))
     for _ in range(NS_STEPS):
         grams = [mm(z, z, NT) for z in zs]
         zs = [1.5 * z - 0.5 * mm(g, z) for g, z in zip(grams, zs)]
-    pieces = []
-    for z in zs:
-        z = z.astype(BF16)
-        pieces += [z[:, b * rows : (b + 1) * rows] for b in range(VBLOCKS)]
-    numer = jnp.zeros((rank, rank), F32)
-    for z, p, weight in zip(zs, prods, weights):
-        projected = mm(z, p, NT)
-        numer += projected * weight
-        pieces.append(jnp.concatenate(split(projected), axis=1))
-    numer_ref[...] = jnp.concatenate([numer[: rank // 2], numer[rank // 2 :]], axis=1)
+    projected = [halves(mm(z, p, NT)) for z, p in zip(zs, prods)]
+    polar = [z.astype(BF16) for z in zs]
+    low = rank // 2
     for d in range(dests):
-        for i, piece in enumerate(pieces):
-            out_ref[d, i * rank : (i + 1) * rank, :] = piece
-
-
-def mix_kernel(sum_a, sum_b, inverse_ref, code_gram_ref, mix_ref, mgram_ref, out_ref):
+        for j in range(own):
+            proj_ref[d, j * low : (j + 1) * low, :] = projected[j]
+            for b in range(VBLOCKS):
+                at = (VBLOCKS * j + b) * rank
+                polar_ref[d, at : at + rank, :] = polar[j][:, b * rows : (b + 1) * rows]
+
+
+def partial_kernel(got_ref, weight_ref, out_ref):
+    sources = got_ref.shape[0]
+    low = out_ref.shape[0]
+    weight = weight_ref[...]
+    twice = jnp.concatenate([weight, weight], axis=1)
+    own = weight.shape[0] // sources
+    total = jnp.zeros(out_ref.shape, F32)
+    for d in range(sources):
+        for j in range(own):
+            k = d * own + j
+            total += got_ref[d, j * low : (j + 1) * low, :] * twice[k : k + 1, :]
+    out_ref[...] = total
+
+
+def mix_kernel(
+    place_ref, sum_a, sum_b, inverse_ref, code_gram_ref, got_ref,
+    mix_ref, mgram_ref, weight_ref, wgram_ref, own_ref,
+):
+    sources = got_ref.shape[0]
+    rank = mix_ref.shape[0]
+    own = own_ref.shape[0]
+    low = rank // 2
     sums = sum_a[...] + sum_b[...]
-    rank = mix_ref.shape[0]
     numer = jnp.concatenate([sums[:, :rank], sums[:, rank:]], axis=0)
     mix = mm(numer, inverse_ref[...])
     mix_ref[...] = mix
     mix_gram = mm(mix, mix, TN)
     mgram_ref[...] = mix_gram
-    out_ref[...] = damped_inverse(mix_gram * code_gram_ref[...])
-
-
-def weight_kernel(place_ref, got_ref, mix_ref, inverse_ref, weight_ref, wgram_ref, own_ref):
-    sources = got_ref.shape[0]
-    rank = mix_ref.shape[0]
-    own = own_ref.shape[0]
-    first = own * VBLOCKS * rank
-    mix = mix_ref[...]
-    twice = jnp.concatenate([mix, mix], axis=1)
+    inverse = damped_inverse(mix_gram * code_gram_ref[...])
+    beside = halves(mix)
     terms = []
     for d in range(sources):
         for j in range(own):
-            at = first + j * rank
-            terms.append(
-                jnp.sum(got_ref[d, at : at + rank, :].astype(F32) * twice, axis=0, keepdims=True)
-            )
-    weight = jnp.maximum(mm(fold(jnp.concatenate(terms, axis=0)), inverse_ref[...]), 0.0)
+            part = got_ref[d, j * low : (j + 1) * low, :] * beside
+            terms.append(jnp.sum(part, axis=0, keepdims=True))
+    weight = jnp.maximum(mm(fold(jnp.concatenate(terms, axis=0)), inverse), 0.0)
     weight_ref[...] = weight
     for j in range(own):
         own_ref[j : j + 1, :] = weight_ref[pl.ds(place_ref[0] * own + j, 1), :]
-    wgram_ref[...] = mm(weight, weight, TN)
+    wgram_ref[...] = halves(mm(weight, weight, TN))
 
 
 def numer_kernel(
@@ -225,12 +236,31 @@
         send_ref[j] = acc_ref[2 * j + 1 - parity]
 
 
-def factor_kernel(got_ref, inverse_ref, out_ref):
-    sources = got_ref.shape[0]
-    total = got_ref[0].astype(F32)
-    for d in range(1, sources):
-        total += got_ref[d].astype(F32)
-    code = jnp.maximum(mm(inverse_ref[...], total), 0.0).astype(BF16)
+def pair_kernel(keep_ref, came_ref, gram_a, gram_b, out_ref):
+    low, lanes = gram_a.shape
+    slabs = keep_ref.shape[2] // lanes
+    piece = jnp.concatenate(split(gram_a[...] + gram_b[...]), axis=0)
+    for j in range(keep_ref.shape[0]):
+        both = (keep_ref[j] + came_ref[j]).astype(BF16)
+        for i in range(slabs):
+            out_ref[j, i] = both[:, i * lanes : (i + 1) * lanes]
+        out_ref[j, slabs] = piece
+
+
+def factor_kernel(got_ref, mgram_ref, out_ref):
+    sources, slabs = got_ref.shape[0], got_ref.shape[1] - 1
+    sums = []
+    for i in range(slabs + 1):
+        total = got_ref[0, i].astype(F32)
+        for d in range(1, sources):
+            total += got_ref[d, i].astype(F32)
+        sums.append(total)
+    low = sums[slabs].shape[0] // 2
+    gram = sums[slabs][:low] + sums[slabs][low:]
+    rank = mgram_ref.shape[0]
+    gram = jnp.concatenate([gram[:, :rank], gram[:, rank:]], axis=0)
+    inverse = damped_inverse(mgram_ref[...] * gram)
+    code = jnp.maximum(mm(inverse, jnp.concatenate(sums[:slabs], axis=1)), 0.0).astype(BF16)
     for d in range(sources):
         out_ref[d] = code
 
@@ -261,16 +291,6 @@
 def swap(x, axis, bit):
     size = lax.axis_size(axis)
     return lax.ppermute(x, axis, [(i, i ^ bit) for i in range(size)])
-
-
-def swap_z(x, high, low):
-    n_pat, n_code = lax.axis_size("pat"), lax.axis_size("code")
-    pairs = [
-        (p * n_code + c, (p ^ (high * n_pat // 2)) * n_code + (c ^ (low * n_code // 2)))
-        for p in range(n_pat)
-        for c in range(n_code)
-    ]
-    return lax.ppermute(x, ("pat", "code"), pairs)
 
 
 def plus(x, parts):
@@ -304,39 +324,46 @@
         [SM, SM, SM, VM, VM], (listing, tile_count, visit_counts, tiles, code_factor_t),
     )
     sent = partial.astype(F16).reshape(n_code, own * VBLOCKS * rank, rows)
+    sent, weight_after = lax.optimization_barrier((sent, patient_weight))
     got = lax.all_to_all(sent, "code", 0, 0, tiled=True)
     code_gram, weight_gram = call(
-        gram_kernel, (square, square), [VM, VM], (code_factor_t, patient_weight)
+        gram_kernel, (square, square), [VM, VM], (code_factor_t, weight_after)
     )
     code_gram = plus(code_gram, [swap(code_gram, "code", bit) for bit in (1, 2, 3)])
     code_gram = code_gram + swap(code_gram, "code", 4)
     inverse_mix = call(
         inverse_kernel, square, [VM, VM], (code_gram, sum_pat(weight_gram)), flops=4e9
     )
+    got, inverse_mix = lax.optimization_barrier((got, inverse_mix))
     products = jnp.sum(got.astype(F32), axis=0).reshape(own * VBLOCKS, rank, rows)
 
-    length = (own * VBLOCKS + own) * rank
-    sums, message = call(
+    proj, polar = call(
         polar_kernel,
-        (shape((rank // 2, 2 * rank), F32), shape((n_code, length, rows), BF16)),
+        (
+            shape((n_code, own * rank // 2, 2 * rank), F32),
+            shape((n_code, own * VBLOCKS * rank, rows), BF16),
+        ),
         [SM, VM, VM, VM], (place, products, visit_mix, patient_weight), flops=5e9,
     )
-    shared = lax.all_to_all(message, "code", 0, 0, tiled=True)
-    sums = plus(sums, [swap(sums, "code", bit) for bit in (1, 2, 3)])
-    sums = plus(sums, [swap_z(sums, high, low) for high, low in ((0, 1), (1, 0), (1, 1))])
+    proj = lax.all_to_all(proj, "code", 0, 0, tiled=True)
+    proj, polar = lax.optimization_barrier((proj, polar))
+    polar = lax.all_to_all(polar, "code", 0, 0, tiled=True)
+    sums = call(partial_kernel, shape((rank // 2, 2 * rank), F32), [VM, VM], (proj, patient_weight))
     sums = plus(sums, [swap(sums, "pat", bit) for bit in (2, 4, 6)])
-    mix_new, mix_gram, inverse_weight = call(
-        mix_kernel, (square,) * 3, [VM] * 4,
-        (sums, swap(sums, "pat", 1), inverse_mix, code_gram), flops=4e9,
-    )
-    weights, wgram, weight_new = call(
-        weight_kernel, (shape((patients, rank), F32), square, shape((own, rank), F32)),
-        [SM, VM, VM, VM], (place, shared, mix_new, inverse_weight),
+    sums = sums + swap(sums, "pat", 8)
+    mix_new, mix_gram, weights, wgram, weight_new = call(
+        mix_kernel,
+        (
+            square, square, shape((patients, rank), F32),
+            shape((rank // 2, 2 * rank), F32), shape((own, rank), F32),
+        ),
+        [SM] + [VM] * 5,
+        (place, sums, swap(sums, "pat", 1), inverse_mix, code_gram, proj), flops=5e9,
     )
     block = shape((half, rank, cols), F32)
     keep, send = call(
         numer_kernel, (block, block), [SM, SM, SM, SM, VM, VM, VM, VM],
-        (place, listing, tile_count, visit_counts, shared, mix_new, weights, tiles),
+        (place, listing, tile_count, visit_counts, polar, mix_new, weights, tiles),
         [pltpu.VMEM((n_pat, rank, cols), F32)], flops=4e9,
     )
     groups = [[core + 2 * i for i in range(half)] for core in (0, 1)]
@@ -344,10 +371,13 @@
     def exchange(x):
         return lax.all_to_all(x, "pat", 0, 0, axis_index_groups=groups, tiled=True)
 
-    summed = exchange((keep + swap(send, "pat", 1)).astype(BF16))
-    inverse_code = call(inverse_kernel, square, [VM, VM], (mix_gram, sum_pat(wgram)), flops=4e9)
+    lanes = 2 * rank
+    packed = call(
+        pair_kernel, shape((half, cols // lanes + 1, rank, lanes), BF16), [VM] * 4,
+        (keep, swap(send, "pat", 1), wgram, swap(wgram, "pat", 1)),
+    )
     code = call(
-        factor_kernel, shape((half, rank, cols), BF16), [VM, VM], (summed, inverse_code)
+        factor_kernel, shape((half, rank, cols), BF16), [VM, VM], (exchange(packed), mix_gram)
     )
     mine = exchange(code)
     code_new = call(

time: 135 us -> 135 us (level)
  blocking collectives: 17.4 us -> 46 us
  starting transfers between devices: 54.4 us -> 32 us
  waiting for transfers between devices: 25.7 us -> 21.7 us
  Pallas kernels: 27.3 us -> 25.1 us
  local copies, waits for them, and re-layouts: 3.86 us -> 5.47 us
    all_to_all x0 -> x1, blocking collectives: none -> 15.3 us  [body(): proj = lax.all_to_all(proj, 'code', 0, 0, tiled=True)]
    all_to_all x1 -> x2, blocking collectives: 17.4 us -> 30.6 us  [exchange(): return lax.all_to_all(x, 'pat', 0, 0, axis_index_groups=groups, tiled=True)]
    ppermute x23 -> x17, starting transfers between devices: 34 us -> 22.8 us  [swap(): return lax.ppermute(x, axis, [(i, i ^ bit) for i in range(size)])]
    all_to_all x1, waiting for transfers between devices: 7.58 us -> 0.01 us  [body(): got = lax.all_to_all(sent, 'code', 0, 0, tiled=True)]
    all_to_all x2 -> x1, starting transfers between devices: 11.4 us -> 4.26 us  [body(): polar = lax.all_to_all(polar, 'code', 0, 0, tiled=True)]
    ppermute x23 -> x17, waiting for transfers between devices: 18.1 us -> 21.7 us  [swap(): return lax.ppermute(x, axis, [(i, i ^ bit) for i in range(size)])]
    ppermute x3 -> x0, starting transfers between devices: 3.33 us -> none  [swap_z(): return lax.ppermute(x, ('pat', 'code'), pairs)]
    pallas_call x10, Pallas kernels: 27.3 us -> 25.1 us  [call(): pl.pallas_call(kernel, out_shape=outs, in_specs=specs, out_specs=(VM,) *...]
  transfers between devices with their start and end apart: 29 -> 19, of which waited for: 7 -> 9; matrix products, arithmetic and copies ran while one was open for 1% -> 0% of each run, Pallas kernels for 12% -> 6%
where the time goes in v3:
time: 135 us; the launch traced here: 133 us
  blocking collectives  46 us (34%)
  starting transfers between devices  32 us (24%)
  Pallas kernels  25.1 us (19%)
  waiting for transfers between devices  21.7 us (16%)
  local copies, waits for them, and re-layouts  5.47 us (4%)
  other arithmetic  1.49 us (1%)
  between operations  1.42 us (1%)
    all_to_all x2, blocking collectives, exchange(): return lax.all_to_all(x, 'pat', 0, 0, axis_index_groups=groups, tiled=True)  30.6 us
    pallas_call x10, Pallas kernels, call(): pl.pallas_call(kernel, out_shape=outs, in_specs=specs, out_specs=(VM,) *...  25.1 us
    ppermute x17, starting transfers between devices, swap(): return lax.ppermute(x, axis, [(i, i ^ bit) for i in range(size)])  22.8 us
    ppermute x17, waiting for transfers between devices, swap(): return lax.ppermute(x, axis, [(i, i ^ bit) for i in range(size)])  21.7 us
    all_to_all x1, blocking collectives, body(): proj = lax.all_to_all(proj, 'code', 0, 0, tiled=True)  15.3 us
    unnamed x21, local copies, waits for them, and re-layouts  5.47 us
    all_to_all x1, starting transfers between devices, body(): got = lax.all_to_all(sent, 'code', 0, 0, tiled=True)  4.99 us
    all_to_all x1, starting transfers between devices, body(): polar = lax.all_to_all(polar, 'code', 0, 0, tiled=True)  4.26 us
  transfers between devices with their start and end apart: 19, of which 9 were waited for; matrix products, arithmetic and copies ran while one was open for 0% of the time, Pallas kernels for 6%

profile of v3, /device:TPU:3, one launch (start us, length us, event | category | flops | bytes accessed | tf_op | source)
XLA Modules:
  0.0 133.2 jit_solution(3650995229992773617)
XLA Ops:
  0.6 0.7 copy.12
  2.0 1.6 %copy-done.1 = bf16[1,1,16,128,512]{4,3,2,1,0:T(8,128)(2,1)S(1)} copy-done((bf16[1,1,16,128,512]{4,3,2,1,0:T(8,128)(2,1)S(1)}, bf16[1,1,16,128,512]{4,3,2,1,0:T(8,128)(2,1)}, u32[]{:S(2)}) %copy-start.1) | copy-done | bytes 2097176
  3.6 0.7 copy-done.5
  4.2 2.5 %shard_map.94 = f32[64,64,128]{2,1,0:T(8,128)S(1)} custom-call(s32[3,16]{1,0:T(4,128)S(1)} %bitcast.11, s32[1,1]{1,0:T(1,128)S(6)} %copy.13.count_ref, s32[32]{0:T(128)S(1)} %copy-done.5, bf16[16,128,512]{2,1,0:T(8,128)(2,1)S(1)} %bitcast.8, f32[64,8192]{1,0:T(8,128)} %code_ref.3), custom_call_target="tpu_custom_call" | custom-call | flops 1000000000 | bytes 65536 | tf_op jit(solution)/shard_map/pallas_call | solution.py:280
  6.7 1.2 convert_element_type.6
  7.9 0.7 copy-done
  8.7 0.8 shard_map.95
  9.4 1.4 %collective-permute-start.4 = (f32[64,64]{1,0:T(8,128)S(1)}, f32[64,64]{1,0:T(8,128)S(1)}, u32[]{:S(2)}, u32[]{:S(2)}) collective-permute-start(f32[64,64]{1,0:T(8,128)S(1)} %get-tuple-element.23), channel_id=1, source_target_pairs={{0,16},{8,24},{16,0},{24,8},{32,48},{40,56},{48,32},{56,40},{64,80... | collective-permute-start | bytes 49160 | tf_op jit(solution)/shard_map/ppermute | solution.py:293
  10.8 2.6 %collective-permute-start.5 = (f32[64,64]{1,0:T(8,128)S(1)}, f32[64,64]{1,0:T(8,128)S(1)}, u32[]{:S(2)}, u32[]{:S(2)}) collective-permute-start(f32[64,64]{1,0:T(8,128)S(1)} %get-tuple-element.23), channel_id=1, source_target_pairs={{0,32},{8,40},{16,48},{24,56},{32,0},{40,8},{48,16},{56,24},{64,96... | collective-permute-start | bytes 49160 | tf_op jit(solution)/shard_map/ppermute | solution.py:293
  13.4 0.3 collective-permute-start
  13.7 2.1 %collective-permute-start.1 = (f32[64,64]{1,0:T(8,128)S(1)}, f32[64,64]{1,0:T(8,128)S(1)}, u32[]{:S(2)}, u32[]{:S(2)}) collective-permute-start(f32[64,64]{1,0:T(8,128)S(1)} %get-tuple-element.22), channel_id=1, source_target_pairs={{0,2},{1,3},{2,0},{3,1},{4,6},{5,7},{6,4},{7,5},{8,10},{9,11},{10,... | collective-permute-start | bytes 49160 | tf_op jit(solution)/shard_map/ppermute | solution.py:293
  15.8 5.0 %all-to-all-start = ((f16[8,512,128]{2,1,0:T(8,128)(2,1)}), f16[8,512,128]{2,1,0:T(8,128)(2,1)S(1)}, u32[]{:S(2)}, u32[]{:S(2)}) async-start(f16[8,512,128]{2,1,0:T(8,128)(2,1)} %bitcast.3), calls=%async_computation | async-start | bytes 2097152 | tf_op jit(solution)/shard_map/all_to_all | solution.py:328
  20.8 1.2 collective-permute-start.2
  22.0 3.7 %collective-permute-start.7 = (f32[64,64]{1,0:T(8,128)S(1)}, f32[64,64]{1,0:T(8,128)S(1)}, u32[]{:S(2)}, u32[]{:S(2)}) collective-permute-start(f32[64,64]{1,0:T(8,128)S(1)} %add_add_fusion), channel_id=1, source_target_pairs={{0,64},{8,72},{16,80},{24,88},{32,96},{40,104},{48,112},{56,120},{... | collective-permute-start | bytes 49160 | tf_op jit(solution)/shard_map/ppermute | solution.py:293
  25.7 7.4 %collective-permute-done.2 = f32[64,64]{1,0:T(8,128)S(1)} collective-permute-done((f32[64,64]{1,0:T(8,128)S(1)}, f32[64,64]{1,0:T(8,128)S(1)}, u32[]{:S(2)}, u32[]{:S(2)}) %collective-permute-start.2) | collective-permute-done | bytes 16416 | tf_op jit(solution)/shard_map/ppermute | solution.py:293
  33.2 1.3 collective-permute-start.3
  34.5 1.0 collective-permute-start.8
  35.6 0.8 collective-permute-done.3
  36.4 2.8 %shard_map.96.inverse_ref = f32[64,64]{1,0:T(8,128)S(1)} custom-call(f32[64,64]{1,0:T(8,128)S(1)} %add.42.a_ref.code_gram_ref, f32[64,64]{1,0:T(8,128)S(1)} %add.47.b_ref), custom_call_target="tpu_custom_call" | custom-call | flops 4000000000 | bytes 65536 | tf_op jit(solution)/shard_map/pallas_call | solution.py:280
  39.2 0.1 convert_reduce_fusion
  39.4 5.8 %shard_map.97 = (f32[8,128,128]{2,1,0:T(8,128)S(1)}, bf16[8,512,128]{2,1,0:T(8,128)(2,1)}) custom-call(s32[2]{0:T(128)S(1)} %pad_add_fusion.at_ref.place_ref, f32[8,64,128]{2,1,0:T(8,128)S(1)} %bitcast.10, f32[64,64]{1,0:T(8,128)S(1)} %copy-done.7, f32[32,64]{1,0:T(8,128)S(1)} %copy-done.8), custom_call_target="tpu_custom_call" | custom-call | flops 5000000000 | bytes 65536 | tf_op jit(solution)/shard_map/pallas_call | solution.py:280
  45.2 15.3 %all_to_all.25.got_ref = f32[8,128,128]{2,1,0:T(8,128)S(1)} all-to-all(f32[8,128,128]{2,1,0:T(8,128)S(1)} %get-tuple-element.25), channel_id=1, replica_groups=mesh['pat'=16,'code'=8] {'code'}, dimensions={0} | all-to-all | bytes 1048576 | tf_op jit(solution)/shard_map/all_to_all | solution.py:348
  60.5 4.3 %all-to-all-start.2 = ((bf16[8,512,128]{2,1,0:T(8,128)(2,1)}), bf16[8,512,128]{2,1,0:T(8,128)(2,1)S(1)}, u32[]{:S(2)}, u32[]{:S(2)}) async-start(bf16[8,512,128]{2,1,0:T(8,128)(2,1)} %get-tuple-element.27), calls=%async_computation.2 | async-start | bytes 2097152 | tf_op jit(solution)/shard_map/all_to_all | solution.py:350
  64.8 0.1 shard_map.98
  64.9 1.7 %collective-permute-start.10 = (f32[32,128]{1,0:T(8,128)S(1)}, f32[32,128]{1,0:T(8,128)S(1)}, u32[]{:S(2)}, u32[]{:S(2)}) collective-permute-start(f32[32,128]{1,0:T(8,128)S(1)} %shard_map.98), channel_id=1, source_target_pairs={{0,32},{8,40},{16,48},{24,56},{32,0},{40,8},{48,16},{56,24},{64,96... | collective-permute-start | bytes 49160 | tf_op jit(solution)/shard_map/ppermute | solution.py:293
  66.6 1.1 collective-permute-start.11
  67.7 0.5 collective-permute-start.9
  68.2 0.8 collective-permute-done.10
  69.1 1.3 %collective-permute-done.11 = f32[32,128]{1,0:T(8,128)S(1)} collective-permute-done((f32[32,128]{1,0:T(8,128)S(1)}, f32[32,128]{1,0:T(8,128)S(1)}, u32[]{:S(2)}, u32[]{:S(2)}) %collective-permute-start.11) | collective-permute-done | bytes 16416 | tf_op jit(solution)/shard_map/ppermute | solution.py:293
  70.4 0.2 collective-permute-done.9
  70.6 1.8 %collective-permute-start.12 = (f32[32,128]{1,0:T(8,128)S(1)}, f32[32,128]{1,0:T(8,128)S(1)}, u32[]{:S(2)}, u32[]{:S(2)}) collective-permute-start(f32[32,128]{1,0:T(8,128)S(1)} %add_add_fusion.2), channel_id=1, source_target_pairs={{0,64},{8,72},{16,80},{24,88},{32,96},{40,104},{48,112},{56,120},{... | collective-permute-start | bytes 49160 | tf_op jit(solution)/shard_map/ppermute | solution.py:293
  72.4 6.5 %collective-permute-done.12 = f32[32,128]{1,0:T(8,128)S(1)} collective-permute-done((f32[32,128]{1,0:T(8,128)S(1)}, f32[32,128]{1,0:T(8,128)S(1)}, u32[]{:S(2)}, u32[]{:S(2)}) %collective-permute-start.12) | collective-permute-done | bytes 16416 | tf_op jit(solution)/shard_map/ppermute | solution.py:293
  78.9 1.2 collective-permute-start.13
  80.1 0.8 collective-permute-done.13.sum_b
  80.9 1.0 copy-done.4
  82.0 4.6 %shard_map.99 = (f32[64,64]{1,0:T(8,128)}, f32[64,64]{1,0:T(8,128)S(1)}, f32[32,64]{1,0:T(8,128)S(1)}, f32[32,128]{1,0:T(8,128)S(1)}, f32[4,64]{1,0:T(4,128)}) custom-call(s32[2]{0:T(128)S(1)} %pad_add_fusion.at_ref.place_ref, f32[32,128]{1,0:T(8,128)S(1)} %add.51.sum_a, f32[32,128]{1,0:T(8,128)S(1)} %collective-permute-done.13.sum_b, ...), custom_call_target="tpu_custom_call" | custom-call | flops 5000000000 | bytes 65536 | tf_op jit(solution)/shard_map/pallas_call | solution.py:280
  86.6 0.7 copy-done.9
  87.3 3.3 %shard_map.100 = (f32[8,64,512]{2,1,0:T(8,128)S(1)}, f32[8,64,512]{2,1,0:T(8,128)S(1)}) custom-call(s32[2]{0:T(128)S(1)} %pad_add_fusion.at_ref.place_ref, s32[3,16]{1,0:T(4,128)S(1)} %bitcast.12, s32[1,1]{1,0:T(1,128)S(6)} %copy.13.count_ref, s32[32]{0:T(128)S(1)} %copy-done.6, bf16[8,512,128]{2,1,0:T(8,128)(2,1)S(1)} %all-to-all-done.2.got_ref, ...), custom_call_target="tpu_custom_call" | custom-call | flops 4000000000 | bytes 65536 | tf_op jit(solution)/shard_map/pallas_call | solution.py:280
  90.7 0.4 collective-permute-start.14
  91.1 0.2 collective-permute-start.15
  91.3 2.2 %collective-permute-done.15.gram_b = f32[32,128]{1,0:T(8,128)S(1)} collective-permute-done((f32[32,128]{1,0:T(8,128)S(1)}, f32[32,128]{1,0:T(8,128)S(1)}, u32[]{:S(2)}, u32[]{:S(2)}) %collective-permute-start.15) | collective-permute-done | bytes 16416 | tf_op jit(solution)/shard_map/ppermute | solution.py:293
  93.4 0.1 shard_map.101
  93.6 18.0 %all_to_all.26.got_ref = bf16[8,5,64,128]{3,2,1,0:T(8,128)(2,1)S(1)} all-to-all(bf16[8,5,64,128]{3,2,1,0:T(8,128)(2,1)S(1)} %shard_map.101), channel_id=1, replica_groups={{0,16,32,48,64,80,96,112},{8,24,40,56,72,88,104,120},{1,17,33,49,65,81,..., dimensions={0} | all-to-all | bytes 1310720 | tf_op jit(solution)/shard_map/all_to_all | solution.py:372
  111.6 3.1 %shard_map.102 = bf16[8,64,512]{2,1,0:T(8,128)(2,1)S(1)} custom-call(bf16[8,5,64,128]{3,2,1,0:T(8,128)(2,1)S(1)} %all_to_all.26.got_ref, f32[64,64]{1,0:T(8,128)S(1)} %get-tuple-element.35.mgram_ref), custom_call_target="tpu_custom_call" | custom-call | flops 1000000000 | bytes 65536 | tf_op jit(solution)/shard_map/pallas_call | solution.py:280
  114.7 12.6 %all_to_all.27.mine_ref = bf16[8,64,512]{2,1,0:T(8,128)(2,1)S(1)} all-to-all(bf16[8,64,512]{2,1,0:T(8,128)(2,1)S(1)} %shard_map.102), channel_id=1, replica_groups={{0,16,32,48,64,80,96,112},{8,24,40,56,72,88,104,120},{1,17,33,49,65,81,..., dimensions={0} | all-to-all | bytes 1048576 | tf_op jit(solution)/shard_map/all_to_all | solution.py:372
  127.3 2.3 %collective-permute-start.16 = (bf16[8,64,512]{2,1,0:T(8,128)(2,1)S(1)}, bf16[8,64,512]{2,1,0:T(8,128)(2,1)S(1)}, u32[]{:S(2)}, u32[]{:S(2)}) collective-permute-start(bf16[8,64,512]{2,1,0:T(8,128)(2,1)S(1)} %all_to_all.27.mine_ref), channel_id=1, source_target_pairs={{0,8},{8,0},{16,24},{24,16},{32,40},{40,32},{48,56},{56,48},{64,72... | collective-permute-start | bytes 1572872 | tf_op jit(solution)/shard_map/ppermute | solution.py:293
  129.7 1.5 %collective-permute-done.16.came_ref = bf16[8,64,512]{2,1,0:T(8,128)(2,1)S(1)} collective-permute-done((bf16[8,64,512]{2,1,0:T(8,128)(2,1)S(1)}, bf16[8,64,512]{2,1,0:T(8,128)(2,1)S(1)}, u32[]{:S(2)}, u32[]{:S(2)}) %collective-permute-start.16) | collective-permute-done | bytes 524320 | tf_op jit(solution)/shard_map/ppermute | solution.py:293
  131.2 2.0 %shard_map.103 = f32[64,8192]{1,0:T(8,128)} custom-call(s32[2]{0:T(128)S(1)} %pad_add_fusion.at_ref.place_ref, bf16[8,64,512]{2,1,0:T(8,128)(2,1)S(1)} %all_to_all.27.mine_ref, bf16[8,64,512]{2,1,0:T(8,128)(2,1)S(1)} %collective-permute-done.16.came_ref), custom_call_target="tpu_custom_call" | custom-call | flops 1000000000 | bytes 65536 | tf_op jit(solution)/shard_map/pallas_call | solution.py:280
  (34 shorter events, 0.2 us)
Async XLA Ops:
  2.0 1.6 %copy-start.1 = (bf16[1,1,16,128,512]{4,3,2,1,0:T(8,128)(2,1)S(1)}, bf16[1,1,16,128,512]{4,3,2,1,0:T(8,128)(2,1)}, u32[]{:S(2)}) copy-start(bf16[1,1,16,128,512]{4,3,2,1,0:T(8,128)(2,1)} %param.7) | copy-start | bytes 6291460
  3.6 0.7 copy-start.5
  6.7 2.0 %copy-start = (f32[64,8192]{1,0:T(8,128)S(1)}, f32[64,8192]{1,0:T(8,128)}, u32[]{:S(2)}) copy-start(f32[64,8192]{1,0:T(8,128)} %code_ref.3) | copy-start | bytes 6291460
  6.7 2.0 %copy-start.8 = (f32[32,64]{1,0:T(8,128)S(1)}, f32[32,64]{1,0:T(8,128)}, u32[]{:S(2)}) copy-start(f32[32,64]{1,0:T(8,128)} %weight_ref.4) | copy-start | bytes 24580
  9.4 11.4 %collective-permute-start.4 = (f32[64,64]{1,0:T(8,128)S(1)}, f32[64,64]{1,0:T(8,128)S(1)}, u32[]{:S(2)}, u32[]{:S(2)}) collective-permute-start(f32[64,64]{1,0:T(8,128)S(1)} %get-tuple-element.23), channel_id=1, source_target_pairs={{0,16},{8,24},{16,0},{24,8},{32,48},{40,56},{48,32},{56,40},{64,80... | collective-permute-start | bytes 49160 | tf_op jit(solution)/shard_map/ppermute | solution.py:293
  10.8 11.2 %collective-permute-start.5 = (f32[64,64]{1,0:T(8,128)S(1)}, f32[64,64]{1,0:T(8,128)S(1)}, u32[]{:S(2)}, u32[]{:S(2)}) collective-permute-start(f32[64,64]{1,0:T(8,128)S(1)} %get-tuple-element.23), channel_id=1, source_target_pairs={{0,32},{8,40},{16,48},{24,56},{32,0},{40,8},{48,16},{56,24},{64,96... | collective-permute-start | bytes 49160 | tf_op jit(solution)/shard_map/ppermute | solution.py:293
  13.4 8.6 %collective-permute-start.6 = (f32[64,64]{1,0:T(8,128)S(1)}, f32[64,64]{1,0:T(8,128)S(1)}, u32[]{:S(2)}, u32[]{:S(2)}) collective-permute-start(f32[64,64]{1,0:T(8,128)S(1)} %get-tuple-element.23), channel_id=1, source_target_pairs={{0,48},{8,56},{16,32},{24,40},{32,16},{40,24},{48,0},{56,8},{64,11... | collective-permute-start | bytes 49160 | tf_op jit(solution)/shard_map/ppermute | solution.py:293
  13.4 12.3 %collective-permute-start = (f32[64,64]{1,0:T(8,128)S(1)}, f32[64,64]{1,0:T(8,128)S(1)}, u32[]{:S(2)}, u32[]{:S(2)}) collective-permute-start(f32[64,64]{1,0:T(8,128)S(1)} %get-tuple-element.22), channel_id=1, source_target_pairs={{0,1},{1,0},{2,3},{3,2},{4,5},{5,4},{6,7},{7,6},{8,9},{9,8},{10,11... | collective-permute-start | bytes 49160 | tf_op jit(solution)/shard_map/ppermute | solution.py:293
  13.7 12.0 %collective-permute-start.1 = (f32[64,64]{1,0:T(8,128)S(1)}, f32[64,64]{1,0:T(8,128)S(1)}, u32[]{:S(2)}, u32[]{:S(2)}) collective-permute-start(f32[64,64]{1,0:T(8,128)S(1)} %get-tuple-element.22), channel_id=1, source_target_pairs={{0,2},{1,3},{2,0},{3,1},{4,6},{5,7},{6,4},{7,5},{8,10},{9,11},{10,... | collective-permute-start | bytes 49160 | tf_op jit(solution)/shard_map/ppermute | solution.py:293
  15.8 23.4 %all-to-all-start = ((f16[8,512,128]{2,1,0:T(8,128)(2,1)}), f16[8,512,128]{2,1,0:T(8,128)(2,1)S(1)}, u32[]{:S(2)}, u32[]{:S(2)}) async-start(f16[8,512,128]{2,1,0:T(8,128)(2,1)} %bitcast.3), calls=%async_computation | async-start | bytes 2097152 | tf_op jit(solution)/shard_map/all_to_all | solution.py:328
  20.8 12.3 %collective-permute-start.2 = (f32[64,64]{1,0:T(8,128)S(1)}, f32[64,64]{1,0:T(8,128)S(1)}, u32[]{:S(2)}, u32[]{:S(2)}) collective-permute-start(f32[64,64]{1,0:T(8,128)S(1)} %get-tuple-element.22), channel_id=1, source_target_pairs={{0,3},{1,2},{2,1},{3,0},{4,7},{5,6},{6,5},{7,4},{8,11},{9,10},{10,... | collective-permute-start | bytes 49160 | tf_op jit(solution)/shard_map/ppermute | solution.py:293
  22.0 12.5 %collective-permute-start.7 = (f32[64,64]{1,0:T(8,128)S(1)}, f32[64,64]{1,0:T(8,128)S(1)}, u32[]{:S(2)}, u32[]{:S(2)}) collective-permute-start(f32[64,64]{1,0:T(8,128)S(1)} %add_add_fusion), channel_id=1, source_target_pairs={{0,64},{8,72},{16,80},{24,88},{32,96},{40,104},{48,112},{56,120},{... | collective-permute-start | bytes 49160 | tf_op jit(solution)/shard_map/ppermute | solution.py:293
  33.2 3.2 %collective-permute-start.3 = (f32[64,64]{1,0:T(8,128)S(1)}, f32[64,64]{1,0:T(8,128)S(1)}, u32[]{:S(2)}, u32[]{:S(2)}) collective-permute-start(f32[64,64]{1,0:T(8,128)S(1)} %add_add_fusion.1), channel_id=1, source_target_pairs={{0,4},{1,5},{2,6},{3,7},{4,0},{5,1},{6,2},{7,3},{8,12},{9,13},{10,... | collective-permute-start | bytes 49160 | tf_op jit(solution)/shard_map/ppermute | solution.py:293
  34.5 1.9 %collective-permute-start.8 = (f32[64,64]{1,0:T(8,128)S(1)}, f32[64,64]{1,0:T(8,128)S(1)}, u32[]{:S(2)}, u32[]{:S(2)}) collective-permute-start(f32[64,64]{1,0:T(8,128)S(1)} %add.46), channel_id=1, source_target_pairs={{0,8},{8,0},{16,24},{24,16},{32,40},{40,32},{48,56},{56,48},{64,72... | collective-permute-start | bytes 49160 | tf_op jit(solution)/shard_map/ppermute | solution.py:293
  36.4 2.9 %copy-start.7 = (f32[64,64]{1,0:T(8,128)S(1)}, f32[64,64]{1,0:T(8,128)}, u32[]{:S(2)}) copy-start(f32[64,64]{1,0:T(8,128)} %mix_ref.1) | copy-start | bytes 49156
  60.5 4.4 %copy-start.3 = (f32[8,128,128]{2,1,0:T(8,128)}, f32[8,128,128]{2,1,0:T(8,128)S(1)}, u32[]{:S(2)}) copy-start(f32[8,128,128]{2,1,0:T(8,128)S(1)} %all_to_all.25.got_ref) | copy-start | bytes 1572868
  60.5 26.1 %all-to-all-start.2 = ((bf16[8,512,128]{2,1,0:T(8,128)(2,1)}), bf16[8,512,128]{2,1,0:T(8,128)(2,1)S(1)}, u32[]{:S(2)}, u32[]{:S(2)}) async-start(bf16[8,512,128]{2,1,0:T(8,128)(2,1)} %get-tuple-element.27), calls=%async_computation.2 | async-start | bytes 2097152 | tf_op jit(solution)/shard_map/all_to_all | solution.py:350
  64.9 4.2 %collective-permute-start.10 = (f32[32,128]{1,0:T(8,128)S(1)}, f32[32,128]{1,0:T(8,128)S(1)}, u32[]{:S(2)}, u32[]{:S(2)}) collective-permute-start(f32[32,128]{1,0:T(8,128)S(1)} %shard_map.98), channel_id=1, source_target_pairs={{0,32},{8,40},{16,48},{24,56},{32,0},{40,8},{48,16},{56,24},{64,96... | collective-permute-start | bytes 49160 | tf_op jit(solution)/shard_map/ppermute | solution.py:293
  66.6 3.8 %collective-permute-start.11 = (f32[32,128]{1,0:T(8,128)S(1)}, f32[32,128]{1,0:T(8,128)S(1)}, u32[]{:S(2)}, u32[]{:S(2)}) collective-permute-start(f32[32,128]{1,0:T(8,128)S(1)} %shard_map.98), channel_id=1, source_target_pairs={{0,48},{8,56},{16,32},{24,40},{32,16},{40,24},{48,0},{56,8},{64,11... | collective-permute-start | bytes 49160 | tf_op jit(solution)/shard_map/ppermute | solution.py:293
  67.7 2.9 %collective-permute-start.9 = (f32[32,128]{1,0:T(8,128)S(1)}, f32[32,128]{1,0:T(8,128)S(1)}, u32[]{:S(2)}, u32[]{:S(2)}) collective-permute-start(f32[32,128]{1,0:T(8,128)S(1)} %shard_map.98), channel_id=1, source_target_pairs={{0,16},{8,24},{16,0},{24,8},{32,48},{40,56},{48,32},{56,40},{64,80... | collective-permute-start | bytes 49160 | tf_op jit(solution)/shard_map/ppermute | solution.py:293
  70.6 8.3 %collective-permute-start.12 = (f32[32,128]{1,0:T(8,128)S(1)}, f32[32,128]{1,0:T(8,128)S(1)}, u32[]{:S(2)}, u32[]{:S(2)}) collective-permute-start(f32[32,128]{1,0:T(8,128)S(1)} %add_add_fusion.2), channel_id=1, source_target_pairs={{0,64},{8,72},{16,80},{24,88},{32,96},{40,104},{48,112},{56,120},{... | collective-permute-start | bytes 49160 | tf_op jit(solution)/shard_map/ppermute | solution.py:293
  78.9 7.7 %copy-start.6 = (s32[32]{0:T(128)S(1)}, s32[32]{0:T(128)}, u32[]{:S(2)}) copy-start(s32[32]{0:T(128)} %visits_ref.3) | copy-start | bytes 388
  78.9 7.7 %copy-start.2 = (bf16[1,1,16,128,512]{4,3,2,1,0:T(8,128)(2,1)S(1)}, bf16[1,1,16,128,512]{4,3,2,1,0:T(8,128)(2,1)}, u32[]{:S(2)}) copy-start(bf16[1,1,16,128,512]{4,3,2,1,0:T(8,128)(2,1)} %param.7) | copy-start | bytes 6291460
  78.9 2.0 %collective-permute-start.13 = (f32[32,128]{1,0:T(8,128)S(1)}, f32[32,128]{1,0:T(8,128)S(1)}, u32[]{:S(2)}, u32[]{:S(2)}) collective-permute-start(f32[32,128]{1,0:T(8,128)S(1)} %add.51.sum_a), channel_id=1, source_target_pairs={{0,8},{8,0},{16,24},{24,16},{32,40},{40,32},{48,56},{56,48},{64,72... | collective-permute-start | bytes 49160 | tf_op jit(solution)/shard_map/ppermute | solution.py:293
  80.9 1.0 copy-start.4
  86.6 0.8 copy-start.9
  90.7 2.8 %collective-permute-start.14 = (f32[8,64,512]{2,1,0:T(8,128)S(1)}, f32[8,64,512]{2,1,0:T(8,128)S(1)}, u32[]{:S(2)}, u32[]{:S(2)}) collective-permute-start(f32[8,64,512]{2,1,0:T(8,128)S(1)} %get-tuple-element.33), channel_id=1, source_target_pairs={{0,8},{8,0},{16,24},{24,16},{32,40},{40,32},{48,56},{56,48},{64,72... | collective-permute-start | bytes 3145736 | tf_op jit(solution)/shard_map/ppermute | solution.py:293
  91.1 2.3 %collective-permute-start.15 = (f32[32,128]{1,0:T(8,128)S(1)}, f32[32,128]{1,0:T(8,128)S(1)}, u32[]{:S(2)}, u32[]{:S(2)}) collective-permute-start(f32[32,128]{1,0:T(8,128)S(1)} %get-tuple-element.34.gram_a), channel_id=1, source_target_pairs={{0,8},{8,0},{16,24},{24,16},{32,40},{40,32},{48,56},{56,48},{64,72... | collective-permute-start | bytes 49160 | tf_op jit(solution)/shard_map/ppermute | solution.py:293
  127.3 3.9 %collective-permute-start.16 = (bf16[8,64,512]{2,1,0:T(8,128)(2,1)S(1)}, bf16[8,64,512]{2,1,0:T(8,128)(2,1)S(1)}, u32[]{:S(2)}, u32[]{:S(2)}) collective-permute-start(bf16[8,64,512]{2,1,0:T(8,128)(2,1)S(1)} %all_to_all.27.mine_ref), channel_id=1, source_target_pairs={{0,8},{8,0},{16,24},{24,16},{32,40},{40,32},{48,56},{56,48},{64,72... | collective-permute-start | bytes 1572872 | tf_op jit(solution)/shard_map/ppermute | solution.py:293

commit v4 on v3

--- a/solution.py
+++ b/solution.py
@@ -1,3 +1,5 @@
+import functools
+
 import jax
 import jax.numpy as jnp
 from jax import lax
@@ -11,6 +13,7 @@
 epsilon = 1e-06
 F32, BF16, F16 = jnp.float32, jnp.bfloat16, jnp.float16
 VM = pl.BlockSpec(memory_space=pltpu.VMEM)
+HBM = pl.BlockSpec(memory_space=pl.ANY)
 SM = pl.BlockSpec(memory_space=pltpu.SMEM)
 PARAMS = pltpu.CompilerParams(vmem_limit_bytes=48 * 1024 * 1024)
 
@@ -114,36 +117,45 @@
 
 
 def live_rows(t, list_ref, count_ref, visits_ref, tile_rows):
-    k, b, g = list_ref[0, t], list_ref[1, t], list_ref[2, t]
+    k, b, g = list_ref[0, 0, 0, t], list_ref[0, 0, 1, t], list_ref[0, 0, 2, t]
     kept = jnp.where(t < count_ref[0, 0], visits_ref[k] - tile_rows * b, 0)
     return k, b, g, kept
 
 
-def products_kernel(list_ref, count_ref, visits_ref, tile_ref, code_ref, out_ref):
+def products_kernel(
+    list_ref, count_ref, visits_ref, tile_hbm, code_hbm, out_ref, acc_ref, tile_ref, code_ref, sems
+):
     slots, rows, cols = tile_ref.shape
     rank = code_ref.shape[0]
-    out_ref[...] = jnp.zeros(out_ref.shape, F32)
+    parts = sems.shape[0] - 1
+    each = slots // parts
+    code_copy = pltpu.make_async_copy(code_hbm, code_ref, sems.at[parts])
+    code_copy.start()
+    copies = []
+    for i in range(parts):
+        at = pl.ds(i * each, each)
+        copies.append(pltpu.make_async_copy(tile_hbm.at[0, 0, at], tile_ref.at[at], sems.at[i]))
+        copies[-1].start()
+    acc_ref[...] = jnp.zeros(acc_ref.shape, F32)
     lane = lax.broadcasted_iota(jnp.int32, (rank, rows), 1)
+    code_copy.wait()
     for t in range(slots):
+        if t % each == 0:
+            copies[t // each].wait()
         k, b, g, kept = live_rows(t, list_ref, count_ref, visits_ref, rows)
         codes = code_ref[:, pl.ds(pl.multiple_of(g * cols, cols), cols)].astype(BF16)
         part = mm16(codes, tile_ref[t], NT)
-        out_ref[k * VBLOCKS + b] += jnp.where(lane < kept, part, 0.0)
-
-
-def gram_kernel(code_ref, weight_ref, code_gram_ref, weight_gram_ref):
+        acc_ref[k * VBLOCKS + b] += jnp.where(lane < kept, part, 0.0)
+    out_ref[...] = acc_ref[...].astype(out_ref.dtype)
+
+
+def gram_kernel(code_ref, out_ref):
     high, low = split(code_ref[...])
     cross = mm16(high, low, NT)
-    code_gram_ref[...] = mm16(high, high, NT) + cross + cross.T
-    weight = weight_ref[...]
-    weight_gram_ref[...] = mm(weight, weight, TN)
-
-
-def inverse_kernel(a_ref, b_ref, out_ref):
-    out_ref[...] = damped_inverse(a_ref[...] * b_ref[...])
-
-
-def polar_kernel(at_ref, prod_ref, mix_ref, weight_ref, proj_ref, polar_ref):
+    out_ref[...] = halves(mm16(high, high, NT) + cross + cross.T)
+
+
+def polar_kernel(at_ref, prod_ref, mix_ref, weight_ref, gram_ref, proj_ref, polar_ref):
     dests = polar_ref.shape[0]
     segs, rank, rows = prod_ref.shape
     own = segs // VBLOCKS
@@ -163,6 +175,7 @@
     polar = [z.astype(BF16) for z in zs]
     low = rank // 2
     for d in range(dests):
+        proj_ref[d, own * low :, :] = gram_ref[...]
         for j in range(own):
             proj_ref[d, j * low : (j + 1) * low, :] = projected[j]
             for b in range(VBLOCKS):
@@ -172,33 +185,42 @@
 
 def partial_kernel(got_ref, weight_ref, out_ref):
     sources = got_ref.shape[0]
-    low = out_ref.shape[0]
+    low = out_ref.shape[0] // 2
     weight = weight_ref[...]
     twice = jnp.concatenate([weight, weight], axis=1)
     own = weight.shape[0] // sources
-    total = jnp.zeros(out_ref.shape, F32)
+    total = jnp.zeros((low, out_ref.shape[1]), F32)
     for d in range(sources):
         for j in range(own):
             k = d * own + j
             total += got_ref[d, j * low : (j + 1) * low, :] * twice[k : k + 1, :]
-    out_ref[...] = total
+    out_ref[:low, :] = total
+    out_ref[low:, :] = halves(mm(weight, weight, TN))
+
+
+def whole(x):
+    rank = x.shape[1] // 2
+    return jnp.concatenate([x[:, :rank], x[:, rank:]], axis=0)
 
 
 def mix_kernel(
-    place_ref, sum_a, sum_b, inverse_ref, code_gram_ref, got_ref,
-    mix_ref, mgram_ref, weight_ref, wgram_ref, own_ref,
+    place_ref, sum_a, sum_b, got_ref, mix_ref, mgram_ref, weight_ref, wgram_ref, own_ref
 ):
     sources = got_ref.shape[0]
     rank = mix_ref.shape[0]
     own = own_ref.shape[0]
     low = rank // 2
-    sums = sum_a[...] + sum_b[...]
-    numer = jnp.concatenate([sums[:, :rank], sums[:, rank:]], axis=0)
-    mix = mm(numer, inverse_ref[...])
+    code_gram = got_ref[0, own * low :, :]
+    for d in range(1, sources):
+        code_gram += got_ref[d, own * low :, :]
+    code_gram = whole(code_gram)
+    numer = whole(sum_a[:low, :] + sum_b[:low, :])
+    weight_gram = whole(sum_a[low:, :] + sum_b[low:, :])
+    mix = mm(numer, damped_inverse(code_gram * weight_gram))
     mix_ref[...] = mix
     mix_gram = mm(mix, mix, TN)
     mgram_ref[...] = mix_gram
-    inverse = damped_inverse(mix_gram * code_gram_ref[...])
+    inverse = damped_inverse(mix_gram * code_gram)
     beside = halves(mix)
     terms = []
     for d in range(sources):
@@ -256,32 +278,37 @@
             total += got_ref[d, i].astype(F32)
         sums.append(total)
     low = sums[slabs].shape[0] // 2
-    gram = sums[slabs][:low] + sums[slabs][low:]
-    rank = mgram_ref.shape[0]
-    gram = jnp.concatenate([gram[:, :rank], gram[:, rank:]], axis=0)
+    gram = whole(sums[slabs][:low] + sums[slabs][low:])
     inverse = damped_inverse(mgram_ref[...] * gram)
     code = jnp.maximum(mm(inverse, jnp.concatenate(sums[:slabs], axis=1)), 0.0).astype(BF16)
     for d in range(sources):
         out_ref[d] = code
 
 
-def place_kernel(place_ref, mine_ref, came_ref, out_ref):
-    parity = place_ref[1]
-    cols = mine_ref.shape[2]
-    for j in range(mine_ref.shape[0]):
+def place_kernel(flip, place_ref, from_ref, *refs):
+    out_hbm, wide_ref, sems = refs[-3:]
+    parity = place_ref[1] if not flip else 1 - place_ref[1]
+    cols = from_ref.shape[2]
+    copies = []
+    for j in range(from_ref.shape[0]):
+        wide_ref[j] = from_ref[j].astype(F32)
         at = pl.multiple_of((2 * j + parity) * cols, cols)
-        out_ref[:, pl.ds(at, cols)] = mine_ref[j].astype(F32)
-        at = pl.multiple_of((2 * j + 1 - parity) * cols, cols)
-        out_ref[:, pl.ds(at, cols)] = came_ref[j].astype(F32)
-
-
-def call(kernel, outs, specs, args, scratch=(), flops=1e9):
+        copies.append(
+            pltpu.make_async_copy(wide_ref.at[j], out_hbm.at[:, pl.ds(at, cols)], sems.at[j])
+        )
+        copies[-1].start()
+    for copy in copies:
+        copy.wait()
+
+
+def call(kernel, outs, specs, args, scratch=(), flops=1e9, spec=VM, alias=None):
     many = isinstance(outs, tuple)
     return pl.pallas_call(
         kernel,
         out_shape=outs,
         in_specs=specs,
-        out_specs=(VM,) * len(outs) if many else VM,
+        out_specs=(spec,) * len(outs) if many else spec,
+        input_output_aliases=alias or {},
         scratch_shapes=scratch,
         compiler_params=PARAMS,
         cost_estimate=pl.CostEstimate(flops=int(flops), bytes_accessed=65536, transcendentals=0),
@@ -299,15 +326,8 @@
     return x
 
 
-def sum_pat(x):
-    x = plus(x, [swap(x, "pat", bit) for bit in (2, 4, 6)])
-    x = x + swap(x, "pat", 8)
-    return x + swap(x, "pat", 1)
-
-
 def body(tile_data, tile_list, tile_count, visit_counts, code_factor_t, visit_mix, patient_weight):
     tiles = tile_data[0, 0]
-    listing = tile_list[0, 0]
     slots, rows, cols = tiles.shape
     rank = visit_mix.shape[0]
     patients = visit_counts.shape[0]
@@ -320,35 +340,30 @@
     square = shape((rank, rank), F32)
 
     partial = call(
-        products_kernel, shape((patients * VBLOCKS, rank, rows), F32),
-        [SM, SM, SM, VM, VM], (listing, tile_count, visit_counts, tiles, code_factor_t),
+        products_kernel, shape((patients * VBLOCKS, rank, rows), F32), [SM, SM, SM, HBM, HBM],
+        (tile_list, tile_count, visit_counts, tile_data, code_factor_t),
+        [
+            pltpu.VMEM((patients * VBLOCKS, rank, rows), F32), pltpu.VMEM(tiles.shape, BF16),
+            pltpu.VMEM(code_factor_t.shape, F32), pltpu.SemaphoreType.DMA((5,)),
+        ],
     )
     sent = partial.astype(F16).reshape(n_code, own * VBLOCKS * rank, rows)
-    sent, weight_after = lax.optimization_barrier((sent, patient_weight))
     got = lax.all_to_all(sent, "code", 0, 0, tiled=True)
-    code_gram, weight_gram = call(
-        gram_kernel, (square, square), [VM, VM], (code_factor_t, weight_after)
-    )
-    code_gram = plus(code_gram, [swap(code_gram, "code", bit) for bit in (1, 2, 3)])
-    code_gram = code_gram + swap(code_gram, "code", 4)
-    inverse_mix = call(
-        inverse_kernel, square, [VM, VM], (code_gram, sum_pat(weight_gram)), flops=4e9
-    )
-    got, inverse_mix = lax.optimization_barrier((got, inverse_mix))
+    gram = call(gram_kernel, shape((rank // 2, 2 * rank), F32), [VM], (code_factor_t,))
     products = jnp.sum(got.astype(F32), axis=0).reshape(own * VBLOCKS, rank, rows)
 
     proj, polar = call(
         polar_kernel,
         (
-            shape((n_code, own * rank // 2, 2 * rank), F32),
+            shape((n_code, (own + 1) * rank // 2, 2 * rank), F32),
             shape((n_code, own * VBLOCKS * rank, rows), BF16),
         ),
-        [SM, VM, VM, VM], (place, products, visit_mix, patient_weight), flops=5e9,
+        [SM, VM, VM, VM, VM], (place, products, visit_mix, patient_weight, gram), flops=5e9,
     )
     proj = lax.all_to_all(proj, "code", 0, 0, tiled=True)
     proj, polar = lax.optimization_barrier((proj, polar))
     polar = lax.all_to_all(polar, "code", 0, 0, tiled=True)
-    sums = call(partial_kernel, shape((rank // 2, 2 * rank), F32), [VM, VM], (proj, patient_weight))
+    sums = call(partial_kernel, shape((rank, 2 * rank), F32), [VM, VM], (proj, patient_weight))
     sums = plus(sums, [swap(sums, "pat", bit) for bit in (2, 4, 6)])
     sums = sums + swap(sums, "pat", 8)
     mix_new, mix_gram, weights, wgram, weight_new = call(
@@ -357,13 +372,13 @@
             square, square, shape((patients, rank), F32),
             shape((rank // 2, 2 * rank), F32), shape((own, rank), F32),
         ),
-        [SM] + [VM] * 5,
-        (place, sums, swap(sums, "pat", 1), inverse_mix, code_gram, proj), flops=5e9,
+        [SM] + [VM] * 3,
+        (place, sums, swap(sums, "pat", 1), proj), flops=8e9,
     )
     block = shape((half, rank, cols), F32)
     keep, send = call(
         numer_kernel, (block, block), [SM, SM, SM, SM, VM, VM, VM, VM],
-        (place, listing, tile_count, visit_counts, polar, mix_new, weights, tiles),
+        (place, tile_list, tile_count, visit_counts, polar, mix_new, weights, tiles),
         [pltpu.VMEM((n_pat, rank, cols), F32)], flops=4e9,
     )
     groups = [[core + 2 * i for i in range(half)] for core in (0, 1)]
@@ -380,9 +395,16 @@
         factor_kernel, shape((half, rank, cols), BF16), [VM, VM], (exchange(packed), mix_gram)
     )
     mine = exchange(code)
+    place_scratch = [pltpu.VMEM(mine.shape, F32), pltpu.SemaphoreType.DMA((half,))]
+    result = shape((rank, n_pat * cols), F32)
+    came = swap(mine, "pat", 1)
     code_new = call(
-        place_kernel, shape((rank, n_pat * cols), F32),
-        [SM, VM, VM], (place, mine, swap(mine, "pat", 1)),
+        functools.partial(place_kernel, False), result, [SM, VM], (place, mine), place_scratch,
+        spec=HBM,
+    )
+    code_new = call(
+        functools.partial(place_kernel, True), result, [SM, VM, HBM], (place, came, code_new),
+        place_scratch, spec=HBM, alias={2: 0},
     )
     return (code_new, mix_new, weight_new)
 

time: 135 us -> 132 us (0.978)
  waiting for transfers between devices: 21.7 us -> 18.7 us
  Pallas kernels: 25.1 us -> 27.7 us
  starting transfers between devices: 32 us -> 30.3 us
  blocking collectives: 46 us -> 44.5 us
    ppermute x17 -> x8, waiting for transfers between devices: 21.7 us -> 5.91 us  [swap(): return lax.ppermute(x, axis, [(i, i ^ bit) for i in range(size)])]
    all_to_all x1, waiting for transfers between devices: 0.01 us -> 12.8 us  [body(): got = lax.all_to_all(sent, 'code', 0, 0, tiled=True)]
    ppermute x17 -> x8, starting transfers between devices: 22.8 us -> 19.8 us  [swap(): return lax.ppermute(x, axis, [(i, i ^ bit) for i in range(size)])]
    pallas_call x10, Pallas kernels: 25.1 us -> 27.7 us  [call(): pl.pallas_call(kernel, out_shape=outs, in_specs=specs, out_specs=(spec,)...]
    all_to_all x1, blocking collectives: 15.3 us -> 14 us  [body(): proj = lax.all_to_all(proj, 'code', 0, 0, tiled=True)]
  transfers between devices with their start and end apart: 19 -> 10, of which waited for: 9 -> 4; matrix products, arithmetic and copies ran while one was open for 0% -> 0% of each run, Pallas kernels for 6% -> 8%
where the time goes in v4:
time: 132 us; the launch traced here: 131 us
  blocking collectives  44.5 us (34%)
  starting transfers between devices  30.3 us (23%)
  Pallas kernels  27.7 us (21%)
  waiting for transfers between devices  18.7 us (14%)
  local copies, waits for them, and re-layouts  5.67 us (4%)
  other arithmetic  2.7 us (2%)
  between operations  1.57 us (1%)
    all_to_all x2, blocking collectives, exchange(): return lax.all_to_all(x, 'pat', 0, 0, axis_index_groups=groups, tiled=True)  30.5 us
    pallas_call x10, Pallas kernels, call(): pl.pallas_call(kernel, out_shape=outs, in_specs=specs, out_specs=(spec,)...  27.7 us
    ppermute x8, starting transfers between devices, swap(): return lax.ppermute(x, axis, [(i, i ^ bit) for i in range(size)])  19.8 us
    all_to_all x1, blocking collectives, body(): proj = lax.all_to_all(proj, 'code', 0, 0, tiled=True)  14 us
    all_to_all x1, waiting for transfers between devices, body(): got = lax.all_to_all(sent, 'code', 0, 0, tiled=True)  12.8 us
    ppermute x8, waiting for transfers between devices, swap(): return lax.ppermute(x, axis, [(i, i ^ bit) for i in range(size)])  5.91 us
    unnamed x21, local copies, waits for them, and re-layouts  5.67 us
    all_to_all x1, starting transfers between devices, body(): got = lax.all_to_all(sent, 'code', 0, 0, tiled=True)  5.63 us
  transfers between devices with their start and end apart: 10, of which 4 were waited for; matrix products, arithmetic and copies ran while one was open for 0% of the time, Pallas kernels for 8%

profile of v4, /device:TPU:3, one launch (start us, length us, event | category | flops | bytes accessed | tf_op | source)
XLA Modules:
  0.0 131.1 jit_solution(1518369531727104090)
XLA Ops:
  1.3 0.7 copy.12.list_ref
  2.0 1.6 %copy-done.1 = bf16[1,1,16,128,512]{4,3,2,1,0:T(8,128)(2,1)S(1)} copy-done((bf16[1,1,16,128,512]{4,3,2,1,0:T(8,128)(2,1)S(1)}, bf16[1,1,16,128,512]{4,3,2,1,0:T(8,128)(2,1)}, u32[]{:S(2)}) %copy-start.1) | copy-done | bytes 2097176
  3.6 0.7 copy-done.5
  4.2 3.5 %shard_map.94 = f32[64,64,128]{2,1,0:T(8,128)S(1)} custom-call(s32[1,1,3,16]{3,2,1,0:T(4,128)S(1)} %copy.12.list_ref, s32[1,1]{1,0:T(1,128)S(6)} %copy.14.count_ref, s32[32]{0:T(128)S(1)} %copy-done.5, bf16[1,1,16,128,512]{4,3,2,1,0:T(8,128)(2,1)S(1)} %copy-done.1, f32[64,8192]{1,0:T(8,128)} %code_ref.1), custom_call_target="tpu_custom_call" | custom-call | flops 1000000000 | bytes 65536 | tf_op jit(solution)/shard_map/pallas_call | solution.py:306
  7.8 0.0 copy-start
  7.8 1.2 convert_element_type.6
  9.0 5.6 %all-to-all-start = ((f16[8,512,128]{2,1,0:T(8,128)(2,1)}), f16[8,512,128]{2,1,0:T(8,128)(2,1)}, u32[]{:S(2)}, u32[]{:S(2)}) async-start(f16[8,512,128]{2,1,0:T(8,128)(2,1)} %bitcast.2), calls=%async_computation | async-start | bytes 2097152 | tf_op jit(solution)/shard_map/all_to_all | solution.py:351
  14.6 0.0 copy-done
  14.6 0.8 shard_map.95.gram_ref
  15.5 0.1 pad_add_fusion.at_ref.place_ref
  15.5 12.8 %all-to-all-done = f16[8,512,128]{2,1,0:T(8,128)(2,1)} async-done(((f16[8,512,128]{2,1,0:T(8,128)(2,1)}), f16[8,512,128]{2,1,0:T(8,128)(2,1)}, u32[]{:S(2)}, u32[]{:S(2)}) %all-to-all-start) | async-done | bytes 1048608 | tf_op jit(solution)/shard_map/all_to_all | solution.py:351
  28.3 1.4 %convert_reduce_fusion = f32[512,128]{1,0:T(8,128)S(1)} fusion(f16[8,512,128]{2,1,0:T(8,128)(2,1)} %all-to-all-done), kind=kLoop, calls=%fused_computation | loop fusion | flops 983040 | bytes 1310720 | tf_op jit(solution)/shard_map/reduce_sum | solution.py:353
  29.7 0.0 copy-done.7
  29.7 0.0 copy-done.8
  29.7 5.9 %shard_map.96 = (f32[8,160,128]{2,1,0:T(8,128)S(1)}, bf16[8,512,128]{2,1,0:T(8,128)(2,1)}) custom-call(s32[2]{0:T(128)S(1)} %pad_add_fusion.at_ref.place_ref, f32[8,64,128]{2,1,0:T(8,128)S(1)} %bitcast.6, f32[64,64]{1,0:T(8,128)S(1)} %copy-done.7, f32[32,64]{1,0:T(8,128)S(1)} %copy-done.8, f32[32,128]{1,0:T(8,128)S(1)} %shard_map.95.gram_ref), custom_call_target="tpu_custom_call" | custom-call | flops 5000000000 | bytes 65536 | tf_op jit(solution)/shard_map/pallas_call | solution.py:306
  35.6 14.0 %all_to_all.25.got_ref = f32[8,160,128]{2,1,0:T(8,128)S(1)} all-to-all(f32[8,160,128]{2,1,0:T(8,128)S(1)} %get-tuple-element.14), channel_id=1, replica_groups=mesh['pat'=16,'code'=8] {'code'}, dimensions={0} | all-to-all | bytes 1310720 | tf_op jit(solution)/shard_map/all_to_all | solution.py:363
  49.6 0.3 shard_map.97
  49.9 0.9 copy-done.3
  50.8 2.8 %collective-permute-start.2 = (f32[64,128]{1,0:T(8,128)S(1)}, f32[64,128]{1,0:T(8,128)S(1)}, u32[]{:S(2)}, u32[]{:S(2)}) collective-permute-start(f32[64,128]{1,0:T(8,128)S(1)} %shard_map.97), channel_id=1, source_target_pairs={{0,48},{8,56},{16,32},{24,40},{32,16},{40,24},{48,0},{56,8},{64,11... | collective-permute-start | bytes 98312 | tf_op jit(solution)/shard_map/ppermute | solution.py:320
  53.6 0.3 collective-permute-start.1
  53.9 0.2 collective-permute-start
  54.1 4.8 %all-to-all-start.2 = ((bf16[8,512,128]{2,1,0:T(8,128)(2,1)}), bf16[8,512,128]{2,1,0:T(8,128)(2,1)S(1)}, u32[]{:S(2)}, u32[]{:S(2)}) async-start(bf16[8,512,128]{2,1,0:T(8,128)(2,1)} %get-tuple-element.16), calls=%async_computation.2 | async-start | bytes 2097152 | tf_op jit(solution)/shard_map/all_to_all | solution.py:365
  59.0 0.0 collective-permute-done.2
  59.0 0.0 collective-permute-done.1
  59.0 0.0 collective-permute-done
  59.0 3.4 %collective-permute-start.3 = (f32[64,128]{1,0:T(8,128)S(1)}, f32[64,128]{1,0:T(8,128)S(1)}, u32[]{:S(2)}, u32[]{:S(2)}) collective-permute-start(f32[64,128]{1,0:T(8,128)S(1)} %add_add_fusion), channel_id=1, source_target_pairs={{0,64},{8,72},{16,80},{24,88},{32,96},{40,104},{48,112},{56,120},{... | collective-permute-start | bytes 98312 | tf_op jit(solution)/shard_map/ppermute | solution.py:320
  62.4 2.9 %collective-permute-done.3 = f32[64,128]{1,0:T(8,128)S(1)} collective-permute-done((f32[64,128]{1,0:T(8,128)S(1)}, f32[64,128]{1,0:T(8,128)S(1)}, u32[]{:S(2)}, u32[]{:S(2)}) %collective-permute-start.3) | collective-permute-done | bytes 32800 | tf_op jit(solution)/shard_map/ppermute | solution.py:320
  65.3 10.2 %collective-permute-start.4 = (f32[64,128]{1,0:T(8,128)S(1)}, f32[64,128]{1,0:T(8,128)S(1)}, u32[]{:S(2)}, u32[]{:S(2)}) collective-permute-start(f32[64,128]{1,0:T(8,128)S(1)} %add.15.sum_a), channel_id=1, source_target_pairs={{0,8},{8,0},{16,24},{24,16},{32,40},{40,32},{48,56},{56,48},{64,72... | collective-permute-start | bytes 98312 | tf_op jit(solution)/shard_map/ppermute | solution.py:320
  75.5 0.9 collective-permute-done.4.sum_b
  76.3 1.1 copy-done.4
  77.4 7.4 %shard_map.98 = (f32[64,64]{1,0:T(8,128)}, f32[64,64]{1,0:T(8,128)S(1)}, f32[32,64]{1,0:T(8,128)S(1)}, f32[32,128]{1,0:T(8,128)S(1)}, f32[4,64]{1,0:T(4,128)}) custom-call(s32[2]{0:T(128)S(1)} %pad_add_fusion.at_ref.place_ref, f32[64,128]{1,0:T(8,128)S(1)} %add.15.sum_a, f32[64,128]{1,0:T(8,128)S(1)} %collective-permute-done.4.sum_b, ...), custom_call_target="tpu_custom_call" | custom-call | flops 8000000000 | bytes 65536 | tf_op jit(solution)/shard_map/pallas_call | solution.py:306
  84.9 0.0 all-to-all-done.2.got_ref
  84.9 0.0 copy-done.2
  84.9 0.0 copy-start.9
  84.9 0.7 copy-done.9
  85.6 3.3 %shard_map.99 = (f32[8,64,512]{2,1,0:T(8,128)S(1)}, f32[8,64,512]{2,1,0:T(8,128)S(1)}) custom-call(s32[2]{0:T(128)S(1)} %pad_add_fusion.at_ref.place_ref, s32[1,1,3,16]{3,2,1,0:T(4,128)S(1)} %copy.12.list_ref, s32[1,1]{1,0:T(1,128)S(6)} %copy.14.count_ref, s32[32]{0:T(128)S(1)} %copy-done.6, bf16[8,512,128]{2,1,0:T(8,128)(2,1)S(1)} %all-to-all-done.2.got_ref, ...), custom_call_target="tpu_custom_call" | custom-call | flops 4000000000 | bytes 65536 | tf_op jit(solution)/shard_map/pallas_call | solution.py:306
  89.0 0.4 collective-permute-start.5
  89.4 0.2 collective-permute-start.6
  89.6 2.2 %collective-permute-done.6.gram_b = f32[32,128]{1,0:T(8,128)S(1)} collective-permute-done((f32[32,128]{1,0:T(8,128)S(1)}, f32[32,128]{1,0:T(8,128)S(1)}, u32[]{:S(2)}, u32[]{:S(2)}) %collective-permute-start.6) | collective-permute-done | bytes 16416 | tf_op jit(solution)/shard_map/ppermute | solution.py:320
  91.7 0.0 collective-permute-done.5.came_ref
  91.7 0.1 shard_map.100
  91.9 17.9 %all_to_all.26.got_ref = bf16[8,5,64,128]{3,2,1,0:T(8,128)(2,1)S(1)} all-to-all(bf16[8,5,64,128]{3,2,1,0:T(8,128)(2,1)S(1)} %shard_map.100), channel_id=1, replica_groups={{0,16,32,48,64,80,96,112},{8,24,40,56,72,88,104,120},{1,17,33,49,65,81,..., dimensions={0} | all-to-all | bytes 1310720 | tf_op jit(solution)/shard_map/all_to_all | solution.py:387
  109.7 3.1 %shard_map.101 = bf16[8,64,512]{2,1,0:T(8,128)(2,1)S(1)} custom-call(bf16[8,5,64,128]{3,2,1,0:T(8,128)(2,1)S(1)} %all_to_all.26.got_ref, f32[64,64]{1,0:T(8,128)S(1)} %get-tuple-element.23.mgram_ref), custom_call_target="tpu_custom_call" | custom-call | flops 1000000000 | bytes 65536 | tf_op jit(solution)/shard_map/pallas_call | solution.py:306
  112.9 12.6 %all_to_all.27.from_ref = bf16[8,64,512]{2,1,0:T(8,128)(2,1)S(1)} all-to-all(bf16[8,64,512]{2,1,0:T(8,128)(2,1)S(1)} %shard_map.101), channel_id=1, replica_groups={{0,16,32,48,64,80,96,112},{8,24,40,56,72,88,104,120},{1,17,33,49,65,81,..., dimensions={0} | all-to-all | bytes 1048576 | tf_op jit(solution)/shard_map/all_to_all | solution.py:387
  125.5 2.3 %collective-permute-start.7 = (bf16[8,64,512]{2,1,0:T(8,128)(2,1)S(1)}, bf16[8,64,512]{2,1,0:T(8,128)(2,1)S(1)}, u32[]{:S(2)}, u32[]{:S(2)}) collective-permute-start(bf16[8,64,512]{2,1,0:T(8,128)(2,1)S(1)} %all_to_all.27.from_ref), channel_id=1, source_target_pairs={{0,8},{8,0},{16,24},{24,16},{32,40},{40,32},{48,56},{56,48},{64,72... | collective-permute-start | bytes 1572872 | tf_op jit(solution)/shard_map/ppermute | solution.py:320
  127.8 1.6 %shard_map.102.refs_0_ = f32[64,8192]{1,0:T(8,128)} custom-call(s32[2]{0:T(128)S(1)} %pad_add_fusion.at_ref.place_ref, bf16[8,64,512]{2,1,0:T(8,128)(2,1)S(1)} %all_to_all.27.from_ref), custom_call_target="tpu_custom_call" | custom-call | flops 1000000000 | bytes 65536 | tf_op jit(solution)/shard_map/pallas_call | solution.py:306
  129.4 0.0 collective-permute-done.7.from_ref
  129.4 1.6 %shard_map.103 = f32[64,8192]{1,0:T(8,128)} custom-call(s32[2]{0:T(128)S(1)} %pad_add_fusion.at_ref.place_ref, bf16[8,64,512]{2,1,0:T(8,128)(2,1)S(1)} %collective-permute-done.7.from_ref, f32[64,8192]{1,0:T(8,128)} %shard_map.102.refs_0_), custom_call_target="tpu_custom_call", output_to_operand_aliasing={{}: (2, {})} | custom-call | flops 1000000000 | bytes 65536 | tf_op jit(solution)/shard_map/pallas_call | solution.py:306
  (11 shorter events, 0.0 us)
Async XLA Ops:
  2.0 1.6 %copy-start.1 = (bf16[1,1,16,128,512]{4,3,2,1,0:T(8,128)(2,1)S(1)}, bf16[1,1,16,128,512]{4,3,2,1,0:T(8,128)(2,1)}, u32[]{:S(2)}) copy-start(bf16[1,1,16,128,512]{4,3,2,1,0:T(8,128)(2,1)} %tile_hbm.1) | copy-start | bytes 6291460
  3.6 0.7 copy-start.5
  7.8 6.9 %copy-start = (f32[64,8192]{1,0:T(8,128)S(1)}, f32[64,8192]{1,0:T(8,128)}, u32[]{:S(2)}) copy-start(f32[64,8192]{1,0:T(8,128)} %code_ref.1) | copy-start | bytes 6291460
  9.0 19.3 %all-to-all-start = ((f16[8,512,128]{2,1,0:T(8,128)(2,1)}), f16[8,512,128]{2,1,0:T(8,128)(2,1)}, u32[]{:S(2)}, u32[]{:S(2)}) async-start(f16[8,512,128]{2,1,0:T(8,128)(2,1)} %bitcast.2), calls=%async_computation | async-start | bytes 2097152 | tf_op jit(solution)/shard_map/all_to_all | solution.py:351
  14.6 15.1 %copy-start.7 = (f32[64,64]{1,0:T(8,128)S(1)}, f32[64,64]{1,0:T(8,128)}, u32[]{:S(2)}) copy-start(f32[64,64]{1,0:T(8,128)} %mix_ref.1) | copy-start | bytes 49156
  14.6 15.1 %copy-start.8 = (f32[32,64]{1,0:T(8,128)S(1)}, f32[32,64]{1,0:T(8,128)}, u32[]{:S(2)}) copy-start(f32[32,64]{1,0:T(8,128)} %weight_ref.3) | copy-start | bytes 24580
  49.9 0.9 copy-start.3
  50.8 8.2 %collective-permute-start.2 = (f32[64,128]{1,0:T(8,128)S(1)}, f32[64,128]{1,0:T(8,128)S(1)}, u32[]{:S(2)}, u32[]{:S(2)}) collective-permute-start(f32[64,128]{1,0:T(8,128)S(1)} %shard_map.97), channel_id=1, source_target_pairs={{0,48},{8,56},{16,32},{24,40},{32,16},{40,24},{48,0},{56,8},{64,11... | collective-permute-start | bytes 98312 | tf_op jit(solution)/shard_map/ppermute | solution.py:320
  53.6 5.4 %collective-permute-start.1 = (f32[64,128]{1,0:T(8,128)S(1)}, f32[64,128]{1,0:T(8,128)S(1)}, u32[]{:S(2)}, u32[]{:S(2)}) collective-permute-start(f32[64,128]{1,0:T(8,128)S(1)} %shard_map.97), channel_id=1, source_target_pairs={{0,32},{8,40},{16,48},{24,56},{32,0},{40,8},{48,16},{56,24},{64,96... | collective-permute-start | bytes 98312 | tf_op jit(solution)/shard_map/ppermute | solution.py:320
  53.9 5.1 %collective-permute-start = (f32[64,128]{1,0:T(8,128)S(1)}, f32[64,128]{1,0:T(8,128)S(1)}, u32[]{:S(2)}, u32[]{:S(2)}) collective-permute-start(f32[64,128]{1,0:T(8,128)S(1)} %shard_map.97), channel_id=1, source_target_pairs={{0,16},{8,24},{16,0},{24,8},{32,48},{40,56},{48,32},{56,40},{64,80... | collective-permute-start | bytes 98312 | tf_op jit(solution)/shard_map/ppermute | solution.py:320
  54.1 30.7 %all-to-all-start.2 = ((bf16[8,512,128]{2,1,0:T(8,128)(2,1)}), bf16[8,512,128]{2,1,0:T(8,128)(2,1)S(1)}, u32[]{:S(2)}, u32[]{:S(2)}) async-start(bf16[8,512,128]{2,1,0:T(8,128)(2,1)} %get-tuple-element.16), calls=%async_computation.2 | async-start | bytes 2097152 | tf_op jit(solution)/shard_map/all_to_all | solution.py:365
  59.0 6.2 %collective-permute-start.3 = (f32[64,128]{1,0:T(8,128)S(1)}, f32[64,128]{1,0:T(8,128)S(1)}, u32[]{:S(2)}, u32[]{:S(2)}) collective-permute-start(f32[64,128]{1,0:T(8,128)S(1)} %add_add_fusion), channel_id=1, source_target_pairs={{0,64},{8,72},{16,80},{24,88},{32,96},{40,104},{48,112},{56,120},{... | collective-permute-start | bytes 98312 | tf_op jit(solution)/shard_map/ppermute | solution.py:320
  65.3 19.6 %copy-start.6 = (s32[32]{0:T(128)S(1)}, s32[32]{0:T(128)}, u32[]{:S(2)}) copy-start(s32[32]{0:T(128)} %visits_ref.3) | copy-start | bytes 388
  65.3 19.6 %copy-start.2 = (bf16[1,1,16,128,512]{4,3,2,1,0:T(8,128)(2,1)S(1)}, bf16[1,1,16,128,512]{4,3,2,1,0:T(8,128)(2,1)}, u32[]{:S(2)}) copy-start(bf16[1,1,16,128,512]{4,3,2,1,0:T(8,128)(2,1)} %tile_hbm.1) | copy-start | bytes 6291460
  65.3 11.1 %collective-permute-start.4 = (f32[64,128]{1,0:T(8,128)S(1)}, f32[64,128]{1,0:T(8,128)S(1)}, u32[]{:S(2)}, u32[]{:S(2)}) collective-permute-start(f32[64,128]{1,0:T(8,128)S(1)} %add.15.sum_a), channel_id=1, source_target_pairs={{0,8},{8,0},{16,24},{24,16},{32,40},{40,32},{48,56},{56,48},{64,72... | collective-permute-start | bytes 98312 | tf_op jit(solution)/shard_map/ppermute | solution.py:320
  76.3 1.1 copy-start.4
  84.9 0.8 copy-start.9
  89.0 2.8 %collective-permute-start.5 = (f32[8,64,512]{2,1,0:T(8,128)S(1)}, f32[8,64,512]{2,1,0:T(8,128)S(1)}, u32[]{:S(2)}, u32[]{:S(2)}) collective-permute-start(f32[8,64,512]{2,1,0:T(8,128)S(1)} %get-tuple-element.21), channel_id=1, source_target_pairs={{0,8},{8,0},{16,24},{24,16},{32,40},{40,32},{48,56},{56,48},{64,72... | collective-permute-start | bytes 3145736 | tf_op jit(solution)/shard_map/ppermute | solution.py:320
  89.4 2.3 %collective-permute-start.6 = (f32[32,128]{1,0:T(8,128)S(1)}, f32[32,128]{1,0:T(8,128)S(1)}, u32[]{:S(2)}, u32[]{:S(2)}) collective-permute-start(f32[32,128]{1,0:T(8,128)S(1)} %get-tuple-element.22.gram_a), channel_id=1, source_target_pairs={{0,8},{8,0},{16,24},{24,16},{32,40},{40,32},{48,56},{56,48},{64,72... | collective-permute-start | bytes 49160 | tf_op jit(solution)/shard_map/ppermute | solution.py:320
  125.5 3.9 %collective-permute-start.7 = (bf16[8,64,512]{2,1,0:T(8,128)(2,1)S(1)}, bf16[8,64,512]{2,1,0:T(8,128)(2,1)S(1)}, u32[]{:S(2)}, u32[]{:S(2)}) collective-permute-start(bf16[8,64,512]{2,1,0:T(8,128)(2,1)S(1)} %all_to_all.27.from_ref), channel_id=1, source_target_pairs={{0,8},{8,0},{16,24},{24,16},{32,40},{40,32},{48,56},{56,48},{64,72... | collective-permute-start | bytes 1572872 | tf_op jit(solution)/shard_map/ppermute | solution.py:320

commit v5 on v4

--- a/solution.py
+++ b/solution.py
@@ -15,7 +15,7 @@
 VM = pl.BlockSpec(memory_space=pltpu.VMEM)
 HBM = pl.BlockSpec(memory_space=pl.ANY)
 SM = pl.BlockSpec(memory_space=pltpu.SMEM)
-PARAMS = pltpu.CompilerParams(vmem_limit_bytes=48 * 1024 * 1024)
+MIB = 1024 * 1024
 
 
 def mm(a, b, dims=((1,), (0,))):
@@ -37,6 +37,10 @@
     return high, (x - high.astype(F32)).astype(BF16)
 
 
+def mm3(a, b, dims=((1,), (0,))):
+    return mm16(a[0], b[0], dims) + (mm16(a[0], b[1], dims) + mm16(a[1], b[0], dims))
+
+
 def fold(x):
     half = x.shape[1] // 2
     return x[:, :half] + x[:, half:]
@@ -46,29 +50,29 @@
     return [[x[i][0] * y[0][j] + x[i][1] * y[1][j] for j in (0, 1)] for i in (0, 1)]
 
 
-def flip2(x):
-    return [[x[0][0], x[1][0]], [x[0][1], x[1][1]]]
-
-
-def inverse2(x):
-    r = 1.0 / (x[0][0] * x[1][1] - x[0][1] * x[1][0])
-    return [[x[1][1] * r, -x[0][1] * r], [-x[1][0] * r, x[0][0] * r]]
-
-
 def inverse4(p):
-    a = [[p[0][0], p[0][1]], [p[0][1], p[1][1]]]
+    a = [[p[1][1], -p[0][1]], [-p[0][1], p[0][0]]]
+    det = p[0][0] * p[1][1] - p[0][1] * p[0][1]
     b = [[p[0][2], p[0][3]], [p[1][2], p[1][3]]]
-    ai = inverse2(a)
-    t = times2(ai, b)
-    bt = times2(flip2(b), t)
-    si = inverse2([[p[2][2] - bt[0][0], p[2][3] - bt[0][1]], [p[2][3] - bt[1][0], p[3][3] - bt[1][1]]])
-    r = times2(t, si)
-    u = times2(r, flip2(t))
+    t = times2(a, b)
+    s00 = det * p[2][2] - (b[0][0] * t[0][0] + b[1][0] * t[1][0])
+    s01 = det * p[2][3] - (b[0][0] * t[0][1] + b[1][0] * t[1][1])
+    s11 = det * p[3][3] - (b[0][1] * t[0][1] + b[1][1] * t[1][1])
+    over = 1.0 / (s00 * s11 - s01 * s01)
+    over_det = 1.0 / det
+    flip = [[s11, -s01], [-s01, s00]]
+    u = times2(t, flip)
+    v = times2(u, [[t[0][0], t[1][0]], [t[0][1], t[1][1]]])
+    side = [[u[i][j] * over for j in (0, 1)] for i in (0, 1)]
+    last = [[flip[i][j] * (det * over) for j in (0, 1)] for i in (0, 1)]
+    first = [
+        [a[i][j] * over_det + v[i][j] * (over * over_det) for j in (0, 1)] for i in (0, 1)
+    ]
     return [
-        [ai[0][0] + u[0][0], ai[0][1] + u[0][1], -r[0][0], -r[0][1]],
-        [ai[1][0] + u[1][0], ai[1][1] + u[1][1], -r[1][0], -r[1][1]],
-        [-r[0][0], -r[1][0], si[0][0], si[0][1]],
-        [-r[0][1], -r[1][1], si[1][0], si[1][1]],
+        [first[0][0], first[0][1], -side[0][0], -side[0][1]],
+        [first[0][1], first[1][1], -side[1][0], -side[1][1]],
+        [-side[0][0], -side[1][0], last[0][0], last[0][1]],
+        [-side[0][1], -side[1][1], last[0][1], last[1][1]],
     ]
 
 
@@ -82,13 +86,13 @@
     eye = lax.broadcasted_iota(jnp.int32, (size, size), 0) == lax.broadcasted_iota(
         jnp.int32, (size, size), 1
     )
-    mean = jnp.sum(jnp.where(eye, gram, 0.0), keepdims=True) / size
+    scale = size / jnp.sum(jnp.where(eye, gram, 0.0), keepdims=True)
     work = jnp.concatenate(
-        [gram + jnp.where(eye, damping * mean, 0.0), eye.astype(F32)], axis=1
+        [gram * scale + jnp.where(eye, damping, 0.0), eye.astype(F32)], axis=1
     )
     lanes = 2 * size
     blocks = [work[i : i + 8] for i in range(0, size, 8)]
-    row_at = lax.broadcasted_iota(jnp.int32, (8, lanes), 0)
+    raw, fresh = [], []
     for j in range(0, size, 4):
         owner, at = j // 8, j % 8
         rows = [blocks[owner][at + i : at + i + 1] for i in range(4)]
@@ -97,38 +101,42 @@
             for row in rows
         ]
         inverse = inverse4(pivot)
-        fresh = []
-        for i in range(4):
-            total = inverse[i][0] * rows[0]
-            for k in range(1, 4):
-                total = total + inverse[i][k] * rows[k]
-            fresh.append(total)
-        after = []
-        for m, block in enumerate(blocks):
-            value = block
-            for k in range(4):
-                value = value - block[:, j + k : j + k + 1] * fresh[k]
-            if m == owner:
-                for k in range(4):
-                    value = jnp.where(row_at == at + k, fresh[k], value)
-            after.append(value)
-        blocks = after
-    return jnp.concatenate(blocks, axis=0)[:, size:]
+        new = [
+            (inverse[i][0] * rows[0] + inverse[i][1] * rows[1])
+            + (inverse[i][2] * rows[2] + inverse[i][3] * rows[3])
+            for i in range(4)
+        ]
+        raw += rows
+        fresh += new
+        for m in range(owner if at == 0 else owner + 1, len(blocks)):
+            block = blocks[m]
+            part = [block[:, j + k : j + k + 1] * new[k] for k in range(4)]
+            blocks[m] = block - ((part[0] + part[1]) + (part[2] + part[3]))
+    raw = jnp.concatenate(raw, axis=0)[:, size:]
+    fresh = jnp.concatenate(fresh, axis=0)[:, size:]
+    return scale * mm(raw, fresh, TN)
 
 
 def live_rows(t, list_ref, count_ref, visits_ref, tile_rows):
-    k, b, g = list_ref[0, 0, 0, t], list_ref[0, 0, 1, t], list_ref[0, 0, 2, t]
+    k, b, g = list_ref[0, 0, 0, t], list_ref[0, 1, 0, t], list_ref[0, 2, 0, t]
     kept = jnp.where(t < count_ref[0, 0], visits_ref[k] - tile_rows * b, 0)
     return k, b, g, kept
 
 
 def products_kernel(
-    list_ref, count_ref, visits_ref, tile_hbm, code_hbm, out_ref, acc_ref, tile_ref, code_ref, sems
+    list_hbm, count_hbm, visits_hbm, tile_hbm, code_hbm, out_ref,
+    list_ref, count_ref, visits_ref, tile_ref, code_ref, small_sems, sems,
 ):
     slots, rows, cols = tile_ref.shape
     rank = code_ref.shape[0]
     parts = sems.shape[0] - 1
     each = slots // parts
+    small = []
+    for i, (src, dst) in enumerate(
+        ((list_hbm, list_ref), (count_hbm, count_ref), (visits_hbm, visits_ref))
+    ):
+        small.append(pltpu.make_async_copy(src, dst, small_sems.at[i]))
+        small[-1].start()
     code_copy = pltpu.make_async_copy(code_hbm, code_ref, sems.at[parts])
     code_copy.start()
     copies = []
@@ -136,8 +144,10 @@
         at = pl.ds(i * each, each)
         copies.append(pltpu.make_async_copy(tile_hbm.at[0, 0, at], tile_ref.at[at], sems.at[i]))
         copies[-1].start()
-    acc_ref[...] = jnp.zeros(acc_ref.shape, F32)
+    out_ref[...] = jnp.zeros(out_ref.shape, F32)
     lane = lax.broadcasted_iota(jnp.int32, (rank, rows), 1)
+    for copy in small:
+        copy.wait()
     code_copy.wait()
     for t in range(slots):
         if t % each == 0:
@@ -145,8 +155,7 @@
         k, b, g, kept = live_rows(t, list_ref, count_ref, visits_ref, rows)
         codes = code_ref[:, pl.ds(pl.multiple_of(g * cols, cols), cols)].astype(BF16)
         part = mm16(codes, tile_ref[t], NT)
-        acc_ref[k * VBLOCKS + b] += jnp.where(lane < kept, part, 0.0)
-    out_ref[...] = acc_ref[...].astype(out_ref.dtype)
+        out_ref[k * VBLOCKS + b] += jnp.where(lane < kept, part, 0.0)
 
 
 def gram_kernel(code_ref, out_ref):
@@ -159,20 +168,23 @@
     dests = polar_ref.shape[0]
     segs, rank, rows = prod_ref.shape
     own = segs // VBLOCKS
-    prods = [
-        jnp.concatenate([prod_ref[VBLOCKS * j + b] for b in range(VBLOCKS)], axis=1)
-        for j in range(own)
-    ]
-    zs = []
+    eye = lax.broadcasted_iota(jnp.int32, (rank, rank), 0) == lax.broadcasted_iota(
+        jnp.int32, (rank, rank), 1
+    )
+    prods, zs = [], []
     for j in range(own):
+        prods.append(
+            split(jnp.concatenate([prod_ref[VBLOCKS * j + b] for b in range(VBLOCKS)], axis=1))
+        )
         weight = weight_ref[pl.ds(at_ref[0] * own + j, 1), :]
-        target = mm(mix_ref[...] * weight, prods[j])
+        target = mm3(split(mix_ref[...] * weight), prods[j])
         zs.append(target / jnp.sqrt(jnp.sum(target * target, keepdims=True) + epsilon))
+    zs = [split(z) for z in zs]
     for _ in range(NS_STEPS):
-        grams = [mm(z, z, NT) for z in zs]
-        zs = [1.5 * z - 0.5 * mm(g, z) for g, z in zip(grams, zs)]
-    projected = [halves(mm(z, p, NT)) for z, p in zip(zs, prods)]
-    polar = [z.astype(BF16) for z in zs]
+        factors = [split(jnp.where(eye, 1.5, 0.0) - 0.5 * mm3(z, z, NT)) for z in zs]
+        zs = [split(mm3(q, z)) for q, z in zip(factors, zs)]
+    projected = [halves(mm3(z, p, NT)) for z, p in zip(zs, prods)]
+    polar = [z[0] for z in zs]
     low = rank // 2
     for d in range(dests):
         proj_ref[d, own * low :, :] = gram_ref[...]
@@ -183,19 +195,22 @@
                 polar_ref[d, at : at + rank, :] = polar[j][:, b * rows : (b + 1) * rows]
 
 
-def partial_kernel(got_ref, weight_ref, out_ref):
+def partial_kernel(got_ref, weight_ref, out_ref, gram_ref):
     sources = got_ref.shape[0]
-    low = out_ref.shape[0] // 2
+    low = gram_ref.shape[0]
     weight = weight_ref[...]
     twice = jnp.concatenate([weight, weight], axis=1)
     own = weight.shape[0] // sources
-    total = jnp.zeros((low, out_ref.shape[1]), F32)
+    total = jnp.zeros(gram_ref.shape, F32)
+    gram = jnp.zeros(gram_ref.shape, F32)
     for d in range(sources):
         for j in range(own):
             k = d * own + j
             total += got_ref[d, j * low : (j + 1) * low, :] * twice[k : k + 1, :]
+        gram += got_ref[d, own * low :, :]
     out_ref[:low, :] = total
     out_ref[low:, :] = halves(mm(weight, weight, TN))
+    gram_ref[...] = gram
 
 
 def whole(x):
@@ -204,24 +219,26 @@
 
 
 def mix_kernel(
-    place_ref, sum_a, sum_b, got_ref, mix_ref, mgram_ref, weight_ref, wgram_ref, own_ref
+    place_ref, sum_a, sum_b, gram_ref, got_hbm,
+    mix_ref, again_ref, mgram_ref, weight_ref, wgram_ref, own_ref, got_ref, sem,
 ):
+    copy = pltpu.make_async_copy(got_hbm, got_ref, sem)
+    copy.start()
     sources = got_ref.shape[0]
     rank = mix_ref.shape[0]
     own = own_ref.shape[0]
     low = rank // 2
-    code_gram = got_ref[0, own * low :, :]
-    for d in range(1, sources):
-        code_gram += got_ref[d, own * low :, :]
-    code_gram = whole(code_gram)
+    code_gram = whole(gram_ref[...])
     numer = whole(sum_a[:low, :] + sum_b[:low, :])
     weight_gram = whole(sum_a[low:, :] + sum_b[low:, :])
     mix = mm(numer, damped_inverse(code_gram * weight_gram))
+    again_ref[...] = mix
     mix_ref[...] = mix
     mix_gram = mm(mix, mix, TN)
     mgram_ref[...] = mix_gram
     inverse = damped_inverse(mix_gram * code_gram)
     beside = halves(mix)
+    copy.wait()
     terms = []
     for d in range(sources):
         for j in range(own):
@@ -301,7 +318,7 @@
         copy.wait()
 
 
-def call(kernel, outs, specs, args, scratch=(), flops=1e9, spec=VM, alias=None):
+def call(kernel, outs, specs, args, scratch=(), flops=1e9, spec=VM, alias=None, vmem=16):
     many = isinstance(outs, tuple)
     return pl.pallas_call(
         kernel,
@@ -310,7 +327,7 @@
         out_specs=(spec,) * len(outs) if many else spec,
         input_output_aliases=alias or {},
         scratch_shapes=scratch,
-        compiler_params=PARAMS,
+        compiler_params=pltpu.CompilerParams(vmem_limit_bytes=vmem * MIB),
         cost_estimate=pl.CostEstimate(flops=int(flops), bytes_accessed=65536, transcendentals=0),
     )(*args)
 
@@ -328,6 +345,7 @@
 
 def body(tile_data, tile_list, tile_count, visit_counts, code_factor_t, visit_mix, patient_weight):
     tiles = tile_data[0, 0]
+    tile_list = jnp.transpose(tile_list, (0, 2, 1, 3))
     slots, rows, cols = tiles.shape
     rank = visit_mix.shape[0]
     patients = visit_counts.shape[0]
@@ -340,12 +358,15 @@
     square = shape((rank, rank), F32)
 
     partial = call(
-        products_kernel, shape((patients * VBLOCKS, rank, rows), F32), [SM, SM, SM, HBM, HBM],
+        products_kernel, shape((patients * VBLOCKS, rank, rows), F32), [HBM] * 5,
         (tile_list, tile_count, visit_counts, tile_data, code_factor_t),
         [
-            pltpu.VMEM((patients * VBLOCKS, rank, rows), F32), pltpu.VMEM(tiles.shape, BF16),
-            pltpu.VMEM(code_factor_t.shape, F32), pltpu.SemaphoreType.DMA((5,)),
+            pltpu.SMEM(tile_list.shape, jnp.int32), pltpu.SMEM(tile_count.shape, jnp.int32),
+            pltpu.SMEM(visit_counts.shape, jnp.int32), pltpu.VMEM(tiles.shape, BF16),
+            pltpu.VMEM(code_factor_t.shape, F32), pltpu.SemaphoreType.DMA((3,)),
+            pltpu.SemaphoreType.DMA((5,)),
         ],
+        vmem=60,
     )
     sent = partial.astype(F16).reshape(n_code, own * VBLOCKS * rank, rows)
     got = lax.all_to_all(sent, "code", 0, 0, tiled=True)
@@ -361,24 +382,28 @@
         [SM, VM, VM, VM, VM], (place, products, visit_mix, patient_weight, gram), flops=5e9,
     )
     proj = lax.all_to_all(proj, "code", 0, 0, tiled=True)
-    proj, polar = lax.optimization_barrier((proj, polar))
+    sums, code_gram = call(
+        partial_kernel, (shape((rank, 2 * rank), F32), shape((rank // 2, 2 * rank), F32)),
+        [VM, VM], (proj, patient_weight), vmem=60,
+    )
+    sums = sums + swap(sums, "pat", 8)
+    sums, polar = lax.optimization_barrier((sums, polar))
     polar = lax.all_to_all(polar, "code", 0, 0, tiled=True)
-    sums = call(partial_kernel, shape((rank, 2 * rank), F32), [VM, VM], (proj, patient_weight))
     sums = plus(sums, [swap(sums, "pat", bit) for bit in (2, 4, 6)])
-    sums = sums + swap(sums, "pat", 8)
-    mix_new, mix_gram, weights, wgram, weight_new = call(
+    mix_new, mix_again, mix_gram, weights, wgram, weight_new = call(
         mix_kernel,
         (
-            square, square, shape((patients, rank), F32),
+            square, square, square, shape((patients, rank), F32),
             shape((rank // 2, 2 * rank), F32), shape((own, rank), F32),
         ),
-        [SM] + [VM] * 3,
-        (place, sums, swap(sums, "pat", 1), proj), flops=8e9,
+        [SM, VM, VM, VM, HBM],
+        (place, sums, swap(sums, "pat", 1), code_gram, proj),
+        [pltpu.VMEM(proj.shape, F32), pltpu.SemaphoreType.DMA(())], flops=8e9, vmem=60,
     )
     block = shape((half, rank, cols), F32)
     keep, send = call(
         numer_kernel, (block, block), [SM, SM, SM, SM, VM, VM, VM, VM],
-        (place, tile_list, tile_count, visit_counts, polar, mix_new, weights, tiles),
+        (place, tile_list, tile_count, visit_counts, polar, mix_again, weights, tiles),
         [pltpu.VMEM((n_pat, rank, cols), F32)], flops=4e9,
     )
     groups = [[core + 2 * i for i in range(half)] for core in (0, 1)]

time: 132 us -> 129 us (0.977)
  starting transfers between devices: 30.3 us -> 26.5 us
  local copies, waits for them, and re-layouts: 5.67 us -> 2.12 us
  blocking collectives: 44.5 us -> 47 us
    ppermute x8, starting transfers between devices: 19.8 us -> 15.9 us  [swap(): return lax.ppermute(x, axis, [(i, i ^ bit) for i in range(size)])]
    unnamed x21 -> x28, local copies, waits for them, and re-layouts: 5.67 us -> 2.12 us
    convert_element_type x1, other arithmetic: 1.22 us -> 3 us  [body(): sent = partial.astype(F16).reshape(n_code, own * VBLOCKS * rank, rows)]
    all_to_all x2, blocking collectives: 30.5 us -> 32.1 us  [exchange(): return lax.all_to_all(x, 'pat', 0, 0, axis_index_groups=groups, tiled=True)]
  transfers between devices with their start and end apart: 10 -> 10, of which waited for: 4 -> 5; matrix products, arithmetic and copies ran while one was open for 0% -> 0% of each run, Pallas kernels for 8% -> 8%
where the time goes in v5:
time: 129 us; the launch traced here: 127 us
  blocking collectives  47 us (36%)
  Pallas kernels  28.5 us (22%)
  starting transfers between devices  26.5 us (21%)
  waiting for transfers between devices  17.6 us (14%)
  other arithmetic  4 us (3%)
  local copies, waits for them, and re-layouts  2.12 us (2%)
  between operations  1.43 us (1%)
    all_to_all x2, blocking collectives, exchange(): return lax.all_to_all(x, 'pat', 0, 0, axis_index_groups=groups, tiled=True)  32.1 us
    pallas_call x10, Pallas kernels, call(): pl.pallas_call(kernel, out_shape=outs, in_specs=specs, out_specs=(spec,)...  28.5 us
    ppermute x8, starting transfers between devices, swap(): return lax.ppermute(x, axis, [(i, i ^ bit) for i in range(size)])  15.9 us
    all_to_all x1, blocking collectives, body(): proj = lax.all_to_all(proj, 'code', 0, 0, tiled=True)  14.8 us
    all_to_all x1, waiting for transfers between devices, body(): got = lax.all_to_all(sent, 'code', 0, 0, tiled=True)  12.7 us
    all_to_all x1, starting transfers between devices, body(): got = lax.all_to_all(sent, 'code', 0, 0, tiled=True)  5.62 us
    all_to_all x1, starting transfers between devices, body(): polar = lax.all_to_all(polar, 'code', 0, 0, tiled=True)  4.95 us
    ppermute x8, waiting for transfers between devices, swap(): return lax.ppermute(x, axis, [(i, i ^ bit) for i in range(size)])  4.59 us
  transfers between devices with their start and end apart: 10, of which 5 were waited for; matrix products, arithmetic and copies ran while one was open for 0% of the time, Pallas kernels for 8%

profile of v5, /device:TPU:3, one launch (start us, length us, event | category | flops | bytes accessed | tf_op | source)
XLA Modules:
  0.0 127.1 jit_solution(15829950042117667523)
XLA Ops:
  1.3 4.3 %shard_map.94 = f32[64,64,128]{2,1,0:T(8,128)} custom-call(s32[1,3,1,16]{3,2,1,0:T(1,128)} %bitcast.8, s32[1,1]{1,0:T(1,128)S(6)} %copy.12.count_hbm.count_ref, s32[32]{0:T(128)} %visits_ref.1, bf16[1,1,16,128,512]{4,3,2,1,0:T(8,128)(2,1)} %tile_hbm.1, f32[64,8192]{1,0:T(8,128)} %code_ref.1), custom_call_target="tpu_custom_call" | custom-call | flops 1000000000 | bytes 65536 | tf_op jit(solution)/shard_map/pallas_call | solution.py:323
  5.6 0.0 copy-start
  5.6 3.0 %convert_element_type.6 = f16[64,64,128]{2,1,0:T(8,128)(2,1)} convert(f32[64,64,128]{2,1,0:T(8,128)} %shard_map.94) | non-fusion elementwise | flops 524288 | bytes 3145728 | tf_op jit(solution)/shard_map/convert_element_type | solution.py:371
  8.6 5.6 %all-to-all-start = ((f16[8,512,128]{2,1,0:T(8,128)(2,1)}), f16[8,512,128]{2,1,0:T(8,128)(2,1)S(1)}, u32[]{:S(2)}, u32[]{:S(2)}) async-start(f16[8,512,128]{2,1,0:T(8,128)(2,1)} %bitcast.3), calls=%async_computation | async-start | bytes 2097152 | tf_op jit(solution)/shard_map/all_to_all | solution.py:372
  14.2 0.0 copy-done
  14.2 0.8 shard_map.95.gram_ref
  15.0 0.1 pad_add_fusion.at_ref.place_ref
  15.1 12.7 %all-to-all-done = f16[8,512,128]{2,1,0:T(8,128)(2,1)S(1)} async-done(((f16[8,512,128]{2,1,0:T(8,128)(2,1)}), f16[8,512,128]{2,1,0:T(8,128)(2,1)S(1)}, u32[]{:S(2)}, u32[]{:S(2)}) %all-to-all-start) | async-done | bytes 1048608 | tf_op jit(solution)/shard_map/all_to_all | solution.py:372
  27.8 0.1 convert_reduce_fusion
  27.9 0.0 copy-done.6
  28.0 0.0 copy-done.7
  28.0 4.9 %shard_map.96 = (f32[8,160,128]{2,1,0:T(8,128)S(1)}, bf16[8,512,128]{2,1,0:T(8,128)(2,1)}) custom-call(s32[2]{0:T(128)S(1)} %pad_add_fusion.at_ref.place_ref, f32[8,64,128]{2,1,0:T(8,128)S(1)} %bitcast.7, f32[64,64]{1,0:T(8,128)S(1)} %copy-done.6, f32[32,64]{1,0:T(8,128)S(1)} %copy-done.7, f32[32,128]{1,0:T(8,128)S(1)} %shard_map.95.gram_ref), custom_call_target="tpu_custom_call" | custom-call | flops 5000000000 | bytes 65536 | tf_op jit(solution)/shard_map/pallas_call | solution.py:323
  32.9 0.0 copy-done.4
  32.9 14.8 %all_to_all.25.got_ref.got_hbm = f32[8,160,128]{2,1,0:T(8,128)} all-to-all(f32[8,160,128]{2,1,0:T(8,128)S(1)} %get-tuple-element.17), channel_id=1, replica_groups=mesh['pat'=16,'code'=8] {'code'}, dimensions={0} | all-to-all | bytes 1310720 | tf_op jit(solution)/shard_map/all_to_all | solution.py:384
  47.7 2.0 %shard_map.97 = (f32[64,128]{1,0:T(8,128)}, f32[32,128]{1,0:T(8,128)}) custom-call(f32[8,160,128]{2,1,0:T(8,128)} %all_to_all.25.got_ref.got_hbm, f32[32,64]{1,0:T(8,128)} %weight_ref.3), custom_call_target="tpu_custom_call" | custom-call | flops 1000000000 | bytes 65536 | tf_op jit(solution)/shard_map/pallas_call | solution.py:323
  49.7 3.3 %collective-permute-start = (f32[64,128]{1,0:T(8,128)}, f32[64,128]{1,0:T(8,128)S(1)}, u32[]{:S(2)}, u32[]{:S(2)}) collective-permute-start(f32[64,128]{1,0:T(8,128)} %get-tuple-element.18), channel_id=1, source_target_pairs={{0,64},{8,72},{16,80},{24,88},{32,96},{40,104},{48,112},{56,120},{... | collective-permute-start | bytes 98312 | tf_op jit(solution)/shard_map/ppermute | solution.py:337
  53.0 1.5 %collective-permute-done = f32[64,128]{1,0:T(8,128)S(1)} collective-permute-done((f32[64,128]{1,0:T(8,128)}, f32[64,128]{1,0:T(8,128)S(1)}, u32[]{:S(2)}, u32[]{:S(2)}) %collective-permute-start) | collective-permute-done | bytes 32800 | tf_op jit(solution)/shard_map/ppermute | solution.py:337
  54.5 0.8 add.12
  55.3 2.7 %collective-permute-start.3 = (f32[64,128]{1,0:T(8,128)S(1)}, f32[64,128]{1,0:T(8,128)S(1)}, u32[]{:S(2)}, u32[]{:S(2)}) collective-permute-start(f32[64,128]{1,0:T(8,128)S(1)} %add.12), channel_id=1, source_target_pairs={{0,48},{8,56},{16,32},{24,40},{32,16},{40,24},{48,0},{56,8},{64,11... | collective-permute-start | bytes 98312 | tf_op jit(solution)/shard_map/ppermute | solution.py:337
  58.0 0.3 collective-permute-start.2
  58.4 0.3 collective-permute-start.1
  58.7 5.0 %all-to-all-start.2 = ((bf16[8,512,128]{2,1,0:T(8,128)(2,1)}), bf16[8,512,128]{2,1,0:T(8,128)(2,1)S(1)}, u32[]{:S(2)}, u32[]{:S(2)}) async-start(bf16[8,512,128]{2,1,0:T(8,128)(2,1)} %get-tuple-element.20), calls=%async_computation.2 | async-start | bytes 2097152 | tf_op jit(solution)/shard_map/all_to_all | solution.py:391
  63.6 0.0 collective-permute-done.3
  63.6 0.0 collective-permute-done.2
  63.6 0.0 collective-permute-done.1
  63.7 0.0 copy-start.12
  63.7 3.3 %collective-permute-start.4 = (f32[64,128]{1,0:T(8,128)S(1)}, f32[64,128]{1,0:T(8,128)S(1)}, u32[]{:S(2)}, u32[]{:S(2)}) collective-permute-start(f32[64,128]{1,0:T(8,128)S(1)} %add_add_fusion.sum_a), channel_id=1, source_target_pairs={{0,8},{8,0},{16,24},{24,16},{32,40},{40,32},{48,56},{56,48},{64,72... | collective-permute-start | bytes 98312 | tf_op jit(solution)/shard_map/ppermute | solution.py:337
  67.0 0.9 collective-permute-done.4.sum_b
  67.9 0.0 copy-done.12
  67.9 0.6 copy-done.13
  68.5 7.2 %shard_map.98 = (f32[64,64]{1,0:T(8,128)}, f32[64,64]{1,0:T(8,128)}, f32[64,64]{1,0:T(8,128)}, f32[32,64]{1,0:T(8,128)}, f32[32,128]{1,0:T(8,128)}, /*index=5*/f32[4,64]{1,0:T(4,128)}) custom-call(s32[2]{0:T(128)} %copy-done.4, f32[64,128]{1,0:T(8,128)} %copy-done.12, f32[64,128]{1,0:T(8,128)} %copy-done.13, f32[32,128]{1,0:T(8,128)} %get-tuple-element.22.gram_ref, ...), custom_call_target="tpu_custom_call" | custom-call | flops 8000000000 | bytes 65536 | tf_op jit(solution)/shard_map/pallas_call | solution.py:323
  75.7 0.3 all-to-all-done.2.got_ref
  76.1 0.0 copy-done.2
  76.1 0.7 copy-done.10
  76.8 0.7 copy-done.11
  77.6 3.3 %shard_map.99 = (f32[8,64,512]{2,1,0:T(8,128)S(1)}, f32[8,64,512]{2,1,0:T(8,128)S(1)}) custom-call(s32[2]{0:T(128)S(1)} %copy-done.5, s32[1,3,1,16]{3,2,1,0:T(1,128)S(1)} %bitcast.9, s32[1,1]{1,0:T(1,128)S(6)} %copy.12.count_hbm.count_ref, s32[32]{0:T(128)S(1)} %copy-done.3, bf16[8,512,128]{2,1,0:T(8,128)(2,1)S(1)} %all-to-all-done.2.got_ref, ...), custom_call_target="tpu_custom_call" | custom-call | flops 4000000000 | bytes 65536 | tf_op jit(solution)/shard_map/pallas_call | solution.py:323
  80.9 3.5 %collective-permute-start.5 = (f32[8,64,512]{2,1,0:T(8,128)S(1)}, f32[8,64,512]{2,1,0:T(8,128)S(1)}, u32[]{:S(2)}, u32[]{:S(2)}) collective-permute-start(f32[8,64,512]{2,1,0:T(8,128)S(1)} %get-tuple-element.26), channel_id=1, source_target_pairs={{0,8},{8,0},{16,24},{24,16},{32,40},{40,32},{48,56},{56,48},{64,72... | collective-permute-start | bytes 3145736 | tf_op jit(solution)/shard_map/ppermute | solution.py:337
  84.4 0.1 collective-permute-start.6
  84.5 2.2 %collective-permute-done.6.gram_b = f32[32,128]{1,0:T(8,128)S(1)} collective-permute-done((f32[32,128]{1,0:T(8,128)S(1)}, f32[32,128]{1,0:T(8,128)S(1)}, u32[]{:S(2)}, u32[]{:S(2)}) %collective-permute-start.6) | collective-permute-done | bytes 16416 | tf_op jit(solution)/shard_map/ppermute | solution.py:337
  86.7 0.0 collective-permute-done.5.came_ref
  86.7 0.1 shard_map.100
  86.8 19.5 %all_to_all.26.got_ref = bf16[8,5,64,128]{3,2,1,0:T(8,128)(2,1)S(1)} all-to-all(bf16[8,5,64,128]{3,2,1,0:T(8,128)(2,1)S(1)} %shard_map.100), channel_id=1, replica_groups={{0,16,32,48,64,80,96,112},{8,24,40,56,72,88,104,120},{1,17,33,49,65,81,..., dimensions={0} | all-to-all | bytes 1310720 | tf_op jit(solution)/shard_map/all_to_all | solution.py:412
  106.3 2.7 %shard_map.101 = bf16[8,64,512]{2,1,0:T(8,128)(2,1)S(1)} custom-call(bf16[8,5,64,128]{3,2,1,0:T(8,128)(2,1)S(1)} %all_to_all.26.got_ref, f32[64,64]{1,0:T(8,128)S(1)} %copy-done.9), custom_call_target="tpu_custom_call" | custom-call | flops 1000000000 | bytes 65536 | tf_op jit(solution)/shard_map/pallas_call | solution.py:323
  108.9 12.6 %all_to_all.27.from_ref = bf16[8,64,512]{2,1,0:T(8,128)(2,1)S(1)} all-to-all(bf16[8,64,512]{2,1,0:T(8,128)(2,1)S(1)} %shard_map.101), channel_id=1, replica_groups={{0,16,32,48,64,80,96,112},{8,24,40,56,72,88,104,120},{1,17,33,49,65,81,..., dimensions={0} | all-to-all | bytes 1048576 | tf_op jit(solution)/shard_map/all_to_all | solution.py:412
  121.6 2.3 %collective-permute-start.7 = (bf16[8,64,512]{2,1,0:T(8,128)(2,1)S(1)}, bf16[8,64,512]{2,1,0:T(8,128)(2,1)S(1)}, u32[]{:S(2)}, u32[]{:S(2)}) collective-permute-start(bf16[8,64,512]{2,1,0:T(8,128)(2,1)S(1)} %all_to_all.27.from_ref), channel_id=1, source_target_pairs={{0,8},{8,0},{16,24},{24,16},{32,40},{40,32},{48,56},{56,48},{64,72... | collective-permute-start | bytes 1572872 | tf_op jit(solution)/shard_map/ppermute | solution.py:337
  123.9 1.6 %shard_map.102.refs_0_ = f32[64,8192]{1,0:T(8,128)} custom-call(s32[2]{0:T(128)S(1)} %copy-done.5, bf16[8,64,512]{2,1,0:T(8,128)(2,1)S(1)} %all_to_all.27.from_ref), custom_call_target="tpu_custom_call" | custom-call | flops 1000000000 | bytes 65536 | tf_op jit(solution)/shard_map/pallas_call | solution.py:323
  125.5 0.0 collective-permute-done.7.from_ref
  125.5 1.6 %shard_map.103 = f32[64,8192]{1,0:T(8,128)} custom-call(s32[2]{0:T(128)S(1)} %copy-done.5, bf16[8,64,512]{2,1,0:T(8,128)(2,1)S(1)} %collective-permute-done.7.from_ref, f32[64,8192]{1,0:T(8,128)} %shard_map.102.refs_0_), custom_call_target="tpu_custom_call", output_to_operand_aliasing={{}: (2, {})} | custom-call | flops 1000000000 | bytes 65536 | tf_op jit(solution)/shard_map/pallas_call | solution.py:323
  (18 shorter events, 0.0 us)
Async XLA Ops:
  5.6 8.6 %copy-start = (f32[64,8192]{1,0:T(8,128)S(1)}, f32[64,8192]{1,0:T(8,128)}, u32[]{:S(2)}) copy-start(f32[64,8192]{1,0:T(8,128)} %code_ref.1) | copy-start | bytes 6291460
  8.6 19.2 %all-to-all-start = ((f16[8,512,128]{2,1,0:T(8,128)(2,1)}), f16[8,512,128]{2,1,0:T(8,128)(2,1)S(1)}, u32[]{:S(2)}, u32[]{:S(2)}) async-start(f16[8,512,128]{2,1,0:T(8,128)(2,1)} %bitcast.3), calls=%async_computation | async-start | bytes 2097152 | tf_op jit(solution)/shard_map/all_to_all | solution.py:372
  14.2 13.8 %copy-start.6 = (f32[64,64]{1,0:T(8,128)S(1)}, f32[64,64]{1,0:T(8,128)}, u32[]{:S(2)}) copy-start(f32[64,64]{1,0:T(8,128)} %mix_ref.1) | copy-start | bytes 49156
  14.2 13.8 %copy-start.7 = (f32[32,64]{1,0:T(8,128)S(1)}, f32[32,64]{1,0:T(8,128)}, u32[]{:S(2)}) copy-start(f32[32,64]{1,0:T(8,128)} %weight_ref.3) | copy-start | bytes 24580
  15.1 17.7 %copy-start.4 = (s32[2]{0:T(128)}, s32[2]{0:T(128)S(1)}, u32[]{:S(2)}) copy-start(s32[2]{0:T(128)S(1)} %pad_add_fusion.at_ref.place_ref) | copy-start | bytes 28
  49.7 4.8 %collective-permute-start = (f32[64,128]{1,0:T(8,128)}, f32[64,128]{1,0:T(8,128)S(1)}, u32[]{:S(2)}, u32[]{:S(2)}) collective-permute-start(f32[64,128]{1,0:T(8,128)} %get-tuple-element.18), channel_id=1, source_target_pairs={{0,64},{8,72},{16,80},{24,88},{32,96},{40,104},{48,112},{56,120},{... | collective-permute-start | bytes 98312 | tf_op jit(solution)/shard_map/ppermute | solution.py:337
  55.3 8.3 %collective-permute-start.3 = (f32[64,128]{1,0:T(8,128)S(1)}, f32[64,128]{1,0:T(8,128)S(1)}, u32[]{:S(2)}, u32[]{:S(2)}) collective-permute-start(f32[64,128]{1,0:T(8,128)S(1)} %add.12), channel_id=1, source_target_pairs={{0,48},{8,56},{16,32},{24,40},{32,16},{40,24},{48,0},{56,8},{64,11... | collective-permute-start | bytes 98312 | tf_op jit(solution)/shard_map/ppermute | solution.py:337
  58.0 5.6 %collective-permute-start.2 = (f32[64,128]{1,0:T(8,128)S(1)}, f32[64,128]{1,0:T(8,128)S(1)}, u32[]{:S(2)}, u32[]{:S(2)}) collective-permute-start(f32[64,128]{1,0:T(8,128)S(1)} %add.12), channel_id=1, source_target_pairs={{0,32},{8,40},{16,48},{24,56},{32,0},{40,8},{48,16},{56,24},{64,96... | collective-permute-start | bytes 98312 | tf_op jit(solution)/shard_map/ppermute | solution.py:337
  58.4 5.3 %collective-permute-start.1 = (f32[64,128]{1,0:T(8,128)S(1)}, f32[64,128]{1,0:T(8,128)S(1)}, u32[]{:S(2)}, u32[]{:S(2)}) collective-permute-start(f32[64,128]{1,0:T(8,128)S(1)} %add.12), channel_id=1, source_target_pairs={{0,16},{8,24},{16,0},{24,8},{32,48},{40,56},{48,32},{56,40},{64,80... | collective-permute-start | bytes 98312 | tf_op jit(solution)/shard_map/ppermute | solution.py:337
  58.7 17.4 %all-to-all-start.2 = ((bf16[8,512,128]{2,1,0:T(8,128)(2,1)}), bf16[8,512,128]{2,1,0:T(8,128)(2,1)S(1)}, u32[]{:S(2)}, u32[]{:S(2)}) async-start(bf16[8,512,128]{2,1,0:T(8,128)(2,1)} %get-tuple-element.20), calls=%async_computation.2 | async-start | bytes 2097152 | tf_op jit(solution)/shard_map/all_to_all | solution.py:391
  63.7 4.2 %copy-start.12 = (f32[64,128]{1,0:T(8,128)}, f32[64,128]{1,0:T(8,128)S(1)}, u32[]{:S(2)}) copy-start(f32[64,128]{1,0:T(8,128)S(1)} %add_add_fusion.sum_a) | copy-start | bytes 98308
  63.7 4.2 %collective-permute-start.4 = (f32[64,128]{1,0:T(8,128)S(1)}, f32[64,128]{1,0:T(8,128)S(1)}, u32[]{:S(2)}, u32[]{:S(2)}) collective-permute-start(f32[64,128]{1,0:T(8,128)S(1)} %add_add_fusion.sum_a), channel_id=1, source_target_pairs={{0,8},{8,0},{16,24},{24,16},{32,40},{40,32},{48,56},{56,48},{64,72... | collective-permute-start | bytes 98312 | tf_op jit(solution)/shard_map/ppermute | solution.py:337
  67.9 0.6 copy-start.13
  68.5 7.6 %copy-start.1 = (bf16[1,1,16,128,512]{4,3,2,1,0:T(8,128)(2,1)S(1)}, bf16[1,1,16,128,512]{4,3,2,1,0:T(8,128)(2,1)}, u32[]{:S(2)}) copy-start(bf16[1,1,16,128,512]{4,3,2,1,0:T(8,128)(2,1)} %tile_hbm.1) | copy-start | bytes 6291460
  68.5 7.6 %copy-start.2 = (s32[1,1,3,16]{3,1,2,0:T(1,128)S(1)}, s32[1,1,3,16]{3,1,2,0:T(1,128)}, u32[]{:S(2)}) copy-start(s32[1,1,3,16]{3,1,2,0:T(1,128)} %param.8) | copy-start | bytes 580
  68.5 7.6 %copy-start.3 = (s32[32]{0:T(128)S(1)}, s32[32]{0:T(128)}, u32[]{:S(2)}) copy-start(s32[32]{0:T(128)} %visits_ref.1) | copy-start | bytes 388
  68.5 7.6 %copy-start.5 = (s32[2]{0:T(128)S(1)}, s32[2]{0:T(128)}, u32[]{:S(2)}) copy-start(s32[2]{0:T(128)} %copy-done.4) | copy-start | bytes 28
  76.1 0.8 copy-start.10
  76.8 0.7 copy-start.11
  77.6 6.8 %copy-start.8 = (f32[32,128]{1,0:T(8,128)S(1)}, f32[32,128]{1,0:T(8,128)}, u32[]{:S(2)}) copy-start(f32[32,128]{1,0:T(8,128)} %get-tuple-element.27.gram_a) | copy-start | bytes 49156
  80.9 5.8 %collective-permute-start.5 = (f32[8,64,512]{2,1,0:T(8,128)S(1)}, f32[8,64,512]{2,1,0:T(8,128)S(1)}, u32[]{:S(2)}, u32[]{:S(2)}) collective-permute-start(f32[8,64,512]{2,1,0:T(8,128)S(1)} %get-tuple-element.26), channel_id=1, source_target_pairs={{0,8},{8,0},{16,24},{24,16},{32,40},{40,32},{48,56},{56,48},{64,72... | collective-permute-start | bytes 3145736 | tf_op jit(solution)/shard_map/ppermute | solution.py:337
  84.4 2.3 %collective-permute-start.6 = (f32[32,128]{1,0:T(8,128)S(1)}, f32[32,128]{1,0:T(8,128)S(1)}, u32[]{:S(2)}, u32[]{:S(2)}) collective-permute-start(f32[32,128]{1,0:T(8,128)S(1)} %copy-done.8), channel_id=1, source_target_pairs={{0,8},{8,0},{16,24},{24,16},{32,40},{40,32},{48,56},{56,48},{64,72... | collective-permute-start | bytes 49160 | tf_op jit(solution)/shard_map/ppermute | solution.py:337
  86.7 19.6 %copy-start.9 = (f32[64,64]{1,0:T(8,128)S(1)}, f32[64,64]{1,0:T(8,128)}, u32[]{:S(2)}) copy-start(f32[64,64]{1,0:T(8,128)} %get-tuple-element.28.mgram_ref) | copy-start | bytes 49156
  121.6 3.9 %collective-permute-start.7 = (bf16[8,64,512]{2,1,0:T(8,128)(2,1)S(1)}, bf16[8,64,512]{2,1,0:T(8,128)(2,1)S(1)}, u32[]{:S(2)}, u32[]{:S(2)}) collective-permute-start(bf16[8,64,512]{2,1,0:T(8,128)(2,1)S(1)} %all_to_all.27.from_ref), channel_id=1, source_target_pairs={{0,8},{8,0},{16,24},{24,16},{32,40},{40,32},{48,56},{56,48},{64,72... | collective-permute-start | bytes 1572872 | tf_op jit(solution)/shard_map/ppermute | solution.py:337

commit v6 on v5

--- a/solution.py
+++ b/solution.py
@@ -124,34 +124,16 @@
 
 
 def products_kernel(
-    list_hbm, count_hbm, visits_hbm, tile_hbm, code_hbm, out_ref,
-    list_ref, count_ref, visits_ref, tile_ref, code_ref, small_sems, sems,
+    list_ref, count_ref, visits_hbm, tile_ref, code_ref, out_ref, visits_ref, sem
 ):
+    copy = pltpu.make_async_copy(visits_hbm, visits_ref, sem)
+    copy.start()
     slots, rows, cols = tile_ref.shape
     rank = code_ref.shape[0]
-    parts = sems.shape[0] - 1
-    each = slots // parts
-    small = []
-    for i, (src, dst) in enumerate(
-        ((list_hbm, list_ref), (count_hbm, count_ref), (visits_hbm, visits_ref))
-    ):
-        small.append(pltpu.make_async_copy(src, dst, small_sems.at[i]))
-        small[-1].start()
-    code_copy = pltpu.make_async_copy(code_hbm, code_ref, sems.at[parts])
-    code_copy.start()
-    copies = []
-    for i in range(parts):
-        at = pl.ds(i * each, each)
-        copies.append(pltpu.make_async_copy(tile_hbm.at[0, 0, at], tile_ref.at[at], sems.at[i]))
-        copies[-1].start()
     out_ref[...] = jnp.zeros(out_ref.shape, F32)
     lane = lax.broadcasted_iota(jnp.int32, (rank, rows), 1)
-    for copy in small:
-        copy.wait()
-    code_copy.wait()
+    copy.wait()
     for t in range(slots):
-        if t % each == 0:
-            copies[t // each].wait()
         k, b, g, kept = live_rows(t, list_ref, count_ref, visits_ref, rows)
         codes = code_ref[:, pl.ds(pl.multiple_of(g * cols, cols), cols)].astype(BF16)
         part = mm16(codes, tile_ref[t], NT)
@@ -164,53 +146,41 @@
     out_ref[...] = halves(mm16(high, high, NT) + cross + cross.T)
 
 
-def polar_kernel(at_ref, prod_ref, mix_ref, weight_ref, gram_ref, proj_ref, polar_ref):
-    dests = polar_ref.shape[0]
+def polar_kernel(
+    scales, at_ref, prod_ref, mix_ref, weight_ref, gram_ref, sums_ref, out_ref
+):
+    dests = out_ref.shape[0]
     segs, rank, rows = prod_ref.shape
     own = segs // VBLOCKS
     eye = lax.broadcasted_iota(jnp.int32, (rank, rank), 0) == lax.broadcasted_iota(
         jnp.int32, (rank, rank), 1
     )
-    prods, zs = [], []
+    prods, zs, weights = [], [], []
     for j in range(own):
         prods.append(
             split(jnp.concatenate([prod_ref[VBLOCKS * j + b] for b in range(VBLOCKS)], axis=1))
         )
-        weight = weight_ref[pl.ds(at_ref[0] * own + j, 1), :]
-        target = mm3(split(mix_ref[...] * weight), prods[j])
+        weights.append(weight_ref[pl.ds(at_ref[0] * own + j, 1), :])
+        target = mm3(split(mix_ref[...] * weights[j]), prods[j])
         zs.append(target / jnp.sqrt(jnp.sum(target * target, keepdims=True) + epsilon))
     zs = [split(z) for z in zs]
     for _ in range(NS_STEPS):
         factors = [split(jnp.where(eye, 1.5, 0.0) - 0.5 * mm3(z, z, NT)) for z in zs]
         zs = [split(mm3(q, z)) for q, z in zip(factors, zs)]
-    projected = [halves(mm3(z, p, NT)) for z, p in zip(zs, prods)]
-    polar = [z[0] for z in zs]
+    pieces = [z[0][:, b * rows : (b + 1) * rows] for z in zs for b in range(VBLOCKS)]
+    numer = jnp.zeros((rank, rank), F32)
+    for z, p, weight in zip(zs, prods, weights):
+        projected = mm3(z, p, NT)
+        numer += projected * weight
+        pieces.append(jnp.concatenate(split(projected), axis=1))
     low = rank // 2
+    weight = weight_ref[...]
+    sums_ref[:low, :] = halves(numer)
+    sums_ref[low:rank, :] = halves(mm(weight, weight, TN)) * scales[0]
+    sums_ref[rank:, :] = gram_ref[...] * scales[1]
     for d in range(dests):
-        proj_ref[d, own * low :, :] = gram_ref[...]
-        for j in range(own):
-            proj_ref[d, j * low : (j + 1) * low, :] = projected[j]
-            for b in range(VBLOCKS):
-                at = (VBLOCKS * j + b) * rank
-                polar_ref[d, at : at + rank, :] = polar[j][:, b * rows : (b + 1) * rows]
-
-
-def partial_kernel(got_ref, weight_ref, out_ref, gram_ref):
-    sources = got_ref.shape[0]
-    low = gram_ref.shape[0]
-    weight = weight_ref[...]
-    twice = jnp.concatenate([weight, weight], axis=1)
-    own = weight.shape[0] // sources
-    total = jnp.zeros(gram_ref.shape, F32)
-    gram = jnp.zeros(gram_ref.shape, F32)
-    for d in range(sources):
-        for j in range(own):
-            k = d * own + j
-            total += got_ref[d, j * low : (j + 1) * low, :] * twice[k : k + 1, :]
-        gram += got_ref[d, own * low :, :]
-    out_ref[:low, :] = total
-    out_ref[low:, :] = halves(mm(weight, weight, TN))
-    gram_ref[...] = gram
+        for i, piece in enumerate(pieces):
+            out_ref[d, i * rank : (i + 1) * rank, :] = piece
 
 
 def whole(x):
@@ -218,55 +188,49 @@
     return jnp.concatenate([x[:, :rank], x[:, rank:]], axis=0)
 
 
-def mix_kernel(
-    place_ref, sum_a, sum_b, gram_ref, got_hbm,
-    mix_ref, again_ref, mgram_ref, weight_ref, wgram_ref, own_ref, got_ref, sem,
-):
-    copy = pltpu.make_async_copy(got_hbm, got_ref, sem)
-    copy.start()
-    sources = got_ref.shape[0]
+def mix_kernel(a_ref, b_ref, c_ref, d_ref, mix_ref, again_ref, mgram_ref, inverse_ref):
+    sums = (a_ref[...] + b_ref[...]) + (c_ref[...] + d_ref[...])
     rank = mix_ref.shape[0]
-    own = own_ref.shape[0]
     low = rank // 2
-    code_gram = whole(gram_ref[...])
-    numer = whole(sum_a[:low, :] + sum_b[:low, :])
-    weight_gram = whole(sum_a[low:, :] + sum_b[low:, :])
-    mix = mm(numer, damped_inverse(code_gram * weight_gram))
+    weight_gram, code_gram = whole(sums[low:rank]), whole(sums[rank:])
+    mix = mm(whole(sums[:low]), damped_inverse(code_gram * weight_gram))
     again_ref[...] = mix
     mix_ref[...] = mix
     mix_gram = mm(mix, mix, TN)
     mgram_ref[...] = mix_gram
-    inverse = damped_inverse(mix_gram * code_gram)
-    beside = halves(mix)
-    copy.wait()
+    inverse_ref[...] = damped_inverse(mix_gram * code_gram)
+
+
+def numer_kernel(
+    place_ref, list_ref, count_ref, visits_ref, got_ref, mix_ref, inverse_ref, tile_ref,
+    keep_ref, send_ref, wgram_ref, own_ref, acc_ref, weight_ref,
+):
+    slots, rows, cols = tile_ref.shape
+    sources = got_ref.shape[0]
+    rank = mix_ref.shape[0]
+    own = own_ref.shape[0]
+    first = own * VBLOCKS * rank
+    mix = mix_ref[...]
+    twice = jnp.concatenate([mix, mix], axis=1)
     terms = []
     for d in range(sources):
         for j in range(own):
-            part = got_ref[d, j * low : (j + 1) * low, :] * beside
+            at = first + j * rank
+            part = got_ref[d, at : at + rank, :].astype(F32) * twice
             terms.append(jnp.sum(part, axis=0, keepdims=True))
-    weight = jnp.maximum(mm(fold(jnp.concatenate(terms, axis=0)), inverse), 0.0)
+    weight = jnp.maximum(mm(fold(jnp.concatenate(terms, axis=0)), inverse_ref[...]), 0.0)
     weight_ref[...] = weight
     for j in range(own):
         own_ref[j : j + 1, :] = weight_ref[pl.ds(place_ref[0] * own + j, 1), :]
     wgram_ref[...] = halves(mm(weight, weight, TN))
-
-
-def numer_kernel(
-    place_ref, list_ref, count_ref, visits_ref, got_ref, mix_ref, weight_ref, tile_ref,
-    keep_ref, send_ref, acc_ref,
-):
-    slots, rows, cols = tile_ref.shape
-    rank = mix_ref.shape[0]
-    own = weight_ref.shape[0] // got_ref.shape[0]
-    mix = mix_ref[...]
     acc_ref[...] = jnp.zeros(acc_ref.shape, F32)
     lane = lax.broadcasted_iota(jnp.int32, (rank, rows), 1)
     for t in range(slots):
         k, b, g, kept = live_rows(t, list_ref, count_ref, visits_ref, rows)
-        high, low = split(mix * weight_ref[pl.ds(k, 1), :])
+        both = jnp.concatenate(split(mix * weight_ref[pl.ds(k, 1), :]), axis=0)
         at = pl.multiple_of((lax.rem(k, own) * VBLOCKS + b) * rank, rank)
         polar = got_ref[lax.div(k, own), pl.ds(at, rank), :]
-        spread = mm16(high, polar, TN) + mm16(low, polar, TN)
+        spread = mm16(both, jnp.concatenate([polar, polar], axis=0), TN)
         spread = jnp.where(lane < kept, spread, 0.0).astype(BF16)
         acc_ref[g] += mm16(spread, tile_ref[t])
     parity = place_ref[1]
@@ -337,6 +301,16 @@
     return lax.ppermute(x, axis, [(i, i ^ bit) for i in range(size)])
 
 
+def swap_z(x, high, low):
+    n_pat, n_code = lax.axis_size("pat"), lax.axis_size("code")
+    pairs = [
+        (p * n_code + c, (p ^ (high * n_pat // 2)) * n_code + (c ^ (low * n_code // 2)))
+        for p in range(n_pat)
+        for c in range(n_code)
+    ]
+    return lax.ppermute(x, ("pat", "code"), pairs)
+
+
 def plus(x, parts):
     for part in parts:
         x = x + part
@@ -358,53 +332,37 @@
     square = shape((rank, rank), F32)
 
     partial = call(
-        products_kernel, shape((patients * VBLOCKS, rank, rows), F32), [HBM] * 5,
-        (tile_list, tile_count, visit_counts, tile_data, code_factor_t),
-        [
-            pltpu.SMEM(tile_list.shape, jnp.int32), pltpu.SMEM(tile_count.shape, jnp.int32),
-            pltpu.SMEM(visit_counts.shape, jnp.int32), pltpu.VMEM(tiles.shape, BF16),
-            pltpu.VMEM(code_factor_t.shape, F32), pltpu.SemaphoreType.DMA((3,)),
-            pltpu.SemaphoreType.DMA((5,)),
-        ],
-        vmem=60,
+        products_kernel, shape((patients * VBLOCKS, rank, rows), F32), [SM, SM, HBM, VM, VM],
+        (tile_list, tile_count, visit_counts, tiles, code_factor_t),
+        [pltpu.SMEM(visit_counts.shape, jnp.int32), pltpu.SemaphoreType.DMA(())],
     )
     sent = partial.astype(F16).reshape(n_code, own * VBLOCKS * rank, rows)
     got = lax.all_to_all(sent, "code", 0, 0, tiled=True)
     gram = call(gram_kernel, shape((rank // 2, 2 * rank), F32), [VM], (code_factor_t,))
     products = jnp.sum(got.astype(F32), axis=0).reshape(own * VBLOCKS, rank, rows)
 
-    proj, polar = call(
-        polar_kernel,
-        (
-            shape((n_code, (own + 1) * rank // 2, 2 * rank), F32),
-            shape((n_code, own * VBLOCKS * rank, rows), BF16),
-        ),
+    scales = (1.0 / n_code, 1.0 / n_pat)
+    length = (own * VBLOCKS + own) * rank
+    sums, message = call(
+        functools.partial(polar_kernel, scales),
+        (shape((3 * rank // 2, 2 * rank), F32), shape((n_code, length, rows), BF16)),
         [SM, VM, VM, VM, VM], (place, products, visit_mix, patient_weight, gram), flops=5e9,
     )
-    proj = lax.all_to_all(proj, "code", 0, 0, tiled=True)
-    sums, code_gram = call(
-        partial_kernel, (shape((rank, 2 * rank), F32), shape((rank // 2, 2 * rank), F32)),
-        [VM, VM], (proj, patient_weight), vmem=60,
-    )
-    sums = sums + swap(sums, "pat", 8)
-    sums, polar = lax.optimization_barrier((sums, polar))
-    polar = lax.all_to_all(polar, "code", 0, 0, tiled=True)
+    shared = lax.all_to_all(message, "code", 0, 0, tiled=True)
     sums = plus(sums, [swap(sums, "pat", bit) for bit in (2, 4, 6)])
-    mix_new, mix_again, mix_gram, weights, wgram, weight_new = call(
-        mix_kernel,
-        (
-            square, square, square, shape((patients, rank), F32),
-            shape((rank // 2, 2 * rank), F32), shape((own, rank), F32),
-        ),
-        [SM, VM, VM, VM, HBM],
-        (place, sums, swap(sums, "pat", 1), code_gram, proj),
-        [pltpu.VMEM(proj.shape, F32), pltpu.SemaphoreType.DMA(())], flops=8e9, vmem=60,
+    sums = sums + swap(sums, "pat", 1)
+    sums = plus(sums, [swap_z(sums, high, low) for high, low in ((0, 1), (1, 0), (1, 1))])
+    mix_new, mix_again, mix_gram, inverse = call(
+        mix_kernel, (square,) * 4, [VM] * 4,
+        (sums, *(swap(sums, "code", bit) for bit in (1, 2, 3))), flops=5e9,
     )
     block = shape((half, rank, cols), F32)
-    keep, send = call(
-        numer_kernel, (block, block), [SM, SM, SM, SM, VM, VM, VM, VM],
-        (place, tile_list, tile_count, visit_counts, polar, mix_again, weights, tiles),
-        [pltpu.VMEM((n_pat, rank, cols), F32)], flops=4e9,
+    keep, send, wgram, weight_new = call(
+        numer_kernel,
+        (block, block, shape((rank // 2, 2 * rank), F32), shape((own, rank), F32)),
+        [SM, SM, SM, SM, VM, VM, VM, VM],
+        (place, tile_list, tile_count, visit_counts, shared, mix_again, inverse, tiles),
+        [pltpu.VMEM((n_pat, rank, cols), F32), pltpu.VMEM((patients, rank), F32)], flops=5e9,
     )
     groups = [[core + 2 * i for i in range(half)] for core in (0, 1)]
 

time: 129 us -> 125 us (0.969)
  blocking collectives: 47 us -> 30.9 us
  waiting for transfers between devices: 17.6 us -> 30.9 us
  Pallas kernels: 28.5 us -> 23.9 us
  starting transfers between devices: 26.5 us -> 29.6 us
  other arithmetic: 4 us -> 1.47 us
  local copies, waits for them, and re-layouts: 2.12 us -> 4.54 us
    all_to_all x1 -> x0, blocking collectives: 14.8 us -> none  [body(): proj = lax.all_to_all(proj, 'code', 0, 0, tiled=True)]
    ppermute x0 -> x3, waiting for transfers between devices: none -> 8.86 us  [swap_z(): return lax.ppermute(x, ('pat', 'code'), pairs)]
    ppermute x8 -> x10, waiting for transfers between devices: 4.59 us -> 9.34 us  [swap(): return lax.ppermute(x, axis, [(i, i ^ bit) for i in range(size)])]
    pallas_call x10 -> x9, Pallas kernels: 28.5 us -> 23.9 us  [call(): pl.pallas_call(kernel, out_shape=outs, in_specs=specs, out_specs=(spec,)...]
    ppermute x0 -> x3, starting transfers between devices: none -> 4 us  [swap_z(): return lax.ppermute(x, ('pat', 'code'), pairs)]
    unnamed x28 -> x20, local copies, waits for them, and re-layouts: 2.12 us -> 4.54 us
    ppermute x8 -> x10, starting transfers between devices: 15.9 us -> 13.6 us  [swap(): return lax.ppermute(x, axis, [(i, i ^ bit) for i in range(size)])]
    convert_element_type x1, other arithmetic: 3 us -> 1.22 us  [body(): sent = partial.astype(F16).reshape(n_code, own * VBLOCKS * rank, rows)]
  transfers between devices with their start and end apart: 10 -> 15, of which waited for: 5 -> 9; matrix products, arithmetic and copies ran while one was open for 0% -> 0% of each run, Pallas kernels for 8% -> 6%
where the time goes in v6:
time: 125 us; the launch traced here: 123 us
  waiting for transfers between devices  30.9 us (25%)
  blocking collectives  30.9 us (25%)
  starting transfers between devices  29.6 us (24%)
  Pallas kernels  23.9 us (19%)
  local copies, waits for them, and re-layouts  4.54 us (4%)
  other arithmetic  1.47 us (1%)
  between operations  1.43 us (1%)
    all_to_all x2, blocking collectives, exchange(): return lax.all_to_all(x, 'pat', 0, 0, axis_index_groups=groups, tiled=True)  30.9 us
    pallas_call x9, Pallas kernels, call(): pl.pallas_call(kernel, out_shape=outs, in_specs=specs, out_specs=(spec,)...  23.9 us
    ppermute x10, starting transfers between devices, swap(): return lax.ppermute(x, axis, [(i, i ^ bit) for i in range(size)])  13.6 us
    all_to_all x1, waiting for transfers between devices, body(): got = lax.all_to_all(sent, 'code', 0, 0, tiled=True)  12.7 us
    ppermute x10, waiting for transfers between devices, swap(): return lax.ppermute(x, axis, [(i, i ^ bit) for i in range(size)])  9.34 us
    ppermute x3, waiting for transfers between devices, swap_z(): return lax.ppermute(x, ('pat', 'code'), pairs)  8.86 us
    all_to_all x1, starting transfers between devices, body(): shared = lax.all_to_all(message, 'code', 0, 0, tiled=True)  6.38 us
    all_to_all x1, starting transfers between devices, body(): got = lax.all_to_all(sent, 'code', 0, 0, tiled=True)  5.62 us
  transfers between devices with their start and end apart: 15, of which 9 were waited for; matrix products, arithmetic and copies ran while one was open for 0% of the time, Pallas kernels for 6%

profile of v6, /device:TPU:3, one launch (start us, length us, event | category | flops | bytes accessed | tf_op | source)
XLA Modules:
  0.0 122.8 jit_solution(15603753019887368039)
XLA Ops:
  1.3 0.0 copy-start
  1.3 1.6 %copy-done = f32[64,8192]{1,0:T(8,128)S(1)} copy-done((f32[64,8192]{1,0:T(8,128)S(1)}, f32[64,8192]{1,0:T(8,128)}, u32[]{:S(2)}) %copy-start) | copy-done | bytes 2097176
  2.9 1.6 %copy-done.2 = bf16[1,1,16,128,512]{4,3,2,1,0:T(8,128)(2,1)S(1)} copy-done((bf16[1,1,16,128,512]{4,3,2,1,0:T(8,128)(2,1)S(1)}, bf16[1,1,16,128,512]{4,3,2,1,0:T(8,128)(2,1)}, u32[]{:S(2)}) %copy-start.2) | copy-done | bytes 2097176
  4.5 0.7 copy-done.4
  5.1 0.7 copy-done.6
  5.8 1.9 %shard_map.94 = f32[64,64,128]{2,1,0:T(8,128)S(1)} custom-call(s32[1,3,1,16]{3,2,1,0:T(1,128)S(1)} %bitcast.9, s32[1,1]{1,0:T(1,128)S(6)} %copy.12.count_ref, s32[32]{0:T(128)S(1)} %copy-done.6, bf16[16,128,512]{2,1,0:T(8,128)(2,1)S(1)} %bitcast.6, f32[64,8192]{1,0:T(8,128)S(1)} %copy-done), custom_call_target="tpu_custom_call" | custom-call | flops 1000000000 | bytes 65536 | tf_op jit(solution)/shard_map/pallas_call | solution.py:287
  7.7 0.0 copy-start.1
  7.8 1.2 convert_element_type.6
  9.0 5.6 %all-to-all-start = ((f16[8,512,128]{2,1,0:T(8,128)(2,1)}), f16[8,512,128]{2,1,0:T(8,128)(2,1)S(1)}, u32[]{:S(2)}, u32[]{:S(2)}) async-start(f16[8,512,128]{2,1,0:T(8,128)(2,1)} %bitcast.4), calls=%async_computation | async-start | bytes 2097152 | tf_op jit(solution)/shard_map/all_to_all | solution.py:340
  14.6 0.8 shard_map.95.gram_ref
  15.4 0.1 pad_add_fusion.at_ref.place_ref
  15.5 12.7 %all-to-all-done = f16[8,512,128]{2,1,0:T(8,128)(2,1)S(1)} async-done(((f16[8,512,128]{2,1,0:T(8,128)(2,1)}), f16[8,512,128]{2,1,0:T(8,128)(2,1)S(1)}, u32[]{:S(2)}, u32[]{:S(2)}) %all-to-all-start) | async-done | bytes 1048608 | tf_op jit(solution)/shard_map/all_to_all | solution.py:340
  28.2 0.1 convert_reduce_fusion
  28.4 5.0 %shard_map.96 = (f32[96,128]{1,0:T(8,128)S(1)}, bf16[8,768,128]{2,1,0:T(8,128)(2,1)}) custom-call(s32[2]{0:T(128)S(1)} %pad_add_fusion.at_ref.place_ref, f32[8,64,128]{2,1,0:T(8,128)S(1)} %bitcast.8, f32[64,64]{1,0:T(8,128)S(1)} %copy-done.8, f32[32,64]{1,0:T(8,128)S(1)} %copy-done.9, f32[32,128]{1,0:T(8,128)S(1)} %shard_map.95.gram_ref), custom_call_target="tpu_custom_call" | custom-call | flops 5000000000 | bytes 65536 | tf_op jit(solution)/shard_map/pallas_call | solution.py:287
  33.4 6.4 %all-to-all-start.1 = ((bf16[8,768,128]{2,1,0:T(8,128)(2,1)}), bf16[8,768,128]{2,1,0:T(8,128)(2,1)}, u32[]{:S(2)}, u32[]{:S(2)}) async-start(bf16[8,768,128]{2,1,0:T(8,128)(2,1)} %get-tuple-element.13), calls=%async_computation.1 | async-start | bytes 3145728 | tf_op jit(solution)/shard_map/all_to_all | solution.py:351
  39.8 2.7 %collective-permute-start.2 = (f32[96,128]{1,0:T(8,128)S(1)}, f32[96,128]{1,0:T(8,128)S(1)}, u32[]{:S(2)}, u32[]{:S(2)}) collective-permute-start(f32[96,128]{1,0:T(8,128)S(1)} %get-tuple-element.14), channel_id=1, source_target_pairs={{0,48},{8,56},{16,32},{24,40},{32,16},{40,24},{48,0},{56,8},{64,11... | collective-permute-start | bytes 147464 | tf_op jit(solution)/shard_map/ppermute | solution.py:301
  42.5 0.3 collective-permute-start.1
  42.9 0.2 collective-permute-start
  43.1 0.9 collective-permute-done.2
  44.0 3.0 %collective-permute-done.1 = f32[96,128]{1,0:T(8,128)S(1)} collective-permute-done((f32[96,128]{1,0:T(8,128)S(1)}, f32[96,128]{1,0:T(8,128)S(1)}, u32[]{:S(2)}, u32[]{:S(2)}) %collective-permute-start.1) | collective-permute-done | bytes 49184 | tf_op jit(solution)/shard_map/ppermute | solution.py:301
  47.0 0.0 collective-permute-done
  47.0 2.6 %collective-permute-start.3 = (f32[96,128]{1,0:T(8,128)S(1)}, f32[96,128]{1,0:T(8,128)S(1)}, u32[]{:S(2)}, u32[]{:S(2)}) collective-permute-start(f32[96,128]{1,0:T(8,128)S(1)} %add_add_fusion.1), channel_id=1, source_target_pairs={{0,8},{8,0},{16,24},{24,16},{32,40},{40,32},{48,56},{56,48},{64,72... | collective-permute-start | bytes 147464 | tf_op jit(solution)/shard_map/ppermute | solution.py:301
  49.6 0.9 collective-permute-done.3
  50.5 3.3 %collective-permute-start.6 = (f32[96,128]{1,0:T(8,128)S(1)}, f32[96,128]{1,0:T(8,128)S(1)}, u32[]{:S(2)}, u32[]{:S(2)}) collective-permute-start(f32[96,128]{1,0:T(8,128)S(1)} %add.24), channel_id=1, source_target_pairs={{0,68},{1,69},{2,70},{3,71},{4,64},{5,65},{6,66},{7,67},{8,76},{9,... | collective-permute-start | bytes 147464 | tf_op jit(solution)/shard_map/ppermute | solution.py:311
  53.8 0.1 collective-permute-start.5
  53.9 0.6 collective-permute-start.4
  54.5 1.1 collective-permute-done.6
  55.6 7.8 %collective-permute-done.5 = f32[96,128]{1,0:T(8,128)S(1)} collective-permute-done((f32[96,128]{1,0:T(8,128)S(1)}, f32[96,128]{1,0:T(8,128)S(1)}, u32[]{:S(2)}, u32[]{:S(2)}) %collective-permute-start.5) | collective-permute-done | bytes 49184 | tf_op jit(solution)/shard_map/ppermute | solution.py:311
  63.4 0.0 copy-start.3
  63.4 0.0 copy-start.5
  63.4 0.0 copy-start.7
  63.4 0.1 collective-permute-start.9
  63.5 0.6 collective-permute-start.8
  64.1 2.6 %collective-permute-start.7 = (f32[96,128]{1,0:T(8,128)S(1)}, f32[96,128]{1,0:T(8,128)S(1)}, u32[]{:S(2)}, u32[]{:S(2)}) collective-permute-start(f32[96,128]{1,0:T(8,128)S(1)} %add_add_fusion.a_ref), channel_id=1, source_target_pairs={{0,1},{1,0},{2,3},{3,2},{4,5},{5,4},{6,7},{7,6},{8,9},{9,8},{10,11... | collective-permute-start | bytes 147464 | tf_op jit(solution)/shard_map/ppermute | solution.py:301
  66.8 1.3 %collective-permute-done.8.c_ref = f32[96,128]{1,0:T(8,128)S(1)} collective-permute-done((f32[96,128]{1,0:T(8,128)S(1)}, f32[96,128]{1,0:T(8,128)S(1)}, u32[]{:S(2)}, u32[]{:S(2)}) %collective-permute-start.8) | collective-permute-done | bytes 49184 | tf_op jit(solution)/shard_map/ppermute | solution.py:301
  68.0 1.0 collective-permute-done.7.b_ref
  69.1 5.5 %shard_map.97 = (f32[64,64]{1,0:T(8,128)}, f32[64,64]{1,0:T(8,128)S(1)}, f32[64,64]{1,0:T(8,128)S(1)}, f32[64,64]{1,0:T(8,128)S(1)}) custom-call(f32[96,128]{1,0:T(8,128)S(1)} %add_add_fusion.a_ref, f32[96,128]{1,0:T(8,128)S(1)} %collective-permute-done.7.b_ref, f32[96,128]{1,0:T(8,128)S(1)} %collective-permute-done.8.c_ref, ...), custom_call_target="tpu_custom_call" | custom-call | flops 5000000000 | bytes 65536 | tf_op jit(solution)/shard_map/pallas_call | solution.py:287
  74.6 4.7 %shard_map.98 = (f32[8,64,512]{2,1,0:T(8,128)S(1)}, f32[8,64,512]{2,1,0:T(8,128)S(1)}, f32[32,128]{1,0:T(8,128)S(1)}, f32[4,64]{1,0:T(4,128)}) custom-call(s32[2]{0:T(128)S(1)} %pad_add_fusion.at_ref.place_ref, s32[1,3,1,16]{3,2,1,0:T(1,128)S(1)} %bitcast.10, s32[1,1]{1,0:T(1,128)S(6)} %copy.12.count_ref, s32[32]{0:T(128)S(1)} %copy-done.7, ...), custom_call_target="tpu_custom_call" | custom-call | flops 5000000000 | bytes 65536 | tf_op jit(solution)/shard_map/pallas_call | solution.py:287
  79.3 2.0 %collective-permute-start.10 = (f32[8,64,512]{2,1,0:T(8,128)S(1)}, f32[8,64,512]{2,1,0:T(8,128)S(1)}, u32[]{:S(2)}, u32[]{:S(2)}) collective-permute-start(f32[8,64,512]{2,1,0:T(8,128)S(1)} %get-tuple-element.18), channel_id=1, source_target_pairs={{0,8},{8,0},{16,24},{24,16},{32,40},{40,32},{48,56},{56,48},{64,72... | collective-permute-start | bytes 3145736 | tf_op jit(solution)/shard_map/ppermute | solution.py:301
  81.3 0.0 collective-permute-start.11
  81.3 2.3 %collective-permute-done.11.gram_b = f32[32,128]{1,0:T(8,128)S(1)} collective-permute-done((f32[32,128]{1,0:T(8,128)S(1)}, f32[32,128]{1,0:T(8,128)S(1)}, u32[]{:S(2)}, u32[]{:S(2)}) %collective-permute-start.11) | collective-permute-done | bytes 16416 | tf_op jit(solution)/shard_map/ppermute | solution.py:301
  83.6 0.1 shard_map.99
  83.7 18.2 %all_to_all.20.got_ref = bf16[8,5,64,128]{3,2,1,0:T(8,128)(2,1)S(1)} all-to-all(bf16[8,5,64,128]{3,2,1,0:T(8,128)(2,1)S(1)} %shard_map.99), channel_id=1, replica_groups={{0,16,32,48,64,80,96,112},{8,24,40,56,72,88,104,120},{1,17,33,49,65,81,..., dimensions={0} | all-to-all | bytes 1310720 | tf_op jit(solution)/shard_map/all_to_all | solution.py:370
  101.9 2.7 %shard_map.100 = bf16[8,64,512]{2,1,0:T(8,128)(2,1)S(1)} custom-call(bf16[8,5,64,128]{3,2,1,0:T(8,128)(2,1)S(1)} %all_to_all.20.got_ref, f32[64,64]{1,0:T(8,128)S(1)} %get-tuple-element.20.mgram_ref), custom_call_target="tpu_custom_call" | custom-call | flops 1000000000 | bytes 65536 | tf_op jit(solution)/shard_map/pallas_call | solution.py:287
  104.6 12.6 %all_to_all.21.from_ref = bf16[8,64,512]{2,1,0:T(8,128)(2,1)S(1)} all-to-all(bf16[8,64,512]{2,1,0:T(8,128)(2,1)S(1)} %shard_map.100), channel_id=1, replica_groups={{0,16,32,48,64,80,96,112},{8,24,40,56,72,88,104,120},{1,17,33,49,65,81,..., dimensions={0} | all-to-all | bytes 1048576 | tf_op jit(solution)/shard_map/all_to_all | solution.py:370
  117.3 2.3 %collective-permute-start.12 = (bf16[8,64,512]{2,1,0:T(8,128)(2,1)S(1)}, bf16[8,64,512]{2,1,0:T(8,128)(2,1)S(1)}, u32[]{:S(2)}, u32[]{:S(2)}) collective-permute-start(bf16[8,64,512]{2,1,0:T(8,128)(2,1)S(1)} %all_to_all.21.from_ref), channel_id=1, source_target_pairs={{0,8},{8,0},{16,24},{24,16},{32,40},{40,32},{48,56},{56,48},{64,72... | collective-permute-start | bytes 1572872 | tf_op jit(solution)/shard_map/ppermute | solution.py:301
  119.6 1.6 %shard_map.101.refs_0_ = f32[64,8192]{1,0:T(8,128)} custom-call(s32[2]{0:T(128)S(1)} %pad_add_fusion.at_ref.place_ref, bf16[8,64,512]{2,1,0:T(8,128)(2,1)S(1)} %all_to_all.21.from_ref), custom_call_target="tpu_custom_call" | custom-call | flops 1000000000 | bytes 65536 | tf_op jit(solution)/shard_map/pallas_call | solution.py:287
  121.2 1.6 %shard_map.102 = f32[64,8192]{1,0:T(8,128)} custom-call(s32[2]{0:T(128)S(1)} %pad_add_fusion.at_ref.place_ref, bf16[8,64,512]{2,1,0:T(8,128)(2,1)S(1)} %collective-permute-done.12.from_ref, f32[64,8192]{1,0:T(8,128)} %shard_map.101.refs_0_), custom_call_target="tpu_custom_call", output_to_operand_aliasing={{}: (2, {})} | custom-call | flops 1000000000 | bytes 65536 | tf_op jit(solution)/shard_map/pallas_call | solution.py:287
  (19 shorter events, 0.1 us)
Async XLA Ops:
  1.3 1.6 %copy-start = (f32[64,8192]{1,0:T(8,128)S(1)}, f32[64,8192]{1,0:T(8,128)}, u32[]{:S(2)}) copy-start(f32[64,8192]{1,0:T(8,128)} %code_ref.3) | copy-start | bytes 6291460
  2.9 1.6 %copy-start.2 = (bf16[1,1,16,128,512]{4,3,2,1,0:T(8,128)(2,1)S(1)}, bf16[1,1,16,128,512]{4,3,2,1,0:T(8,128)(2,1)}, u32[]{:S(2)}) copy-start(bf16[1,1,16,128,512]{4,3,2,1,0:T(8,128)(2,1)} %param.7) | copy-start | bytes 6291460
  4.5 0.7 copy-start.4
  5.1 0.7 copy-start.6
  7.7 6.9 %copy-start.1 = (f32[64,8192]{1,0:T(8,128)S(1)}, f32[64,8192]{1,0:T(8,128)}, u32[]{:S(2)}) copy-start(f32[64,8192]{1,0:T(8,128)} %code_ref.3) | copy-start | bytes 6291460
  9.0 19.2 %all-to-all-start = ((f16[8,512,128]{2,1,0:T(8,128)(2,1)}), f16[8,512,128]{2,1,0:T(8,128)(2,1)S(1)}, u32[]{:S(2)}, u32[]{:S(2)}) async-start(f16[8,512,128]{2,1,0:T(8,128)(2,1)} %bitcast.4), calls=%async_computation | async-start | bytes 2097152 | tf_op jit(solution)/shard_map/all_to_all | solution.py:340
  14.6 13.8 %copy-start.8 = (f32[64,64]{1,0:T(8,128)S(1)}, f32[64,64]{1,0:T(8,128)}, u32[]{:S(2)}) copy-start(f32[64,64]{1,0:T(8,128)} %mix_ref.1) | copy-start | bytes 49156
  14.6 13.8 %copy-start.9 = (f32[32,64]{1,0:T(8,128)S(1)}, f32[32,64]{1,0:T(8,128)}, u32[]{:S(2)}) copy-start(f32[32,64]{1,0:T(8,128)} %weight_ref.1) | copy-start | bytes 24580
  33.4 41.1 %all-to-all-start.1 = ((bf16[8,768,128]{2,1,0:T(8,128)(2,1)}), bf16[8,768,128]{2,1,0:T(8,128)(2,1)}, u32[]{:S(2)}, u32[]{:S(2)}) async-start(bf16[8,768,128]{2,1,0:T(8,128)(2,1)} %get-tuple-element.13), calls=%async_computation.1 | async-start | bytes 3145728 | tf_op jit(solution)/shard_map/all_to_all | solution.py:351
  39.8 4.2 %collective-permute-start.2 = (f32[96,128]{1,0:T(8,128)S(1)}, f32[96,128]{1,0:T(8,128)S(1)}, u32[]{:S(2)}, u32[]{:S(2)}) collective-permute-start(f32[96,128]{1,0:T(8,128)S(1)} %get-tuple-element.14), channel_id=1, source_target_pairs={{0,48},{8,56},{16,32},{24,40},{32,16},{40,24},{48,0},{56,8},{64,11... | collective-permute-start | bytes 147464 | tf_op jit(solution)/shard_map/ppermute | solution.py:301
  42.5 4.4 %collective-permute-start.1 = (f32[96,128]{1,0:T(8,128)S(1)}, f32[96,128]{1,0:T(8,128)S(1)}, u32[]{:S(2)}, u32[]{:S(2)}) collective-permute-start(f32[96,128]{1,0:T(8,128)S(1)} %get-tuple-element.14), channel_id=1, source_target_pairs={{0,32},{8,40},{16,48},{24,56},{32,0},{40,8},{48,16},{56,24},{64,96... | collective-permute-start | bytes 147464 | tf_op jit(solution)/shard_map/ppermute | solution.py:301
  42.9 4.1 %collective-permute-start = (f32[96,128]{1,0:T(8,128)S(1)}, f32[96,128]{1,0:T(8,128)S(1)}, u32[]{:S(2)}, u32[]{:S(2)}) collective-permute-start(f32[96,128]{1,0:T(8,128)S(1)} %get-tuple-element.14), channel_id=1, source_target_pairs={{0,16},{8,24},{16,0},{24,8},{32,48},{40,56},{48,32},{56,40},{64,80... | collective-permute-start | bytes 147464 | tf_op jit(solution)/shard_map/ppermute | solution.py:301
  47.0 3.5 %collective-permute-start.3 = (f32[96,128]{1,0:T(8,128)S(1)}, f32[96,128]{1,0:T(8,128)S(1)}, u32[]{:S(2)}, u32[]{:S(2)}) collective-permute-start(f32[96,128]{1,0:T(8,128)S(1)} %add_add_fusion.1), channel_id=1, source_target_pairs={{0,8},{8,0},{16,24},{24,16},{32,40},{40,32},{48,56},{56,48},{64,72... | collective-permute-start | bytes 147464 | tf_op jit(solution)/shard_map/ppermute | solution.py:301
  50.5 5.1 %collective-permute-start.6 = (f32[96,128]{1,0:T(8,128)S(1)}, f32[96,128]{1,0:T(8,128)S(1)}, u32[]{:S(2)}, u32[]{:S(2)}) collective-permute-start(f32[96,128]{1,0:T(8,128)S(1)} %add.24), channel_id=1, source_target_pairs={{0,68},{1,69},{2,70},{3,71},{4,64},{5,65},{6,66},{7,67},{8,76},{9,... | collective-permute-start | bytes 147464 | tf_op jit(solution)/shard_map/ppermute | solution.py:311
  53.8 9.5 %collective-permute-start.5 = (f32[96,128]{1,0:T(8,128)S(1)}, f32[96,128]{1,0:T(8,128)S(1)}, u32[]{:S(2)}, u32[]{:S(2)}) collective-permute-start(f32[96,128]{1,0:T(8,128)S(1)} %add.24), channel_id=1, source_target_pairs={{0,64},{1,65},{2,66},{3,67},{4,68},{5,69},{6,70},{7,71},{8,72},{9,... | collective-permute-start | bytes 147464 | tf_op jit(solution)/shard_map/ppermute | solution.py:311
  53.9 9.5 %collective-permute-start.4 = (f32[96,128]{1,0:T(8,128)S(1)}, f32[96,128]{1,0:T(8,128)S(1)}, u32[]{:S(2)}, u32[]{:S(2)}) collective-permute-start(f32[96,128]{1,0:T(8,128)S(1)} %add.24), channel_id=1, source_target_pairs={{0,4},{1,5},{2,6},{3,7},{4,0},{5,1},{6,2},{7,3},{8,12},{9,13},{10,... | collective-permute-start | bytes 147464 | tf_op jit(solution)/shard_map/ppermute | solution.py:311
  63.4 11.2 %copy-start.3 = (bf16[1,1,16,128,512]{4,3,2,1,0:T(8,128)(2,1)S(1)}, bf16[1,1,16,128,512]{4,3,2,1,0:T(8,128)(2,1)}, u32[]{:S(2)}) copy-start(bf16[1,1,16,128,512]{4,3,2,1,0:T(8,128)(2,1)} %param.7) | copy-start | bytes 6291460
  63.4 11.1 %copy-start.5 = (s32[1,1,3,16]{3,1,2,0:T(1,128)S(1)}, s32[1,1,3,16]{3,1,2,0:T(1,128)}, u32[]{:S(2)}) copy-start(s32[1,1,3,16]{3,1,2,0:T(1,128)} %param.8) | copy-start | bytes 580
  63.4 11.1 %copy-start.7 = (s32[32]{0:T(128)S(1)}, s32[32]{0:T(128)}, u32[]{:S(2)}) copy-start(s32[32]{0:T(128)} %visits_ref.1) | copy-start | bytes 388
  63.4 3.3 %collective-permute-start.9 = (f32[96,128]{1,0:T(8,128)S(1)}, f32[96,128]{1,0:T(8,128)S(1)}, u32[]{:S(2)}, u32[]{:S(2)}) collective-permute-start(f32[96,128]{1,0:T(8,128)S(1)} %add_add_fusion.a_ref), channel_id=1, source_target_pairs={{0,3},{1,2},{2,1},{3,0},{4,7},{5,6},{6,5},{7,4},{8,11},{9,10},{10,... | collective-permute-start | bytes 147464 | tf_op jit(solution)/shard_map/ppermute | solution.py:301
  63.5 4.5 %collective-permute-start.8 = (f32[96,128]{1,0:T(8,128)S(1)}, f32[96,128]{1,0:T(8,128)S(1)}, u32[]{:S(2)}, u32[]{:S(2)}) collective-permute-start(f32[96,128]{1,0:T(8,128)S(1)} %add_add_fusion.a_ref), channel_id=1, source_target_pairs={{0,2},{1,3},{2,0},{3,1},{4,6},{5,7},{6,4},{7,5},{8,10},{9,11},{10,... | collective-permute-start | bytes 147464 | tf_op jit(solution)/shard_map/ppermute | solution.py:301
  64.1 4.9 %collective-permute-start.7 = (f32[96,128]{1,0:T(8,128)S(1)}, f32[96,128]{1,0:T(8,128)S(1)}, u32[]{:S(2)}, u32[]{:S(2)}) collective-permute-start(f32[96,128]{1,0:T(8,128)S(1)} %add_add_fusion.a_ref), channel_id=1, source_target_pairs={{0,1},{1,0},{2,3},{3,2},{4,5},{5,4},{6,7},{7,6},{8,9},{9,8},{10,11... | collective-permute-start | bytes 147464 | tf_op jit(solution)/shard_map/ppermute | solution.py:301
  79.3 4.4 %collective-permute-start.10 = (f32[8,64,512]{2,1,0:T(8,128)S(1)}, f32[8,64,512]{2,1,0:T(8,128)S(1)}, u32[]{:S(2)}, u32[]{:S(2)}) collective-permute-start(f32[8,64,512]{2,1,0:T(8,128)S(1)} %get-tuple-element.18), channel_id=1, source_target_pairs={{0,8},{8,0},{16,24},{24,16},{32,40},{40,32},{48,56},{56,48},{64,72... | collective-permute-start | bytes 3145736 | tf_op jit(solution)/shard_map/ppermute | solution.py:301
  81.3 2.3 %collective-permute-start.11 = (f32[32,128]{1,0:T(8,128)S(1)}, f32[32,128]{1,0:T(8,128)S(1)}, u32[]{:S(2)}, u32[]{:S(2)}) collective-permute-start(f32[32,128]{1,0:T(8,128)S(1)} %get-tuple-element.19.gram_a), channel_id=1, source_target_pairs={{0,8},{8,0},{16,24},{24,16},{32,40},{40,32},{48,56},{56,48},{64,72... | collective-permute-start | bytes 49160 | tf_op jit(solution)/shard_map/ppermute | solution.py:301
  117.3 3.9 %collective-permute-start.12 = (bf16[8,64,512]{2,1,0:T(8,128)(2,1)S(1)}, bf16[8,64,512]{2,1,0:T(8,128)(2,1)S(1)}, u32[]{:S(2)}, u32[]{:S(2)}) collective-permute-start(bf16[8,64,512]{2,1,0:T(8,128)(2,1)S(1)} %all_to_all.21.from_ref), channel_id=1, source_target_pairs={{0,8},{8,0},{16,24},{24,16},{32,40},{40,32},{48,56},{56,48},{64,72... | collective-permute-start | bytes 1572872 | tf_op jit(solution)/shard_map/ppermute | solution.py:301

commit v7 on v6

--- a/solution.py
+++ b/solution.py
@@ -124,16 +124,34 @@
 
 
 def products_kernel(
-    list_ref, count_ref, visits_hbm, tile_ref, code_ref, out_ref, visits_ref, sem
+    list_hbm, count_hbm, visits_hbm, tile_hbm, code_hbm, out_ref,
+    list_ref, count_ref, visits_ref, tile_ref, code_ref, small_sems, sems,
 ):
-    copy = pltpu.make_async_copy(visits_hbm, visits_ref, sem)
-    copy.start()
     slots, rows, cols = tile_ref.shape
     rank = code_ref.shape[0]
+    parts = sems.shape[0] - 1
+    each = slots // parts
+    small = []
+    for i, (src, dst) in enumerate(
+        ((list_hbm, list_ref), (count_hbm, count_ref), (visits_hbm, visits_ref))
+    ):
+        small.append(pltpu.make_async_copy(src, dst, small_sems.at[i]))
+        small[-1].start()
+    code_copy = pltpu.make_async_copy(code_hbm, code_ref, sems.at[parts])
+    code_copy.start()
+    copies = []
+    for i in range(parts):
+        at = pl.ds(i * each, each)
+        copies.append(pltpu.make_async_copy(tile_hbm.at[0, 0, at], tile_ref.at[at], sems.at[i]))
+        copies[-1].start()
     out_ref[...] = jnp.zeros(out_ref.shape, F32)
     lane = lax.broadcasted_iota(jnp.int32, (rank, rows), 1)
-    copy.wait()
+    for copy in small:
+        copy.wait()
+    code_copy.wait()
     for t in range(slots):
+        if t % each == 0:
+            copies[t // each].wait()
         k, b, g, kept = live_rows(t, list_ref, count_ref, visits_ref, rows)
         codes = code_ref[:, pl.ds(pl.multiple_of(g * cols, cols), cols)].astype(BF16)
         part = mm16(codes, tile_ref[t], NT)
@@ -149,7 +167,6 @@
 def polar_kernel(
     scales, at_ref, prod_ref, mix_ref, weight_ref, gram_ref, sums_ref, out_ref
 ):
-    dests = out_ref.shape[0]
     segs, rank, rows = prod_ref.shape
     own = segs // VBLOCKS
     eye = lax.broadcasted_iota(jnp.int32, (rank, rank), 0) == lax.broadcasted_iota(
@@ -178,9 +195,8 @@
     sums_ref[:low, :] = halves(numer)
     sums_ref[low:rank, :] = halves(mm(weight, weight, TN)) * scales[0]
     sums_ref[rank:, :] = gram_ref[...] * scales[1]
-    for d in range(dests):
-        for i, piece in enumerate(pieces):
-            out_ref[d, i * rank : (i + 1) * rank, :] = piece
+    for i, piece in enumerate(pieces):
+        out_ref[i * rank : (i + 1) * rank, :] = piece
 
 
 def whole(x):
@@ -210,6 +226,13 @@
     rank = mix_ref.shape[0]
     own = own_ref.shape[0]
     first = own * VBLOCKS * rank
+    layers = 2
+    z_at = lax.div(place_ref[0], sources // layers)
+
+    def source(d):
+        x_at, layer = lax.rem(d, sources // layers), lax.div(d, sources // layers)
+        return x_at * layers + jnp.where(layer == z_at, 0, 1)
+
     mix = mix_ref[...]
     twice = jnp.concatenate([mix, mix], axis=1)
     terms = []
@@ -221,15 +244,16 @@
     weight = jnp.maximum(mm(fold(jnp.concatenate(terms, axis=0)), inverse_ref[...]), 0.0)
     weight_ref[...] = weight
     for j in range(own):
-        own_ref[j : j + 1, :] = weight_ref[pl.ds(place_ref[0] * own + j, 1), :]
+        own_ref[j : j + 1, :] = weight_ref[pl.ds(source(place_ref[0]) * own + j, 1), :]
     wgram_ref[...] = halves(mm(weight, weight, TN))
     acc_ref[...] = jnp.zeros(acc_ref.shape, F32)
     lane = lax.broadcasted_iota(jnp.int32, (rank, rows), 1)
     for t in range(slots):
         k, b, g, kept = live_rows(t, list_ref, count_ref, visits_ref, rows)
-        both = jnp.concatenate(split(mix * weight_ref[pl.ds(k, 1), :]), axis=0)
-        at = pl.multiple_of((lax.rem(k, own) * VBLOCKS + b) * rank, rank)
-        polar = got_ref[lax.div(k, own), pl.ds(at, rank), :]
+        d, j = source(lax.div(k, own)), lax.rem(k, own)
+        both = jnp.concatenate(split(mix * weight_ref[pl.ds(d * own + j, 1), :]), axis=0)
+        at = pl.multiple_of((j * VBLOCKS + b) * rank, rank)
+        polar = got_ref[d, pl.ds(at, rank), :]
         spread = mm16(both, jnp.concatenate([polar, polar], axis=0), TN)
         spread = jnp.where(lane < kept, spread, 0.0).astype(BF16)
         acc_ref[g] += mm16(spread, tile_ref[t])
@@ -332,9 +356,15 @@
     square = shape((rank, rank), F32)
 
     partial = call(
-        products_kernel, shape((patients * VBLOCKS, rank, rows), F32), [SM, SM, HBM, VM, VM],
-        (tile_list, tile_count, visit_counts, tiles, code_factor_t),
-        [pltpu.SMEM(visit_counts.shape, jnp.int32), pltpu.SemaphoreType.DMA(())],
+        products_kernel, shape((patients * VBLOCKS, rank, rows), F32), [HBM] * 5,
+        (tile_list, tile_count, visit_counts, tile_data, code_factor_t),
+        [
+            pltpu.SMEM(tile_list.shape, jnp.int32), pltpu.SMEM(tile_count.shape, jnp.int32),
+            pltpu.SMEM(visit_counts.shape, jnp.int32), pltpu.VMEM(tiles.shape, BF16),
+            pltpu.VMEM(code_factor_t.shape, F32), pltpu.SemaphoreType.DMA((3,)),
+            pltpu.SemaphoreType.DMA((5,)),
+        ],
+        vmem=50,
     )
     sent = partial.astype(F16).reshape(n_code, own * VBLOCKS * rank, rows)
     got = lax.all_to_all(sent, "code", 0, 0, tiled=True)
@@ -345,16 +375,22 @@
     length = (own * VBLOCKS + own) * rank
     sums, message = call(
         functools.partial(polar_kernel, scales),
-        (shape((3 * rank // 2, 2 * rank), F32), shape((n_code, length, rows), BF16)),
+        (shape((3 * rank // 2, 2 * rank), F32), shape((length, rows), BF16)),
         [SM, VM, VM, VM, VM], (place, products, visit_mix, patient_weight, gram), flops=5e9,
     )
-    shared = lax.all_to_all(message, "code", 0, 0, tiled=True)
+    quarter = n_code // 2
+    other = swap(message, "code", quarter)
+    sums = plus(sums, [swap(sums, "code", bit) for bit in (1, 2, 3)])
+    sums, message, other = lax.optimization_barrier((sums, message, other))
+    message = jnp.broadcast_to(jnp.concatenate([message, other])[None], (quarter, 2 * length, rows))
+    layers = [[z * quarter + i for i in range(quarter)] for z in (0, 1)]
+    shared = lax.all_to_all(message, "code", 0, 0, axis_index_groups=layers, tiled=True)
+    shared = shared.reshape(n_code, length, rows)
     sums = plus(sums, [swap(sums, "pat", bit) for bit in (2, 4, 6)])
     sums = sums + swap(sums, "pat", 1)
-    sums = plus(sums, [swap_z(sums, high, low) for high, low in ((0, 1), (1, 0), (1, 1))])
     mix_new, mix_again, mix_gram, inverse = call(
         mix_kernel, (square,) * 4, [VM] * 4,
-        (sums, *(swap(sums, "code", bit) for bit in (1, 2, 3))), flops=5e9,
+        (sums, *(swap_z(sums, high, low) for high, low in ((0, 1), (1, 0), (1, 1)))), flops=5e9,
     )
     block = shape((half, rank, cols), F32)
     keep, send, wgram, weight_new = call(

time: 125 us -> 119 us (0.952)
  waiting for transfers between devices: 30.9 us -> 27.7 us
  local copies, waits for them, and re-layouts: 4.54 us -> 2.71 us
  starting transfers between devices: 29.6 us -> 31.4 us
  blocking collectives: 30.9 us -> 29.3 us
    ppermute x3, waiting for transfers between devices: 8.86 us -> 3.45 us  [swap_z(): return lax.ppermute(x, ('pat', 'code'), pairs)]
    ppermute x10 -> x11, starting transfers between devices: 13.6 us -> 16.8 us  [swap(): return lax.ppermute(x, axis, [(i, i ^ bit) for i in range(size)])]
    unnamed x20 -> x16, local copies, waits for them, and re-layouts: 4.54 us -> 1.36 us
    ppermute x10 -> x11, waiting for transfers between devices: 9.34 us -> 11.6 us  [swap(): return lax.ppermute(x, axis, [(i, i ^ bit) for i in range(size)])]
    all_to_all x2, blocking collectives: 30.9 us -> 29.3 us  [exchange(): return lax.all_to_all(x, 'pat', 0, 0, axis_index_groups=groups, tiled=True)]
    broadcast_in_dim x0 -> x1, local copies, waits for them, and re-layouts: none -> 1.35 us  [body(): jnp.broadcast_to(jnp.concatenate([message, other])[None], (quarter, 2 * l...]
  transfers between devices with their start and end apart: 15 -> 16, of which waited for: 9 -> 10; matrix products, arithmetic and copies ran while one was open for 0% -> 0% of each run, Pallas kernels for 6% -> 7%
where the time goes in v7:
time: 119 us; the launch traced here: 118 us
  starting transfers between devices  31.4 us (26%)
  blocking collectives  29.3 us (25%)
  waiting for transfers between devices  27.7 us (23%)
  Pallas kernels  23.7 us (20%)
  local copies, waits for them, and re-layouts  2.71 us (2%)
  other arithmetic  1.5 us (1%)
  between operations  1.42 us (1%)
    all_to_all x2, blocking collectives, exchange(): return lax.all_to_all(x, 'pat', 0, 0, axis_index_groups=groups, tiled=True)  29.3 us
    pallas_call x9, Pallas kernels, call(): pl.pallas_call(kernel, out_shape=outs, in_specs=specs, out_specs=(spec,)...  23.7 us
    ppermute x11, starting transfers between devices, swap(): return lax.ppermute(x, axis, [(i, i ^ bit) for i in range(size)])  16.8 us
    all_to_all x1, waiting for transfers between devices, body(): got = lax.all_to_all(sent, 'code', 0, 0, tiled=True)  12.7 us
    ppermute x11, waiting for transfers between devices, swap(): return lax.ppermute(x, axis, [(i, i ^ bit) for i in range(size)])  11.6 us
    all_to_all x1, starting transfers between devices, body(): got = lax.all_to_all(sent, 'code', 0, 0, tiled=True)  5.63 us
    all_to_all x1, starting transfers between devices, body(): lax.all_to_all(message, 'code', 0, 0, axis_index_groups=layers, tiled=True)  5.47 us
    ppermute x3, starting transfers between devices, swap_z(): return lax.ppermute(x, ('pat', 'code'), pairs)  3.48 us
  transfers between devices with their start and end apart: 16, of which 10 were waited for; matrix products, arithmetic and copies ran while one was open for 0% of the time, Pallas kernels for 7%

profile of v7, /device:TPU:3, one launch (start us, length us, event | category | flops | bytes accessed | tf_op | source)
XLA Modules:
  0.0 117.7 jit_solution(4442693198383657933)
XLA Ops:
  1.3 0.0 copy-start.2
  1.3 0.7 copy-done.2
  2.0 0.7 copy-done.4
  2.6 2.9 %shard_map.94 = f32[64,64,128]{2,1,0:T(8,128)S(1)} custom-call(s32[1,3,1,16]{3,2,1,0:T(1,128)S(1)} %bitcast.9, s32[1,1]{1,0:T(1,128)S(6)} %copy.12.count_hbm.count_ref, s32[32]{0:T(128)S(1)} %copy-done.4, bf16[1,1,16,128,512]{4,3,2,1,0:T(8,128)(2,1)} %tile_hbm.1, f32[64,8192]{1,0:T(8,128)} %code_ref.1), custom_call_target="tpu_custom_call" | custom-call | flops 1000000000 | bytes 65536 | tf_op jit(solution)/shard_map/pallas_call | solution.py:311
  5.6 0.0 copy-start
  5.6 1.2 %convert_element_type.6 = f16[64,64,128]{2,1,0:T(8,128)(2,1)} convert(f32[64,64,128]{2,1,0:T(8,128)S(1)} %shard_map.94) | non-fusion elementwise | flops 524288 | bytes 3145728 | tf_op jit(solution)/shard_map/convert_element_type | solution.py:369
  6.8 5.6 %all-to-all-start = ((f16[8,512,128]{2,1,0:T(8,128)(2,1)}), f16[8,512,128]{2,1,0:T(8,128)(2,1)S(1)}, u32[]{:S(2)}, u32[]{:S(2)}) async-start(f16[8,512,128]{2,1,0:T(8,128)(2,1)} %bitcast.3), calls=%async_computation | async-start | bytes 2097152 | tf_op jit(solution)/shard_map/all_to_all | solution.py:370
  12.4 0.8 shard_map.95.gram_ref
  13.3 0.1 pad_add_fusion.at_ref.place_ref
  13.3 12.7 %all-to-all-done = f16[8,512,128]{2,1,0:T(8,128)(2,1)S(1)} async-done(((f16[8,512,128]{2,1,0:T(8,128)(2,1)}), f16[8,512,128]{2,1,0:T(8,128)(2,1)S(1)}, u32[]{:S(2)}, u32[]{:S(2)}) %all-to-all-start) | async-done | bytes 1048608 | tf_op jit(solution)/shard_map/all_to_all | solution.py:370
  26.0 0.1 convert_reduce_fusion
  26.2 3.8 %shard_map.96 = (f32[96,128]{1,0:T(8,128)S(1)}, bf16[768,128]{1,0:T(8,128)(2,1)S(1)}) custom-call(s32[2]{0:T(128)S(1)} %pad_add_fusion.at_ref.place_ref, f32[8,64,128]{2,1,0:T(8,128)S(1)} %bitcast.8, f32[64,64]{1,0:T(8,128)S(1)} %copy-done.6, f32[32,64]{1,0:T(8,128)S(1)} %copy-done.7, f32[32,128]{1,0:T(8,128)S(1)} %shard_map.95.gram_ref), custom_call_target="tpu_custom_call" | custom-call | flops 5000000000 | bytes 65536 | tf_op jit(solution)/shard_map/pallas_call | solution.py:311
  30.0 1.4 %collective-permute-start.2 = (f32[96,128]{1,0:T(8,128)S(1)}, f32[96,128]{1,0:T(8,128)S(1)}, u32[]{:S(2)}, u32[]{:S(2)}) collective-permute-start(f32[96,128]{1,0:T(8,128)S(1)} %get-tuple-element.16), channel_id=1, source_target_pairs={{0,3},{1,2},{2,1},{3,0},{4,7},{5,6},{6,5},{7,4},{8,11},{9,10},{10,... | collective-permute-start | bytes 147464 | tf_op jit(solution)/shard_map/ppermute | solution.py:325
  31.5 2.6 %collective-permute-start.1 = (f32[96,128]{1,0:T(8,128)S(1)}, f32[96,128]{1,0:T(8,128)S(1)}, u32[]{:S(2)}, u32[]{:S(2)}) collective-permute-start(f32[96,128]{1,0:T(8,128)S(1)} %get-tuple-element.16), channel_id=1, source_target_pairs={{0,2},{1,3},{2,0},{3,1},{4,6},{5,7},{6,4},{7,5},{8,10},{9,11},{10,... | collective-permute-start | bytes 147464 | tf_op jit(solution)/shard_map/ppermute | solution.py:325
  34.1 0.3 collective-permute-start.3
  34.4 0.0 collective-permute-done.2
  34.4 1.6 %collective-permute-done.1 = f32[96,128]{1,0:T(8,128)S(1)} collective-permute-done((f32[96,128]{1,0:T(8,128)S(1)}, f32[96,128]{1,0:T(8,128)S(1)}, u32[]{:S(2)}, u32[]{:S(2)}) %collective-permute-start.1) | collective-permute-done | bytes 49184 | tf_op jit(solution)/shard_map/ppermute | solution.py:325
  36.0 1.3 %collective-permute-done = f32[96,128]{1,0:T(8,128)S(1)} collective-permute-done((f32[96,128]{1,0:T(8,128)S(1)}, f32[96,128]{1,0:T(8,128)S(1)}, u32[]{:S(2)}, u32[]{:S(2)}) %collective-permute-start) | collective-permute-done | bytes 49184 | tf_op jit(solution)/shard_map/ppermute | solution.py:325
  37.4 1.6 %collective-permute-done.3 = bf16[768,128]{1,0:T(8,128)(2,1)S(1)} collective-permute-done((bf16[768,128]{1,0:T(8,128)(2,1)S(1)}, bf16[768,128]{1,0:T(8,128)(2,1)S(1)}, u32[]{:S(2)}, u32[]{:S(2)}) %collective-permute-start.3) | collective-permute-done | bytes 196640 | tf_op jit(solution)/shard_map/ppermute | solution.py:325
  39.0 1.3 %broadcast_in_dim.2 = bf16[4,1536,128]{2,1,0:T(8,128)(2,1)} broadcast(bf16[1536,128]{1,0:T(8,128)(2,1)S(1)} %pad_maximum_fusion), dimensions={1,2} | broadcast | bytes 1966080 | tf_op jit(solution)/shard_map/broadcast_in_dim | solution.py:385
  40.3 5.5 %all-to-all-start.1 = ((bf16[4,1536,128]{2,1,0:T(8,128)(2,1)}), bf16[4,1536,128]{2,1,0:T(8,128)(2,1)}, u32[]{:S(2)}, u32[]{:S(2)}) async-start(bf16[4,1536,128]{2,1,0:T(8,128)(2,1)} %broadcast_in_dim.2), calls=%async_computation.1 | async-start | bytes 3145728 | tf_op jit(solution)/shard_map/all_to_all | solution.py:387
  45.8 2.7 %collective-permute-start.6 = (f32[96,128]{1,0:T(8,128)S(1)}, f32[96,128]{1,0:T(8,128)S(1)}, u32[]{:S(2)}, u32[]{:S(2)}) collective-permute-start(f32[96,128]{1,0:T(8,128)S(1)} %add_add_fusion.1), channel_id=1, source_target_pairs={{0,48},{8,56},{16,32},{24,40},{32,16},{40,24},{48,0},{56,8},{64,11... | collective-permute-start | bytes 147464 | tf_op jit(solution)/shard_map/ppermute | solution.py:325
  48.5 0.4 collective-permute-start.5
  48.9 0.2 collective-permute-start.4
  49.1 0.9 collective-permute-done.6
  50.0 3.0 %collective-permute-done.5 = f32[96,128]{1,0:T(8,128)S(1)} collective-permute-done((f32[96,128]{1,0:T(8,128)S(1)}, f32[96,128]{1,0:T(8,128)S(1)}, u32[]{:S(2)}, u32[]{:S(2)}) %collective-permute-start.5) | collective-permute-done | bytes 49184 | tf_op jit(solution)/shard_map/ppermute | solution.py:325
  53.0 4.6 %collective-permute-start.7 = (f32[96,128]{1,0:T(8,128)S(1)}, f32[96,128]{1,0:T(8,128)S(1)}, u32[]{:S(2)}, u32[]{:S(2)}) collective-permute-start(f32[96,128]{1,0:T(8,128)S(1)} %add_add_fusion), channel_id=1, source_target_pairs={{0,8},{8,0},{16,24},{24,16},{32,40},{40,32},{48,56},{56,48},{64,72... | collective-permute-start | bytes 147464 | tf_op jit(solution)/shard_map/ppermute | solution.py:325
  57.6 0.9 collective-permute-done.7
  58.5 0.0 copy-start.3
  58.5 0.0 copy-start.5
  58.5 2.5 %collective-permute-start.10 = (f32[96,128]{1,0:T(8,128)S(1)}, f32[96,128]{1,0:T(8,128)S(1)}, u32[]{:S(2)}, u32[]{:S(2)}) collective-permute-start(f32[96,128]{1,0:T(8,128)S(1)} %add.27.a_ref), channel_id=1, source_target_pairs={{0,68},{1,69},{2,70},{3,71},{4,64},{5,65},{6,66},{7,67},{8,76},{9,... | collective-permute-start | bytes 147464 | tf_op jit(solution)/shard_map/ppermute | solution.py:335
  61.0 1.0 collective-permute-start.9
  62.0 1.0 collective-permute-done.10.d_ref
  63.0 2.5 %collective-permute-done.9.c_ref = f32[96,128]{1,0:T(8,128)S(1)} collective-permute-done((f32[96,128]{1,0:T(8,128)S(1)}, f32[96,128]{1,0:T(8,128)S(1)}, u32[]{:S(2)}, u32[]{:S(2)}) %collective-permute-start.9) | collective-permute-done | bytes 49184 | tf_op jit(solution)/shard_map/ppermute | solution.py:335
  65.5 0.0 collective-permute-done.8.b_ref
  65.5 5.5 %shard_map.97 = (f32[64,64]{1,0:T(8,128)}, f32[64,64]{1,0:T(8,128)S(1)}, f32[64,64]{1,0:T(8,128)S(1)}, f32[64,64]{1,0:T(8,128)S(1)}) custom-call(f32[96,128]{1,0:T(8,128)S(1)} %add.27.a_ref, f32[96,128]{1,0:T(8,128)S(1)} %collective-permute-done.8.b_ref, f32[96,128]{1,0:T(8,128)S(1)} %collective-permute-done.9.c_ref, f32[96,128]{1,0:T(8,128)S(1)} %collective-permute-done.10.d_ref), custom_call_target="tpu_custom_call" | custom-call | flops 5000000000 | bytes 65536 | tf_op jit(solution)/shard_map/pallas_call | solution.py:311
  70.9 0.0 all-to-all-done.1
  71.0 4.7 %shard_map.98 = (f32[8,64,512]{2,1,0:T(8,128)S(1)}, f32[8,64,512]{2,1,0:T(8,128)S(1)}, f32[32,128]{1,0:T(8,128)S(1)}, f32[4,64]{1,0:T(4,128)}) custom-call(s32[2]{0:T(128)S(1)} %pad_add_fusion.at_ref.place_ref, s32[1,3,1,16]{3,2,1,0:T(1,128)S(1)} %bitcast.10, s32[1,1]{1,0:T(1,128)S(6)} %copy.12.count_hbm.count_ref, s32[32]{0:T(128)S(1)} %copy-done.5, ...), custom_call_target="tpu_custom_call" | custom-call | flops 5000000000 | bytes 65536 | tf_op jit(solution)/shard_map/pallas_call | solution.py:311
  75.7 2.2 %collective-permute-start.11 = (f32[8,64,512]{2,1,0:T(8,128)S(1)}, f32[8,64,512]{2,1,0:T(8,128)S(1)}, u32[]{:S(2)}, u32[]{:S(2)}) collective-permute-start(f32[8,64,512]{2,1,0:T(8,128)S(1)} %get-tuple-element.24), channel_id=1, source_target_pairs={{0,8},{8,0},{16,24},{24,16},{32,40},{40,32},{48,56},{56,48},{64,72... | collective-permute-start | bytes 3145736 | tf_op jit(solution)/shard_map/ppermute | solution.py:325
  77.9 0.0 collective-permute-start.12
  77.9 2.3 %collective-permute-done.12.gram_b = f32[32,128]{1,0:T(8,128)S(1)} collective-permute-done((f32[32,128]{1,0:T(8,128)S(1)}, f32[32,128]{1,0:T(8,128)S(1)}, u32[]{:S(2)}, u32[]{:S(2)}) %collective-permute-start.12) | collective-permute-done | bytes 16416 | tf_op jit(solution)/shard_map/ppermute | solution.py:325
  80.2 0.1 shard_map.99
  80.3 16.6 %all_to_all.20.got_ref = bf16[8,5,64,128]{3,2,1,0:T(8,128)(2,1)S(1)} all-to-all(bf16[8,5,64,128]{3,2,1,0:T(8,128)(2,1)S(1)} %shard_map.99), channel_id=1, replica_groups={{0,16,32,48,64,80,96,112},{8,24,40,56,72,88,104,120},{1,17,33,49,65,81,..., dimensions={0} | all-to-all | bytes 1310720 | tf_op jit(solution)/shard_map/all_to_all | solution.py:406
  96.9 2.7 %shard_map.100 = bf16[8,64,512]{2,1,0:T(8,128)(2,1)S(1)} custom-call(bf16[8,5,64,128]{3,2,1,0:T(8,128)(2,1)S(1)} %all_to_all.20.got_ref, f32[64,64]{1,0:T(8,128)S(1)} %get-tuple-element.26.mgram_ref), custom_call_target="tpu_custom_call" | custom-call | flops 1000000000 | bytes 65536 | tf_op jit(solution)/shard_map/pallas_call | solution.py:311
  99.6 12.6 %all_to_all.21.from_ref = bf16[8,64,512]{2,1,0:T(8,128)(2,1)S(1)} all-to-all(bf16[8,64,512]{2,1,0:T(8,128)(2,1)S(1)} %shard_map.100), channel_id=1, replica_groups={{0,16,32,48,64,80,96,112},{8,24,40,56,72,88,104,120},{1,17,33,49,65,81,..., dimensions={0} | all-to-all | bytes 1048576 | tf_op jit(solution)/shard_map/all_to_all | solution.py:406
  112.3 2.3 %collective-permute-start.13 = (bf16[8,64,512]{2,1,0:T(8,128)(2,1)S(1)}, bf16[8,64,512]{2,1,0:T(8,128)(2,1)S(1)}, u32[]{:S(2)}, u32[]{:S(2)}) collective-permute-start(bf16[8,64,512]{2,1,0:T(8,128)(2,1)S(1)} %all_to_all.21.from_ref), channel_id=1, source_target_pairs={{0,8},{8,0},{16,24},{24,16},{32,40},{40,32},{48,56},{56,48},{64,72... | collective-permute-start | bytes 1572872 | tf_op jit(solution)/shard_map/ppermute | solution.py:325
  114.6 1.6 %shard_map.101.refs_0_ = f32[64,8192]{1,0:T(8,128)} custom-call(s32[2]{0:T(128)S(1)} %pad_add_fusion.at_ref.place_ref, bf16[8,64,512]{2,1,0:T(8,128)(2,1)S(1)} %all_to_all.21.from_ref), custom_call_target="tpu_custom_call" | custom-call | flops 1000000000 | bytes 65536 | tf_op jit(solution)/shard_map/pallas_call | solution.py:311
  116.2 1.6 %shard_map.102 = f32[64,8192]{1,0:T(8,128)} custom-call(s32[2]{0:T(128)S(1)} %pad_add_fusion.at_ref.place_ref, bf16[8,64,512]{2,1,0:T(8,128)(2,1)S(1)} %collective-permute-done.13.from_ref, f32[64,8192]{1,0:T(8,128)} %shard_map.101.refs_0_), custom_call_target="tpu_custom_call", output_to_operand_aliasing={{}: (2, {})} | custom-call | flops 1000000000 | bytes 65536 | tf_op jit(solution)/shard_map/pallas_call | solution.py:311
  (19 shorter events, 0.1 us)
Async XLA Ops:
  1.3 0.7 copy-start.2
  2.0 0.7 copy-start.4
  5.6 6.9 %copy-start = (f32[64,8192]{1,0:T(8,128)S(1)}, f32[64,8192]{1,0:T(8,128)}, u32[]{:S(2)}) copy-start(f32[64,8192]{1,0:T(8,128)} %code_ref.1) | copy-start | bytes 6291460
  6.8 19.2 %all-to-all-start = ((f16[8,512,128]{2,1,0:T(8,128)(2,1)}), f16[8,512,128]{2,1,0:T(8,128)(2,1)S(1)}, u32[]{:S(2)}, u32[]{:S(2)}) async-start(f16[8,512,128]{2,1,0:T(8,128)(2,1)} %bitcast.3), calls=%async_computation | async-start | bytes 2097152 | tf_op jit(solution)/shard_map/all_to_all | solution.py:370
  12.4 13.8 %copy-start.6 = (f32[64,64]{1,0:T(8,128)S(1)}, f32[64,64]{1,0:T(8,128)}, u32[]{:S(2)}) copy-start(f32[64,64]{1,0:T(8,128)} %mix_ref.1) | copy-start | bytes 49156
  12.4 13.8 %copy-start.7 = (f32[32,64]{1,0:T(8,128)S(1)}, f32[32,64]{1,0:T(8,128)}, u32[]{:S(2)}) copy-start(f32[32,64]{1,0:T(8,128)} %weight_ref.1) | copy-start | bytes 24580
  30.0 4.4 %collective-permute-start.2 = (f32[96,128]{1,0:T(8,128)S(1)}, f32[96,128]{1,0:T(8,128)S(1)}, u32[]{:S(2)}, u32[]{:S(2)}) collective-permute-start(f32[96,128]{1,0:T(8,128)S(1)} %get-tuple-element.16), channel_id=1, source_target_pairs={{0,3},{1,2},{2,1},{3,0},{4,7},{5,6},{6,5},{7,4},{8,11},{9,10},{10,... | collective-permute-start | bytes 147464 | tf_op jit(solution)/shard_map/ppermute | solution.py:325
  31.5 4.6 %collective-permute-start.1 = (f32[96,128]{1,0:T(8,128)S(1)}, f32[96,128]{1,0:T(8,128)S(1)}, u32[]{:S(2)}, u32[]{:S(2)}) collective-permute-start(f32[96,128]{1,0:T(8,128)S(1)} %get-tuple-element.16), channel_id=1, source_target_pairs={{0,2},{1,3},{2,0},{3,1},{4,6},{5,7},{6,4},{7,5},{8,10},{9,11},{10,... | collective-permute-start | bytes 147464 | tf_op jit(solution)/shard_map/ppermute | solution.py:325
  34.1 3.2 %collective-permute-start = (f32[96,128]{1,0:T(8,128)S(1)}, f32[96,128]{1,0:T(8,128)S(1)}, u32[]{:S(2)}, u32[]{:S(2)}) collective-permute-start(f32[96,128]{1,0:T(8,128)S(1)} %get-tuple-element.16), channel_id=1, source_target_pairs={{0,1},{1,0},{2,3},{3,2},{4,5},{5,4},{6,7},{7,6},{8,9},{9,8},{10,11... | collective-permute-start | bytes 147464 | tf_op jit(solution)/shard_map/ppermute | solution.py:325
  34.1 4.8 %collective-permute-start.3 = (bf16[768,128]{1,0:T(8,128)(2,1)S(1)}, bf16[768,128]{1,0:T(8,128)(2,1)S(1)}, u32[]{:S(2)}, u32[]{:S(2)}) collective-permute-start(bf16[768,128]{1,0:T(8,128)(2,1)S(1)} %get-tuple-element.18), channel_id=1, source_target_pairs={{0,4},{1,5},{2,6},{3,7},{4,0},{5,1},{6,2},{7,3},{8,12},{9,13},{10,... | collective-permute-start | bytes 589832 | tf_op jit(solution)/shard_map/ppermute | solution.py:325
  40.3 30.6 %all-to-all-start.1 = ((bf16[4,1536,128]{2,1,0:T(8,128)(2,1)}), bf16[4,1536,128]{2,1,0:T(8,128)(2,1)}, u32[]{:S(2)}, u32[]{:S(2)}) async-start(bf16[4,1536,128]{2,1,0:T(8,128)(2,1)} %broadcast_in_dim.2), calls=%async_computation.1 | async-start | bytes 3145728 | tf_op jit(solution)/shard_map/all_to_all | solution.py:387
  45.8 4.2 %collective-permute-start.6 = (f32[96,128]{1,0:T(8,128)S(1)}, f32[96,128]{1,0:T(8,128)S(1)}, u32[]{:S(2)}, u32[]{:S(2)}) collective-permute-start(f32[96,128]{1,0:T(8,128)S(1)} %add_add_fusion.1), channel_id=1, source_target_pairs={{0,48},{8,56},{16,32},{24,40},{32,16},{40,24},{48,0},{56,8},{64,11... | collective-permute-start | bytes 147464 | tf_op jit(solution)/shard_map/ppermute | solution.py:325
  48.5 4.4 %collective-permute-start.5 = (f32[96,128]{1,0:T(8,128)S(1)}, f32[96,128]{1,0:T(8,128)S(1)}, u32[]{:S(2)}, u32[]{:S(2)}) collective-permute-start(f32[96,128]{1,0:T(8,128)S(1)} %add_add_fusion.1), channel_id=1, source_target_pairs={{0,32},{8,40},{16,48},{24,56},{32,0},{40,8},{48,16},{56,24},{64,96... | collective-permute-start | bytes 147464 | tf_op jit(solution)/shard_map/ppermute | solution.py:325
  48.9 4.1 %collective-permute-start.4 = (f32[96,128]{1,0:T(8,128)S(1)}, f32[96,128]{1,0:T(8,128)S(1)}, u32[]{:S(2)}, u32[]{:S(2)}) collective-permute-start(f32[96,128]{1,0:T(8,128)S(1)} %add_add_fusion.1), channel_id=1, source_target_pairs={{0,16},{8,24},{16,0},{24,8},{32,48},{40,56},{48,32},{56,40},{64,80... | collective-permute-start | bytes 147464 | tf_op jit(solution)/shard_map/ppermute | solution.py:325
  53.0 5.5 %collective-permute-start.7 = (f32[96,128]{1,0:T(8,128)S(1)}, f32[96,128]{1,0:T(8,128)S(1)}, u32[]{:S(2)}, u32[]{:S(2)}) collective-permute-start(f32[96,128]{1,0:T(8,128)S(1)} %add_add_fusion), channel_id=1, source_target_pairs={{0,8},{8,0},{16,24},{24,16},{32,40},{40,32},{48,56},{56,48},{64,72... | collective-permute-start | bytes 147464 | tf_op jit(solution)/shard_map/ppermute | solution.py:325
  58.5 12.4 %copy-start.1 = (bf16[1,1,16,128,512]{4,3,2,1,0:T(8,128)(2,1)S(1)}, bf16[1,1,16,128,512]{4,3,2,1,0:T(8,128)(2,1)}, u32[]{:S(2)}) copy-start(bf16[1,1,16,128,512]{4,3,2,1,0:T(8,128)(2,1)} %tile_hbm.1) | copy-start | bytes 6291460
  58.5 12.4 %copy-start.3 = (s32[1,1,3,16]{3,1,2,0:T(1,128)S(1)}, s32[1,1,3,16]{3,1,2,0:T(1,128)}, u32[]{:S(2)}) copy-start(s32[1,1,3,16]{3,1,2,0:T(1,128)} %param.8) | copy-start | bytes 580
  58.5 12.4 %copy-start.5 = (s32[32]{0:T(128)S(1)}, s32[32]{0:T(128)}, u32[]{:S(2)}) copy-start(s32[32]{0:T(128)} %visits_ref.1) | copy-start | bytes 388
  58.5 4.5 %collective-permute-start.10 = (f32[96,128]{1,0:T(8,128)S(1)}, f32[96,128]{1,0:T(8,128)S(1)}, u32[]{:S(2)}, u32[]{:S(2)}) collective-permute-start(f32[96,128]{1,0:T(8,128)S(1)} %add.27.a_ref), channel_id=1, source_target_pairs={{0,68},{1,69},{2,70},{3,71},{4,64},{5,65},{6,66},{7,67},{8,76},{9,... | collective-permute-start | bytes 147464 | tf_op jit(solution)/shard_map/ppermute | solution.py:335
  61.0 4.4 %collective-permute-start.9 = (f32[96,128]{1,0:T(8,128)S(1)}, f32[96,128]{1,0:T(8,128)S(1)}, u32[]{:S(2)}, u32[]{:S(2)}) collective-permute-start(f32[96,128]{1,0:T(8,128)S(1)} %add.27.a_ref), channel_id=1, source_target_pairs={{0,64},{1,65},{2,66},{3,67},{4,68},{5,69},{6,70},{7,71},{8,72},{9,... | collective-permute-start | bytes 147464 | tf_op jit(solution)/shard_map/ppermute | solution.py:335
  62.0 3.5 %collective-permute-start.8 = (f32[96,128]{1,0:T(8,128)S(1)}, f32[96,128]{1,0:T(8,128)S(1)}, u32[]{:S(2)}, u32[]{:S(2)}) collective-permute-start(f32[96,128]{1,0:T(8,128)S(1)} %add.27.a_ref), channel_id=1, source_target_pairs={{0,4},{1,5},{2,6},{3,7},{4,0},{5,1},{6,2},{7,3},{8,12},{9,13},{10,... | collective-permute-start | bytes 147464 | tf_op jit(solution)/shard_map/ppermute | solution.py:335
  75.7 4.5 %collective-permute-start.11 = (f32[8,64,512]{2,1,0:T(8,128)S(1)}, f32[8,64,512]{2,1,0:T(8,128)S(1)}, u32[]{:S(2)}, u32[]{:S(2)}) collective-permute-start(f32[8,64,512]{2,1,0:T(8,128)S(1)} %get-tuple-element.24), channel_id=1, source_target_pairs={{0,8},{8,0},{16,24},{24,16},{32,40},{40,32},{48,56},{56,48},{64,72... | collective-permute-start | bytes 3145736 | tf_op jit(solution)/shard_map/ppermute | solution.py:325
  77.9 2.3 %collective-permute-start.12 = (f32[32,128]{1,0:T(8,128)S(1)}, f32[32,128]{1,0:T(8,128)S(1)}, u32[]{:S(2)}, u32[]{:S(2)}) collective-permute-start(f32[32,128]{1,0:T(8,128)S(1)} %get-tuple-element.25.gram_a), channel_id=1, source_target_pairs={{0,8},{8,0},{16,24},{24,16},{32,40},{40,32},{48,56},{56,48},{64,72... | collective-permute-start | bytes 49160 | tf_op jit(solution)/shard_map/ppermute | solution.py:325
  112.3 3.9 %collective-permute-start.13 = (bf16[8,64,512]{2,1,0:T(8,128)(2,1)S(1)}, bf16[8,64,512]{2,1,0:T(8,128)(2,1)S(1)}, u32[]{:S(2)}, u32[]{:S(2)}) collective-permute-start(bf16[8,64,512]{2,1,0:T(8,128)(2,1)S(1)} %all_to_all.21.from_ref), channel_id=1, source_target_pairs={{0,8},{8,0},{16,24},{24,16},{32,40},{40,32},{48,56},{56,48},{64,72... | collective-permute-start | bytes 1572872 | tf_op jit(solution)/shard_map/ppermute | solution.py:325

commit v8 on v7

--- a/solution.py
+++ b/solution.py
@@ -380,9 +380,10 @@
     )
     quarter = n_code // 2
     other = swap(message, "code", quarter)
-    sums = plus(sums, [swap(sums, "code", bit) for bit in (1, 2, 3)])
-    sums, message, other = lax.optimization_barrier((sums, message, other))
+    parts = [swap(sums, "code", bit) for bit in (1, 2, 3)]
     message = jnp.broadcast_to(jnp.concatenate([message, other])[None], (quarter, 2 * length, rows))
+    message, *parts = lax.optimization_barrier((message, *parts))
+    sums = plus(sums, parts)
     layers = [[z * quarter + i for i in range(quarter)] for z in (0, 1)]
     shared = lax.all_to_all(message, "code", 0, 0, axis_index_groups=layers, tiled=True)
     shared = shared.reshape(n_code, length, rows)

time: 119 us -> 117 us (0.983)
    ppermute x11, waiting for transfers between devices: 11.6 us -> 10.2 us  [swap(): return lax.ppermute(x, axis, [(i, i ^ bit) for i in range(size)])]
where the time goes in v8:
time: 117 us
  starting transfers between devices  30.8 us (26%)
  blocking collectives  29.7 us (25%)
  waiting for transfers between devices  26.6 us (23%)
  Pallas kernels  23.7 us (20%)
  local copies, waits for them, and re-layouts  2.71 us (2%)
  other arithmetic  1.5 us (1%)
  between operations  1.43 us (1%)
    all_to_all x2, blocking collectives, exchange(): return lax.all_to_all(x, 'pat', 0, 0, axis_index_groups=groups, tiled=True)  29.7 us
    pallas_call x9, Pallas kernels, call(): pl.pallas_call(kernel, out_shape=outs, in_specs=specs, out_specs=(spec,)...  23.7 us
    ppermute x11, starting transfers between devices, swap(): return lax.ppermute(x, axis, [(i, i ^ bit) for i in range(size)])  16.4 us
    all_to_all x1, waiting for transfers between devices, body(): got = lax.all_to_all(sent, 'code', 0, 0, tiled=True)  12.7 us
    ppermute x11, waiting for transfers between devices, swap(): return lax.ppermute(x, axis, [(i, i ^ bit) for i in range(size)])  10.2 us
    all_to_all x1, starting transfers between devices, body(): got = lax.all_to_all(sent, 'code', 0, 0, tiled=True)  5.63 us
    all_to_all x1, starting transfers between devices, body(): lax.all_to_all(message, 'code', 0, 0, axis_index_groups=layers, tiled=True)  4.83 us
    ppermute x3, starting transfers between devices, swap_z(): return lax.ppermute(x, ('pat', 'code'), pairs)  4.01 us
  transfers between devices with their start and end apart: 16, of which 10 were waited for; matrix products, arithmetic and copies ran while one was open for 0% of the time, Pallas kernels for 7%

profile of v8, /device:TPU:3, one launch (start us, length us, event | category | flops | bytes accessed | tf_op | source)
XLA Modules:
  0.0 116.5 jit_solution(16385048701587203835)
XLA Ops:
  1.3 0.0 copy-start.2
  1.3 0.7 copy-done.2
  2.0 0.7 copy-done.4
  2.6 2.9 %shard_map.94 = f32[64,64,128]{2,1,0:T(8,128)S(1)} custom-call(s32[1,3,1,16]{3,2,1,0:T(1,128)S(1)} %bitcast.9, s32[1,1]{1,0:T(1,128)S(6)} %copy.12.count_hbm.count_ref, s32[32]{0:T(128)S(1)} %copy-done.4, bf16[1,1,16,128,512]{4,3,2,1,0:T(8,128)(2,1)} %tile_hbm.1, f32[64,8192]{1,0:T(8,128)} %code_ref.1), custom_call_target="tpu_custom_call" | custom-call | flops 1000000000 | bytes 65536 | tf_op jit(solution)/shard_map/pallas_call | solution.py:311
  5.6 0.0 copy-start
  5.6 1.2 %convert_element_type.6 = f16[64,64,128]{2,1,0:T(8,128)(2,1)} convert(f32[64,64,128]{2,1,0:T(8,128)S(1)} %shard_map.94) | non-fusion elementwise | flops 524288 | bytes 3145728 | tf_op jit(solution)/shard_map/convert_element_type | solution.py:369
  6.8 5.6 %all-to-all-start = ((f16[8,512,128]{2,1,0:T(8,128)(2,1)}), f16[8,512,128]{2,1,0:T(8,128)(2,1)S(1)}, u32[]{:S(2)}, u32[]{:S(2)}) async-start(f16[8,512,128]{2,1,0:T(8,128)(2,1)} %bitcast.3), calls=%async_computation | async-start | bytes 2097152 | tf_op jit(solution)/shard_map/all_to_all | solution.py:370
  12.4 0.8 shard_map.95.gram_ref
  13.3 0.1 pad_add_fusion.at_ref.place_ref
  13.3 12.7 %all-to-all-done = f16[8,512,128]{2,1,0:T(8,128)(2,1)S(1)} async-done(((f16[8,512,128]{2,1,0:T(8,128)(2,1)}), f16[8,512,128]{2,1,0:T(8,128)(2,1)S(1)}, u32[]{:S(2)}, u32[]{:S(2)}) %all-to-all-start) | async-done | bytes 1048608 | tf_op jit(solution)/shard_map/all_to_all | solution.py:370
  26.0 0.1 convert_reduce_fusion
  26.2 3.8 %shard_map.96 = (f32[96,128]{1,0:T(8,128)S(1)}, bf16[768,128]{1,0:T(8,128)(2,1)S(1)}) custom-call(s32[2]{0:T(128)S(1)} %pad_add_fusion.at_ref.place_ref, f32[8,64,128]{2,1,0:T(8,128)S(1)} %bitcast.8, f32[64,64]{1,0:T(8,128)S(1)} %copy-done.6, f32[32,64]{1,0:T(8,128)S(1)} %copy-done.7, f32[32,128]{1,0:T(8,128)S(1)} %shard_map.95.gram_ref), custom_call_target="tpu_custom_call" | custom-call | flops 5000000000 | bytes 65536 | tf_op jit(solution)/shard_map/pallas_call | solution.py:311
  30.1 0.4 collective-permute-start
  30.4 1.5 %collective-permute-start.3 = (f32[96,128]{1,0:T(8,128)S(1)}, f32[96,128]{1,0:T(8,128)S(1)}, u32[]{:S(2)}, u32[]{:S(2)}) collective-permute-start(f32[96,128]{1,0:T(8,128)S(1)} %get-tuple-element.18), channel_id=1, source_target_pairs={{0,3},{1,2},{2,1},{3,0},{4,7},{5,6},{6,5},{7,4},{8,11},{9,10},{10,... | collective-permute-start | bytes 147464 | tf_op jit(solution)/shard_map/ppermute | solution.py:325
  31.9 2.5 %collective-permute-start.2 = (f32[96,128]{1,0:T(8,128)S(1)}, f32[96,128]{1,0:T(8,128)S(1)}, u32[]{:S(2)}, u32[]{:S(2)}) collective-permute-start(f32[96,128]{1,0:T(8,128)S(1)} %get-tuple-element.18), channel_id=1, source_target_pairs={{0,2},{1,3},{2,0},{3,1},{4,6},{5,7},{6,4},{7,5},{8,10},{9,11},{10,... | collective-permute-start | bytes 147464 | tf_op jit(solution)/shard_map/ppermute | solution.py:325
  34.4 0.2 collective-permute-done
  34.7 0.0 collective-permute-done.3
  34.7 1.7 %collective-permute-done.2 = f32[96,128]{1,0:T(8,128)S(1)} collective-permute-done((f32[96,128]{1,0:T(8,128)S(1)}, f32[96,128]{1,0:T(8,128)S(1)}, u32[]{:S(2)}, u32[]{:S(2)}) %collective-permute-start.2) | collective-permute-done | bytes 49184 | tf_op jit(solution)/shard_map/ppermute | solution.py:325
  36.4 1.2 %collective-permute-done.1 = f32[96,128]{1,0:T(8,128)S(1)} collective-permute-done((f32[96,128]{1,0:T(8,128)S(1)}, f32[96,128]{1,0:T(8,128)S(1)}, u32[]{:S(2)}, u32[]{:S(2)}) %collective-permute-start.1) | collective-permute-done | bytes 49184 | tf_op jit(solution)/shard_map/ppermute | solution.py:325
  37.6 1.3 %broadcast_in_dim.2 = bf16[4,1536,128]{2,1,0:T(8,128)(2,1)} broadcast(bf16[1536,128]{1,0:T(8,128)(2,1)S(1)} %pad_maximum_fusion), dimensions={1,2} | broadcast | bytes 1966080 | tf_op jit(solution)/shard_map/broadcast_in_dim | solution.py:384
  39.0 4.8 %all-to-all-start.1 = ((bf16[4,1536,128]{2,1,0:T(8,128)(2,1)}), bf16[4,1536,128]{2,1,0:T(8,128)(2,1)}, u32[]{:S(2)}, u32[]{:S(2)}) async-start(bf16[4,1536,128]{2,1,0:T(8,128)(2,1)} %broadcast_in_dim.2), calls=%async_computation.1 | async-start | bytes 3145728 | tf_op jit(solution)/shard_map/all_to_all | solution.py:388
  43.8 2.8 %collective-permute-start.6 = (f32[96,128]{1,0:T(8,128)S(1)}, f32[96,128]{1,0:T(8,128)S(1)}, u32[]{:S(2)}, u32[]{:S(2)}) collective-permute-start(f32[96,128]{1,0:T(8,128)S(1)} %add_add_fusion.1), channel_id=1, source_target_pairs={{0,48},{8,56},{16,32},{24,40},{32,16},{40,24},{48,0},{56,8},{64,11... | collective-permute-start | bytes 147464 | tf_op jit(solution)/shard_map/ppermute | solution.py:325
  46.6 0.3 collective-permute-start.5
  47.0 0.3 collective-permute-start.4
  47.3 0.8 collective-permute-done.6
  48.1 3.0 %collective-permute-done.5 = f32[96,128]{1,0:T(8,128)S(1)} collective-permute-done((f32[96,128]{1,0:T(8,128)S(1)}, f32[96,128]{1,0:T(8,128)S(1)}, u32[]{:S(2)}, u32[]{:S(2)}) %collective-permute-start.5) | collective-permute-done | bytes 49184 | tf_op jit(solution)/shard_map/ppermute | solution.py:325
  51.1 0.0 collective-permute-done.4
  51.1 4.4 %collective-permute-start.7 = (f32[96,128]{1,0:T(8,128)S(1)}, f32[96,128]{1,0:T(8,128)S(1)}, u32[]{:S(2)}, u32[]{:S(2)}) collective-permute-start(f32[96,128]{1,0:T(8,128)S(1)} %add_add_fusion), channel_id=1, source_target_pairs={{0,8},{8,0},{16,24},{24,16},{32,40},{40,32},{48,56},{56,48},{64,72... | collective-permute-start | bytes 147464 | tf_op jit(solution)/shard_map/ppermute | solution.py:325
  55.5 0.9 collective-permute-done.7
  56.4 0.0 copy-start.3
  56.4 0.0 copy-start.5
  56.5 3.3 %collective-permute-start.10 = (f32[96,128]{1,0:T(8,128)S(1)}, f32[96,128]{1,0:T(8,128)S(1)}, u32[]{:S(2)}, u32[]{:S(2)}) collective-permute-start(f32[96,128]{1,0:T(8,128)S(1)} %add.27.a_ref), channel_id=1, source_target_pairs={{0,68},{1,69},{2,70},{3,71},{4,64},{5,65},{6,66},{7,67},{8,76},{9,... | collective-permute-start | bytes 147464 | tf_op jit(solution)/shard_map/ppermute | solution.py:335
  59.8 0.1 collective-permute-start.9
  59.9 0.5 collective-permute-start.8
  60.5 1.1 collective-permute-done.10.d_ref
  61.5 2.7 %collective-permute-done.9.c_ref = f32[96,128]{1,0:T(8,128)S(1)} collective-permute-done((f32[96,128]{1,0:T(8,128)S(1)}, f32[96,128]{1,0:T(8,128)S(1)}, u32[]{:S(2)}, u32[]{:S(2)}) %collective-permute-start.9) | collective-permute-done | bytes 49184 | tf_op jit(solution)/shard_map/ppermute | solution.py:335
  64.2 5.5 %shard_map.97 = (f32[64,64]{1,0:T(8,128)}, f32[64,64]{1,0:T(8,128)S(1)}, f32[64,64]{1,0:T(8,128)S(1)}, f32[64,64]{1,0:T(8,128)S(1)}) custom-call(f32[96,128]{1,0:T(8,128)S(1)} %add.27.a_ref, f32[96,128]{1,0:T(8,128)S(1)} %collective-permute-done.8.b_ref, f32[96,128]{1,0:T(8,128)S(1)} %collective-permute-done.9.c_ref, f32[96,128]{1,0:T(8,128)S(1)} %collective-permute-done.10.d_ref), custom_call_target="tpu_custom_call" | custom-call | flops 5000000000 | bytes 65536 | tf_op jit(solution)/shard_map/pallas_call | solution.py:311
  69.7 4.7 %shard_map.98 = (f32[8,64,512]{2,1,0:T(8,128)S(1)}, f32[8,64,512]{2,1,0:T(8,128)S(1)}, f32[32,128]{1,0:T(8,128)S(1)}, f32[4,64]{1,0:T(4,128)}) custom-call(s32[2]{0:T(128)S(1)} %pad_add_fusion.at_ref.place_ref, s32[1,3,1,16]{3,2,1,0:T(1,128)S(1)} %bitcast.10, s32[1,1]{1,0:T(1,128)S(6)} %copy.12.count_hbm.count_ref, s32[32]{0:T(128)S(1)} %copy-done.5, ...), custom_call_target="tpu_custom_call" | custom-call | flops 5000000000 | bytes 65536 | tf_op jit(solution)/shard_map/pallas_call | solution.py:311
  74.5 1.8 %collective-permute-start.11 = (f32[8,64,512]{2,1,0:T(8,128)S(1)}, f32[8,64,512]{2,1,0:T(8,128)S(1)}, u32[]{:S(2)}, u32[]{:S(2)}) collective-permute-start(f32[8,64,512]{2,1,0:T(8,128)S(1)} %get-tuple-element.26), channel_id=1, source_target_pairs={{0,8},{8,0},{16,24},{24,16},{32,40},{40,32},{48,56},{56,48},{64,72... | collective-permute-start | bytes 3145736 | tf_op jit(solution)/shard_map/ppermute | solution.py:325
  76.2 0.0 collective-permute-start.12
  76.3 2.3 %collective-permute-done.12.gram_b = f32[32,128]{1,0:T(8,128)S(1)} collective-permute-done((f32[32,128]{1,0:T(8,128)S(1)}, f32[32,128]{1,0:T(8,128)S(1)}, u32[]{:S(2)}, u32[]{:S(2)}) %collective-permute-start.12) | collective-permute-done | bytes 16416 | tf_op jit(solution)/shard_map/ppermute | solution.py:325
  78.5 0.1 shard_map.99
  78.7 17.1 %all_to_all.20.got_ref = bf16[8,5,64,128]{3,2,1,0:T(8,128)(2,1)S(1)} all-to-all(bf16[8,5,64,128]{3,2,1,0:T(8,128)(2,1)S(1)} %shard_map.99), channel_id=1, replica_groups={{0,16,32,48,64,80,96,112},{8,24,40,56,72,88,104,120},{1,17,33,49,65,81,..., dimensions={0} | all-to-all | bytes 1310720 | tf_op jit(solution)/shard_map/all_to_all | solution.py:407
  95.7 2.7 %shard_map.100 = bf16[8,64,512]{2,1,0:T(8,128)(2,1)S(1)} custom-call(bf16[8,5,64,128]{3,2,1,0:T(8,128)(2,1)S(1)} %all_to_all.20.got_ref, f32[64,64]{1,0:T(8,128)S(1)} %get-tuple-element.28.mgram_ref), custom_call_target="tpu_custom_call" | custom-call | flops 1000000000 | bytes 65536 | tf_op jit(solution)/shard_map/pallas_call | solution.py:311
  98.4 12.6 %all_to_all.21.from_ref = bf16[8,64,512]{2,1,0:T(8,128)(2,1)S(1)} all-to-all(bf16[8,64,512]{2,1,0:T(8,128)(2,1)S(1)} %shard_map.100), channel_id=1, replica_groups={{0,16,32,48,64,80,96,112},{8,24,40,56,72,88,104,120},{1,17,33,49,65,81,..., dimensions={0} | all-to-all | bytes 1048576 | tf_op jit(solution)/shard_map/all_to_all | solution.py:407
  111.0 2.3 %collective-permute-start.13 = (bf16[8,64,512]{2,1,0:T(8,128)(2,1)S(1)}, bf16[8,64,512]{2,1,0:T(8,128)(2,1)S(1)}, u32[]{:S(2)}, u32[]{:S(2)}) collective-permute-start(bf16[8,64,512]{2,1,0:T(8,128)(2,1)S(1)} %all_to_all.21.from_ref), channel_id=1, source_target_pairs={{0,8},{8,0},{16,24},{24,16},{32,40},{40,32},{48,56},{56,48},{64,72... | collective-permute-start | bytes 1572872 | tf_op jit(solution)/shard_map/ppermute | solution.py:325
  113.4 1.6 %shard_map.101.refs_0_ = f32[64,8192]{1,0:T(8,128)} custom-call(s32[2]{0:T(128)S(1)} %pad_add_fusion.at_ref.place_ref, bf16[8,64,512]{2,1,0:T(8,128)(2,1)S(1)} %all_to_all.21.from_ref), custom_call_target="tpu_custom_call" | custom-call | flops 1000000000 | bytes 65536 | tf_op jit(solution)/shard_map/pallas_call | solution.py:311
  114.9 1.6 %shard_map.102 = f32[64,8192]{1,0:T(8,128)} custom-call(s32[2]{0:T(128)S(1)} %pad_add_fusion.at_ref.place_ref, bf16[8,64,512]{2,1,0:T(8,128)(2,1)S(1)} %collective-permute-done.13.from_ref, f32[64,8192]{1,0:T(8,128)} %shard_map.101.refs_0_), custom_call_target="tpu_custom_call", output_to_operand_aliasing={{}: (2, {})} | custom-call | flops 1000000000 | bytes 65536 | tf_op jit(solution)/shard_map/pallas_call | solution.py:311
  (19 shorter events, 0.1 us)
Async XLA Ops:
  1.3 0.7 copy-start.2
  2.0 0.7 copy-start.4
  5.6 6.9 %copy-start = (f32[64,8192]{1,0:T(8,128)S(1)}, f32[64,8192]{1,0:T(8,128)}, u32[]{:S(2)}) copy-start(f32[64,8192]{1,0:T(8,128)} %code_ref.1) | copy-start | bytes 6291460
  6.8 19.2 %all-to-all-start = ((f16[8,512,128]{2,1,0:T(8,128)(2,1)}), f16[8,512,128]{2,1,0:T(8,128)(2,1)S(1)}, u32[]{:S(2)}, u32[]{:S(2)}) async-start(f16[8,512,128]{2,1,0:T(8,128)(2,1)} %bitcast.3), calls=%async_computation | async-start | bytes 2097152 | tf_op jit(solution)/shard_map/all_to_all | solution.py:370
  12.4 13.8 %copy-start.6 = (f32[64,64]{1,0:T(8,128)S(1)}, f32[64,64]{1,0:T(8,128)}, u32[]{:S(2)}) copy-start(f32[64,64]{1,0:T(8,128)} %mix_ref.1) | copy-start | bytes 49156
  12.4 13.8 %copy-start.7 = (f32[32,64]{1,0:T(8,128)S(1)}, f32[32,64]{1,0:T(8,128)}, u32[]{:S(2)}) copy-start(f32[32,64]{1,0:T(8,128)} %weight_ref.1) | copy-start | bytes 24580
  30.1 4.6 %collective-permute-start = (bf16[768,128]{1,0:T(8,128)(2,1)S(1)}, bf16[768,128]{1,0:T(8,128)(2,1)S(1)}, u32[]{:S(2)}, u32[]{:S(2)}) collective-permute-start(bf16[768,128]{1,0:T(8,128)(2,1)S(1)} %get-tuple-element.17), channel_id=1, source_target_pairs={{0,4},{1,5},{2,6},{3,7},{4,0},{5,1},{6,2},{7,3},{8,12},{9,13},{10,... | collective-permute-start | bytes 589832 | tf_op jit(solution)/shard_map/ppermute | solution.py:325
  30.4 4.3 %collective-permute-start.3 = (f32[96,128]{1,0:T(8,128)S(1)}, f32[96,128]{1,0:T(8,128)S(1)}, u32[]{:S(2)}, u32[]{:S(2)}) collective-permute-start(f32[96,128]{1,0:T(8,128)S(1)} %get-tuple-element.18), channel_id=1, source_target_pairs={{0,3},{1,2},{2,1},{3,0},{4,7},{5,6},{6,5},{7,4},{8,11},{9,10},{10,... | collective-permute-start | bytes 147464 | tf_op jit(solution)/shard_map/ppermute | solution.py:325
  31.9 4.6 %collective-permute-start.2 = (f32[96,128]{1,0:T(8,128)S(1)}, f32[96,128]{1,0:T(8,128)S(1)}, u32[]{:S(2)}, u32[]{:S(2)}) collective-permute-start(f32[96,128]{1,0:T(8,128)S(1)} %get-tuple-element.18), channel_id=1, source_target_pairs={{0,2},{1,3},{2,0},{3,1},{4,6},{5,7},{6,4},{7,5},{8,10},{9,11},{10,... | collective-permute-start | bytes 147464 | tf_op jit(solution)/shard_map/ppermute | solution.py:325
  34.4 3.2 %collective-permute-start.1 = (f32[96,128]{1,0:T(8,128)S(1)}, f32[96,128]{1,0:T(8,128)S(1)}, u32[]{:S(2)}, u32[]{:S(2)}) collective-permute-start(f32[96,128]{1,0:T(8,128)S(1)} %get-tuple-element.18), channel_id=1, source_target_pairs={{0,1},{1,0},{2,3},{3,2},{4,5},{5,4},{6,7},{7,6},{8,9},{9,8},{10,11... | collective-permute-start | bytes 147464 | tf_op jit(solution)/shard_map/ppermute | solution.py:325
  39.0 30.7 %all-to-all-start.1 = ((bf16[4,1536,128]{2,1,0:T(8,128)(2,1)}), bf16[4,1536,128]{2,1,0:T(8,128)(2,1)}, u32[]{:S(2)}, u32[]{:S(2)}) async-start(bf16[4,1536,128]{2,1,0:T(8,128)(2,1)} %broadcast_in_dim.2), calls=%async_computation.1 | async-start | bytes 3145728 | tf_op jit(solution)/shard_map/all_to_all | solution.py:388
  43.8 4.3 %collective-permute-start.6 = (f32[96,128]{1,0:T(8,128)S(1)}, f32[96,128]{1,0:T(8,128)S(1)}, u32[]{:S(2)}, u32[]{:S(2)}) collective-permute-start(f32[96,128]{1,0:T(8,128)S(1)} %add_add_fusion.1), channel_id=1, source_target_pairs={{0,48},{8,56},{16,32},{24,40},{32,16},{40,24},{48,0},{56,8},{64,11... | collective-permute-start | bytes 147464 | tf_op jit(solution)/shard_map/ppermute | solution.py:325
  46.6 4.5 %collective-permute-start.5 = (f32[96,128]{1,0:T(8,128)S(1)}, f32[96,128]{1,0:T(8,128)S(1)}, u32[]{:S(2)}, u32[]{:S(2)}) collective-permute-start(f32[96,128]{1,0:T(8,128)S(1)} %add_add_fusion.1), channel_id=1, source_target_pairs={{0,32},{8,40},{16,48},{24,56},{32,0},{40,8},{48,16},{56,24},{64,96... | collective-permute-start | bytes 147464 | tf_op jit(solution)/shard_map/ppermute | solution.py:325
  47.0 4.1 %collective-permute-start.4 = (f32[96,128]{1,0:T(8,128)S(1)}, f32[96,128]{1,0:T(8,128)S(1)}, u32[]{:S(2)}, u32[]{:S(2)}) collective-permute-start(f32[96,128]{1,0:T(8,128)S(1)} %add_add_fusion.1), channel_id=1, source_target_pairs={{0,16},{8,24},{16,0},{24,8},{32,48},{40,56},{48,32},{56,40},{64,80... | collective-permute-start | bytes 147464 | tf_op jit(solution)/shard_map/ppermute | solution.py:325
  51.1 5.3 %collective-permute-start.7 = (f32[96,128]{1,0:T(8,128)S(1)}, f32[96,128]{1,0:T(8,128)S(1)}, u32[]{:S(2)}, u32[]{:S(2)}) collective-permute-start(f32[96,128]{1,0:T(8,128)S(1)} %add_add_fusion), channel_id=1, source_target_pairs={{0,8},{8,0},{16,24},{24,16},{32,40},{40,32},{48,56},{56,48},{64,72... | collective-permute-start | bytes 147464 | tf_op jit(solution)/shard_map/ppermute | solution.py:325
  56.4 13.3 %copy-start.1 = (bf16[1,1,16,128,512]{4,3,2,1,0:T(8,128)(2,1)S(1)}, bf16[1,1,16,128,512]{4,3,2,1,0:T(8,128)(2,1)}, u32[]{:S(2)}) copy-start(bf16[1,1,16,128,512]{4,3,2,1,0:T(8,128)(2,1)} %tile_hbm.1) | copy-start | bytes 6291460
  56.4 13.3 %copy-start.3 = (s32[1,1,3,16]{3,1,2,0:T(1,128)S(1)}, s32[1,1,3,16]{3,1,2,0:T(1,128)}, u32[]{:S(2)}) copy-start(s32[1,1,3,16]{3,1,2,0:T(1,128)} %param.8) | copy-start | bytes 580
  56.4 13.3 %copy-start.5 = (s32[32]{0:T(128)S(1)}, s32[32]{0:T(128)}, u32[]{:S(2)}) copy-start(s32[32]{0:T(128)} %visits_ref.1) | copy-start | bytes 388
  56.5 5.1 %collective-permute-start.10 = (f32[96,128]{1,0:T(8,128)S(1)}, f32[96,128]{1,0:T(8,128)S(1)}, u32[]{:S(2)}, u32[]{:S(2)}) collective-permute-start(f32[96,128]{1,0:T(8,128)S(1)} %add.27.a_ref), channel_id=1, source_target_pairs={{0,68},{1,69},{2,70},{3,71},{4,64},{5,65},{6,66},{7,67},{8,76},{9,... | collective-permute-start | bytes 147464 | tf_op jit(solution)/shard_map/ppermute | solution.py:335
  59.8 4.4 %collective-permute-start.9 = (f32[96,128]{1,0:T(8,128)S(1)}, f32[96,128]{1,0:T(8,128)S(1)}, u32[]{:S(2)}, u32[]{:S(2)}) collective-permute-start(f32[96,128]{1,0:T(8,128)S(1)} %add.27.a_ref), channel_id=1, source_target_pairs={{0,64},{1,65},{2,66},{3,67},{4,68},{5,69},{6,70},{7,71},{8,72},{9,... | collective-permute-start | bytes 147464 | tf_op jit(solution)/shard_map/ppermute | solution.py:335
  59.9 4.3 %collective-permute-start.8 = (f32[96,128]{1,0:T(8,128)S(1)}, f32[96,128]{1,0:T(8,128)S(1)}, u32[]{:S(2)}, u32[]{:S(2)}) collective-permute-start(f32[96,128]{1,0:T(8,128)S(1)} %add.27.a_ref), channel_id=1, source_target_pairs={{0,4},{1,5},{2,6},{3,7},{4,0},{5,1},{6,2},{7,3},{8,12},{9,13},{10,... | collective-permute-start | bytes 147464 | tf_op jit(solution)/shard_map/ppermute | solution.py:335
  74.5 4.1 %collective-permute-start.11 = (f32[8,64,512]{2,1,0:T(8,128)S(1)}, f32[8,64,512]{2,1,0:T(8,128)S(1)}, u32[]{:S(2)}, u32[]{:S(2)}) collective-permute-start(f32[8,64,512]{2,1,0:T(8,128)S(1)} %get-tuple-element.26), channel_id=1, source_target_pairs={{0,8},{8,0},{16,24},{24,16},{32,40},{40,32},{48,56},{56,48},{64,72... | collective-permute-start | bytes 3145736 | tf_op jit(solution)/shard_map/ppermute | solution.py:325
  76.2 2.3 %collective-permute-start.12 = (f32[32,128]{1,0:T(8,128)S(1)}, f32[32,128]{1,0:T(8,128)S(1)}, u32[]{:S(2)}, u32[]{:S(2)}) collective-permute-start(f32[32,128]{1,0:T(8,128)S(1)} %get-tuple-element.27.gram_a), channel_id=1, source_target_pairs={{0,8},{8,0},{16,24},{24,16},{32,40},{40,32},{48,56},{56,48},{64,72... | collective-permute-start | bytes 49160 | tf_op jit(solution)/shard_map/ppermute | solution.py:325
  111.0 3.9 %collective-permute-start.13 = (bf16[8,64,512]{2,1,0:T(8,128)(2,1)S(1)}, bf16[8,64,512]{2,1,0:T(8,128)(2,1)S(1)}, u32[]{:S(2)}, u32[]{:S(2)}) collective-permute-start(bf16[8,64,512]{2,1,0:T(8,128)(2,1)S(1)} %all_to_all.21.from_ref), channel_id=1, source_target_pairs={{0,8},{8,0},{16,24},{24,16},{32,40},{40,32},{48,56},{56,48},{64,72... | collective-permute-start | bytes 1572872 | tf_op jit(solution)/shard_map/ppermute | solution.py:325

commit v9 on v8

--- a/solution.py
+++ b/solution.py
@@ -117,26 +117,21 @@
     return scale * mm(raw, fresh, TN)
 
 
-def live_rows(t, list_ref, count_ref, visits_ref, tile_rows):
-    k, b, g = list_ref[0, 0, 0, t], list_ref[0, 1, 0, t], list_ref[0, 2, 0, t]
-    kept = jnp.where(t < count_ref[0, 0], visits_ref[k] - tile_rows * b, 0)
+def live_rows(t, meta_ref, tile_rows):
+    width = meta_ref.shape[3]
+    k, b, g = meta_ref[0, 0, 0, t], meta_ref[0, 1, 0, t], meta_ref[0, 2, 0, t]
+    visits = meta_ref[0, 4 + lax.div(k, width), 0, lax.rem(k, width)]
+    kept = jnp.where(t < meta_ref[0, 3, 0, 0], visits - tile_rows * b, 0)
     return k, b, g, kept
 
 
 def products_kernel(
-    list_hbm, count_hbm, visits_hbm, tile_hbm, code_hbm, out_ref,
-    list_ref, count_ref, visits_ref, tile_ref, code_ref, small_sems, sems,
+    meta_ref, tile_hbm, code_hbm, out_ref, tile_ref, code_ref, sems
 ):
     slots, rows, cols = tile_ref.shape
     rank = code_ref.shape[0]
     parts = sems.shape[0] - 1
     each = slots // parts
-    small = []
-    for i, (src, dst) in enumerate(
-        ((list_hbm, list_ref), (count_hbm, count_ref), (visits_hbm, visits_ref))
-    ):
-        small.append(pltpu.make_async_copy(src, dst, small_sems.at[i]))
-        small[-1].start()
     code_copy = pltpu.make_async_copy(code_hbm, code_ref, sems.at[parts])
     code_copy.start()
     copies = []
@@ -146,13 +141,11 @@
         copies[-1].start()
     out_ref[...] = jnp.zeros(out_ref.shape, F32)
     lane = lax.broadcasted_iota(jnp.int32, (rank, rows), 1)
-    for copy in small:
-        copy.wait()
     code_copy.wait()
     for t in range(slots):
         if t % each == 0:
             copies[t // each].wait()
-        k, b, g, kept = live_rows(t, list_ref, count_ref, visits_ref, rows)
+        k, b, g, kept = live_rows(t, meta_ref, rows)
         codes = code_ref[:, pl.ds(pl.multiple_of(g * cols, cols), cols)].astype(BF16)
         part = mm16(codes, tile_ref[t], NT)
         out_ref[k * VBLOCKS + b] += jnp.where(lane < kept, part, 0.0)
@@ -218,7 +211,7 @@
 
 
 def numer_kernel(
-    place_ref, list_ref, count_ref, visits_ref, got_ref, mix_ref, inverse_ref, tile_ref,
+    place_ref, meta_ref, got_ref, mix_ref, inverse_ref, tile_ref,
     keep_ref, send_ref, wgram_ref, own_ref, acc_ref, weight_ref,
 ):
     slots, rows, cols = tile_ref.shape
@@ -249,7 +242,7 @@
     acc_ref[...] = jnp.zeros(acc_ref.shape, F32)
     lane = lax.broadcasted_iota(jnp.int32, (rank, rows), 1)
     for t in range(slots):
-        k, b, g, kept = live_rows(t, list_ref, count_ref, visits_ref, rows)
+        k, b, g, kept = live_rows(t, meta_ref, rows)
         d, j = source(lax.div(k, own)), lax.rem(k, own)
         both = jnp.concatenate(split(mix * weight_ref[pl.ds(d * own + j, 1), :]), axis=0)
         at = pl.multiple_of((j * VBLOCKS + b) * rank, rank)
@@ -260,7 +253,7 @@
     parity = place_ref[1]
     for j in range(keep_ref.shape[0]):
         keep_ref[j] = acc_ref[2 * j + parity]
-        send_ref[j] = acc_ref[2 * j + 1 - parity]
+        send_ref[j] = acc_ref[2 * j + 1 - parity].astype(BF16)
 
 
 def pair_kernel(keep_ref, came_ref, gram_a, gram_b, out_ref):
@@ -343,8 +336,15 @@
 
 def body(tile_data, tile_list, tile_count, visit_counts, code_factor_t, visit_mix, patient_weight):
     tiles = tile_data[0, 0]
-    tile_list = jnp.transpose(tile_list, (0, 2, 1, 3))
     slots, rows, cols = tiles.shape
+    meta = jnp.concatenate(
+        [
+            jnp.transpose(tile_list, (0, 2, 1, 3)),
+            jnp.broadcast_to(tile_count.reshape(1, 1, 1, 1), (1, 1, 1, slots)),
+            visit_counts.reshape(1, -1, 1, slots),
+        ],
+        axis=1,
+    )
     rank = visit_mix.shape[0]
     patients = visit_counts.shape[0]
     n_code, n_pat = lax.axis_size("code"), lax.axis_size("pat")
@@ -356,12 +356,10 @@
     square = shape((rank, rank), F32)
 
     partial = call(
-        products_kernel, shape((patients * VBLOCKS, rank, rows), F32), [HBM] * 5,
-        (tile_list, tile_count, visit_counts, tile_data, code_factor_t),
+        products_kernel, shape((patients * VBLOCKS, rank, rows), F32), [SM, HBM, HBM],
+        (meta, tile_data, code_factor_t),
         [
-            pltpu.SMEM(tile_list.shape, jnp.int32), pltpu.SMEM(tile_count.shape, jnp.int32),
-            pltpu.SMEM(visit_counts.shape, jnp.int32), pltpu.VMEM(tiles.shape, BF16),
-            pltpu.VMEM(code_factor_t.shape, F32), pltpu.SemaphoreType.DMA((3,)),
+            pltpu.VMEM(tiles.shape, BF16), pltpu.VMEM(code_factor_t.shape, F32),
             pltpu.SemaphoreType.DMA((5,)),
         ],
         vmem=50,
@@ -396,9 +394,12 @@
     block = shape((half, rank, cols), F32)
     keep, send, wgram, weight_new = call(
         numer_kernel,
-        (block, block, shape((rank // 2, 2 * rank), F32), shape((own, rank), F32)),
-        [SM, SM, SM, SM, VM, VM, VM, VM],
-        (place, tile_list, tile_count, visit_counts, shared, mix_again, inverse, tiles),
+        (
+            block, shape(block.shape, BF16), shape((rank // 2, 2 * rank), F32),
+            shape((own, rank), F32),
+        ),
+        [SM, SM, VM, VM, VM, VM],
+        (place, meta, shared, mix_again, inverse, tiles),
         [pltpu.VMEM((n_pat, rank, cols), F32), pltpu.VMEM((patients, rank), F32)], flops=5e9,
     )
     groups = [[core + 2 * i for i in range(half)] for core in (0, 1)]

time: 117 us -> 117 us (level)
    unnamed x16 -> x8, local copies, waits for them, and re-layouts: 1.36 us -> 0.02 us
where the time goes in v9:
time: 117 us; the launch traced here: 116 us
  starting transfers between devices  30.9 us (26%)
  blocking collectives  29.7 us (25%)
  waiting for transfers between devices  25.8 us (22%)
  Pallas kernels  24.1 us (21%)
  other arithmetic  2.25 us (2%)
  local copies, waits for them, and re-layouts  2.17 us (2%)
  between operations  1.4 us (1%)
    all_to_all x2, blocking collectives, exchange(): return lax.all_to_all(x, 'pat', 0, 0, axis_index_groups=groups, tiled=True)  29.7 us
    pallas_call x9, Pallas kernels, call(): pl.pallas_call(kernel, out_shape=outs, in_specs=specs, out_specs=(spec,)...  24.1 us
    ppermute x11, starting transfers between devices, swap(): return lax.ppermute(x, axis, [(i, i ^ bit) for i in range(size)])  16.5 us
    all_to_all x1, waiting for transfers between devices, body(): got = lax.all_to_all(sent, 'code', 0, 0, tiled=True)  12.7 us
    ppermute x11, waiting for transfers between devices, swap(): return lax.ppermute(x, axis, [(i, i ^ bit) for i in range(size)])  9.34 us
    all_to_all x1, starting transfers between devices, body(): got = lax.all_to_all(sent, 'code', 0, 0, tiled=True)  5.62 us
    all_to_all x1, starting transfers between devices, body(): lax.all_to_all(message, 'code', 0, 0, axis_index_groups=layers, tiled=True)  4.83 us
    ppermute x3, starting transfers between devices, swap_z(): return lax.ppermute(x, ('pat', 'code'), pairs)  4 us
  transfers between devices with their start and end apart: 16, of which 10 were waited for; matrix products, arithmetic and copies ran while one was open for 0% of the time, Pallas kernels for 7%

profile of v9, /device:TPU:3, one launch (start us, length us, event | category | flops | bytes accessed | tf_op | source)
XLA Modules:
  0.0 116.4 jit_solution(12544260678447282427)
XLA Ops:
  1.3 0.7 reshape.23
  2.0 0.1 pad.3.clone
  2.1 0.8 pad_add_fusion.meta_ref
  2.8 3.5 %shard_map.94 = f32[64,64,128]{2,1,0:T(8,128)S(1)} custom-call(s32[1,6,1,16]{3,2,1,0:T(1,128)S(1)} %pad_add_fusion.meta_ref, bf16[1,1,16,128,512]{4,3,2,1,0:T(8,128)(2,1)} %tile_hbm.1, f32[64,8192]{1,0:T(8,128)} %code_ref.1), custom_call_target="tpu_custom_call" | custom-call | flops 1000000000 | bytes 65536 | tf_op jit(solution)/shard_map/pallas_call | solution.py:304
  6.4 0.0 copy-start
  6.4 1.2 %convert_element_type.6 = f16[64,64,128]{2,1,0:T(8,128)(2,1)} convert(f32[64,64,128]{2,1,0:T(8,128)S(1)} %shard_map.94) | non-fusion elementwise | flops 524288 | bytes 3145728 | tf_op jit(solution)/shard_map/convert_element_type | solution.py:367
  7.6 5.6 %all-to-all-start = ((f16[8,512,128]{2,1,0:T(8,128)(2,1)}), f16[8,512,128]{2,1,0:T(8,128)(2,1)S(1)}, u32[]{:S(2)}, u32[]{:S(2)}) async-start(f16[8,512,128]{2,1,0:T(8,128)(2,1)} %bitcast.5), calls=%async_computation | async-start | bytes 2097152 | tf_op jit(solution)/shard_map/all_to_all | solution.py:368
  13.2 0.8 shard_map.95.gram_ref
  14.1 0.1 pad_add_fusion.1.at_ref.place_ref
  14.1 12.7 %all-to-all-done = f16[8,512,128]{2,1,0:T(8,128)(2,1)S(1)} async-done(((f16[8,512,128]{2,1,0:T(8,128)(2,1)}), f16[8,512,128]{2,1,0:T(8,128)(2,1)S(1)}, u32[]{:S(2)}, u32[]{:S(2)}) %all-to-all-start) | async-done | bytes 1048608 | tf_op jit(solution)/shard_map/all_to_all | solution.py:368
  26.8 0.1 convert_reduce_fusion
  27.0 3.8 %shard_map.96 = (f32[96,128]{1,0:T(8,128)S(1)}, bf16[768,128]{1,0:T(8,128)(2,1)S(1)}) custom-call(s32[2]{0:T(128)S(1)} %pad_add_fusion.1.at_ref.place_ref, f32[8,64,128]{2,1,0:T(8,128)S(1)} %bitcast.13, f32[64,64]{1,0:T(8,128)S(1)} %copy-done.2, f32[32,64]{1,0:T(8,128)S(1)} %copy-done.3, f32[32,128]{1,0:T(8,128)S(1)} %shard_map.95.gram_ref), custom_call_target="tpu_custom_call" | custom-call | flops 5000000000 | bytes 65536 | tf_op jit(solution)/shard_map/pallas_call | solution.py:304
  30.8 0.4 collective-permute-start
  31.2 1.5 %collective-permute-start.3 = (f32[96,128]{1,0:T(8,128)S(1)}, f32[96,128]{1,0:T(8,128)S(1)}, u32[]{:S(2)}, u32[]{:S(2)}) collective-permute-start(f32[96,128]{1,0:T(8,128)S(1)} %get-tuple-element.18), channel_id=1, source_target_pairs={{0,3},{1,2},{2,1},{3,0},{4,7},{5,6},{6,5},{7,4},{8,11},{9,10},{10,... | collective-permute-start | bytes 147464 | tf_op jit(solution)/shard_map/ppermute | solution.py:318
  32.7 2.5 %collective-permute-start.2 = (f32[96,128]{1,0:T(8,128)S(1)}, f32[96,128]{1,0:T(8,128)S(1)}, u32[]{:S(2)}, u32[]{:S(2)}) collective-permute-start(f32[96,128]{1,0:T(8,128)S(1)} %get-tuple-element.18), channel_id=1, source_target_pairs={{0,2},{1,3},{2,0},{3,1},{4,6},{5,7},{6,4},{7,5},{8,10},{9,11},{10,... | collective-permute-start | bytes 147464 | tf_op jit(solution)/shard_map/ppermute | solution.py:318
  35.2 0.0 collective-permute-start.1
  35.2 0.2 collective-permute-done
  35.5 0.0 collective-permute-done.3
  35.5 1.7 %collective-permute-done.2 = f32[96,128]{1,0:T(8,128)S(1)} collective-permute-done((f32[96,128]{1,0:T(8,128)S(1)}, f32[96,128]{1,0:T(8,128)S(1)}, u32[]{:S(2)}, u32[]{:S(2)}) %collective-permute-start.2) | collective-permute-done | bytes 49184 | tf_op jit(solution)/shard_map/ppermute | solution.py:318
  37.2 1.2 %collective-permute-done.1 = f32[96,128]{1,0:T(8,128)S(1)} collective-permute-done((f32[96,128]{1,0:T(8,128)S(1)}, f32[96,128]{1,0:T(8,128)S(1)}, u32[]{:S(2)}, u32[]{:S(2)}) %collective-permute-start.1) | collective-permute-done | bytes 49184 | tf_op jit(solution)/shard_map/ppermute | solution.py:318
  38.4 1.3 %broadcast_in_dim.15 = bf16[4,1536,128]{2,1,0:T(8,128)(2,1)} broadcast(bf16[1536,128]{1,0:T(8,128)(2,1)S(1)} %pad_maximum_fusion), dimensions={1,2} | broadcast | bytes 1966080 | tf_op jit(solution)/shard_map/broadcast_in_dim | solution.py:382
  39.8 4.8 %all-to-all-start.1 = ((bf16[4,1536,128]{2,1,0:T(8,128)(2,1)}), bf16[4,1536,128]{2,1,0:T(8,128)(2,1)}, u32[]{:S(2)}, u32[]{:S(2)}) async-start(bf16[4,1536,128]{2,1,0:T(8,128)(2,1)} %broadcast_in_dim.15), calls=%async_computation.1 | async-start | bytes 3145728 | tf_op jit(solution)/shard_map/all_to_all | solution.py:386
  44.6 2.8 %collective-permute-start.6 = (f32[96,128]{1,0:T(8,128)S(1)}, f32[96,128]{1,0:T(8,128)S(1)}, u32[]{:S(2)}, u32[]{:S(2)}) collective-permute-start(f32[96,128]{1,0:T(8,128)S(1)} %add_add_fusion.1), channel_id=1, source_target_pairs={{0,48},{8,56},{16,32},{24,40},{32,16},{40,24},{48,0},{56,8},{64,11... | collective-permute-start | bytes 147464 | tf_op jit(solution)/shard_map/ppermute | solution.py:318
  47.4 0.3 collective-permute-start.5
  47.8 0.3 collective-permute-start.4
  48.1 0.8 collective-permute-done.6
  48.9 3.0 %collective-permute-done.5 = f32[96,128]{1,0:T(8,128)S(1)} collective-permute-done((f32[96,128]{1,0:T(8,128)S(1)}, f32[96,128]{1,0:T(8,128)S(1)}, u32[]{:S(2)}, u32[]{:S(2)}) %collective-permute-start.5) | collective-permute-done | bytes 49184 | tf_op jit(solution)/shard_map/ppermute | solution.py:318
  51.9 0.0 collective-permute-done.4
  51.9 4.4 %collective-permute-start.7 = (f32[96,128]{1,0:T(8,128)S(1)}, f32[96,128]{1,0:T(8,128)S(1)}, u32[]{:S(2)}, u32[]{:S(2)}) collective-permute-start(f32[96,128]{1,0:T(8,128)S(1)} %add_add_fusion), channel_id=1, source_target_pairs={{0,8},{8,0},{16,24},{24,16},{32,40},{40,32},{48,56},{56,48},{64,72... | collective-permute-start | bytes 147464 | tf_op jit(solution)/shard_map/ppermute | solution.py:318
  56.3 0.9 collective-permute-done.7
  57.2 3.3 %collective-permute-start.10 = (f32[96,128]{1,0:T(8,128)S(1)}, f32[96,128]{1,0:T(8,128)S(1)}, u32[]{:S(2)}, u32[]{:S(2)}) collective-permute-start(f32[96,128]{1,0:T(8,128)S(1)} %add.27.a_ref), channel_id=1, source_target_pairs={{0,68},{1,69},{2,70},{3,71},{4,64},{5,65},{6,66},{7,67},{8,76},{9,... | collective-permute-start | bytes 147464 | tf_op jit(solution)/shard_map/ppermute | solution.py:328
  60.6 0.1 collective-permute-start.9
  60.7 0.5 collective-permute-start.8
  61.2 1.1 collective-permute-done.10.d_ref
  62.3 2.7 %collective-permute-done.9.c_ref = f32[96,128]{1,0:T(8,128)S(1)} collective-permute-done((f32[96,128]{1,0:T(8,128)S(1)}, f32[96,128]{1,0:T(8,128)S(1)}, u32[]{:S(2)}, u32[]{:S(2)}) %collective-permute-start.9) | collective-permute-done | bytes 49184 | tf_op jit(solution)/shard_map/ppermute | solution.py:328
  65.0 5.5 %shard_map.97 = (f32[64,64]{1,0:T(8,128)}, f32[64,64]{1,0:T(8,128)S(1)}, f32[64,64]{1,0:T(8,128)S(1)}, f32[64,64]{1,0:T(8,128)S(1)}) custom-call(f32[96,128]{1,0:T(8,128)S(1)} %add.27.a_ref, f32[96,128]{1,0:T(8,128)S(1)} %collective-permute-done.8.b_ref, f32[96,128]{1,0:T(8,128)S(1)} %collective-permute-done.9.c_ref, f32[96,128]{1,0:T(8,128)S(1)} %collective-permute-done.10.d_ref), custom_call_target="tpu_custom_call" | custom-call | flops 5000000000 | bytes 65536 | tf_op jit(solution)/shard_map/pallas_call | solution.py:304
  70.5 0.0 all-to-all-done.1
  70.5 4.6 %shard_map.98 = (f32[8,64,512]{2,1,0:T(8,128)S(1)}, bf16[8,64,512]{2,1,0:T(8,128)(2,1)S(1)}, f32[32,128]{1,0:T(8,128)S(1)}, f32[4,64]{1,0:T(4,128)}) custom-call(s32[2]{0:T(128)S(1)} %pad_add_fusion.1.at_ref.place_ref, s32[1,6,1,16]{3,2,1,0:T(1,128)S(1)} %pad_add_fusion.meta_ref, bf16[8,768,128]{2,1,0:T(8,128)(2,1)} %bitcast.7.got_ref, ...), custom_call_target="tpu_custom_call" | custom-call | flops 5000000000 | bytes 65536 | tf_op jit(solution)/shard_map/pallas_call | solution.py:304
  75.0 1.8 %collective-permute-start.11 = (bf16[8,64,512]{2,1,0:T(8,128)(2,1)S(1)}, bf16[8,64,512]{2,1,0:T(8,128)(2,1)S(1)}, u32[]{:S(2)}, u32[]{:S(2)}) collective-permute-start(bf16[8,64,512]{2,1,0:T(8,128)(2,1)S(1)} %get-tuple-element.26), channel_id=1, source_target_pairs={{0,8},{8,0},{16,24},{24,16},{32,40},{40,32},{48,56},{56,48},{64,72... | collective-permute-start | bytes 1572872 | tf_op jit(solution)/shard_map/ppermute | solution.py:318
  76.9 0.1 collective-permute-start.12
  77.0 1.5 %collective-permute-done.12.gram_b = f32[32,128]{1,0:T(8,128)S(1)} collective-permute-done((f32[32,128]{1,0:T(8,128)S(1)}, f32[32,128]{1,0:T(8,128)S(1)}, u32[]{:S(2)}, u32[]{:S(2)}) %collective-permute-start.12) | collective-permute-done | bytes 16416 | tf_op jit(solution)/shard_map/ppermute | solution.py:318
  78.4 0.1 shard_map.99
  78.5 17.0 %all_to_all.20.got_ref = bf16[8,5,64,128]{3,2,1,0:T(8,128)(2,1)S(1)} all-to-all(bf16[8,5,64,128]{3,2,1,0:T(8,128)(2,1)S(1)} %shard_map.99), channel_id=1, replica_groups={{0,16,32,48,64,80,96,112},{8,24,40,56,72,88,104,120},{1,17,33,49,65,81,..., dimensions={0} | all-to-all | bytes 1310720 | tf_op jit(solution)/shard_map/all_to_all | solution.py:408
  95.6 2.7 %shard_map.100 = bf16[8,64,512]{2,1,0:T(8,128)(2,1)S(1)} custom-call(bf16[8,5,64,128]{3,2,1,0:T(8,128)(2,1)S(1)} %all_to_all.20.got_ref, f32[64,64]{1,0:T(8,128)S(1)} %get-tuple-element.28.mgram_ref), custom_call_target="tpu_custom_call" | custom-call | flops 1000000000 | bytes 65536 | tf_op jit(solution)/shard_map/pallas_call | solution.py:304
  98.3 12.6 %all_to_all.21.from_ref = bf16[8,64,512]{2,1,0:T(8,128)(2,1)S(1)} all-to-all(bf16[8,64,512]{2,1,0:T(8,128)(2,1)S(1)} %shard_map.100), channel_id=1, replica_groups={{0,16,32,48,64,80,96,112},{8,24,40,56,72,88,104,120},{1,17,33,49,65,81,..., dimensions={0} | all-to-all | bytes 1048576 | tf_op jit(solution)/shard_map/all_to_all | solution.py:408
  110.9 2.3 %collective-permute-start.13 = (bf16[8,64,512]{2,1,0:T(8,128)(2,1)S(1)}, bf16[8,64,512]{2,1,0:T(8,128)(2,1)S(1)}, u32[]{:S(2)}, u32[]{:S(2)}) collective-permute-start(bf16[8,64,512]{2,1,0:T(8,128)(2,1)S(1)} %all_to_all.21.from_ref), channel_id=1, source_target_pairs={{0,8},{8,0},{16,24},{24,16},{32,40},{40,32},{48,56},{56,48},{64,72... | collective-permute-start | bytes 1572872 | tf_op jit(solution)/shard_map/ppermute | solution.py:318
  113.2 1.6 %shard_map.101.refs_0_ = f32[64,8192]{1,0:T(8,128)} custom-call(s32[2]{0:T(128)S(1)} %pad_add_fusion.1.at_ref.place_ref, bf16[8,64,512]{2,1,0:T(8,128)(2,1)S(1)} %all_to_all.21.from_ref), custom_call_target="tpu_custom_call" | custom-call | flops 1000000000 | bytes 65536 | tf_op jit(solution)/shard_map/pallas_call | solution.py:304
  114.8 1.6 %shard_map.102 = f32[64,8192]{1,0:T(8,128)} custom-call(s32[2]{0:T(128)S(1)} %pad_add_fusion.1.at_ref.place_ref, bf16[8,64,512]{2,1,0:T(8,128)(2,1)S(1)} %collective-permute-done.13.from_ref, f32[64,8192]{1,0:T(8,128)} %shard_map.101.refs_0_), custom_call_target="tpu_custom_call", output_to_operand_aliasing={{}: (2, {})} | custom-call | flops 1000000000 | bytes 65536 | tf_op jit(solution)/shard_map/pallas_call | solution.py:304
  (14 shorter events, 0.1 us)
Async XLA Ops:
  6.4 6.9 %copy-start = (f32[64,8192]{1,0:T(8,128)S(1)}, f32[64,8192]{1,0:T(8,128)}, u32[]{:S(2)}) copy-start(f32[64,8192]{1,0:T(8,128)} %code_ref.1) | copy-start | bytes 6291460
  7.6 19.2 %all-to-all-start = ((f16[8,512,128]{2,1,0:T(8,128)(2,1)}), f16[8,512,128]{2,1,0:T(8,128)(2,1)S(1)}, u32[]{:S(2)}, u32[]{:S(2)}) async-start(f16[8,512,128]{2,1,0:T(8,128)(2,1)} %bitcast.5), calls=%async_computation | async-start | bytes 2097152 | tf_op jit(solution)/shard_map/all_to_all | solution.py:368
  13.2 13.8 %copy-start.2 = (f32[64,64]{1,0:T(8,128)S(1)}, f32[64,64]{1,0:T(8,128)}, u32[]{:S(2)}) copy-start(f32[64,64]{1,0:T(8,128)} %mix_ref.1) | copy-start | bytes 49156
  13.2 13.8 %copy-start.3 = (f32[32,64]{1,0:T(8,128)S(1)}, f32[32,64]{1,0:T(8,128)}, u32[]{:S(2)}) copy-start(f32[32,64]{1,0:T(8,128)} %weight_ref.1) | copy-start | bytes 24580
  30.8 4.6 %collective-permute-start = (bf16[768,128]{1,0:T(8,128)(2,1)S(1)}, bf16[768,128]{1,0:T(8,128)(2,1)S(1)}, u32[]{:S(2)}, u32[]{:S(2)}) collective-permute-start(bf16[768,128]{1,0:T(8,128)(2,1)S(1)} %get-tuple-element.17), channel_id=1, source_target_pairs={{0,4},{1,5},{2,6},{3,7},{4,0},{5,1},{6,2},{7,3},{8,12},{9,13},{10,... | collective-permute-start | bytes 589832 | tf_op jit(solution)/shard_map/ppermute | solution.py:318
  31.2 4.3 %collective-permute-start.3 = (f32[96,128]{1,0:T(8,128)S(1)}, f32[96,128]{1,0:T(8,128)S(1)}, u32[]{:S(2)}, u32[]{:S(2)}) collective-permute-start(f32[96,128]{1,0:T(8,128)S(1)} %get-tuple-element.18), channel_id=1, source_target_pairs={{0,3},{1,2},{2,1},{3,0},{4,7},{5,6},{6,5},{7,4},{8,11},{9,10},{10,... | collective-permute-start | bytes 147464 | tf_op jit(solution)/shard_map/ppermute | solution.py:318
  32.7 4.5 %collective-permute-start.2 = (f32[96,128]{1,0:T(8,128)S(1)}, f32[96,128]{1,0:T(8,128)S(1)}, u32[]{:S(2)}, u32[]{:S(2)}) collective-permute-start(f32[96,128]{1,0:T(8,128)S(1)} %get-tuple-element.18), channel_id=1, source_target_pairs={{0,2},{1,3},{2,0},{3,1},{4,6},{5,7},{6,4},{7,5},{8,10},{9,11},{10,... | collective-permute-start | bytes 147464 | tf_op jit(solution)/shard_map/ppermute | solution.py:318
  35.2 3.2 %collective-permute-start.1 = (f32[96,128]{1,0:T(8,128)S(1)}, f32[96,128]{1,0:T(8,128)S(1)}, u32[]{:S(2)}, u32[]{:S(2)}) collective-permute-start(f32[96,128]{1,0:T(8,128)S(1)} %get-tuple-element.18), channel_id=1, source_target_pairs={{0,1},{1,0},{2,3},{3,2},{4,5},{5,4},{6,7},{7,6},{8,9},{9,8},{10,11... | collective-permute-start | bytes 147464 | tf_op jit(solution)/shard_map/ppermute | solution.py:318
  39.8 30.7 %all-to-all-start.1 = ((bf16[4,1536,128]{2,1,0:T(8,128)(2,1)}), bf16[4,1536,128]{2,1,0:T(8,128)(2,1)}, u32[]{:S(2)}, u32[]{:S(2)}) async-start(bf16[4,1536,128]{2,1,0:T(8,128)(2,1)} %broadcast_in_dim.15), calls=%async_computation.1 | async-start | bytes 3145728 | tf_op jit(solution)/shard_map/all_to_all | solution.py:386
  44.6 4.3 %collective-permute-start.6 = (f32[96,128]{1,0:T(8,128)S(1)}, f32[96,128]{1,0:T(8,128)S(1)}, u32[]{:S(2)}, u32[]{:S(2)}) collective-permute-start(f32[96,128]{1,0:T(8,128)S(1)} %add_add_fusion.1), channel_id=1, source_target_pairs={{0,48},{8,56},{16,32},{24,40},{32,16},{40,24},{48,0},{56,8},{64,11... | collective-permute-start | bytes 147464 | tf_op jit(solution)/shard_map/ppermute | solution.py:318
  47.4 4.5 %collective-permute-start.5 = (f32[96,128]{1,0:T(8,128)S(1)}, f32[96,128]{1,0:T(8,128)S(1)}, u32[]{:S(2)}, u32[]{:S(2)}) collective-permute-start(f32[96,128]{1,0:T(8,128)S(1)} %add_add_fusion.1), channel_id=1, source_target_pairs={{0,32},{8,40},{16,48},{24,56},{32,0},{40,8},{48,16},{56,24},{64,96... | collective-permute-start | bytes 147464 | tf_op jit(solution)/shard_map/ppermute | solution.py:318
  47.8 4.1 %collective-permute-start.4 = (f32[96,128]{1,0:T(8,128)S(1)}, f32[96,128]{1,0:T(8,128)S(1)}, u32[]{:S(2)}, u32[]{:S(2)}) collective-permute-start(f32[96,128]{1,0:T(8,128)S(1)} %add_add_fusion.1), channel_id=1, source_target_pairs={{0,16},{8,24},{16,0},{24,8},{32,48},{40,56},{48,32},{56,40},{64,80... | collective-permute-start | bytes 147464 | tf_op jit(solution)/shard_map/ppermute | solution.py:318
  51.9 5.3 %collective-permute-start.7 = (f32[96,128]{1,0:T(8,128)S(1)}, f32[96,128]{1,0:T(8,128)S(1)}, u32[]{:S(2)}, u32[]{:S(2)}) collective-permute-start(f32[96,128]{1,0:T(8,128)S(1)} %add_add_fusion), channel_id=1, source_target_pairs={{0,8},{8,0},{16,24},{24,16},{32,40},{40,32},{48,56},{56,48},{64,72... | collective-permute-start | bytes 147464 | tf_op jit(solution)/shard_map/ppermute | solution.py:318
  57.2 13.3 %copy-start.1 = (bf16[1,1,16,128,512]{4,3,2,1,0:T(8,128)(2,1)S(1)}, bf16[1,1,16,128,512]{4,3,2,1,0:T(8,128)(2,1)}, u32[]{:S(2)}) copy-start(bf16[1,1,16,128,512]{4,3,2,1,0:T(8,128)(2,1)} %tile_hbm.1) | copy-start | bytes 6291460
  57.2 5.1 %collective-permute-start.10 = (f32[96,128]{1,0:T(8,128)S(1)}, f32[96,128]{1,0:T(8,128)S(1)}, u32[]{:S(2)}, u32[]{:S(2)}) collective-permute-start(f32[96,128]{1,0:T(8,128)S(1)} %add.27.a_ref), channel_id=1, source_target_pairs={{0,68},{1,69},{2,70},{3,71},{4,64},{5,65},{6,66},{7,67},{8,76},{9,... | collective-permute-start | bytes 147464 | tf_op jit(solution)/shard_map/ppermute | solution.py:328
  60.6 4.4 %collective-permute-start.9 = (f32[96,128]{1,0:T(8,128)S(1)}, f32[96,128]{1,0:T(8,128)S(1)}, u32[]{:S(2)}, u32[]{:S(2)}) collective-permute-start(f32[96,128]{1,0:T(8,128)S(1)} %add.27.a_ref), channel_id=1, source_target_pairs={{0,64},{1,65},{2,66},{3,67},{4,68},{5,69},{6,70},{7,71},{8,72},{9,... | collective-permute-start | bytes 147464 | tf_op jit(solution)/shard_map/ppermute | solution.py:328
  60.7 4.3 %collective-permute-start.8 = (f32[96,128]{1,0:T(8,128)S(1)}, f32[96,128]{1,0:T(8,128)S(1)}, u32[]{:S(2)}, u32[]{:S(2)}) collective-permute-start(f32[96,128]{1,0:T(8,128)S(1)} %add.27.a_ref), channel_id=1, source_target_pairs={{0,4},{1,5},{2,6},{3,7},{4,0},{5,1},{6,2},{7,3},{8,12},{9,13},{10,... | collective-permute-start | bytes 147464 | tf_op jit(solution)/shard_map/ppermute | solution.py:328
  75.0 3.4 %collective-permute-start.11 = (bf16[8,64,512]{2,1,0:T(8,128)(2,1)S(1)}, bf16[8,64,512]{2,1,0:T(8,128)(2,1)S(1)}, u32[]{:S(2)}, u32[]{:S(2)}) collective-permute-start(bf16[8,64,512]{2,1,0:T(8,128)(2,1)S(1)} %get-tuple-element.26), channel_id=1, source_target_pairs={{0,8},{8,0},{16,24},{24,16},{32,40},{40,32},{48,56},{56,48},{64,72... | collective-permute-start | bytes 1572872 | tf_op jit(solution)/shard_map/ppermute | solution.py:318
  76.9 1.6 %collective-permute-start.12 = (f32[32,128]{1,0:T(8,128)S(1)}, f32[32,128]{1,0:T(8,128)S(1)}, u32[]{:S(2)}, u32[]{:S(2)}) collective-permute-start(f32[32,128]{1,0:T(8,128)S(1)} %get-tuple-element.27.gram_a), channel_id=1, source_target_pairs={{0,8},{8,0},{16,24},{24,16},{32,40},{40,32},{48,56},{56,48},{64,72... | collective-permute-start | bytes 49160 | tf_op jit(solution)/shard_map/ppermute | solution.py:318
  110.9 3.9 %collective-permute-start.13 = (bf16[8,64,512]{2,1,0:T(8,128)(2,1)S(1)}, bf16[8,64,512]{2,1,0:T(8,128)(2,1)S(1)}, u32[]{:S(2)}, u32[]{:S(2)}) collective-permute-start(bf16[8,64,512]{2,1,0:T(8,128)(2,1)S(1)} %all_to_all.21.from_ref), channel_id=1, source_target_pairs={{0,8},{8,0},{16,24},{24,16},{32,40},{40,32},{48,56},{56,48},{64,72... | collective-permute-start | bytes 1572872 | tf_op jit(solution)/shard_map/ppermute | solution.py:318

commit v10 on v8

--- a/solution.py
+++ b/solution.py
@@ -260,7 +260,7 @@
     parity = place_ref[1]
     for j in range(keep_ref.shape[0]):
         keep_ref[j] = acc_ref[2 * j + parity]
-        send_ref[j] = acc_ref[2 * j + 1 - parity]
+        send_ref[j] = acc_ref[2 * j + 1 - parity].astype(BF16)
 
 
 def pair_kernel(keep_ref, came_ref, gram_a, gram_b, out_ref):
@@ -396,7 +396,10 @@
     block = shape((half, rank, cols), F32)
     keep, send, wgram, weight_new = call(
         numer_kernel,
-        (block, block, shape((rank // 2, 2 * rank), F32), shape((own, rank), F32)),
+        (
+            block, shape(block.shape, BF16), shape((rank // 2, 2 * rank), F32),
+            shape((own, rank), F32),
+        ),
         [SM, SM, SM, SM, VM, VM, VM, VM],
         (place, tile_list, tile_count, visit_counts, shared, mix_again, inverse, tiles),
         [pltpu.VMEM((n_pat, rank, cols), F32), pltpu.VMEM((patients, rank), F32)], flops=5e9,

time: 117 us -> 116 us (level)
  no operation moved by 1% of the time
where the time goes in v10:
time: 116 us
  starting transfers between devices  31 us (27%)
  blocking collectives  29.7 us (26%)
  waiting for transfers between devices  25.8 us (22%)
  Pallas kernels  23.6 us (20%)
  local copies, waits for them, and re-layouts  2.71 us (2%)
  other arithmetic  1.5 us (1%)
  between operations  1.44 us (1%)
    all_to_all x2, blocking collectives, exchange(): return lax.all_to_all(x, 'pat', 0, 0, axis_index_groups=groups, tiled=True)  29.7 us
    pallas_call x9, Pallas kernels, call(): pl.pallas_call(kernel, out_shape=outs, in_specs=specs, out_specs=(spec,)...  23.6 us
    ppermute x11, starting transfers between devices, swap(): return lax.ppermute(x, axis, [(i, i ^ bit) for i in range(size)])  16.5 us
    all_to_all x1, waiting for transfers between devices, body(): got = lax.all_to_all(sent, 'code', 0, 0, tiled=True)  12.7 us
    ppermute x11, waiting for transfers between devices, swap(): return lax.ppermute(x, axis, [(i, i ^ bit) for i in range(size)])  9.34 us
    all_to_all x1, starting transfers between devices, body(): got = lax.all_to_all(sent, 'code', 0, 0, tiled=True)  5.63 us
    all_to_all x1, starting transfers between devices, body(): lax.all_to_all(message, 'code', 0, 0, axis_index_groups=layers, tiled=True)  4.83 us
    ppermute x3, starting transfers between devices, swap_z(): return lax.ppermute(x, ('pat', 'code'), pairs)  4.01 us
  transfers between devices with their start and end apart: 16, of which 10 were waited for; matrix products, arithmetic and copies ran while one was open for 0% of the time, Pallas kernels for 7%

profile of v10, /device:TPU:3, one launch (start us, length us, event | category | flops | bytes accessed | tf_op | source)
XLA Modules:
  0.0 115.7 jit_solution(6810500049538643406)
XLA Ops:
  1.3 0.0 copy-start.2
  1.3 0.7 copy-done.2
  2.0 0.7 copy-done.4
  2.6 2.9 %shard_map.94 = f32[64,64,128]{2,1,0:T(8,128)S(1)} custom-call(s32[1,3,1,16]{3,2,1,0:T(1,128)S(1)} %bitcast.9, s32[1,1]{1,0:T(1,128)S(6)} %copy.12.count_hbm.count_ref, s32[32]{0:T(128)S(1)} %copy-done.4, bf16[1,1,16,128,512]{4,3,2,1,0:T(8,128)(2,1)} %tile_hbm.1, f32[64,8192]{1,0:T(8,128)} %code_ref.1), custom_call_target="tpu_custom_call" | custom-call | flops 1000000000 | bytes 65536 | tf_op jit(solution)/shard_map/pallas_call | solution.py:311
  5.6 0.0 copy-start
  5.6 1.2 %convert_element_type.6 = f16[64,64,128]{2,1,0:T(8,128)(2,1)} convert(f32[64,64,128]{2,1,0:T(8,128)S(1)} %shard_map.94) | non-fusion elementwise | flops 524288 | bytes 3145728 | tf_op jit(solution)/shard_map/convert_element_type | solution.py:369
  6.8 5.6 %all-to-all-start = ((f16[8,512,128]{2,1,0:T(8,128)(2,1)}), f16[8,512,128]{2,1,0:T(8,128)(2,1)S(1)}, u32[]{:S(2)}, u32[]{:S(2)}) async-start(f16[8,512,128]{2,1,0:T(8,128)(2,1)} %bitcast.3), calls=%async_computation | async-start | bytes 2097152 | tf_op jit(solution)/shard_map/all_to_all | solution.py:370
  12.4 0.8 shard_map.95.gram_ref
  13.3 0.1 pad_add_fusion.at_ref.place_ref
  13.3 12.7 %all-to-all-done = f16[8,512,128]{2,1,0:T(8,128)(2,1)S(1)} async-done(((f16[8,512,128]{2,1,0:T(8,128)(2,1)}), f16[8,512,128]{2,1,0:T(8,128)(2,1)S(1)}, u32[]{:S(2)}, u32[]{:S(2)}) %all-to-all-start) | async-done | bytes 1048608 | tf_op jit(solution)/shard_map/all_to_all | solution.py:370
  26.0 0.1 convert_reduce_fusion
  26.2 3.8 %shard_map.96 = (f32[96,128]{1,0:T(8,128)S(1)}, bf16[768,128]{1,0:T(8,128)(2,1)S(1)}) custom-call(s32[2]{0:T(128)S(1)} %pad_add_fusion.at_ref.place_ref, f32[8,64,128]{2,1,0:T(8,128)S(1)} %bitcast.8, f32[64,64]{1,0:T(8,128)S(1)} %copy-done.6, f32[32,64]{1,0:T(8,128)S(1)} %copy-done.7, f32[32,128]{1,0:T(8,128)S(1)} %shard_map.95.gram_ref), custom_call_target="tpu_custom_call" | custom-call | flops 5000000000 | bytes 65536 | tf_op jit(solution)/shard_map/pallas_call | solution.py:311
  30.1 0.4 collective-permute-start
  30.4 1.5 %collective-permute-start.3 = (f32[96,128]{1,0:T(8,128)S(1)}, f32[96,128]{1,0:T(8,128)S(1)}, u32[]{:S(2)}, u32[]{:S(2)}) collective-permute-start(f32[96,128]{1,0:T(8,128)S(1)} %get-tuple-element.18), channel_id=1, source_target_pairs={{0,3},{1,2},{2,1},{3,0},{4,7},{5,6},{6,5},{7,4},{8,11},{9,10},{10,... | collective-permute-start | bytes 147464 | tf_op jit(solution)/shard_map/ppermute | solution.py:325
  31.9 2.5 %collective-permute-start.2 = (f32[96,128]{1,0:T(8,128)S(1)}, f32[96,128]{1,0:T(8,128)S(1)}, u32[]{:S(2)}, u32[]{:S(2)}) collective-permute-start(f32[96,128]{1,0:T(8,128)S(1)} %get-tuple-element.18), channel_id=1, source_target_pairs={{0,2},{1,3},{2,0},{3,1},{4,6},{5,7},{6,4},{7,5},{8,10},{9,11},{10,... | collective-permute-start | bytes 147464 | tf_op jit(solution)/shard_map/ppermute | solution.py:325
  34.4 0.2 collective-permute-done
  34.7 1.7 %collective-permute-done.2 = f32[96,128]{1,0:T(8,128)S(1)} collective-permute-done((f32[96,128]{1,0:T(8,128)S(1)}, f32[96,128]{1,0:T(8,128)S(1)}, u32[]{:S(2)}, u32[]{:S(2)}) %collective-permute-start.2) | collective-permute-done | bytes 49184 | tf_op jit(solution)/shard_map/ppermute | solution.py:325
  36.4 1.2 %collective-permute-done.1 = f32[96,128]{1,0:T(8,128)S(1)} collective-permute-done((f32[96,128]{1,0:T(8,128)S(1)}, f32[96,128]{1,0:T(8,128)S(1)}, u32[]{:S(2)}, u32[]{:S(2)}) %collective-permute-start.1) | collective-permute-done | bytes 49184 | tf_op jit(solution)/shard_map/ppermute | solution.py:325
  37.6 1.3 %broadcast_in_dim.2 = bf16[4,1536,128]{2,1,0:T(8,128)(2,1)} broadcast(bf16[1536,128]{1,0:T(8,128)(2,1)S(1)} %pad_maximum_fusion), dimensions={1,2} | broadcast | bytes 1966080 | tf_op jit(solution)/shard_map/broadcast_in_dim | solution.py:384
  39.0 4.8 %all-to-all-start.1 = ((bf16[4,1536,128]{2,1,0:T(8,128)(2,1)}), bf16[4,1536,128]{2,1,0:T(8,128)(2,1)}, u32[]{:S(2)}, u32[]{:S(2)}) async-start(bf16[4,1536,128]{2,1,0:T(8,128)(2,1)} %broadcast_in_dim.2), calls=%async_computation.1 | async-start | bytes 3145728 | tf_op jit(solution)/shard_map/all_to_all | solution.py:388
  43.8 2.8 %collective-permute-start.6 = (f32[96,128]{1,0:T(8,128)S(1)}, f32[96,128]{1,0:T(8,128)S(1)}, u32[]{:S(2)}, u32[]{:S(2)}) collective-permute-start(f32[96,128]{1,0:T(8,128)S(1)} %add_add_fusion.1), channel_id=1, source_target_pairs={{0,48},{8,56},{16,32},{24,40},{32,16},{40,24},{48,0},{56,8},{64,11... | collective-permute-start | bytes 147464 | tf_op jit(solution)/shard_map/ppermute | solution.py:325
  46.6 0.3 collective-permute-start.5
  47.0 0.3 collective-permute-start.4
  47.3 0.8 collective-permute-done.6
  48.1 3.0 %collective-permute-done.5 = f32[96,128]{1,0:T(8,128)S(1)} collective-permute-done((f32[96,128]{1,0:T(8,128)S(1)}, f32[96,128]{1,0:T(8,128)S(1)}, u32[]{:S(2)}, u32[]{:S(2)}) %collective-permute-start.5) | collective-permute-done | bytes 49184 | tf_op jit(solution)/shard_map/ppermute | solution.py:325
  51.1 0.0 collective-permute-done.4
  51.1 4.4 %collective-permute-start.7 = (f32[96,128]{1,0:T(8,128)S(1)}, f32[96,128]{1,0:T(8,128)S(1)}, u32[]{:S(2)}, u32[]{:S(2)}) collective-permute-start(f32[96,128]{1,0:T(8,128)S(1)} %add_add_fusion), channel_id=1, source_target_pairs={{0,8},{8,0},{16,24},{24,16},{32,40},{40,32},{48,56},{56,48},{64,72... | collective-permute-start | bytes 147464 | tf_op jit(solution)/shard_map/ppermute | solution.py:325
  55.5 0.9 collective-permute-done.7
  56.4 0.0 copy-start.3
  56.4 0.0 copy-start.5
  56.5 3.3 %collective-permute-start.10 = (f32[96,128]{1,0:T(8,128)S(1)}, f32[96,128]{1,0:T(8,128)S(1)}, u32[]{:S(2)}, u32[]{:S(2)}) collective-permute-start(f32[96,128]{1,0:T(8,128)S(1)} %add.27.a_ref), channel_id=1, source_target_pairs={{0,68},{1,69},{2,70},{3,71},{4,64},{5,65},{6,66},{7,67},{8,76},{9,... | collective-permute-start | bytes 147464 | tf_op jit(solution)/shard_map/ppermute | solution.py:335
  59.8 0.1 collective-permute-start.9
  59.9 0.5 collective-permute-start.8
  60.5 1.1 collective-permute-done.10.d_ref
  61.5 2.7 %collective-permute-done.9.c_ref = f32[96,128]{1,0:T(8,128)S(1)} collective-permute-done((f32[96,128]{1,0:T(8,128)S(1)}, f32[96,128]{1,0:T(8,128)S(1)}, u32[]{:S(2)}, u32[]{:S(2)}) %collective-permute-start.9) | collective-permute-done | bytes 49184 | tf_op jit(solution)/shard_map/ppermute | solution.py:335
  64.2 5.5 %shard_map.97 = (f32[64,64]{1,0:T(8,128)}, f32[64,64]{1,0:T(8,128)S(1)}, f32[64,64]{1,0:T(8,128)S(1)}, f32[64,64]{1,0:T(8,128)S(1)}) custom-call(f32[96,128]{1,0:T(8,128)S(1)} %add.27.a_ref, f32[96,128]{1,0:T(8,128)S(1)} %collective-permute-done.8.b_ref, f32[96,128]{1,0:T(8,128)S(1)} %collective-permute-done.9.c_ref, f32[96,128]{1,0:T(8,128)S(1)} %collective-permute-done.10.d_ref), custom_call_target="tpu_custom_call" | custom-call | flops 5000000000 | bytes 65536 | tf_op jit(solution)/shard_map/pallas_call | solution.py:311
  69.7 4.5 %shard_map.98 = (f32[8,64,512]{2,1,0:T(8,128)S(1)}, bf16[8,64,512]{2,1,0:T(8,128)(2,1)S(1)}, f32[32,128]{1,0:T(8,128)S(1)}, f32[4,64]{1,0:T(4,128)}) custom-call(s32[2]{0:T(128)S(1)} %pad_add_fusion.at_ref.place_ref, s32[1,3,1,16]{3,2,1,0:T(1,128)S(1)} %bitcast.10, s32[1,1]{1,0:T(1,128)S(6)} %copy.12.count_hbm.count_ref, s32[32]{0:T(128)S(1)} %copy-done.5, ...), custom_call_target="tpu_custom_call" | custom-call | flops 5000000000 | bytes 65536 | tf_op jit(solution)/shard_map/pallas_call | solution.py:311
  74.3 1.9 %collective-permute-start.11 = (bf16[8,64,512]{2,1,0:T(8,128)(2,1)S(1)}, bf16[8,64,512]{2,1,0:T(8,128)(2,1)S(1)}, u32[]{:S(2)}, u32[]{:S(2)}) collective-permute-start(bf16[8,64,512]{2,1,0:T(8,128)(2,1)S(1)} %get-tuple-element.26), channel_id=1, source_target_pairs={{0,8},{8,0},{16,24},{24,16},{32,40},{40,32},{48,56},{56,48},{64,72... | collective-permute-start | bytes 1572872 | tf_op jit(solution)/shard_map/ppermute | solution.py:325
  76.1 0.1 collective-permute-start.12
  76.2 1.5 %collective-permute-done.12.gram_b = f32[32,128]{1,0:T(8,128)S(1)} collective-permute-done((f32[32,128]{1,0:T(8,128)S(1)}, f32[32,128]{1,0:T(8,128)S(1)}, u32[]{:S(2)}, u32[]{:S(2)}) %collective-permute-start.12) | collective-permute-done | bytes 16416 | tf_op jit(solution)/shard_map/ppermute | solution.py:325
  77.7 0.0 collective-permute-done.11.came_ref
  77.7 0.1 shard_map.99
  77.8 17.1 %all_to_all.20.got_ref = bf16[8,5,64,128]{3,2,1,0:T(8,128)(2,1)S(1)} all-to-all(bf16[8,5,64,128]{3,2,1,0:T(8,128)(2,1)S(1)} %shard_map.99), channel_id=1, replica_groups={{0,16,32,48,64,80,96,112},{8,24,40,56,72,88,104,120},{1,17,33,49,65,81,..., dimensions={0} | all-to-all | bytes 1310720 | tf_op jit(solution)/shard_map/all_to_all | solution.py:410
  94.9 2.7 %shard_map.100 = bf16[8,64,512]{2,1,0:T(8,128)(2,1)S(1)} custom-call(bf16[8,5,64,128]{3,2,1,0:T(8,128)(2,1)S(1)} %all_to_all.20.got_ref, f32[64,64]{1,0:T(8,128)S(1)} %get-tuple-element.28.mgram_ref), custom_call_target="tpu_custom_call" | custom-call | flops 1000000000 | bytes 65536 | tf_op jit(solution)/shard_map/pallas_call | solution.py:311
  97.5 12.6 %all_to_all.21.from_ref = bf16[8,64,512]{2,1,0:T(8,128)(2,1)S(1)} all-to-all(bf16[8,64,512]{2,1,0:T(8,128)(2,1)S(1)} %shard_map.100), channel_id=1, replica_groups={{0,16,32,48,64,80,96,112},{8,24,40,56,72,88,104,120},{1,17,33,49,65,81,..., dimensions={0} | all-to-all | bytes 1048576 | tf_op jit(solution)/shard_map/all_to_all | solution.py:410
  110.2 2.3 %collective-permute-start.13 = (bf16[8,64,512]{2,1,0:T(8,128)(2,1)S(1)}, bf16[8,64,512]{2,1,0:T(8,128)(2,1)S(1)}, u32[]{:S(2)}, u32[]{:S(2)}) collective-permute-start(bf16[8,64,512]{2,1,0:T(8,128)(2,1)S(1)} %all_to_all.21.from_ref), channel_id=1, source_target_pairs={{0,8},{8,0},{16,24},{24,16},{32,40},{40,32},{48,56},{56,48},{64,72... | collective-permute-start | bytes 1572872 | tf_op jit(solution)/shard_map/ppermute | solution.py:325
  112.5 1.6 %shard_map.101.refs_0_ = f32[64,8192]{1,0:T(8,128)} custom-call(s32[2]{0:T(128)S(1)} %pad_add_fusion.at_ref.place_ref, bf16[8,64,512]{2,1,0:T(8,128)(2,1)S(1)} %all_to_all.21.from_ref), custom_call_target="tpu_custom_call" | custom-call | flops 1000000000 | bytes 65536 | tf_op jit(solution)/shard_map/pallas_call | solution.py:311
  114.1 1.6 %shard_map.102 = f32[64,8192]{1,0:T(8,128)} custom-call(s32[2]{0:T(128)S(1)} %pad_add_fusion.at_ref.place_ref, bf16[8,64,512]{2,1,0:T(8,128)(2,1)S(1)} %collective-permute-done.13.from_ref, f32[64,8192]{1,0:T(8,128)} %shard_map.101.refs_0_), custom_call_target="tpu_custom_call", output_to_operand_aliasing={{}: (2, {})} | custom-call | flops 1000000000 | bytes 65536 | tf_op jit(solution)/shard_map/pallas_call | solution.py:311
  (19 shorter events, 0.1 us)
Async XLA Ops:
  1.3 0.7 copy-start.2
  2.0 0.7 copy-start.4
  5.6 6.9 %copy-start = (f32[64,8192]{1,0:T(8,128)S(1)}, f32[64,8192]{1,0:T(8,128)}, u32[]{:S(2)}) copy-start(f32[64,8192]{1,0:T(8,128)} %code_ref.1) | copy-start | bytes 6291460
  6.8 19.2 %all-to-all-start = ((f16[8,512,128]{2,1,0:T(8,128)(2,1)}), f16[8,512,128]{2,1,0:T(8,128)(2,1)S(1)}, u32[]{:S(2)}, u32[]{:S(2)}) async-start(f16[8,512,128]{2,1,0:T(8,128)(2,1)} %bitcast.3), calls=%async_computation | async-start | bytes 2097152 | tf_op jit(solution)/shard_map/all_to_all | solution.py:370
  12.4 13.8 %copy-start.6 = (f32[64,64]{1,0:T(8,128)S(1)}, f32[64,64]{1,0:T(8,128)}, u32[]{:S(2)}) copy-start(f32[64,64]{1,0:T(8,128)} %mix_ref.1) | copy-start | bytes 49156
  12.4 13.8 %copy-start.7 = (f32[32,64]{1,0:T(8,128)S(1)}, f32[32,64]{1,0:T(8,128)}, u32[]{:S(2)}) copy-start(f32[32,64]{1,0:T(8,128)} %weight_ref.1) | copy-start | bytes 24580
  30.1 4.6 %collective-permute-start = (bf16[768,128]{1,0:T(8,128)(2,1)S(1)}, bf16[768,128]{1,0:T(8,128)(2,1)S(1)}, u32[]{:S(2)}, u32[]{:S(2)}) collective-permute-start(bf16[768,128]{1,0:T(8,128)(2,1)S(1)} %get-tuple-element.17), channel_id=1, source_target_pairs={{0,4},{1,5},{2,6},{3,7},{4,0},{5,1},{6,2},{7,3},{8,12},{9,13},{10,... | collective-permute-start | bytes 589832 | tf_op jit(solution)/shard_map/ppermute | solution.py:325
  30.4 4.3 %collective-permute-start.3 = (f32[96,128]{1,0:T(8,128)S(1)}, f32[96,128]{1,0:T(8,128)S(1)}, u32[]{:S(2)}, u32[]{:S(2)}) collective-permute-start(f32[96,128]{1,0:T(8,128)S(1)} %get-tuple-element.18), channel_id=1, source_target_pairs={{0,3},{1,2},{2,1},{3,0},{4,7},{5,6},{6,5},{7,4},{8,11},{9,10},{10,... | collective-permute-start | bytes 147464 | tf_op jit(solution)/shard_map/ppermute | solution.py:325
  31.9 4.6 %collective-permute-start.2 = (f32[96,128]{1,0:T(8,128)S(1)}, f32[96,128]{1,0:T(8,128)S(1)}, u32[]{:S(2)}, u32[]{:S(2)}) collective-permute-start(f32[96,128]{1,0:T(8,128)S(1)} %get-tuple-element.18), channel_id=1, source_target_pairs={{0,2},{1,3},{2,0},{3,1},{4,6},{5,7},{6,4},{7,5},{8,10},{9,11},{10,... | collective-permute-start | bytes 147464 | tf_op jit(solution)/shard_map/ppermute | solution.py:325
  34.4 3.2 %collective-permute-start.1 = (f32[96,128]{1,0:T(8,128)S(1)}, f32[96,128]{1,0:T(8,128)S(1)}, u32[]{:S(2)}, u32[]{:S(2)}) collective-permute-start(f32[96,128]{1,0:T(8,128)S(1)} %get-tuple-element.18), channel_id=1, source_target_pairs={{0,1},{1,0},{2,3},{3,2},{4,5},{5,4},{6,7},{7,6},{8,9},{9,8},{10,11... | collective-permute-start | bytes 147464 | tf_op jit(solution)/shard_map/ppermute | solution.py:325
  39.0 30.7 %all-to-all-start.1 = ((bf16[4,1536,128]{2,1,0:T(8,128)(2,1)}), bf16[4,1536,128]{2,1,0:T(8,128)(2,1)}, u32[]{:S(2)}, u32[]{:S(2)}) async-start(bf16[4,1536,128]{2,1,0:T(8,128)(2,1)} %broadcast_in_dim.2), calls=%async_computation.1 | async-start | bytes 3145728 | tf_op jit(solution)/shard_map/all_to_all | solution.py:388
  43.8 4.3 %collective-permute-start.6 = (f32[96,128]{1,0:T(8,128)S(1)}, f32[96,128]{1,0:T(8,128)S(1)}, u32[]{:S(2)}, u32[]{:S(2)}) collective-permute-start(f32[96,128]{1,0:T(8,128)S(1)} %add_add_fusion.1), channel_id=1, source_target_pairs={{0,48},{8,56},{16,32},{24,40},{32,16},{40,24},{48,0},{56,8},{64,11... | collective-permute-start | bytes 147464 | tf_op jit(solution)/shard_map/ppermute | solution.py:325
  46.6 4.5 %collective-permute-start.5 = (f32[96,128]{1,0:T(8,128)S(1)}, f32[96,128]{1,0:T(8,128)S(1)}, u32[]{:S(2)}, u32[]{:S(2)}) collective-permute-start(f32[96,128]{1,0:T(8,128)S(1)} %add_add_fusion.1), channel_id=1, source_target_pairs={{0,32},{8,40},{16,48},{24,56},{32,0},{40,8},{48,16},{56,24},{64,96... | collective-permute-start | bytes 147464 | tf_op jit(solution)/shard_map/ppermute | solution.py:325
  47.0 4.1 %collective-permute-start.4 = (f32[96,128]{1,0:T(8,128)S(1)}, f32[96,128]{1,0:T(8,128)S(1)}, u32[]{:S(2)}, u32[]{:S(2)}) collective-permute-start(f32[96,128]{1,0:T(8,128)S(1)} %add_add_fusion.1), channel_id=1, source_target_pairs={{0,16},{8,24},{16,0},{24,8},{32,48},{40,56},{48,32},{56,40},{64,80... | collective-permute-start | bytes 147464 | tf_op jit(solution)/shard_map/ppermute | solution.py:325
  51.1 5.3 %collective-permute-start.7 = (f32[96,128]{1,0:T(8,128)S(1)}, f32[96,128]{1,0:T(8,128)S(1)}, u32[]{:S(2)}, u32[]{:S(2)}) collective-permute-start(f32[96,128]{1,0:T(8,128)S(1)} %add_add_fusion), channel_id=1, source_target_pairs={{0,8},{8,0},{16,24},{24,16},{32,40},{40,32},{48,56},{56,48},{64,72... | collective-permute-start | bytes 147464 | tf_op jit(solution)/shard_map/ppermute | solution.py:325
  56.4 13.3 %copy-start.1 = (bf16[1,1,16,128,512]{4,3,2,1,0:T(8,128)(2,1)S(1)}, bf16[1,1,16,128,512]{4,3,2,1,0:T(8,128)(2,1)}, u32[]{:S(2)}) copy-start(bf16[1,1,16,128,512]{4,3,2,1,0:T(8,128)(2,1)} %tile_hbm.1) | copy-start | bytes 6291460
  56.4 13.3 %copy-start.3 = (s32[1,1,3,16]{3,1,2,0:T(1,128)S(1)}, s32[1,1,3,16]{3,1,2,0:T(1,128)}, u32[]{:S(2)}) copy-start(s32[1,1,3,16]{3,1,2,0:T(1,128)} %param.8) | copy-start | bytes 580
  56.4 13.3 %copy-start.5 = (s32[32]{0:T(128)S(1)}, s32[32]{0:T(128)}, u32[]{:S(2)}) copy-start(s32[32]{0:T(128)} %visits_ref.1) | copy-start | bytes 388
  56.5 5.1 %collective-permute-start.10 = (f32[96,128]{1,0:T(8,128)S(1)}, f32[96,128]{1,0:T(8,128)S(1)}, u32[]{:S(2)}, u32[]{:S(2)}) collective-permute-start(f32[96,128]{1,0:T(8,128)S(1)} %add.27.a_ref), channel_id=1, source_target_pairs={{0,68},{1,69},{2,70},{3,71},{4,64},{5,65},{6,66},{7,67},{8,76},{9,... | collective-permute-start | bytes 147464 | tf_op jit(solution)/shard_map/ppermute | solution.py:335
  59.8 4.4 %collective-permute-start.9 = (f32[96,128]{1,0:T(8,128)S(1)}, f32[96,128]{1,0:T(8,128)S(1)}, u32[]{:S(2)}, u32[]{:S(2)}) collective-permute-start(f32[96,128]{1,0:T(8,128)S(1)} %add.27.a_ref), channel_id=1, source_target_pairs={{0,64},{1,65},{2,66},{3,67},{4,68},{5,69},{6,70},{7,71},{8,72},{9,... | collective-permute-start | bytes 147464 | tf_op jit(solution)/shard_map/ppermute | solution.py:335
  59.9 4.3 %collective-permute-start.8 = (f32[96,128]{1,0:T(8,128)S(1)}, f32[96,128]{1,0:T(8,128)S(1)}, u32[]{:S(2)}, u32[]{:S(2)}) collective-permute-start(f32[96,128]{1,0:T(8,128)S(1)} %add.27.a_ref), channel_id=1, source_target_pairs={{0,4},{1,5},{2,6},{3,7},{4,0},{5,1},{6,2},{7,3},{8,12},{9,13},{10,... | collective-permute-start | bytes 147464 | tf_op jit(solution)/shard_map/ppermute | solution.py:335
  74.3 3.4 %collective-permute-start.11 = (bf16[8,64,512]{2,1,0:T(8,128)(2,1)S(1)}, bf16[8,64,512]{2,1,0:T(8,128)(2,1)S(1)}, u32[]{:S(2)}, u32[]{:S(2)}) collective-permute-start(bf16[8,64,512]{2,1,0:T(8,128)(2,1)S(1)} %get-tuple-element.26), channel_id=1, source_target_pairs={{0,8},{8,0},{16,24},{24,16},{32,40},{40,32},{48,56},{56,48},{64,72... | collective-permute-start | bytes 1572872 | tf_op jit(solution)/shard_map/ppermute | solution.py:325
  76.1 1.6 %collective-permute-start.12 = (f32[32,128]{1,0:T(8,128)S(1)}, f32[32,128]{1,0:T(8,128)S(1)}, u32[]{:S(2)}, u32[]{:S(2)}) collective-permute-start(f32[32,128]{1,0:T(8,128)S(1)} %get-tuple-element.27.gram_a), channel_id=1, source_target_pairs={{0,8},{8,0},{16,24},{24,16},{32,40},{40,32},{48,56},{56,48},{64,72... | collective-permute-start | bytes 49160 | tf_op jit(solution)/shard_map/ppermute | solution.py:325
  110.2 3.9 %collective-permute-start.13 = (bf16[8,64,512]{2,1,0:T(8,128)(2,1)S(1)}, bf16[8,64,512]{2,1,0:T(8,128)(2,1)S(1)}, u32[]{:S(2)}, u32[]{:S(2)}) collective-permute-start(bf16[8,64,512]{2,1,0:T(8,128)(2,1)S(1)} %all_to_all.21.from_ref), channel_id=1, source_target_pairs={{0,8},{8,0},{16,24},{24,16},{32,40},{40,32},{48,56},{56,48},{64,72... | collective-permute-start | bytes 1572872 | tf_op jit(solution)/shard_map/ppermute | solution.py:325

commit v11 on v9

--- a/solution.py
+++ b/solution.py
@@ -48,6 +48,10 @@
 
 def times2(x, y):
     return [[x[i][0] * y[0][j] + x[i][1] * y[1][j] for j in (0, 1)] for i in (0, 1)]
+
+
+def dot4(x, y):
+    return (x[0] * y[0] + x[1] * y[1]) + (x[2] * y[2] + x[3] * y[3])
 
 
 def inverse4(p):
@@ -91,47 +95,57 @@
         [gram * scale + jnp.where(eye, damping, 0.0), eye.astype(F32)], axis=1
     )
     lanes = 2 * size
+    four = range(4)
     blocks = [work[i : i + 8] for i in range(0, size, 8)]
-    raw, fresh = [], []
-    for j in range(0, size, 4):
-        owner, at = j // 8, j % 8
-        rows = [blocks[owner][at + i : at + i + 1] for i in range(4)]
-        pivot = [
-            [jnp.broadcast_to(row[:, j + k : j + k + 1], (1, lanes)) for k in range(4)]
-            for row in rows
-        ]
-        inverse = inverse4(pivot)
-        new = [
-            (inverse[i][0] * rows[0] + inverse[i][1] * rows[1])
-            + (inverse[i][2] * rows[2] + inverse[i][3] * rows[3])
-            for i in range(4)
-        ]
-        raw += rows
+    fresh = []
+    for step in range(len(blocks)):
+        j = 8 * step
+        rows = [blocks[step][i : i + 1] for i in range(8)]
+
+        def entry(i, k):
+            return jnp.broadcast_to(rows[i][:, j + k : j + k + 1], (1, lanes))
+
+        a = inverse4([[entry(i, k) if k >= i else None for k in four] for i in four])
+        b = [[entry(i, 4 + k) for i in four] for k in four]
+        t = [[dot4(a[i], b[k]) for i in four] for k in four]
+        d = inverse4(
+            [
+                [entry(4 + i, 4 + k) - dot4(b[i], t[k]) if k >= i else None for k in four]
+                for i in four
+            ]
+        )
+        top = [dot4(a[i], rows[:4]) for i in four]
+        rest = [rows[4 + i] - dot4(b[i], top) for i in four]
+        low = [dot4(d[i], rest) for i in four]
+        new = [top[i] - dot4([t[k][i] for k in four], low) for i in four] + low
         fresh += new
-        for m in range(owner if at == 0 else owner + 1, len(blocks)):
+        for m in range(step + 1, len(blocks)):
             block = blocks[m]
-            part = [block[:, j + k : j + k + 1] * new[k] for k in range(4)]
-            blocks[m] = block - ((part[0] + part[1]) + (part[2] + part[3]))
-    raw = jnp.concatenate(raw, axis=0)[:, size:]
+            part = [block[:, j + k : j + k + 1] * new[k] for k in range(8)]
+            blocks[m] = block - (
+                ((part[0] + part[1]) + (part[2] + part[3]))
+                + ((part[4] + part[5]) + (part[6] + part[7]))
+            )
+    raw = jnp.concatenate(blocks, axis=0)[:, size:]
     fresh = jnp.concatenate(fresh, axis=0)[:, size:]
     return scale * mm(raw, fresh, TN)
 
 
 def live_rows(t, meta_ref, tile_rows):
-    width = meta_ref.shape[3]
     k, b, g = meta_ref[0, 0, 0, t], meta_ref[0, 1, 0, t], meta_ref[0, 2, 0, t]
-    visits = meta_ref[0, 4 + lax.div(k, width), 0, lax.rem(k, width)]
-    kept = jnp.where(t < meta_ref[0, 3, 0, 0], visits - tile_rows * b, 0)
+    kept = jnp.where(t < meta_ref[0, 3, 0, 0], meta_ref[0, 4, 0, k] - tile_rows * b, 0)
     return k, b, g, kept
 
 
 def products_kernel(
-    meta_ref, tile_hbm, code_hbm, out_ref, tile_ref, code_ref, sems
+    meta_hbm, tile_hbm, code_hbm, out_ref, meta_ref, tile_ref, code_ref, small_sem, sems
 ):
     slots, rows, cols = tile_ref.shape
     rank = code_ref.shape[0]
     parts = sems.shape[0] - 1
     each = slots // parts
+    small = pltpu.make_async_copy(meta_hbm, meta_ref, small_sem)
+    small.start()
     code_copy = pltpu.make_async_copy(code_hbm, code_ref, sems.at[parts])
     code_copy.start()
     copies = []
@@ -141,6 +155,7 @@
         copies[-1].start()
     out_ref[...] = jnp.zeros(out_ref.shape, F32)
     lane = lax.broadcasted_iota(jnp.int32, (rank, rows), 1)
+    small.wait()
     code_copy.wait()
     for t in range(slots):
         if t % each == 0:
@@ -337,29 +352,33 @@
 def body(tile_data, tile_list, tile_count, visit_counts, code_factor_t, visit_mix, patient_weight):
     tiles = tile_data[0, 0]
     slots, rows, cols = tiles.shape
-    meta = jnp.concatenate(
-        [
-            jnp.transpose(tile_list, (0, 2, 1, 3)),
-            jnp.broadcast_to(tile_count.reshape(1, 1, 1, 1), (1, 1, 1, slots)),
-            visit_counts.reshape(1, -1, 1, slots),
-        ],
-        axis=1,
-    )
     rank = visit_mix.shape[0]
     patients = visit_counts.shape[0]
     n_code, n_pat = lax.axis_size("code"), lax.axis_size("pat")
     half = n_pat // 2
     own = patients // n_code
     code_at, pat_at = lax.axis_index("code"), lax.axis_index("pat")
+    meta = jnp.concatenate(
+        [
+            jnp.pad(
+                jnp.transpose(tile_list, (0, 2, 1, 3)),
+                ((0, 0), (0, 0), (0, 0), (0, patients - slots)),
+            ),
+            jnp.broadcast_to(tile_count[0, 0], (1, 1, 1, patients)),
+            visit_counts.reshape(1, 1, 1, patients),
+        ],
+        axis=1,
+    )
     place = jnp.stack([code_at, lax.rem(pat_at, 2)]).astype(jnp.int32)
     shape = jax.ShapeDtypeStruct
     square = shape((rank, rank), F32)
 
     partial = call(
-        products_kernel, shape((patients * VBLOCKS, rank, rows), F32), [SM, HBM, HBM],
+        products_kernel, shape((patients * VBLOCKS, rank, rows), F32), [HBM] * 3,
         (meta, tile_data, code_factor_t),
         [
-            pltpu.VMEM(tiles.shape, BF16), pltpu.VMEM(code_factor_t.shape, F32),
+            pltpu.SMEM(meta.shape, jnp.int32), pltpu.VMEM(tiles.shape, BF16),
+            pltpu.VMEM(code_factor_t.shape, F32), pltpu.SemaphoreType.DMA(()),
             pltpu.SemaphoreType.DMA((5,)),
         ],
         vmem=50,

time: 117 us -> 115 us (0.983)
  Pallas kernels: 24.1 us -> 22.7 us
    pallas_call x9, Pallas kernels: 24.1 us -> 22.7 us  [call(): pl.pallas_call(kernel, out_shape=outs, in_specs=specs, out_specs=(spec,)...]
  transfers between devices with their start and end apart: 16 -> 16, of which waited for: 10 -> 10; matrix products, arithmetic and copies ran while one was open for 0% -> 0% of each run, Pallas kernels for 7% -> 6%
where the time goes in v11:
time: 115 us; the launch traced here: 114 us
  starting transfers between devices  31 us (27%)
  blocking collectives  29.7 us (26%)
  waiting for transfers between devices  25.8 us (22%)
  Pallas kernels  22.7 us (20%)
  other arithmetic  2.25 us (2%)
  between operations  1.56 us (1%)
  local copies, waits for them, and re-layouts  1.44 us (1%)
    all_to_all x2, blocking collectives, exchange(): return lax.all_to_all(x, 'pat', 0, 0, axis_index_groups=groups, tiled=True)  29.7 us
    pallas_call x9, Pallas kernels, call(): pl.pallas_call(kernel, out_shape=outs, in_specs=specs, out_specs=(spec,)...  22.7 us
    ppermute x11, starting transfers between devices, swap(): return lax.ppermute(x, axis, [(i, i ^ bit) for i in range(size)])  16.5 us
    all_to_all x1, waiting for transfers between devices, body(): got = lax.all_to_all(sent, 'code', 0, 0, tiled=True)  12.7 us
    ppermute x11, waiting for transfers between devices, swap(): return lax.ppermute(x, axis, [(i, i ^ bit) for i in range(size)])  9.34 us
    all_to_all x1, starting transfers between devices, body(): got = lax.all_to_all(sent, 'code', 0, 0, tiled=True)  5.62 us
    all_to_all x1, starting transfers between devices, body(): lax.all_to_all(message, 'code', 0, 0, axis_index_groups=layers, tiled=True)  4.83 us
    ppermute x3, starting transfers between devices, swap_z(): return lax.ppermute(x, ('pat', 'code'), pairs)  4.01 us
  transfers between devices with their start and end apart: 16, of which 10 were waited for; matrix products, arithmetic and copies ran while one was open for 0% of the time, Pallas kernels for 6%

profile of v11, /device:TPU:3, one launch (start us, length us, event | category | flops | bytes accessed | tf_op | source)
XLA Modules:
  0.0 114.5 jit_solution(10672786610243919725)
XLA Ops:
  1.3 0.1 pad.8.clone
  1.4 0.8 fusion.meta_hbm.meta_ref
  2.1 2.9 %shard_map.94 = f32[64,64,128]{2,1,0:T(8,128)S(1)} custom-call(s32[1,5,1,32]{3,2,1,0:T(1,128)S(1)} %fusion.meta_hbm.meta_ref, bf16[1,1,16,128,512]{4,3,2,1,0:T(8,128)(2,1)} %tile_hbm.1, f32[64,8192]{1,0:T(8,128)} %code_ref.1), custom_call_target="tpu_custom_call" | custom-call | flops 1000000000 | bytes 65536 | tf_op jit(solution)/shard_map/pallas_call | solution.py:319
  5.0 0.0 copy-start
  5.1 1.2 %convert_element_type.6 = f16[64,64,128]{2,1,0:T(8,128)(2,1)} convert(f32[64,64,128]{2,1,0:T(8,128)S(1)} %shard_map.94) | non-fusion elementwise | flops 524288 | bytes 3145728 | tf_op jit(solution)/shard_map/convert_element_type | solution.py:386
  6.3 5.6 %all-to-all-start = ((f16[8,512,128]{2,1,0:T(8,128)(2,1)}), f16[8,512,128]{2,1,0:T(8,128)(2,1)S(1)}, u32[]{:S(2)}, u32[]{:S(2)}) async-start(f16[8,512,128]{2,1,0:T(8,128)(2,1)} %bitcast.5), calls=%async_computation | async-start | bytes 2097152 | tf_op jit(solution)/shard_map/all_to_all | solution.py:387
  11.9 0.8 shard_map.95.gram_ref
  12.7 0.1 pad_add_fusion.1.at_ref.place_ref
  12.8 12.7 %all-to-all-done = f16[8,512,128]{2,1,0:T(8,128)(2,1)S(1)} async-done(((f16[8,512,128]{2,1,0:T(8,128)(2,1)}), f16[8,512,128]{2,1,0:T(8,128)(2,1)S(1)}, u32[]{:S(2)}, u32[]{:S(2)}) %all-to-all-start) | async-done | bytes 1048608 | tf_op jit(solution)/shard_map/all_to_all | solution.py:387
  25.5 0.1 convert_reduce_fusion
  25.7 3.8 %shard_map.96 = (f32[96,128]{1,0:T(8,128)S(1)}, bf16[768,128]{1,0:T(8,128)(2,1)S(1)}) custom-call(s32[2]{0:T(128)S(1)} %pad_add_fusion.1.at_ref.place_ref, f32[8,64,128]{2,1,0:T(8,128)S(1)} %bitcast.13, f32[64,64]{1,0:T(8,128)S(1)} %copy-done.2, f32[32,64]{1,0:T(8,128)S(1)} %copy-done.3, f32[32,128]{1,0:T(8,128)S(1)} %shard_map.95.gram_ref), custom_call_target="tpu_custom_call" | custom-call | flops 5000000000 | bytes 65536 | tf_op jit(solution)/shard_map/pallas_call | solution.py:319
  29.5 0.4 collective-permute-start
  29.9 1.5 %collective-permute-start.3 = (f32[96,128]{1,0:T(8,128)S(1)}, f32[96,128]{1,0:T(8,128)S(1)}, u32[]{:S(2)}, u32[]{:S(2)}) collective-permute-start(f32[96,128]{1,0:T(8,128)S(1)} %get-tuple-element.18), channel_id=1, source_target_pairs={{0,3},{1,2},{2,1},{3,0},{4,7},{5,6},{6,5},{7,4},{8,11},{9,10},{10,... | collective-permute-start | bytes 147464 | tf_op jit(solution)/shard_map/ppermute | solution.py:333
  31.4 2.5 %collective-permute-start.2 = (f32[96,128]{1,0:T(8,128)S(1)}, f32[96,128]{1,0:T(8,128)S(1)}, u32[]{:S(2)}, u32[]{:S(2)}) collective-permute-start(f32[96,128]{1,0:T(8,128)S(1)} %get-tuple-element.18), channel_id=1, source_target_pairs={{0,2},{1,3},{2,0},{3,1},{4,6},{5,7},{6,4},{7,5},{8,10},{9,11},{10,... | collective-permute-start | bytes 147464 | tf_op jit(solution)/shard_map/ppermute | solution.py:333
  33.9 0.0 collective-permute-start.1
  33.9 0.2 collective-permute-done
  34.2 0.0 collective-permute-done.3
  34.2 1.7 %collective-permute-done.2 = f32[96,128]{1,0:T(8,128)S(1)} collective-permute-done((f32[96,128]{1,0:T(8,128)S(1)}, f32[96,128]{1,0:T(8,128)S(1)}, u32[]{:S(2)}, u32[]{:S(2)}) %collective-permute-start.2) | collective-permute-done | bytes 49184 | tf_op jit(solution)/shard_map/ppermute | solution.py:333
  35.9 1.2 %collective-permute-done.1 = f32[96,128]{1,0:T(8,128)S(1)} collective-permute-done((f32[96,128]{1,0:T(8,128)S(1)}, f32[96,128]{1,0:T(8,128)S(1)}, u32[]{:S(2)}, u32[]{:S(2)}) %collective-permute-start.1) | collective-permute-done | bytes 49184 | tf_op jit(solution)/shard_map/ppermute | solution.py:333
  37.1 1.3 %broadcast_in_dim.10 = bf16[4,1536,128]{2,1,0:T(8,128)(2,1)} broadcast(bf16[1536,128]{1,0:T(8,128)(2,1)S(1)} %pad_maximum_fusion), dimensions={1,2} | broadcast | bytes 1966080 | tf_op jit(solution)/shard_map/broadcast_in_dim | solution.py:401
  38.5 4.8 %all-to-all-start.1 = ((bf16[4,1536,128]{2,1,0:T(8,128)(2,1)}), bf16[4,1536,128]{2,1,0:T(8,128)(2,1)}, u32[]{:S(2)}, u32[]{:S(2)}) async-start(bf16[4,1536,128]{2,1,0:T(8,128)(2,1)} %broadcast_in_dim.10), calls=%async_computation.1 | async-start | bytes 3145728 | tf_op jit(solution)/shard_map/all_to_all | solution.py:405
  43.3 2.8 %collective-permute-start.6 = (f32[96,128]{1,0:T(8,128)S(1)}, f32[96,128]{1,0:T(8,128)S(1)}, u32[]{:S(2)}, u32[]{:S(2)}) collective-permute-start(f32[96,128]{1,0:T(8,128)S(1)} %add_add_fusion.1), channel_id=1, source_target_pairs={{0,48},{8,56},{16,32},{24,40},{32,16},{40,24},{48,0},{56,8},{64,11... | collective-permute-start | bytes 147464 | tf_op jit(solution)/shard_map/ppermute | solution.py:333
  46.1 0.3 collective-permute-start.5
  46.5 0.3 collective-permute-start.4
  46.8 0.8 collective-permute-done.6
  47.6 3.0 %collective-permute-done.5 = f32[96,128]{1,0:T(8,128)S(1)} collective-permute-done((f32[96,128]{1,0:T(8,128)S(1)}, f32[96,128]{1,0:T(8,128)S(1)}, u32[]{:S(2)}, u32[]{:S(2)}) %collective-permute-start.5) | collective-permute-done | bytes 49184 | tf_op jit(solution)/shard_map/ppermute | solution.py:333
  50.6 0.0 collective-permute-done.4
  50.6 4.4 %collective-permute-start.7 = (f32[96,128]{1,0:T(8,128)S(1)}, f32[96,128]{1,0:T(8,128)S(1)}, u32[]{:S(2)}, u32[]{:S(2)}) collective-permute-start(f32[96,128]{1,0:T(8,128)S(1)} %add_add_fusion), channel_id=1, source_target_pairs={{0,8},{8,0},{16,24},{24,16},{32,40},{40,32},{48,56},{56,48},{64,72... | collective-permute-start | bytes 147464 | tf_op jit(solution)/shard_map/ppermute | solution.py:333
  55.0 0.9 collective-permute-done.7
  55.9 3.3 %collective-permute-start.10 = (f32[96,128]{1,0:T(8,128)S(1)}, f32[96,128]{1,0:T(8,128)S(1)}, u32[]{:S(2)}, u32[]{:S(2)}) collective-permute-start(f32[96,128]{1,0:T(8,128)S(1)} %add.29.a_ref), channel_id=1, source_target_pairs={{0,68},{1,69},{2,70},{3,71},{4,64},{5,65},{6,66},{7,67},{8,76},{9,... | collective-permute-start | bytes 147464 | tf_op jit(solution)/shard_map/ppermute | solution.py:343
  59.3 0.1 collective-permute-start.9
  59.4 0.5 collective-permute-start.8
  59.9 1.1 collective-permute-done.10.d_ref
  61.0 2.7 %collective-permute-done.9.c_ref = f32[96,128]{1,0:T(8,128)S(1)} collective-permute-done((f32[96,128]{1,0:T(8,128)S(1)}, f32[96,128]{1,0:T(8,128)S(1)}, u32[]{:S(2)}, u32[]{:S(2)}) %collective-permute-start.9) | collective-permute-done | bytes 49184 | tf_op jit(solution)/shard_map/ppermute | solution.py:343
  63.7 4.8 %shard_map.97 = (f32[64,64]{1,0:T(8,128)}, f32[64,64]{1,0:T(8,128)S(1)}, f32[64,64]{1,0:T(8,128)S(1)}, f32[64,64]{1,0:T(8,128)S(1)}) custom-call(f32[96,128]{1,0:T(8,128)S(1)} %add.29.a_ref, f32[96,128]{1,0:T(8,128)S(1)} %collective-permute-done.8.b_ref, f32[96,128]{1,0:T(8,128)S(1)} %collective-permute-done.9.c_ref, f32[96,128]{1,0:T(8,128)S(1)} %collective-permute-done.10.d_ref), custom_call_target="tpu_custom_call" | custom-call | flops 5000000000 | bytes 65536 | tf_op jit(solution)/shard_map/pallas_call | solution.py:319
  68.5 4.7 %shard_map.98 = (f32[8,64,512]{2,1,0:T(8,128)S(1)}, bf16[8,64,512]{2,1,0:T(8,128)(2,1)S(1)}, f32[32,128]{1,0:T(8,128)S(1)}, f32[4,64]{1,0:T(4,128)}) custom-call(s32[2]{0:T(128)S(1)} %pad_add_fusion.1.at_ref.place_ref, s32[1,5,1,32]{3,2,1,0:T(1,128)S(1)} %fusion.meta_hbm.meta_ref, bf16[8,768,128]{2,1,0:T(8,128)(2,1)} %bitcast.7.got_ref, ...), custom_call_target="tpu_custom_call" | custom-call | flops 5000000000 | bytes 65536 | tf_op jit(solution)/shard_map/pallas_call | solution.py:319
  73.2 1.9 %collective-permute-start.11 = (bf16[8,64,512]{2,1,0:T(8,128)(2,1)S(1)}, bf16[8,64,512]{2,1,0:T(8,128)(2,1)S(1)}, u32[]{:S(2)}, u32[]{:S(2)}) collective-permute-start(bf16[8,64,512]{2,1,0:T(8,128)(2,1)S(1)} %get-tuple-element.26), channel_id=1, source_target_pairs={{0,8},{8,0},{16,24},{24,16},{32,40},{40,32},{48,56},{56,48},{64,72... | collective-permute-start | bytes 1572872 | tf_op jit(solution)/shard_map/ppermute | solution.py:333
  75.1 0.1 collective-permute-start.12
  75.2 1.5 %collective-permute-done.12.gram_b = f32[32,128]{1,0:T(8,128)S(1)} collective-permute-done((f32[32,128]{1,0:T(8,128)S(1)}, f32[32,128]{1,0:T(8,128)S(1)}, u32[]{:S(2)}, u32[]{:S(2)}) %collective-permute-start.12) | collective-permute-done | bytes 16416 | tf_op jit(solution)/shard_map/ppermute | solution.py:333
  76.7 0.0 collective-permute-done.11.came_ref
  76.7 0.1 shard_map.99
  76.8 17.0 %all_to_all.20.got_ref = bf16[8,5,64,128]{3,2,1,0:T(8,128)(2,1)S(1)} all-to-all(bf16[8,5,64,128]{3,2,1,0:T(8,128)(2,1)S(1)} %shard_map.99), channel_id=1, replica_groups={{0,16,32,48,64,80,96,112},{8,24,40,56,72,88,104,120},{1,17,33,49,65,81,..., dimensions={0} | all-to-all | bytes 1310720 | tf_op jit(solution)/shard_map/all_to_all | solution.py:427
  93.8 2.4 %shard_map.100 = bf16[8,64,512]{2,1,0:T(8,128)(2,1)S(1)} custom-call(bf16[8,5,64,128]{3,2,1,0:T(8,128)(2,1)S(1)} %all_to_all.20.got_ref, f32[64,64]{1,0:T(8,128)S(1)} %get-tuple-element.28.mgram_ref), custom_call_target="tpu_custom_call" | custom-call | flops 1000000000 | bytes 65536 | tf_op jit(solution)/shard_map/pallas_call | solution.py:319
  96.2 12.6 %all_to_all.21.from_ref = bf16[8,64,512]{2,1,0:T(8,128)(2,1)S(1)} all-to-all(bf16[8,64,512]{2,1,0:T(8,128)(2,1)S(1)} %shard_map.100), channel_id=1, replica_groups={{0,16,32,48,64,80,96,112},{8,24,40,56,72,88,104,120},{1,17,33,49,65,81,..., dimensions={0} | all-to-all | bytes 1048576 | tf_op jit(solution)/shard_map/all_to_all | solution.py:427
  108.8 2.3 %collective-permute-start.13 = (bf16[8,64,512]{2,1,0:T(8,128)(2,1)S(1)}, bf16[8,64,512]{2,1,0:T(8,128)(2,1)S(1)}, u32[]{:S(2)}, u32[]{:S(2)}) collective-permute-start(bf16[8,64,512]{2,1,0:T(8,128)(2,1)S(1)} %all_to_all.21.from_ref), channel_id=1, source_target_pairs={{0,8},{8,0},{16,24},{24,16},{32,40},{40,32},{48,56},{56,48},{64,72... | collective-permute-start | bytes 1572872 | tf_op jit(solution)/shard_map/ppermute | solution.py:333
  111.1 1.6 %shard_map.101.refs_0_ = f32[64,8192]{1,0:T(8,128)} custom-call(s32[2]{0:T(128)S(1)} %pad_add_fusion.1.at_ref.place_ref, bf16[8,64,512]{2,1,0:T(8,128)(2,1)S(1)} %all_to_all.21.from_ref), custom_call_target="tpu_custom_call" | custom-call | flops 1000000000 | bytes 65536 | tf_op jit(solution)/shard_map/pallas_call | solution.py:319
  112.7 0.0 collective-permute-done.13.from_ref
  112.7 1.6 %shard_map.102 = f32[64,8192]{1,0:T(8,128)} custom-call(s32[2]{0:T(128)S(1)} %pad_add_fusion.1.at_ref.place_ref, bf16[8,64,512]{2,1,0:T(8,128)(2,1)S(1)} %collective-permute-done.13.from_ref, f32[64,8192]{1,0:T(8,128)} %shard_map.101.refs_0_), custom_call_target="tpu_custom_call", output_to_operand_aliasing={{}: (2, {})} | custom-call | flops 1000000000 | bytes 65536 | tf_op jit(solution)/shard_map/pallas_call | solution.py:319
  (13 shorter events, 0.1 us)
Async XLA Ops:
  5.0 6.9 %copy-start = (f32[64,8192]{1,0:T(8,128)S(1)}, f32[64,8192]{1,0:T(8,128)}, u32[]{:S(2)}) copy-start(f32[64,8192]{1,0:T(8,128)} %code_ref.1) | copy-start | bytes 6291460
  6.3 19.2 %all-to-all-start = ((f16[8,512,128]{2,1,0:T(8,128)(2,1)}), f16[8,512,128]{2,1,0:T(8,128)(2,1)S(1)}, u32[]{:S(2)}, u32[]{:S(2)}) async-start(f16[8,512,128]{2,1,0:T(8,128)(2,1)} %bitcast.5), calls=%async_computation | async-start | bytes 2097152 | tf_op jit(solution)/shard_map/all_to_all | solution.py:387
  11.9 13.8 %copy-start.2 = (f32[64,64]{1,0:T(8,128)S(1)}, f32[64,64]{1,0:T(8,128)}, u32[]{:S(2)}) copy-start(f32[64,64]{1,0:T(8,128)} %mix_ref.1) | copy-start | bytes 49156
  11.9 13.8 %copy-start.3 = (f32[32,64]{1,0:T(8,128)S(1)}, f32[32,64]{1,0:T(8,128)}, u32[]{:S(2)}) copy-start(f32[32,64]{1,0:T(8,128)} %weight_ref.1) | copy-start | bytes 24580
  29.5 4.6 %collective-permute-start = (bf16[768,128]{1,0:T(8,128)(2,1)S(1)}, bf16[768,128]{1,0:T(8,128)(2,1)S(1)}, u32[]{:S(2)}, u32[]{:S(2)}) collective-permute-start(bf16[768,128]{1,0:T(8,128)(2,1)S(1)} %get-tuple-element.17), channel_id=1, source_target_pairs={{0,4},{1,5},{2,6},{3,7},{4,0},{5,1},{6,2},{7,3},{8,12},{9,13},{10,... | collective-permute-start | bytes 589832 | tf_op jit(solution)/shard_map/ppermute | solution.py:333
  29.9 4.3 %collective-permute-start.3 = (f32[96,128]{1,0:T(8,128)S(1)}, f32[96,128]{1,0:T(8,128)S(1)}, u32[]{:S(2)}, u32[]{:S(2)}) collective-permute-start(f32[96,128]{1,0:T(8,128)S(1)} %get-tuple-element.18), channel_id=1, source_target_pairs={{0,3},{1,2},{2,1},{3,0},{4,7},{5,6},{6,5},{7,4},{8,11},{9,10},{10,... | collective-permute-start | bytes 147464 | tf_op jit(solution)/shard_map/ppermute | solution.py:333
  31.4 4.5 %collective-permute-start.2 = (f32[96,128]{1,0:T(8,128)S(1)}, f32[96,128]{1,0:T(8,128)S(1)}, u32[]{:S(2)}, u32[]{:S(2)}) collective-permute-start(f32[96,128]{1,0:T(8,128)S(1)} %get-tuple-element.18), channel_id=1, source_target_pairs={{0,2},{1,3},{2,0},{3,1},{4,6},{5,7},{6,4},{7,5},{8,10},{9,11},{10,... | collective-permute-start | bytes 147464 | tf_op jit(solution)/shard_map/ppermute | solution.py:333
  33.9 3.2 %collective-permute-start.1 = (f32[96,128]{1,0:T(8,128)S(1)}, f32[96,128]{1,0:T(8,128)S(1)}, u32[]{:S(2)}, u32[]{:S(2)}) collective-permute-start(f32[96,128]{1,0:T(8,128)S(1)} %get-tuple-element.18), channel_id=1, source_target_pairs={{0,1},{1,0},{2,3},{3,2},{4,5},{5,4},{6,7},{7,6},{8,9},{9,8},{10,11... | collective-permute-start | bytes 147464 | tf_op jit(solution)/shard_map/ppermute | solution.py:333
  38.5 30.1 %all-to-all-start.1 = ((bf16[4,1536,128]{2,1,0:T(8,128)(2,1)}), bf16[4,1536,128]{2,1,0:T(8,128)(2,1)}, u32[]{:S(2)}, u32[]{:S(2)}) async-start(bf16[4,1536,128]{2,1,0:T(8,128)(2,1)} %broadcast_in_dim.10), calls=%async_computation.1 | async-start | bytes 3145728 | tf_op jit(solution)/shard_map/all_to_all | solution.py:405
  43.3 4.3 %collective-permute-start.6 = (f32[96,128]{1,0:T(8,128)S(1)}, f32[96,128]{1,0:T(8,128)S(1)}, u32[]{:S(2)}, u32[]{:S(2)}) collective-permute-start(f32[96,128]{1,0:T(8,128)S(1)} %add_add_fusion.1), channel_id=1, source_target_pairs={{0,48},{8,56},{16,32},{24,40},{32,16},{40,24},{48,0},{56,8},{64,11... | collective-permute-start | bytes 147464 | tf_op jit(solution)/shard_map/ppermute | solution.py:333
  46.1 4.5 %collective-permute-start.5 = (f32[96,128]{1,0:T(8,128)S(1)}, f32[96,128]{1,0:T(8,128)S(1)}, u32[]{:S(2)}, u32[]{:S(2)}) collective-permute-start(f32[96,128]{1,0:T(8,128)S(1)} %add_add_fusion.1), channel_id=1, source_target_pairs={{0,32},{8,40},{16,48},{24,56},{32,0},{40,8},{48,16},{56,24},{64,96... | collective-permute-start | bytes 147464 | tf_op jit(solution)/shard_map/ppermute | solution.py:333
  46.5 4.1 %collective-permute-start.4 = (f32[96,128]{1,0:T(8,128)S(1)}, f32[96,128]{1,0:T(8,128)S(1)}, u32[]{:S(2)}, u32[]{:S(2)}) collective-permute-start(f32[96,128]{1,0:T(8,128)S(1)} %add_add_fusion.1), channel_id=1, source_target_pairs={{0,16},{8,24},{16,0},{24,8},{32,48},{40,56},{48,32},{56,40},{64,80... | collective-permute-start | bytes 147464 | tf_op jit(solution)/shard_map/ppermute | solution.py:333
  50.6 5.3 %collective-permute-start.7 = (f32[96,128]{1,0:T(8,128)S(1)}, f32[96,128]{1,0:T(8,128)S(1)}, u32[]{:S(2)}, u32[]{:S(2)}) collective-permute-start(f32[96,128]{1,0:T(8,128)S(1)} %add_add_fusion), channel_id=1, source_target_pairs={{0,8},{8,0},{16,24},{24,16},{32,40},{40,32},{48,56},{56,48},{64,72... | collective-permute-start | bytes 147464 | tf_op jit(solution)/shard_map/ppermute | solution.py:333
  55.9 12.6 %copy-start.1 = (bf16[1,1,16,128,512]{4,3,2,1,0:T(8,128)(2,1)S(1)}, bf16[1,1,16,128,512]{4,3,2,1,0:T(8,128)(2,1)}, u32[]{:S(2)}) copy-start(bf16[1,1,16,128,512]{4,3,2,1,0:T(8,128)(2,1)} %tile_hbm.1) | copy-start | bytes 6291460
  55.9 5.1 %collective-permute-start.10 = (f32[96,128]{1,0:T(8,128)S(1)}, f32[96,128]{1,0:T(8,128)S(1)}, u32[]{:S(2)}, u32[]{:S(2)}) collective-permute-start(f32[96,128]{1,0:T(8,128)S(1)} %add.29.a_ref), channel_id=1, source_target_pairs={{0,68},{1,69},{2,70},{3,71},{4,64},{5,65},{6,66},{7,67},{8,76},{9,... | collective-permute-start | bytes 147464 | tf_op jit(solution)/shard_map/ppermute | solution.py:343
  59.3 4.4 %collective-permute-start.9 = (f32[96,128]{1,0:T(8,128)S(1)}, f32[96,128]{1,0:T(8,128)S(1)}, u32[]{:S(2)}, u32[]{:S(2)}) collective-permute-start(f32[96,128]{1,0:T(8,128)S(1)} %add.29.a_ref), channel_id=1, source_target_pairs={{0,64},{1,65},{2,66},{3,67},{4,68},{5,69},{6,70},{7,71},{8,72},{9,... | collective-permute-start | bytes 147464 | tf_op jit(solution)/shard_map/ppermute | solution.py:343
  59.4 4.3 %collective-permute-start.8 = (f32[96,128]{1,0:T(8,128)S(1)}, f32[96,128]{1,0:T(8,128)S(1)}, u32[]{:S(2)}, u32[]{:S(2)}) collective-permute-start(f32[96,128]{1,0:T(8,128)S(1)} %add.29.a_ref), channel_id=1, source_target_pairs={{0,4},{1,5},{2,6},{3,7},{4,0},{5,1},{6,2},{7,3},{8,12},{9,13},{10,... | collective-permute-start | bytes 147464 | tf_op jit(solution)/shard_map/ppermute | solution.py:343
  73.2 3.5 %collective-permute-start.11 = (bf16[8,64,512]{2,1,0:T(8,128)(2,1)S(1)}, bf16[8,64,512]{2,1,0:T(8,128)(2,1)S(1)}, u32[]{:S(2)}, u32[]{:S(2)}) collective-permute-start(bf16[8,64,512]{2,1,0:T(8,128)(2,1)S(1)} %get-tuple-element.26), channel_id=1, source_target_pairs={{0,8},{8,0},{16,24},{24,16},{32,40},{40,32},{48,56},{56,48},{64,72... | collective-permute-start | bytes 1572872 | tf_op jit(solution)/shard_map/ppermute | solution.py:333
  75.1 1.6 %collective-permute-start.12 = (f32[32,128]{1,0:T(8,128)S(1)}, f32[32,128]{1,0:T(8,128)S(1)}, u32[]{:S(2)}, u32[]{:S(2)}) collective-permute-start(f32[32,128]{1,0:T(8,128)S(1)} %get-tuple-element.27.gram_a), channel_id=1, source_target_pairs={{0,8},{8,0},{16,24},{24,16},{32,40},{40,32},{48,56},{56,48},{64,72... | collective-permute-start | bytes 49160 | tf_op jit(solution)/shard_map/ppermute | solution.py:333
  108.8 3.9 %collective-permute-start.13 = (bf16[8,64,512]{2,1,0:T(8,128)(2,1)S(1)}, bf16[8,64,512]{2,1,0:T(8,128)(2,1)S(1)}, u32[]{:S(2)}, u32[]{:S(2)}) collective-permute-start(bf16[8,64,512]{2,1,0:T(8,128)(2,1)S(1)} %all_to_all.21.from_ref), channel_id=1, source_target_pairs={{0,8},{8,0},{16,24},{24,16},{32,40},{40,32},{48,56},{56,48},{64,72... | collective-permute-start | bytes 1572872 | tf_op jit(solution)/shard_map/ppermute | solution.py:333

commit v12 on v11

--- a/solution.py
+++ b/solution.py
@@ -138,16 +138,23 @@
 
 
 def products_kernel(
-    meta_hbm, tile_hbm, code_hbm, out_ref, meta_ref, tile_ref, code_ref, small_sem, sems
+    meta_hbm, tile_hbm, code_hbm, out_ref, meta_ref, tile_ref, code_ref, small_sem, band_sems, sems
 ):
     slots, rows, cols = tile_ref.shape
     rank = code_ref.shape[0]
-    parts = sems.shape[0] - 1
+    parts = sems.shape[0]
     each = slots // parts
     small = pltpu.make_async_copy(meta_hbm, meta_ref, small_sem)
     small.start()
-    code_copy = pltpu.make_async_copy(code_hbm, code_ref, sems.at[parts])
-    code_copy.start()
+    bands = band_sems.shape[0]
+    band = rank // bands
+    band_copies = []
+    for i in range(bands):
+        at = pl.ds(i * band, band)
+        band_copies.append(
+            pltpu.make_async_copy(code_hbm.at[at], code_ref.at[at], band_sems.at[i])
+        )
+        band_copies[-1].start()
     copies = []
     for i in range(parts):
         at = pl.ds(i * each, each)
@@ -156,7 +163,8 @@
     out_ref[...] = jnp.zeros(out_ref.shape, F32)
     lane = lax.broadcasted_iota(jnp.int32, (rank, rows), 1)
     small.wait()
-    code_copy.wait()
+    for copy in band_copies:
+        copy.wait()
     for t in range(slots):
         if t % each == 0:
             copies[t // each].wait()
@@ -379,7 +387,7 @@
         [
             pltpu.SMEM(meta.shape, jnp.int32), pltpu.VMEM(tiles.shape, BF16),
             pltpu.VMEM(code_factor_t.shape, F32), pltpu.SemaphoreType.DMA(()),
-            pltpu.SemaphoreType.DMA((5,)),
+            pltpu.SemaphoreType.DMA((8,)), pltpu.SemaphoreType.DMA((4,)),
         ],
         vmem=50,
     )

time: 115 us -> 116 us (level)
  no operation moved by 1% of the time
where the time goes in v12:
time: 116 us; the launch traced here: 115 us
  starting transfers between devices  31 us (27%)
  blocking collectives  29.7 us (26%)
  waiting for transfers between devices  25.8 us (22%)
  Pallas kernels  23.1 us (20%)
  other arithmetic  2.25 us (2%)
  between operations  1.56 us (1%)
  local copies, waits for them, and re-layouts  1.44 us (1%)
    all_to_all x2, blocking collectives, exchange(): return lax.all_to_all(x, 'pat', 0, 0, axis_index_groups=groups, tiled=True)  29.7 us
    pallas_call x9, Pallas kernels, call(): pl.pallas_call(kernel, out_shape=outs, in_specs=specs, out_specs=(spec,)...  23.1 us
    ppermute x11, starting transfers between devices, swap(): return lax.ppermute(x, axis, [(i, i ^ bit) for i in range(size)])  16.5 us
    all_to_all x1, waiting for transfers between devices, body(): got = lax.all_to_all(sent, 'code', 0, 0, tiled=True)  12.7 us
    ppermute x11, waiting for transfers between devices, swap(): return lax.ppermute(x, axis, [(i, i ^ bit) for i in range(size)])  9.34 us
    all_to_all x1, starting transfers between devices, body(): got = lax.all_to_all(sent, 'code', 0, 0, tiled=True)  5.62 us
    all_to_all x1, starting transfers between devices, body(): lax.all_to_all(message, 'code', 0, 0, axis_index_groups=layers, tiled=True)  4.83 us
    ppermute x3, starting transfers between devices, swap_z(): return lax.ppermute(x, ('pat', 'code'), pairs)  4.01 us
  transfers between devices with their start and end apart: 16, of which 10 were waited for; matrix products, arithmetic and copies ran while one was open for 0% of the time, Pallas kernels for 6%

profile of v12, /device:TPU:3, one launch (start us, length us, event | category | flops | bytes accessed | tf_op | source)
XLA Modules:
  0.0 114.8 jit_solution(8319153989008968219)
XLA Ops:
  1.3 0.1 pad.8.clone
  1.4 0.8 fusion.meta_hbm.meta_ref
  2.1 3.3 %shard_map.94 = f32[64,64,128]{2,1,0:T(8,128)S(1)} custom-call(s32[1,5,1,32]{3,2,1,0:T(1,128)S(1)} %fusion.meta_hbm.meta_ref, bf16[1,1,16,128,512]{4,3,2,1,0:T(8,128)(2,1)} %tile_hbm.1, f32[64,8192]{1,0:T(8,128)} %code_ref.1), custom_call_target="tpu_custom_call" | custom-call | flops 1000000000 | bytes 65536 | tf_op jit(solution)/shard_map/pallas_call | solution.py:327
  5.4 0.0 copy-start
  5.4 1.2 %convert_element_type.6 = f16[64,64,128]{2,1,0:T(8,128)(2,1)} convert(f32[64,64,128]{2,1,0:T(8,128)S(1)} %shard_map.94) | non-fusion elementwise | flops 524288 | bytes 3145728 | tf_op jit(solution)/shard_map/convert_element_type | solution.py:394
  6.6 5.6 %all-to-all-start = ((f16[8,512,128]{2,1,0:T(8,128)(2,1)}), f16[8,512,128]{2,1,0:T(8,128)(2,1)S(1)}, u32[]{:S(2)}, u32[]{:S(2)}) async-start(f16[8,512,128]{2,1,0:T(8,128)(2,1)} %bitcast.5), calls=%async_computation | async-start | bytes 2097152 | tf_op jit(solution)/shard_map/all_to_all | solution.py:395
  12.3 0.8 shard_map.95.gram_ref
  13.1 0.1 pad_add_fusion.1.at_ref.place_ref
  13.2 12.7 %all-to-all-done = f16[8,512,128]{2,1,0:T(8,128)(2,1)S(1)} async-done(((f16[8,512,128]{2,1,0:T(8,128)(2,1)}), f16[8,512,128]{2,1,0:T(8,128)(2,1)S(1)}, u32[]{:S(2)}, u32[]{:S(2)}) %all-to-all-start) | async-done | bytes 1048608 | tf_op jit(solution)/shard_map/all_to_all | solution.py:395
  25.9 0.1 convert_reduce_fusion
  26.0 3.8 %shard_map.96 = (f32[96,128]{1,0:T(8,128)S(1)}, bf16[768,128]{1,0:T(8,128)(2,1)S(1)}) custom-call(s32[2]{0:T(128)S(1)} %pad_add_fusion.1.at_ref.place_ref, f32[8,64,128]{2,1,0:T(8,128)S(1)} %bitcast.13, f32[64,64]{1,0:T(8,128)S(1)} %copy-done.2, f32[32,64]{1,0:T(8,128)S(1)} %copy-done.3, f32[32,128]{1,0:T(8,128)S(1)} %shard_map.95.gram_ref), custom_call_target="tpu_custom_call" | custom-call | flops 5000000000 | bytes 65536 | tf_op jit(solution)/shard_map/pallas_call | solution.py:327
  29.9 0.4 collective-permute-start
  30.2 1.5 %collective-permute-start.3 = (f32[96,128]{1,0:T(8,128)S(1)}, f32[96,128]{1,0:T(8,128)S(1)}, u32[]{:S(2)}, u32[]{:S(2)}) collective-permute-start(f32[96,128]{1,0:T(8,128)S(1)} %get-tuple-element.18), channel_id=1, source_target_pairs={{0,3},{1,2},{2,1},{3,0},{4,7},{5,6},{6,5},{7,4},{8,11},{9,10},{10,... | collective-permute-start | bytes 147464 | tf_op jit(solution)/shard_map/ppermute | solution.py:341
  31.7 2.5 %collective-permute-start.2 = (f32[96,128]{1,0:T(8,128)S(1)}, f32[96,128]{1,0:T(8,128)S(1)}, u32[]{:S(2)}, u32[]{:S(2)}) collective-permute-start(f32[96,128]{1,0:T(8,128)S(1)} %get-tuple-element.18), channel_id=1, source_target_pairs={{0,2},{1,3},{2,0},{3,1},{4,6},{5,7},{6,4},{7,5},{8,10},{9,11},{10,... | collective-permute-start | bytes 147464 | tf_op jit(solution)/shard_map/ppermute | solution.py:341
  34.2 0.0 collective-permute-start.1
  34.3 0.2 collective-permute-done
  34.5 0.0 collective-permute-done.3
  34.5 1.7 %collective-permute-done.2 = f32[96,128]{1,0:T(8,128)S(1)} collective-permute-done((f32[96,128]{1,0:T(8,128)S(1)}, f32[96,128]{1,0:T(8,128)S(1)}, u32[]{:S(2)}, u32[]{:S(2)}) %collective-permute-start.2) | collective-permute-done | bytes 49184 | tf_op jit(solution)/shard_map/ppermute | solution.py:341
  36.3 1.2 %collective-permute-done.1 = f32[96,128]{1,0:T(8,128)S(1)} collective-permute-done((f32[96,128]{1,0:T(8,128)S(1)}, f32[96,128]{1,0:T(8,128)S(1)}, u32[]{:S(2)}, u32[]{:S(2)}) %collective-permute-start.1) | collective-permute-done | bytes 49184 | tf_op jit(solution)/shard_map/ppermute | solution.py:341
  37.5 1.3 %broadcast_in_dim.10 = bf16[4,1536,128]{2,1,0:T(8,128)(2,1)} broadcast(bf16[1536,128]{1,0:T(8,128)(2,1)S(1)} %pad_maximum_fusion), dimensions={1,2} | broadcast | bytes 1966080 | tf_op jit(solution)/shard_map/broadcast_in_dim | solution.py:409
  38.8 4.8 %all-to-all-start.1 = ((bf16[4,1536,128]{2,1,0:T(8,128)(2,1)}), bf16[4,1536,128]{2,1,0:T(8,128)(2,1)}, u32[]{:S(2)}, u32[]{:S(2)}) async-start(bf16[4,1536,128]{2,1,0:T(8,128)(2,1)} %broadcast_in_dim.10), calls=%async_computation.1 | async-start | bytes 3145728 | tf_op jit(solution)/shard_map/all_to_all | solution.py:413
  43.7 2.8 %collective-permute-start.6 = (f32[96,128]{1,0:T(8,128)S(1)}, f32[96,128]{1,0:T(8,128)S(1)}, u32[]{:S(2)}, u32[]{:S(2)}) collective-permute-start(f32[96,128]{1,0:T(8,128)S(1)} %add_add_fusion.1), channel_id=1, source_target_pairs={{0,48},{8,56},{16,32},{24,40},{32,16},{40,24},{48,0},{56,8},{64,11... | collective-permute-start | bytes 147464 | tf_op jit(solution)/shard_map/ppermute | solution.py:341
  46.5 0.3 collective-permute-start.5
  46.8 0.3 collective-permute-start.4
  47.2 0.8 collective-permute-done.6
  48.0 3.0 %collective-permute-done.5 = f32[96,128]{1,0:T(8,128)S(1)} collective-permute-done((f32[96,128]{1,0:T(8,128)S(1)}, f32[96,128]{1,0:T(8,128)S(1)}, u32[]{:S(2)}, u32[]{:S(2)}) %collective-permute-start.5) | collective-permute-done | bytes 49184 | tf_op jit(solution)/shard_map/ppermute | solution.py:341
  51.0 0.0 collective-permute-done.4
  51.0 4.4 %collective-permute-start.7 = (f32[96,128]{1,0:T(8,128)S(1)}, f32[96,128]{1,0:T(8,128)S(1)}, u32[]{:S(2)}, u32[]{:S(2)}) collective-permute-start(f32[96,128]{1,0:T(8,128)S(1)} %add_add_fusion), channel_id=1, source_target_pairs={{0,8},{8,0},{16,24},{24,16},{32,40},{40,32},{48,56},{56,48},{64,72... | collective-permute-start | bytes 147464 | tf_op jit(solution)/shard_map/ppermute | solution.py:341
  55.4 0.9 collective-permute-done.7
  56.3 3.3 %collective-permute-start.10 = (f32[96,128]{1,0:T(8,128)S(1)}, f32[96,128]{1,0:T(8,128)S(1)}, u32[]{:S(2)}, u32[]{:S(2)}) collective-permute-start(f32[96,128]{1,0:T(8,128)S(1)} %add.29.a_ref), channel_id=1, source_target_pairs={{0,68},{1,69},{2,70},{3,71},{4,64},{5,65},{6,66},{7,67},{8,76},{9,... | collective-permute-start | bytes 147464 | tf_op jit(solution)/shard_map/ppermute | solution.py:351
  59.6 0.1 collective-permute-start.9
  59.8 0.5 collective-permute-start.8
  60.3 1.1 collective-permute-done.10.d_ref
  61.3 2.7 %collective-permute-done.9.c_ref = f32[96,128]{1,0:T(8,128)S(1)} collective-permute-done((f32[96,128]{1,0:T(8,128)S(1)}, f32[96,128]{1,0:T(8,128)S(1)}, u32[]{:S(2)}, u32[]{:S(2)}) %collective-permute-start.9) | collective-permute-done | bytes 49184 | tf_op jit(solution)/shard_map/ppermute | solution.py:351
  64.1 0.0 collective-permute-done.8.b_ref
  64.1 4.8 %shard_map.97 = (f32[64,64]{1,0:T(8,128)}, f32[64,64]{1,0:T(8,128)S(1)}, f32[64,64]{1,0:T(8,128)S(1)}, f32[64,64]{1,0:T(8,128)S(1)}) custom-call(f32[96,128]{1,0:T(8,128)S(1)} %add.29.a_ref, f32[96,128]{1,0:T(8,128)S(1)} %collective-permute-done.8.b_ref, f32[96,128]{1,0:T(8,128)S(1)} %collective-permute-done.9.c_ref, f32[96,128]{1,0:T(8,128)S(1)} %collective-permute-done.10.d_ref), custom_call_target="tpu_custom_call" | custom-call | flops 5000000000 | bytes 65536 | tf_op jit(solution)/shard_map/pallas_call | solution.py:327
  68.9 4.7 %shard_map.98 = (f32[8,64,512]{2,1,0:T(8,128)S(1)}, bf16[8,64,512]{2,1,0:T(8,128)(2,1)S(1)}, f32[32,128]{1,0:T(8,128)S(1)}, f32[4,64]{1,0:T(4,128)}) custom-call(s32[2]{0:T(128)S(1)} %pad_add_fusion.1.at_ref.place_ref, s32[1,5,1,32]{3,2,1,0:T(1,128)S(1)} %fusion.meta_hbm.meta_ref, bf16[8,768,128]{2,1,0:T(8,128)(2,1)} %bitcast.7.got_ref, ...), custom_call_target="tpu_custom_call" | custom-call | flops 5000000000 | bytes 65536 | tf_op jit(solution)/shard_map/pallas_call | solution.py:327
  73.6 1.9 %collective-permute-start.11 = (bf16[8,64,512]{2,1,0:T(8,128)(2,1)S(1)}, bf16[8,64,512]{2,1,0:T(8,128)(2,1)S(1)}, u32[]{:S(2)}, u32[]{:S(2)}) collective-permute-start(bf16[8,64,512]{2,1,0:T(8,128)(2,1)S(1)} %get-tuple-element.26), channel_id=1, source_target_pairs={{0,8},{8,0},{16,24},{24,16},{32,40},{40,32},{48,56},{56,48},{64,72... | collective-permute-start | bytes 1572872 | tf_op jit(solution)/shard_map/ppermute | solution.py:341
  75.5 0.1 collective-permute-start.12
  75.6 1.5 %collective-permute-done.12.gram_b = f32[32,128]{1,0:T(8,128)S(1)} collective-permute-done((f32[32,128]{1,0:T(8,128)S(1)}, f32[32,128]{1,0:T(8,128)S(1)}, u32[]{:S(2)}, u32[]{:S(2)}) %collective-permute-start.12) | collective-permute-done | bytes 16416 | tf_op jit(solution)/shard_map/ppermute | solution.py:341
  77.0 0.1 shard_map.99
  77.1 17.1 %all_to_all.20.got_ref = bf16[8,5,64,128]{3,2,1,0:T(8,128)(2,1)S(1)} all-to-all(bf16[8,5,64,128]{3,2,1,0:T(8,128)(2,1)S(1)} %shard_map.99), channel_id=1, replica_groups={{0,16,32,48,64,80,96,112},{8,24,40,56,72,88,104,120},{1,17,33,49,65,81,..., dimensions={0} | all-to-all | bytes 1310720 | tf_op jit(solution)/shard_map/all_to_all | solution.py:435
  94.2 2.4 %shard_map.100 = bf16[8,64,512]{2,1,0:T(8,128)(2,1)S(1)} custom-call(bf16[8,5,64,128]{3,2,1,0:T(8,128)(2,1)S(1)} %all_to_all.20.got_ref, f32[64,64]{1,0:T(8,128)S(1)} %get-tuple-element.28.mgram_ref), custom_call_target="tpu_custom_call" | custom-call | flops 1000000000 | bytes 65536 | tf_op jit(solution)/shard_map/pallas_call | solution.py:327
  96.5 12.6 %all_to_all.21.from_ref = bf16[8,64,512]{2,1,0:T(8,128)(2,1)S(1)} all-to-all(bf16[8,64,512]{2,1,0:T(8,128)(2,1)S(1)} %shard_map.100), channel_id=1, replica_groups={{0,16,32,48,64,80,96,112},{8,24,40,56,72,88,104,120},{1,17,33,49,65,81,..., dimensions={0} | all-to-all | bytes 1048576 | tf_op jit(solution)/shard_map/all_to_all | solution.py:435
  109.2 2.3 %collective-permute-start.13 = (bf16[8,64,512]{2,1,0:T(8,128)(2,1)S(1)}, bf16[8,64,512]{2,1,0:T(8,128)(2,1)S(1)}, u32[]{:S(2)}, u32[]{:S(2)}) collective-permute-start(bf16[8,64,512]{2,1,0:T(8,128)(2,1)S(1)} %all_to_all.21.from_ref), channel_id=1, source_target_pairs={{0,8},{8,0},{16,24},{24,16},{32,40},{40,32},{48,56},{56,48},{64,72... | collective-permute-start | bytes 1572872 | tf_op jit(solution)/shard_map/ppermute | solution.py:341
  111.5 1.6 %shard_map.101.refs_0_ = f32[64,8192]{1,0:T(8,128)} custom-call(s32[2]{0:T(128)S(1)} %pad_add_fusion.1.at_ref.place_ref, bf16[8,64,512]{2,1,0:T(8,128)(2,1)S(1)} %all_to_all.21.from_ref), custom_call_target="tpu_custom_call" | custom-call | flops 1000000000 | bytes 65536 | tf_op jit(solution)/shard_map/pallas_call | solution.py:327
  113.1 0.0 collective-permute-done.13.from_ref
  113.1 1.6 %shard_map.102 = f32[64,8192]{1,0:T(8,128)} custom-call(s32[2]{0:T(128)S(1)} %pad_add_fusion.1.at_ref.place_ref, bf16[8,64,512]{2,1,0:T(8,128)(2,1)S(1)} %collective-permute-done.13.from_ref, f32[64,8192]{1,0:T(8,128)} %shard_map.101.refs_0_), custom_call_target="tpu_custom_call", output_to_operand_aliasing={{}: (2, {})} | custom-call | flops 1000000000 | bytes 65536 | tf_op jit(solution)/shard_map/pallas_call | solution.py:327
  (13 shorter events, 0.1 us)
Async XLA Ops:
  5.4 6.9 %copy-start = (f32[64,8192]{1,0:T(8,128)S(1)}, f32[64,8192]{1,0:T(8,128)}, u32[]{:S(2)}) copy-start(f32[64,8192]{1,0:T(8,128)} %code_ref.1) | copy-start | bytes 6291460
  6.6 19.2 %all-to-all-start = ((f16[8,512,128]{2,1,0:T(8,128)(2,1)}), f16[8,512,128]{2,1,0:T(8,128)(2,1)S(1)}, u32[]{:S(2)}, u32[]{:S(2)}) async-start(f16[8,512,128]{2,1,0:T(8,128)(2,1)} %bitcast.5), calls=%async_computation | async-start | bytes 2097152 | tf_op jit(solution)/shard_map/all_to_all | solution.py:395
  12.3 13.8 %copy-start.2 = (f32[64,64]{1,0:T(8,128)S(1)}, f32[64,64]{1,0:T(8,128)}, u32[]{:S(2)}) copy-start(f32[64,64]{1,0:T(8,128)} %mix_ref.1) | copy-start | bytes 49156
  12.3 13.8 %copy-start.3 = (f32[32,64]{1,0:T(8,128)S(1)}, f32[32,64]{1,0:T(8,128)}, u32[]{:S(2)}) copy-start(f32[32,64]{1,0:T(8,128)} %weight_ref.1) | copy-start | bytes 24580
  29.9 4.6 %collective-permute-start = (bf16[768,128]{1,0:T(8,128)(2,1)S(1)}, bf16[768,128]{1,0:T(8,128)(2,1)S(1)}, u32[]{:S(2)}, u32[]{:S(2)}) collective-permute-start(bf16[768,128]{1,0:T(8,128)(2,1)S(1)} %get-tuple-element.17), channel_id=1, source_target_pairs={{0,4},{1,5},{2,6},{3,7},{4,0},{5,1},{6,2},{7,3},{8,12},{9,13},{10,... | collective-permute-start | bytes 589832 | tf_op jit(solution)/shard_map/ppermute | solution.py:341
  30.2 4.3 %collective-permute-start.3 = (f32[96,128]{1,0:T(8,128)S(1)}, f32[96,128]{1,0:T(8,128)S(1)}, u32[]{:S(2)}, u32[]{:S(2)}) collective-permute-start(f32[96,128]{1,0:T(8,128)S(1)} %get-tuple-element.18), channel_id=1, source_target_pairs={{0,3},{1,2},{2,1},{3,0},{4,7},{5,6},{6,5},{7,4},{8,11},{9,10},{10,... | collective-permute-start | bytes 147464 | tf_op jit(solution)/shard_map/ppermute | solution.py:341
  31.7 4.5 %collective-permute-start.2 = (f32[96,128]{1,0:T(8,128)S(1)}, f32[96,128]{1,0:T(8,128)S(1)}, u32[]{:S(2)}, u32[]{:S(2)}) collective-permute-start(f32[96,128]{1,0:T(8,128)S(1)} %get-tuple-element.18), channel_id=1, source_target_pairs={{0,2},{1,3},{2,0},{3,1},{4,6},{5,7},{6,4},{7,5},{8,10},{9,11},{10,... | collective-permute-start | bytes 147464 | tf_op jit(solution)/shard_map/ppermute | solution.py:341
  34.2 3.2 %collective-permute-start.1 = (f32[96,128]{1,0:T(8,128)S(1)}, f32[96,128]{1,0:T(8,128)S(1)}, u32[]{:S(2)}, u32[]{:S(2)}) collective-permute-start(f32[96,128]{1,0:T(8,128)S(1)} %get-tuple-element.18), channel_id=1, source_target_pairs={{0,1},{1,0},{2,3},{3,2},{4,5},{5,4},{6,7},{7,6},{8,9},{9,8},{10,11... | collective-permute-start | bytes 147464 | tf_op jit(solution)/shard_map/ppermute | solution.py:341
  38.8 30.1 %all-to-all-start.1 = ((bf16[4,1536,128]{2,1,0:T(8,128)(2,1)}), bf16[4,1536,128]{2,1,0:T(8,128)(2,1)}, u32[]{:S(2)}, u32[]{:S(2)}) async-start(bf16[4,1536,128]{2,1,0:T(8,128)(2,1)} %broadcast_in_dim.10), calls=%async_computation.1 | async-start | bytes 3145728 | tf_op jit(solution)/shard_map/all_to_all | solution.py:413
  43.7 4.3 %collective-permute-start.6 = (f32[96,128]{1,0:T(8,128)S(1)}, f32[96,128]{1,0:T(8,128)S(1)}, u32[]{:S(2)}, u32[]{:S(2)}) collective-permute-start(f32[96,128]{1,0:T(8,128)S(1)} %add_add_fusion.1), channel_id=1, source_target_pairs={{0,48},{8,56},{16,32},{24,40},{32,16},{40,24},{48,0},{56,8},{64,11... | collective-permute-start | bytes 147464 | tf_op jit(solution)/shard_map/ppermute | solution.py:341
  46.5 4.5 %collective-permute-start.5 = (f32[96,128]{1,0:T(8,128)S(1)}, f32[96,128]{1,0:T(8,128)S(1)}, u32[]{:S(2)}, u32[]{:S(2)}) collective-permute-start(f32[96,128]{1,0:T(8,128)S(1)} %add_add_fusion.1), channel_id=1, source_target_pairs={{0,32},{8,40},{16,48},{24,56},{32,0},{40,8},{48,16},{56,24},{64,96... | collective-permute-start | bytes 147464 | tf_op jit(solution)/shard_map/ppermute | solution.py:341
  46.8 4.1 %collective-permute-start.4 = (f32[96,128]{1,0:T(8,128)S(1)}, f32[96,128]{1,0:T(8,128)S(1)}, u32[]{:S(2)}, u32[]{:S(2)}) collective-permute-start(f32[96,128]{1,0:T(8,128)S(1)} %add_add_fusion.1), channel_id=1, source_target_pairs={{0,16},{8,24},{16,0},{24,8},{32,48},{40,56},{48,32},{56,40},{64,80... | collective-permute-start | bytes 147464 | tf_op jit(solution)/shard_map/ppermute | solution.py:341
  51.0 5.3 %collective-permute-start.7 = (f32[96,128]{1,0:T(8,128)S(1)}, f32[96,128]{1,0:T(8,128)S(1)}, u32[]{:S(2)}, u32[]{:S(2)}) collective-permute-start(f32[96,128]{1,0:T(8,128)S(1)} %add_add_fusion), channel_id=1, source_target_pairs={{0,8},{8,0},{16,24},{24,16},{32,40},{40,32},{48,56},{56,48},{64,72... | collective-permute-start | bytes 147464 | tf_op jit(solution)/shard_map/ppermute | solution.py:341
  56.3 12.6 %copy-start.1 = (bf16[1,1,16,128,512]{4,3,2,1,0:T(8,128)(2,1)S(1)}, bf16[1,1,16,128,512]{4,3,2,1,0:T(8,128)(2,1)}, u32[]{:S(2)}) copy-start(bf16[1,1,16,128,512]{4,3,2,1,0:T(8,128)(2,1)} %tile_hbm.1) | copy-start | bytes 6291460
  56.3 5.1 %collective-permute-start.10 = (f32[96,128]{1,0:T(8,128)S(1)}, f32[96,128]{1,0:T(8,128)S(1)}, u32[]{:S(2)}, u32[]{:S(2)}) collective-permute-start(f32[96,128]{1,0:T(8,128)S(1)} %add.29.a_ref), channel_id=1, source_target_pairs={{0,68},{1,69},{2,70},{3,71},{4,64},{5,65},{6,66},{7,67},{8,76},{9,... | collective-permute-start | bytes 147464 | tf_op jit(solution)/shard_map/ppermute | solution.py:351
  59.6 4.4 %collective-permute-start.9 = (f32[96,128]{1,0:T(8,128)S(1)}, f32[96,128]{1,0:T(8,128)S(1)}, u32[]{:S(2)}, u32[]{:S(2)}) collective-permute-start(f32[96,128]{1,0:T(8,128)S(1)} %add.29.a_ref), channel_id=1, source_target_pairs={{0,64},{1,65},{2,66},{3,67},{4,68},{5,69},{6,70},{7,71},{8,72},{9,... | collective-permute-start | bytes 147464 | tf_op jit(solution)/shard_map/ppermute | solution.py:351
  59.8 4.3 %collective-permute-start.8 = (f32[96,128]{1,0:T(8,128)S(1)}, f32[96,128]{1,0:T(8,128)S(1)}, u32[]{:S(2)}, u32[]{:S(2)}) collective-permute-start(f32[96,128]{1,0:T(8,128)S(1)} %add.29.a_ref), channel_id=1, source_target_pairs={{0,4},{1,5},{2,6},{3,7},{4,0},{5,1},{6,2},{7,3},{8,12},{9,13},{10,... | collective-permute-start | bytes 147464 | tf_op jit(solution)/shard_map/ppermute | solution.py:351
  73.6 3.5 %collective-permute-start.11 = (bf16[8,64,512]{2,1,0:T(8,128)(2,1)S(1)}, bf16[8,64,512]{2,1,0:T(8,128)(2,1)S(1)}, u32[]{:S(2)}, u32[]{:S(2)}) collective-permute-start(bf16[8,64,512]{2,1,0:T(8,128)(2,1)S(1)} %get-tuple-element.26), channel_id=1, source_target_pairs={{0,8},{8,0},{16,24},{24,16},{32,40},{40,32},{48,56},{56,48},{64,72... | collective-permute-start | bytes 1572872 | tf_op jit(solution)/shard_map/ppermute | solution.py:341
  75.5 1.6 %collective-permute-start.12 = (f32[32,128]{1,0:T(8,128)S(1)}, f32[32,128]{1,0:T(8,128)S(1)}, u32[]{:S(2)}, u32[]{:S(2)}) collective-permute-start(f32[32,128]{1,0:T(8,128)S(1)} %get-tuple-element.27.gram_a), channel_id=1, source_target_pairs={{0,8},{8,0},{16,24},{24,16},{32,40},{40,32},{48,56},{56,48},{64,72... | collective-permute-start | bytes 49160 | tf_op jit(solution)/shard_map/ppermute | solution.py:341
  109.2 3.9 %collective-permute-start.13 = (bf16[8,64,512]{2,1,0:T(8,128)(2,1)S(1)}, bf16[8,64,512]{2,1,0:T(8,128)(2,1)S(1)}, u32[]{:S(2)}, u32[]{:S(2)}) collective-permute-start(bf16[8,64,512]{2,1,0:T(8,128)(2,1)S(1)} %all_to_all.21.from_ref), channel_id=1, source_target_pairs={{0,8},{8,0},{16,24},{24,16},{32,40},{40,32},{48,56},{56,48},{64,72... | collective-permute-start | bytes 1572872 | tf_op jit(solution)/shard_map/ppermute | solution.py:341

commit v13 on v11

--- a/solution.py
+++ b/solution.py
@@ -200,8 +200,8 @@
         pieces.append(jnp.concatenate(split(projected), axis=1))
     low = rank // 2
     weight = weight_ref[...]
-    sums_ref[:low, :] = halves(numer)
-    sums_ref[low:rank, :] = halves(mm(weight, weight, TN)) * scales[0]
+    sums_ref[:low, :] = halves(mm(weight, weight, TN)) * scales[0]
+    sums_ref[low:rank, :] = halves(numer)
     sums_ref[rank:, :] = gram_ref[...] * scales[1]
     for i, piece in enumerate(pieces):
         out_ref[i * rank : (i + 1) * rank, :] = piece
@@ -216,8 +216,8 @@
     sums = (a_ref[...] + b_ref[...]) + (c_ref[...] + d_ref[...])
     rank = mix_ref.shape[0]
     low = rank // 2
-    weight_gram, code_gram = whole(sums[low:rank]), whole(sums[rank:])
-    mix = mm(whole(sums[:low]), damped_inverse(code_gram * weight_gram))
+    weight_gram, code_gram = whole(sums[:low]), whole(sums[rank:])
+    mix = mm(whole(sums[low:rank]), damped_inverse(code_gram * weight_gram))
     again_ref[...] = mix
     mix_ref[...] = mix
     mix_gram = mm(mix, mix, TN)
@@ -388,7 +388,7 @@
     gram = call(gram_kernel, shape((rank // 2, 2 * rank), F32), [VM], (code_factor_t,))
     products = jnp.sum(got.astype(F32), axis=0).reshape(own * VBLOCKS, rank, rows)
 
-    scales = (1.0 / n_code, 1.0 / n_pat)
+    scales = (0.5, 0.5)
     length = (own * VBLOCKS + own) * rank
     sums, message = call(
         functools.partial(polar_kernel, scales),
@@ -397,15 +397,19 @@
     )
     quarter = n_code // 2
     other = swap(message, "code", quarter)
+    low = rank // 2
+    weight_gram, sums = sums[:low], sums[low:]
     parts = [swap(sums, "code", bit) for bit in (1, 2, 3)]
     message = jnp.broadcast_to(jnp.concatenate([message, other])[None], (quarter, 2 * length, rows))
     message, *parts = lax.optimization_barrier((message, *parts))
     sums = plus(sums, parts)
+    code_gram, sums = sums[low:], jnp.concatenate([weight_gram, sums[:low]])
     layers = [[z * quarter + i for i in range(quarter)] for z in (0, 1)]
     shared = lax.all_to_all(message, "code", 0, 0, axis_index_groups=layers, tiled=True)
     shared = shared.reshape(n_code, length, rows)
     sums = plus(sums, [swap(sums, "pat", bit) for bit in (2, 4, 6)])
     sums = sums + swap(sums, "pat", 1)
+    sums = jnp.concatenate([sums, code_gram])
     mix_new, mix_again, mix_gram, inverse = call(
         mix_kernel, (square,) * 4, [VM] * 4,
         (sums, *(swap_z(sums, high, low) for high, low in ((0, 1), (1, 0), (1, 1)))), flops=5e9,

time: 115 us -> 115 us (level)
  no operation moved by 1% of the time
where the time goes in v13:
time: 115 us; the launch traced here: 114 us
  starting transfers between devices  31.3 us (27%)
  blocking collectives  29.7 us (26%)
  waiting for transfers between devices  25 us (22%)
  Pallas kernels  22.7 us (20%)
  other arithmetic  2.26 us (2%)
  between operations  1.58 us (1%)
  local copies, waits for them, and re-layouts  1.45 us (1%)
    all_to_all x2, blocking collectives, exchange(): return lax.all_to_all(x, 'pat', 0, 0, axis_index_groups=groups, tiled=True)  29.7 us
    pallas_call x9, Pallas kernels, call(): pl.pallas_call(kernel, out_shape=outs, in_specs=specs, out_specs=(spec,)...  22.7 us
    ppermute x11, starting transfers between devices, swap(): return lax.ppermute(x, axis, [(i, i ^ bit) for i in range(size)])  16.9 us
    all_to_all x1, waiting for transfers between devices, body(): got = lax.all_to_all(sent, 'code', 0, 0, tiled=True)  12.7 us
    ppermute x11, waiting for transfers between devices, swap(): return lax.ppermute(x, axis, [(i, i ^ bit) for i in range(size)])  8.54 us
    all_to_all x1, starting transfers between devices, body(): got = lax.all_to_all(sent, 'code', 0, 0, tiled=True)  5.62 us
    all_to_all x1, starting transfers between devices, body(): lax.all_to_all(message, 'code', 0, 0, axis_index_groups=layers, tiled=True)  4.8 us
    ppermute x3, starting transfers between devices, swap_z(): return lax.ppermute(x, ('pat', 'code'), pairs)  4.01 us
  transfers between devices with their start and end apart: 16, of which 10 were waited for; matrix products, arithmetic and copies ran while one was open for 0% of the time, Pallas kernels for 6%

profile of v13, /device:TPU:3, one launch (start us, length us, event | category | flops | bytes accessed | tf_op | source)
XLA Modules:
  0.0 114.0 jit_solution(18379661702582441691)
XLA Ops:
  1.3 0.1 pad.12.clone
  1.4 0.8 fusion.meta_hbm.meta_ref
  2.1 2.9 %shard_map.94 = f32[64,64,128]{2,1,0:T(8,128)S(1)} custom-call(s32[1,5,1,32]{3,2,1,0:T(1,128)S(1)} %fusion.meta_hbm.meta_ref, bf16[1,1,16,128,512]{4,3,2,1,0:T(8,128)(2,1)} %tile_hbm.1, f32[64,8192]{1,0:T(8,128)} %code_ref.1), custom_call_target="tpu_custom_call" | custom-call | flops 1000000000 | bytes 65536 | tf_op jit(solution)/shard_map/pallas_call | solution.py:319
  5.0 0.0 copy-start
  5.1 1.2 %convert_element_type.6 = f16[64,64,128]{2,1,0:T(8,128)(2,1)} convert(f32[64,64,128]{2,1,0:T(8,128)S(1)} %shard_map.94) | non-fusion elementwise | flops 524288 | bytes 3145728 | tf_op jit(solution)/shard_map/convert_element_type | solution.py:386
  6.3 5.6 %all-to-all-start = ((f16[8,512,128]{2,1,0:T(8,128)(2,1)}), f16[8,512,128]{2,1,0:T(8,128)(2,1)S(1)}, u32[]{:S(2)}, u32[]{:S(2)}) async-start(f16[8,512,128]{2,1,0:T(8,128)(2,1)} %bitcast.5), calls=%async_computation | async-start | bytes 2097152 | tf_op jit(solution)/shard_map/all_to_all | solution.py:387
  11.9 0.8 shard_map.95.gram_ref
  12.7 0.1 pad_add_fusion.1.at_ref.place_ref
  12.8 12.7 %all-to-all-done = f16[8,512,128]{2,1,0:T(8,128)(2,1)S(1)} async-done(((f16[8,512,128]{2,1,0:T(8,128)(2,1)}), f16[8,512,128]{2,1,0:T(8,128)(2,1)S(1)}, u32[]{:S(2)}, u32[]{:S(2)}) %all-to-all-start) | async-done | bytes 1048608 | tf_op jit(solution)/shard_map/all_to_all | solution.py:387
  25.5 0.1 convert_reduce_fusion
  25.7 3.8 %shard_map.96 = (f32[96,128]{1,0:T(8,128)S(1)}, bf16[768,128]{1,0:T(8,128)(2,1)S(1)}) custom-call(s32[2]{0:T(128)S(1)} %pad_add_fusion.1.at_ref.place_ref, f32[8,64,128]{2,1,0:T(8,128)S(1)} %bitcast.13, f32[64,64]{1,0:T(8,128)S(1)} %copy-done.2, f32[32,64]{1,0:T(8,128)S(1)} %copy-done.3, f32[32,128]{1,0:T(8,128)S(1)} %shard_map.95.gram_ref), custom_call_target="tpu_custom_call" | custom-call | flops 5000000000 | bytes 65536 | tf_op jit(solution)/shard_map/pallas_call | solution.py:319
  29.5 0.4 collective-permute-start
  29.9 1.5 %collective-permute-start.3 = (f32[64,128]{1,0:T(8,128)S(1)}, f32[64,128]{1,0:T(8,128)S(1)}, u32[]{:S(2)}, u32[]{:S(2)}) collective-permute-start(f32[64,128]{1,0:T(8,128)S(1)} %slice.12), channel_id=1, source_target_pairs={{0,3},{1,2},{2,1},{3,0},{4,7},{5,6},{6,5},{7,4},{8,11},{9,10},{10,... | collective-permute-start | bytes 98312 | tf_op jit(solution)/shard_map/ppermute | solution.py:333
  31.4 2.5 %collective-permute-start.2 = (f32[64,128]{1,0:T(8,128)S(1)}, f32[64,128]{1,0:T(8,128)S(1)}, u32[]{:S(2)}, u32[]{:S(2)}) collective-permute-start(f32[64,128]{1,0:T(8,128)S(1)} %slice.12), channel_id=1, source_target_pairs={{0,2},{1,3},{2,0},{3,1},{4,6},{5,7},{6,4},{7,5},{8,10},{9,11},{10,... | collective-permute-start | bytes 98312 | tf_op jit(solution)/shard_map/ppermute | solution.py:333
  33.9 0.0 collective-permute-start.1
  33.9 0.2 collective-permute-done
  34.2 0.0 collective-permute-done.3
  34.2 1.6 %collective-permute-done.2 = f32[64,128]{1,0:T(8,128)S(1)} collective-permute-done((f32[64,128]{1,0:T(8,128)S(1)}, f32[64,128]{1,0:T(8,128)S(1)}, u32[]{:S(2)}, u32[]{:S(2)}) %collective-permute-start.2) | collective-permute-done | bytes 32800 | tf_op jit(solution)/shard_map/ppermute | solution.py:333
  35.7 1.2 %collective-permute-done.1 = f32[64,128]{1,0:T(8,128)S(1)} collective-permute-done((f32[64,128]{1,0:T(8,128)S(1)}, f32[64,128]{1,0:T(8,128)S(1)}, u32[]{:S(2)}, u32[]{:S(2)}) %collective-permute-start.1) | collective-permute-done | bytes 32800 | tf_op jit(solution)/shard_map/ppermute | solution.py:333
  37.0 1.3 %broadcast_in_dim.10 = bf16[4,1536,128]{2,1,0:T(8,128)(2,1)} broadcast(bf16[1536,128]{1,0:T(8,128)(2,1)S(1)} %pad_maximum_fusion), dimensions={1,2} | broadcast | bytes 1966080 | tf_op jit(solution)/shard_map/broadcast_in_dim | solution.py:403
  38.3 4.8 %all-to-all-start.1 = ((bf16[4,1536,128]{2,1,0:T(8,128)(2,1)}), bf16[4,1536,128]{2,1,0:T(8,128)(2,1)}, u32[]{:S(2)}, u32[]{:S(2)}) async-start(bf16[4,1536,128]{2,1,0:T(8,128)(2,1)} %broadcast_in_dim.10), calls=%async_computation.1 | async-start | bytes 3145728 | tf_op jit(solution)/shard_map/all_to_all | solution.py:408
  43.1 3.0 %collective-permute-start.5 = (f32[64,128]{1,0:T(8,128)S(1)}, f32[64,128]{1,0:T(8,128)S(1)}, u32[]{:S(2)}, u32[]{:S(2)}) collective-permute-start(f32[64,128]{1,0:T(8,128)S(1)} %pad_maximum_fusion.2), channel_id=1, source_target_pairs={{0,32},{8,40},{16,48},{24,56},{32,0},{40,8},{48,16},{56,24},{64,96... | collective-permute-start | bytes 98312 | tf_op jit(solution)/shard_map/ppermute | solution.py:333
  46.1 0.8 collective-permute-start.6
  46.9 0.0 collective-permute-start.4
  46.9 0.6 collective-permute-done.5
  47.5 2.6 %collective-permute-done.6 = f32[64,128]{1,0:T(8,128)S(1)} collective-permute-done((f32[64,128]{1,0:T(8,128)S(1)}, f32[64,128]{1,0:T(8,128)S(1)}, u32[]{:S(2)}, u32[]{:S(2)}) %collective-permute-start.6) | collective-permute-done | bytes 32800 | tf_op jit(solution)/shard_map/ppermute | solution.py:333
  50.1 0.0 collective-permute-done.4
  50.1 4.5 %collective-permute-start.7 = (f32[64,128]{1,0:T(8,128)S(1)}, f32[64,128]{1,0:T(8,128)S(1)}, u32[]{:S(2)}, u32[]{:S(2)}) collective-permute-start(f32[64,128]{1,0:T(8,128)S(1)} %add_add_fusion), channel_id=1, source_target_pairs={{0,8},{8,0},{16,24},{24,16},{32,40},{40,32},{48,56},{56,48},{64,72... | collective-permute-start | bytes 98312 | tf_op jit(solution)/shard_map/ppermute | solution.py:333
  54.6 0.9 collective-permute-done.7
  55.4 0.0 copy-start.1
  55.5 3.3 %collective-permute-start.10 = (f32[96,128]{1,0:T(8,128)S(1)}, f32[96,128]{1,0:T(8,128)S(1)}, u32[]{:S(2)}, u32[]{:S(2)}) collective-permute-start(f32[96,128]{1,0:T(8,128)S(1)} %pad_maximum_fusion.1.a_ref), channel_id=1, source_target_pairs={{0,68},{1,69},{2,70},{3,71},{4,64},{5,65},{6,66},{7,67},{8,76},{9,... | collective-permute-start | bytes 147464 | tf_op jit(solution)/shard_map/ppermute | solution.py:343
  58.8 0.1 collective-permute-start.9
  58.9 0.5 collective-permute-start.8
  59.5 1.1 collective-permute-done.10.d_ref
  60.5 2.7 %collective-permute-done.9.c_ref = f32[96,128]{1,0:T(8,128)S(1)} collective-permute-done((f32[96,128]{1,0:T(8,128)S(1)}, f32[96,128]{1,0:T(8,128)S(1)}, u32[]{:S(2)}, u32[]{:S(2)}) %collective-permute-start.9) | collective-permute-done | bytes 49184 | tf_op jit(solution)/shard_map/ppermute | solution.py:343
  63.2 4.8 %shard_map.97 = (f32[64,64]{1,0:T(8,128)}, f32[64,64]{1,0:T(8,128)S(1)}, f32[64,64]{1,0:T(8,128)S(1)}, f32[64,64]{1,0:T(8,128)S(1)}) custom-call(f32[96,128]{1,0:T(8,128)S(1)} %pad_maximum_fusion.1.a_ref, f32[96,128]{1,0:T(8,128)S(1)} %collective-permute-done.8.b_ref, f32[96,128]{1,0:T(8,128)S(1)} %collective-permute-done.9.c_ref, ...), custom_call_target="tpu_custom_call" | custom-call | flops 5000000000 | bytes 65536 | tf_op jit(solution)/shard_map/pallas_call | solution.py:319
  68.1 4.7 %shard_map.98 = (f32[8,64,512]{2,1,0:T(8,128)S(1)}, bf16[8,64,512]{2,1,0:T(8,128)(2,1)S(1)}, f32[32,128]{1,0:T(8,128)S(1)}, f32[4,64]{1,0:T(4,128)}) custom-call(s32[2]{0:T(128)S(1)} %pad_add_fusion.1.at_ref.place_ref, s32[1,5,1,32]{3,2,1,0:T(1,128)S(1)} %fusion.meta_hbm.meta_ref, bf16[8,768,128]{2,1,0:T(8,128)(2,1)} %bitcast.7.got_ref, ...), custom_call_target="tpu_custom_call" | custom-call | flops 5000000000 | bytes 65536 | tf_op jit(solution)/shard_map/pallas_call | solution.py:319
  72.8 1.9 %collective-permute-start.11 = (bf16[8,64,512]{2,1,0:T(8,128)(2,1)S(1)}, bf16[8,64,512]{2,1,0:T(8,128)(2,1)S(1)}, u32[]{:S(2)}, u32[]{:S(2)}) collective-permute-start(bf16[8,64,512]{2,1,0:T(8,128)(2,1)S(1)} %get-tuple-element.26), channel_id=1, source_target_pairs={{0,8},{8,0},{16,24},{24,16},{32,40},{40,32},{48,56},{56,48},{64,72... | collective-permute-start | bytes 1572872 | tf_op jit(solution)/shard_map/ppermute | solution.py:333
  74.7 0.1 collective-permute-start.12
  74.7 1.5 %collective-permute-done.12.gram_b = f32[32,128]{1,0:T(8,128)S(1)} collective-permute-done((f32[32,128]{1,0:T(8,128)S(1)}, f32[32,128]{1,0:T(8,128)S(1)}, u32[]{:S(2)}, u32[]{:S(2)}) %collective-permute-start.12) | collective-permute-done | bytes 16416 | tf_op jit(solution)/shard_map/ppermute | solution.py:333
  76.2 0.0 collective-permute-done.11.came_ref
  76.2 0.1 shard_map.99
  76.3 17.0 %all_to_all.20.got_ref = bf16[8,5,64,128]{3,2,1,0:T(8,128)(2,1)S(1)} all-to-all(bf16[8,5,64,128]{3,2,1,0:T(8,128)(2,1)S(1)} %shard_map.99), channel_id=1, replica_groups={{0,16,32,48,64,80,96,112},{8,24,40,56,72,88,104,120},{1,17,33,49,65,81,..., dimensions={0} | all-to-all | bytes 1310720 | tf_op jit(solution)/shard_map/all_to_all | solution.py:431
  93.4 2.4 %shard_map.100 = bf16[8,64,512]{2,1,0:T(8,128)(2,1)S(1)} custom-call(bf16[8,5,64,128]{3,2,1,0:T(8,128)(2,1)S(1)} %all_to_all.20.got_ref, f32[64,64]{1,0:T(8,128)S(1)} %get-tuple-element.28.mgram_ref), custom_call_target="tpu_custom_call" | custom-call | flops 1000000000 | bytes 65536 | tf_op jit(solution)/shard_map/pallas_call | solution.py:319
  95.7 12.6 %all_to_all.21.from_ref = bf16[8,64,512]{2,1,0:T(8,128)(2,1)S(1)} all-to-all(bf16[8,64,512]{2,1,0:T(8,128)(2,1)S(1)} %shard_map.100), channel_id=1, replica_groups={{0,16,32,48,64,80,96,112},{8,24,40,56,72,88,104,120},{1,17,33,49,65,81,..., dimensions={0} | all-to-all | bytes 1048576 | tf_op jit(solution)/shard_map/all_to_all | solution.py:431
  108.4 2.3 %collective-permute-start.13 = (bf16[8,64,512]{2,1,0:T(8,128)(2,1)S(1)}, bf16[8,64,512]{2,1,0:T(8,128)(2,1)S(1)}, u32[]{:S(2)}, u32[]{:S(2)}) collective-permute-start(bf16[8,64,512]{2,1,0:T(8,128)(2,1)S(1)} %all_to_all.21.from_ref), channel_id=1, source_target_pairs={{0,8},{8,0},{16,24},{24,16},{32,40},{40,32},{48,56},{56,48},{64,72... | collective-permute-start | bytes 1572872 | tf_op jit(solution)/shard_map/ppermute | solution.py:333
  110.7 1.6 %shard_map.101.refs_0_ = f32[64,8192]{1,0:T(8,128)} custom-call(s32[2]{0:T(128)S(1)} %pad_add_fusion.1.at_ref.place_ref, bf16[8,64,512]{2,1,0:T(8,128)(2,1)S(1)} %all_to_all.21.from_ref), custom_call_target="tpu_custom_call" | custom-call | flops 1000000000 | bytes 65536 | tf_op jit(solution)/shard_map/pallas_call | solution.py:319
  112.3 1.6 %shard_map.102 = f32[64,8192]{1,0:T(8,128)} custom-call(s32[2]{0:T(128)S(1)} %pad_add_fusion.1.at_ref.place_ref, bf16[8,64,512]{2,1,0:T(8,128)(2,1)S(1)} %collective-permute-done.13.from_ref, f32[64,8192]{1,0:T(8,128)} %shard_map.101.refs_0_), custom_call_target="tpu_custom_call", output_to_operand_aliasing={{}: (2, {})} | custom-call | flops 1000000000 | bytes 65536 | tf_op jit(solution)/shard_map/pallas_call | solution.py:319
  (18 shorter events, 0.1 us)
Async XLA Ops:
  5.0 6.9 %copy-start = (f32[64,8192]{1,0:T(8,128)S(1)}, f32[64,8192]{1,0:T(8,128)}, u32[]{:S(2)}) copy-start(f32[64,8192]{1,0:T(8,128)} %code_ref.1) | copy-start | bytes 6291460
  6.3 19.2 %all-to-all-start = ((f16[8,512,128]{2,1,0:T(8,128)(2,1)}), f16[8,512,128]{2,1,0:T(8,128)(2,1)S(1)}, u32[]{:S(2)}, u32[]{:S(2)}) async-start(f16[8,512,128]{2,1,0:T(8,128)(2,1)} %bitcast.5), calls=%async_computation | async-start | bytes 2097152 | tf_op jit(solution)/shard_map/all_to_all | solution.py:387
  11.9 13.8 %copy-start.2 = (f32[64,64]{1,0:T(8,128)S(1)}, f32[64,64]{1,0:T(8,128)}, u32[]{:S(2)}) copy-start(f32[64,64]{1,0:T(8,128)} %mix_ref.1) | copy-start | bytes 49156
  11.9 13.8 %copy-start.3 = (f32[32,64]{1,0:T(8,128)S(1)}, f32[32,64]{1,0:T(8,128)}, u32[]{:S(2)}) copy-start(f32[32,64]{1,0:T(8,128)} %weight_ref.1) | copy-start | bytes 24580
  29.5 4.6 %collective-permute-start = (bf16[768,128]{1,0:T(8,128)(2,1)S(1)}, bf16[768,128]{1,0:T(8,128)(2,1)S(1)}, u32[]{:S(2)}, u32[]{:S(2)}) collective-permute-start(bf16[768,128]{1,0:T(8,128)(2,1)S(1)} %get-tuple-element.17), channel_id=1, source_target_pairs={{0,4},{1,5},{2,6},{3,7},{4,0},{5,1},{6,2},{7,3},{8,12},{9,13},{10,... | collective-permute-start | bytes 589832 | tf_op jit(solution)/shard_map/ppermute | solution.py:333
  29.9 4.3 %collective-permute-start.3 = (f32[64,128]{1,0:T(8,128)S(1)}, f32[64,128]{1,0:T(8,128)S(1)}, u32[]{:S(2)}, u32[]{:S(2)}) collective-permute-start(f32[64,128]{1,0:T(8,128)S(1)} %slice.12), channel_id=1, source_target_pairs={{0,3},{1,2},{2,1},{3,0},{4,7},{5,6},{6,5},{7,4},{8,11},{9,10},{10,... | collective-permute-start | bytes 98312 | tf_op jit(solution)/shard_map/ppermute | solution.py:333
  31.4 4.4 %collective-permute-start.2 = (f32[64,128]{1,0:T(8,128)S(1)}, f32[64,128]{1,0:T(8,128)S(1)}, u32[]{:S(2)}, u32[]{:S(2)}) collective-permute-start(f32[64,128]{1,0:T(8,128)S(1)} %slice.12), channel_id=1, source_target_pairs={{0,2},{1,3},{2,0},{3,1},{4,6},{5,7},{6,4},{7,5},{8,10},{9,11},{10,... | collective-permute-start | bytes 98312 | tf_op jit(solution)/shard_map/ppermute | solution.py:333
  33.9 3.1 %collective-permute-start.1 = (f32[64,128]{1,0:T(8,128)S(1)}, f32[64,128]{1,0:T(8,128)S(1)}, u32[]{:S(2)}, u32[]{:S(2)}) collective-permute-start(f32[64,128]{1,0:T(8,128)S(1)} %slice.12), channel_id=1, source_target_pairs={{0,1},{1,0},{2,3},{3,2},{4,5},{5,4},{6,7},{7,6},{8,9},{9,8},{10,11... | collective-permute-start | bytes 98312 | tf_op jit(solution)/shard_map/ppermute | solution.py:333
  38.3 29.8 %all-to-all-start.1 = ((bf16[4,1536,128]{2,1,0:T(8,128)(2,1)}), bf16[4,1536,128]{2,1,0:T(8,128)(2,1)}, u32[]{:S(2)}, u32[]{:S(2)}) async-start(bf16[4,1536,128]{2,1,0:T(8,128)(2,1)} %broadcast_in_dim.10), calls=%async_computation.1 | async-start | bytes 3145728 | tf_op jit(solution)/shard_map/all_to_all | solution.py:408
  43.1 4.3 %collective-permute-start.5 = (f32[64,128]{1,0:T(8,128)S(1)}, f32[64,128]{1,0:T(8,128)S(1)}, u32[]{:S(2)}, u32[]{:S(2)}) collective-permute-start(f32[64,128]{1,0:T(8,128)S(1)} %pad_maximum_fusion.2), channel_id=1, source_target_pairs={{0,32},{8,40},{16,48},{24,56},{32,0},{40,8},{48,16},{56,24},{64,96... | collective-permute-start | bytes 98312 | tf_op jit(solution)/shard_map/ppermute | solution.py:333
  46.1 4.0 %collective-permute-start.6 = (f32[64,128]{1,0:T(8,128)S(1)}, f32[64,128]{1,0:T(8,128)S(1)}, u32[]{:S(2)}, u32[]{:S(2)}) collective-permute-start(f32[64,128]{1,0:T(8,128)S(1)} %pad_maximum_fusion.2), channel_id=1, source_target_pairs={{0,48},{8,56},{16,32},{24,40},{32,16},{40,24},{48,0},{56,8},{64,11... | collective-permute-start | bytes 98312 | tf_op jit(solution)/shard_map/ppermute | solution.py:333
  46.9 3.2 %collective-permute-start.4 = (f32[64,128]{1,0:T(8,128)S(1)}, f32[64,128]{1,0:T(8,128)S(1)}, u32[]{:S(2)}, u32[]{:S(2)}) collective-permute-start(f32[64,128]{1,0:T(8,128)S(1)} %pad_maximum_fusion.2), channel_id=1, source_target_pairs={{0,16},{8,24},{16,0},{24,8},{32,48},{40,56},{48,32},{56,40},{64,80... | collective-permute-start | bytes 98312 | tf_op jit(solution)/shard_map/ppermute | solution.py:333
  50.1 5.3 %collective-permute-start.7 = (f32[64,128]{1,0:T(8,128)S(1)}, f32[64,128]{1,0:T(8,128)S(1)}, u32[]{:S(2)}, u32[]{:S(2)}) collective-permute-start(f32[64,128]{1,0:T(8,128)S(1)} %add_add_fusion), channel_id=1, source_target_pairs={{0,8},{8,0},{16,24},{24,16},{32,40},{40,32},{48,56},{56,48},{64,72... | collective-permute-start | bytes 98312 | tf_op jit(solution)/shard_map/ppermute | solution.py:333
  55.4 12.6 %copy-start.1 = (bf16[1,1,16,128,512]{4,3,2,1,0:T(8,128)(2,1)S(1)}, bf16[1,1,16,128,512]{4,3,2,1,0:T(8,128)(2,1)}, u32[]{:S(2)}) copy-start(bf16[1,1,16,128,512]{4,3,2,1,0:T(8,128)(2,1)} %tile_hbm.1) | copy-start | bytes 6291460
  55.5 5.1 %collective-permute-start.10 = (f32[96,128]{1,0:T(8,128)S(1)}, f32[96,128]{1,0:T(8,128)S(1)}, u32[]{:S(2)}, u32[]{:S(2)}) collective-permute-start(f32[96,128]{1,0:T(8,128)S(1)} %pad_maximum_fusion.1.a_ref), channel_id=1, source_target_pairs={{0,68},{1,69},{2,70},{3,71},{4,64},{5,65},{6,66},{7,67},{8,76},{9,... | collective-permute-start | bytes 147464 | tf_op jit(solution)/shard_map/ppermute | solution.py:343
  58.8 4.4 %collective-permute-start.9 = (f32[96,128]{1,0:T(8,128)S(1)}, f32[96,128]{1,0:T(8,128)S(1)}, u32[]{:S(2)}, u32[]{:S(2)}) collective-permute-start(f32[96,128]{1,0:T(8,128)S(1)} %pad_maximum_fusion.1.a_ref), channel_id=1, source_target_pairs={{0,64},{1,65},{2,66},{3,67},{4,68},{5,69},{6,70},{7,71},{8,72},{9,... | collective-permute-start | bytes 147464 | tf_op jit(solution)/shard_map/ppermute | solution.py:343
  58.9 4.3 %collective-permute-start.8 = (f32[96,128]{1,0:T(8,128)S(1)}, f32[96,128]{1,0:T(8,128)S(1)}, u32[]{:S(2)}, u32[]{:S(2)}) collective-permute-start(f32[96,128]{1,0:T(8,128)S(1)} %pad_maximum_fusion.1.a_ref), channel_id=1, source_target_pairs={{0,4},{1,5},{2,6},{3,7},{4,0},{5,1},{6,2},{7,3},{8,12},{9,13},{10,... | collective-permute-start | bytes 147464 | tf_op jit(solution)/shard_map/ppermute | solution.py:343
  72.8 3.5 %collective-permute-start.11 = (bf16[8,64,512]{2,1,0:T(8,128)(2,1)S(1)}, bf16[8,64,512]{2,1,0:T(8,128)(2,1)S(1)}, u32[]{:S(2)}, u32[]{:S(2)}) collective-permute-start(bf16[8,64,512]{2,1,0:T(8,128)(2,1)S(1)} %get-tuple-element.26), channel_id=1, source_target_pairs={{0,8},{8,0},{16,24},{24,16},{32,40},{40,32},{48,56},{56,48},{64,72... | collective-permute-start | bytes 1572872 | tf_op jit(solution)/shard_map/ppermute | solution.py:333
  74.7 1.6 %collective-permute-start.12 = (f32[32,128]{1,0:T(8,128)S(1)}, f32[32,128]{1,0:T(8,128)S(1)}, u32[]{:S(2)}, u32[]{:S(2)}) collective-permute-start(f32[32,128]{1,0:T(8,128)S(1)} %get-tuple-element.27.gram_a), channel_id=1, source_target_pairs={{0,8},{8,0},{16,24},{24,16},{32,40},{40,32},{48,56},{56,48},{64,72... | collective-permute-start | bytes 49160 | tf_op jit(solution)/shard_map/ppermute | solution.py:333
  108.4 3.9 %collective-permute-start.13 = (bf16[8,64,512]{2,1,0:T(8,128)(2,1)S(1)}, bf16[8,64,512]{2,1,0:T(8,128)(2,1)S(1)}, u32[]{:S(2)}, u32[]{:S(2)}) collective-permute-start(bf16[8,64,512]{2,1,0:T(8,128)(2,1)S(1)} %all_to_all.21.from_ref), channel_id=1, source_target_pairs={{0,8},{8,0},{16,24},{24,16},{32,40},{40,32},{48,56},{56,48},{64,72... | collective-permute-start | bytes 1572872 | tf_op jit(solution)/shard_map/ppermute | solution.py:333

commit v14 on v13

--- a/solution.py
+++ b/solution.py
@@ -229,6 +229,7 @@
     place_ref, meta_ref, got_ref, mix_ref, inverse_ref, tile_ref,
     keep_ref, send_ref, wgram_ref, own_ref, acc_ref, weight_ref,
 ):
+    acc_ref[...] = jnp.zeros(acc_ref.shape, F32)
     slots, rows, cols = tile_ref.shape
     sources = got_ref.shape[0]
     rank = mix_ref.shape[0]
@@ -254,7 +255,6 @@
     for j in range(own):
         own_ref[j : j + 1, :] = weight_ref[pl.ds(source(place_ref[0]) * own + j, 1), :]
     wgram_ref[...] = halves(mm(weight, weight, TN))
-    acc_ref[...] = jnp.zeros(acc_ref.shape, F32)
     lane = lax.broadcasted_iota(jnp.int32, (rank, rows), 1)
     for t in range(slots):
         k, b, g, kept = live_rows(t, meta_ref, rows)

time: 115 us -> 115 us (level)
  no operation moved by 1% of the time
where the time goes in v14:
time: 115 us; the launch traced here: 114 us
  starting transfers between devices  31.3 us (27%)
  blocking collectives  29.7 us (26%)
  waiting for transfers between devices  25 us (22%)
  Pallas kernels  22.7 us (20%)
  other arithmetic  2.26 us (2%)
  between operations  1.58 us (1%)
  local copies, waits for them, and re-layouts  1.45 us (1%)
    all_to_all x2, blocking collectives, exchange(): return lax.all_to_all(x, 'pat', 0, 0, axis_index_groups=groups, tiled=True)  29.7 us
    pallas_call x9, Pallas kernels, call(): pl.pallas_call(kernel, out_shape=outs, in_specs=specs, out_specs=(spec,)...  22.7 us
    ppermute x11, starting transfers between devices, swap(): return lax.ppermute(x, axis, [(i, i ^ bit) for i in range(size)])  16.9 us
    all_to_all x1, waiting for transfers between devices, body(): got = lax.all_to_all(sent, 'code', 0, 0, tiled=True)  12.7 us
    ppermute x11, waiting for transfers between devices, swap(): return lax.ppermute(x, axis, [(i, i ^ bit) for i in range(size)])  8.54 us
    all_to_all x1, starting transfers between devices, body(): got = lax.all_to_all(sent, 'code', 0, 0, tiled=True)  5.62 us
    all_to_all x1, starting transfers between devices, body(): lax.all_to_all(message, 'code', 0, 0, axis_index_groups=layers, tiled=True)  4.8 us
    ppermute x3, starting transfers between devices, swap_z(): return lax.ppermute(x, ('pat', 'code'), pairs)  4.01 us
  transfers between devices with their start and end apart: 16, of which 10 were waited for; matrix products, arithmetic and copies ran while one was open for 0% of the time, Pallas kernels for 6%

profile of v14, /device:TPU:3, one launch (start us, length us, event | category | flops | bytes accessed | tf_op | source)
XLA Modules:
  0.0 114.0 jit_solution(18379661702582441691)
XLA Ops:
  1.3 0.1 pad.12.clone
  1.4 0.8 fusion.meta_hbm.meta_ref
  2.1 2.9 %shard_map.94 = f32[64,64,128]{2,1,0:T(8,128)S(1)} custom-call(s32[1,5,1,32]{3,2,1,0:T(1,128)S(1)} %fusion.meta_hbm.meta_ref, bf16[1,1,16,128,512]{4,3,2,1,0:T(8,128)(2,1)} %tile_hbm.1, f32[64,8192]{1,0:T(8,128)} %code_ref.1), custom_call_target="tpu_custom_call" | custom-call | flops 1000000000 | bytes 65536 | tf_op jit(solution)/shard_map/pallas_call | solution.py:319
  5.0 0.0 copy-start
  5.1 1.2 %convert_element_type.6 = f16[64,64,128]{2,1,0:T(8,128)(2,1)} convert(f32[64,64,128]{2,1,0:T(8,128)S(1)} %shard_map.94) | non-fusion elementwise | flops 524288 | bytes 3145728 | tf_op jit(solution)/shard_map/convert_element_type | solution.py:386
  6.3 5.6 %all-to-all-start = ((f16[8,512,128]{2,1,0:T(8,128)(2,1)}), f16[8,512,128]{2,1,0:T(8,128)(2,1)S(1)}, u32[]{:S(2)}, u32[]{:S(2)}) async-start(f16[8,512,128]{2,1,0:T(8,128)(2,1)} %bitcast.5), calls=%async_computation | async-start | bytes 2097152 | tf_op jit(solution)/shard_map/all_to_all | solution.py:387
  11.9 0.8 shard_map.95.gram_ref
  12.7 0.1 pad_add_fusion.1.at_ref.place_ref
  12.8 12.7 %all-to-all-done = f16[8,512,128]{2,1,0:T(8,128)(2,1)S(1)} async-done(((f16[8,512,128]{2,1,0:T(8,128)(2,1)}), f16[8,512,128]{2,1,0:T(8,128)(2,1)S(1)}, u32[]{:S(2)}, u32[]{:S(2)}) %all-to-all-start) | async-done | bytes 1048608 | tf_op jit(solution)/shard_map/all_to_all | solution.py:387
  25.5 0.1 convert_reduce_fusion
  25.7 3.8 %shard_map.96 = (f32[96,128]{1,0:T(8,128)S(1)}, bf16[768,128]{1,0:T(8,128)(2,1)S(1)}) custom-call(s32[2]{0:T(128)S(1)} %pad_add_fusion.1.at_ref.place_ref, f32[8,64,128]{2,1,0:T(8,128)S(1)} %bitcast.13, f32[64,64]{1,0:T(8,128)S(1)} %copy-done.2, f32[32,64]{1,0:T(8,128)S(1)} %copy-done.3, f32[32,128]{1,0:T(8,128)S(1)} %shard_map.95.gram_ref), custom_call_target="tpu_custom_call" | custom-call | flops 5000000000 | bytes 65536 | tf_op jit(solution)/shard_map/pallas_call | solution.py:319
  29.5 0.4 collective-permute-start
  29.9 1.5 %collective-permute-start.3 = (f32[64,128]{1,0:T(8,128)S(1)}, f32[64,128]{1,0:T(8,128)S(1)}, u32[]{:S(2)}, u32[]{:S(2)}) collective-permute-start(f32[64,128]{1,0:T(8,128)S(1)} %slice.12), channel_id=1, source_target_pairs={{0,3},{1,2},{2,1},{3,0},{4,7},{5,6},{6,5},{7,4},{8,11},{9,10},{10,... | collective-permute-start | bytes 98312 | tf_op jit(solution)/shard_map/ppermute | solution.py:333
  31.4 2.5 %collective-permute-start.2 = (f32[64,128]{1,0:T(8,128)S(1)}, f32[64,128]{1,0:T(8,128)S(1)}, u32[]{:S(2)}, u32[]{:S(2)}) collective-permute-start(f32[64,128]{1,0:T(8,128)S(1)} %slice.12), channel_id=1, source_target_pairs={{0,2},{1,3},{2,0},{3,1},{4,6},{5,7},{6,4},{7,5},{8,10},{9,11},{10,... | collective-permute-start | bytes 98312 | tf_op jit(solution)/shard_map/ppermute | solution.py:333
  33.9 0.0 collective-permute-start.1
  33.9 0.2 collective-permute-done
  34.2 0.0 collective-permute-done.3
  34.2 1.6 %collective-permute-done.2 = f32[64,128]{1,0:T(8,128)S(1)} collective-permute-done((f32[64,128]{1,0:T(8,128)S(1)}, f32[64,128]{1,0:T(8,128)S(1)}, u32[]{:S(2)}, u32[]{:S(2)}) %collective-permute-start.2) | collective-permute-done | bytes 32800 | tf_op jit(solution)/shard_map/ppermute | solution.py:333
  35.7 1.2 %collective-permute-done.1 = f32[64,128]{1,0:T(8,128)S(1)} collective-permute-done((f32[64,128]{1,0:T(8,128)S(1)}, f32[64,128]{1,0:T(8,128)S(1)}, u32[]{:S(2)}, u32[]{:S(2)}) %collective-permute-start.1) | collective-permute-done | bytes 32800 | tf_op jit(solution)/shard_map/ppermute | solution.py:333
  37.0 1.3 %broadcast_in_dim.10 = bf16[4,1536,128]{2,1,0:T(8,128)(2,1)} broadcast(bf16[1536,128]{1,0:T(8,128)(2,1)S(1)} %pad_maximum_fusion), dimensions={1,2} | broadcast | bytes 1966080 | tf_op jit(solution)/shard_map/broadcast_in_dim | solution.py:403
  38.3 4.8 %all-to-all-start.1 = ((bf16[4,1536,128]{2,1,0:T(8,128)(2,1)}), bf16[4,1536,128]{2,1,0:T(8,128)(2,1)}, u32[]{:S(2)}, u32[]{:S(2)}) async-start(bf16[4,1536,128]{2,1,0:T(8,128)(2,1)} %broadcast_in_dim.10), calls=%async_computation.1 | async-start | bytes 3145728 | tf_op jit(solution)/shard_map/all_to_all | solution.py:408
  43.1 3.0 %collective-permute-start.5 = (f32[64,128]{1,0:T(8,128)S(1)}, f32[64,128]{1,0:T(8,128)S(1)}, u32[]{:S(2)}, u32[]{:S(2)}) collective-permute-start(f32[64,128]{1,0:T(8,128)S(1)} %pad_maximum_fusion.2), channel_id=1, source_target_pairs={{0,32},{8,40},{16,48},{24,56},{32,0},{40,8},{48,16},{56,24},{64,96... | collective-permute-start | bytes 98312 | tf_op jit(solution)/shard_map/ppermute | solution.py:333
  46.1 0.8 collective-permute-start.6
  46.9 0.0 collective-permute-start.4
  46.9 0.6 collective-permute-done.5
  47.5 2.6 %collective-permute-done.6 = f32[64,128]{1,0:T(8,128)S(1)} collective-permute-done((f32[64,128]{1,0:T(8,128)S(1)}, f32[64,128]{1,0:T(8,128)S(1)}, u32[]{:S(2)}, u32[]{:S(2)}) %collective-permute-start.6) | collective-permute-done | bytes 32800 | tf_op jit(solution)/shard_map/ppermute | solution.py:333
  50.1 0.0 collective-permute-done.4
  50.1 4.5 %collective-permute-start.7 = (f32[64,128]{1,0:T(8,128)S(1)}, f32[64,128]{1,0:T(8,128)S(1)}, u32[]{:S(2)}, u32[]{:S(2)}) collective-permute-start(f32[64,128]{1,0:T(8,128)S(1)} %add_add_fusion), channel_id=1, source_target_pairs={{0,8},{8,0},{16,24},{24,16},{32,40},{40,32},{48,56},{56,48},{64,72... | collective-permute-start | bytes 98312 | tf_op jit(solution)/shard_map/ppermute | solution.py:333
  54.6 0.9 collective-permute-done.7
  55.4 0.0 copy-start.1
  55.5 3.3 %collective-permute-start.10 = (f32[96,128]{1,0:T(8,128)S(1)}, f32[96,128]{1,0:T(8,128)S(1)}, u32[]{:S(2)}, u32[]{:S(2)}) collective-permute-start(f32[96,128]{1,0:T(8,128)S(1)} %pad_maximum_fusion.1.a_ref), channel_id=1, source_target_pairs={{0,68},{1,69},{2,70},{3,71},{4,64},{5,65},{6,66},{7,67},{8,76},{9,... | collective-permute-start | bytes 147464 | tf_op jit(solution)/shard_map/ppermute | solution.py:343
  58.8 0.1 collective-permute-start.9
  58.9 0.5 collective-permute-start.8
  59.5 1.1 collective-permute-done.10.d_ref
  60.5 2.7 %collective-permute-done.9.c_ref = f32[96,128]{1,0:T(8,128)S(1)} collective-permute-done((f32[96,128]{1,0:T(8,128)S(1)}, f32[96,128]{1,0:T(8,128)S(1)}, u32[]{:S(2)}, u32[]{:S(2)}) %collective-permute-start.9) | collective-permute-done | bytes 49184 | tf_op jit(solution)/shard_map/ppermute | solution.py:343
  63.2 4.8 %shard_map.97 = (f32[64,64]{1,0:T(8,128)}, f32[64,64]{1,0:T(8,128)S(1)}, f32[64,64]{1,0:T(8,128)S(1)}, f32[64,64]{1,0:T(8,128)S(1)}) custom-call(f32[96,128]{1,0:T(8,128)S(1)} %pad_maximum_fusion.1.a_ref, f32[96,128]{1,0:T(8,128)S(1)} %collective-permute-done.8.b_ref, f32[96,128]{1,0:T(8,128)S(1)} %collective-permute-done.9.c_ref, ...), custom_call_target="tpu_custom_call" | custom-call | flops 5000000000 | bytes 65536 | tf_op jit(solution)/shard_map/pallas_call | solution.py:319
  68.1 4.7 %shard_map.98 = (f32[8,64,512]{2,1,0:T(8,128)S(1)}, bf16[8,64,512]{2,1,0:T(8,128)(2,1)S(1)}, f32[32,128]{1,0:T(8,128)S(1)}, f32[4,64]{1,0:T(4,128)}) custom-call(s32[2]{0:T(128)S(1)} %pad_add_fusion.1.at_ref.place_ref, s32[1,5,1,32]{3,2,1,0:T(1,128)S(1)} %fusion.meta_hbm.meta_ref, bf16[8,768,128]{2,1,0:T(8,128)(2,1)} %bitcast.7.got_ref, ...), custom_call_target="tpu_custom_call" | custom-call | flops 5000000000 | bytes 65536 | tf_op jit(solution)/shard_map/pallas_call | solution.py:319
  72.8 1.9 %collective-permute-start.11 = (bf16[8,64,512]{2,1,0:T(8,128)(2,1)S(1)}, bf16[8,64,512]{2,1,0:T(8,128)(2,1)S(1)}, u32[]{:S(2)}, u32[]{:S(2)}) collective-permute-start(bf16[8,64,512]{2,1,0:T(8,128)(2,1)S(1)} %get-tuple-element.26), channel_id=1, source_target_pairs={{0,8},{8,0},{16,24},{24,16},{32,40},{40,32},{48,56},{56,48},{64,72... | collective-permute-start | bytes 1572872 | tf_op jit(solution)/shard_map/ppermute | solution.py:333
  74.7 0.1 collective-permute-start.12
  74.7 1.5 %collective-permute-done.12.gram_b = f32[32,128]{1,0:T(8,128)S(1)} collective-permute-done((f32[32,128]{1,0:T(8,128)S(1)}, f32[32,128]{1,0:T(8,128)S(1)}, u32[]{:S(2)}, u32[]{:S(2)}) %collective-permute-start.12) | collective-permute-done | bytes 16416 | tf_op jit(solution)/shard_map/ppermute | solution.py:333
  76.2 0.0 collective-permute-done.11.came_ref
  76.2 0.1 shard_map.99
  76.3 17.0 %all_to_all.20.got_ref = bf16[8,5,64,128]{3,2,1,0:T(8,128)(2,1)S(1)} all-to-all(bf16[8,5,64,128]{3,2,1,0:T(8,128)(2,1)S(1)} %shard_map.99), channel_id=1, replica_groups={{0,16,32,48,64,80,96,112},{8,24,40,56,72,88,104,120},{1,17,33,49,65,81,..., dimensions={0} | all-to-all | bytes 1310720 | tf_op jit(solution)/shard_map/all_to_all | solution.py:431
  93.4 2.4 %shard_map.100 = bf16[8,64,512]{2,1,0:T(8,128)(2,1)S(1)} custom-call(bf16[8,5,64,128]{3,2,1,0:T(8,128)(2,1)S(1)} %all_to_all.20.got_ref, f32[64,64]{1,0:T(8,128)S(1)} %get-tuple-element.28.mgram_ref), custom_call_target="tpu_custom_call" | custom-call | flops 1000000000 | bytes 65536 | tf_op jit(solution)/shard_map/pallas_call | solution.py:319
  95.7 12.6 %all_to_all.21.from_ref = bf16[8,64,512]{2,1,0:T(8,128)(2,1)S(1)} all-to-all(bf16[8,64,512]{2,1,0:T(8,128)(2,1)S(1)} %shard_map.100), channel_id=1, replica_groups={{0,16,32,48,64,80,96,112},{8,24,40,56,72,88,104,120},{1,17,33,49,65,81,..., dimensions={0} | all-to-all | bytes 1048576 | tf_op jit(solution)/shard_map/all_to_all | solution.py:431
  108.4 2.3 %collective-permute-start.13 = (bf16[8,64,512]{2,1,0:T(8,128)(2,1)S(1)}, bf16[8,64,512]{2,1,0:T(8,128)(2,1)S(1)}, u32[]{:S(2)}, u32[]{:S(2)}) collective-permute-start(bf16[8,64,512]{2,1,0:T(8,128)(2,1)S(1)} %all_to_all.21.from_ref), channel_id=1, source_target_pairs={{0,8},{8,0},{16,24},{24,16},{32,40},{40,32},{48,56},{56,48},{64,72... | collective-permute-start | bytes 1572872 | tf_op jit(solution)/shard_map/ppermute | solution.py:333
  110.7 1.6 %shard_map.101.refs_0_ = f32[64,8192]{1,0:T(8,128)} custom-call(s32[2]{0:T(128)S(1)} %pad_add_fusion.1.at_ref.place_ref, bf16[8,64,512]{2,1,0:T(8,128)(2,1)S(1)} %all_to_all.21.from_ref), custom_call_target="tpu_custom_call" | custom-call | flops 1000000000 | bytes 65536 | tf_op jit(solution)/shard_map/pallas_call | solution.py:319
  112.3 1.6 %shard_map.102 = f32[64,8192]{1,0:T(8,128)} custom-call(s32[2]{0:T(128)S(1)} %pad_add_fusion.1.at_ref.place_ref, bf16[8,64,512]{2,1,0:T(8,128)(2,1)S(1)} %collective-permute-done.13.from_ref, f32[64,8192]{1,0:T(8,128)} %shard_map.101.refs_0_), custom_call_target="tpu_custom_call", output_to_operand_aliasing={{}: (2, {})} | custom-call | flops 1000000000 | bytes 65536 | tf_op jit(solution)/shard_map/pallas_call | solution.py:319
  (18 shorter events, 0.1 us)
Async XLA Ops:
  5.0 6.9 %copy-start = (f32[64,8192]{1,0:T(8,128)S(1)}, f32[64,8192]{1,0:T(8,128)}, u32[]{:S(2)}) copy-start(f32[64,8192]{1,0:T(8,128)} %code_ref.1) | copy-start | bytes 6291460
  6.3 19.2 %all-to-all-start = ((f16[8,512,128]{2,1,0:T(8,128)(2,1)}), f16[8,512,128]{2,1,0:T(8,128)(2,1)S(1)}, u32[]{:S(2)}, u32[]{:S(2)}) async-start(f16[8,512,128]{2,1,0:T(8,128)(2,1)} %bitcast.5), calls=%async_computation | async-start | bytes 2097152 | tf_op jit(solution)/shard_map/all_to_all | solution.py:387
  11.9 13.8 %copy-start.2 = (f32[64,64]{1,0:T(8,128)S(1)}, f32[64,64]{1,0:T(8,128)}, u32[]{:S(2)}) copy-start(f32[64,64]{1,0:T(8,128)} %mix_ref.1) | copy-start | bytes 49156
  11.9 13.8 %copy-start.3 = (f32[32,64]{1,0:T(8,128)S(1)}, f32[32,64]{1,0:T(8,128)}, u32[]{:S(2)}) copy-start(f32[32,64]{1,0:T(8,128)} %weight_ref.1) | copy-start | bytes 24580
  29.5 4.6 %collective-permute-start = (bf16[768,128]{1,0:T(8,128)(2,1)S(1)}, bf16[768,128]{1,0:T(8,128)(2,1)S(1)}, u32[]{:S(2)}, u32[]{:S(2)}) collective-permute-start(bf16[768,128]{1,0:T(8,128)(2,1)S(1)} %get-tuple-element.17), channel_id=1, source_target_pairs={{0,4},{1,5},{2,6},{3,7},{4,0},{5,1},{6,2},{7,3},{8,12},{9,13},{10,... | collective-permute-start | bytes 589832 | tf_op jit(solution)/shard_map/ppermute | solution.py:333
  29.9 4.3 %collective-permute-start.3 = (f32[64,128]{1,0:T(8,128)S(1)}, f32[64,128]{1,0:T(8,128)S(1)}, u32[]{:S(2)}, u32[]{:S(2)}) collective-permute-start(f32[64,128]{1,0:T(8,128)S(1)} %slice.12), channel_id=1, source_target_pairs={{0,3},{1,2},{2,1},{3,0},{4,7},{5,6},{6,5},{7,4},{8,11},{9,10},{10,... | collective-permute-start | bytes 98312 | tf_op jit(solution)/shard_map/ppermute | solution.py:333
  31.4 4.4 %collective-permute-start.2 = (f32[64,128]{1,0:T(8,128)S(1)}, f32[64,128]{1,0:T(8,128)S(1)}, u32[]{:S(2)}, u32[]{:S(2)}) collective-permute-start(f32[64,128]{1,0:T(8,128)S(1)} %slice.12), channel_id=1, source_target_pairs={{0,2},{1,3},{2,0},{3,1},{4,6},{5,7},{6,4},{7,5},{8,10},{9,11},{10,... | collective-permute-start | bytes 98312 | tf_op jit(solution)/shard_map/ppermute | solution.py:333
  33.9 3.1 %collective-permute-start.1 = (f32[64,128]{1,0:T(8,128)S(1)}, f32[64,128]{1,0:T(8,128)S(1)}, u32[]{:S(2)}, u32[]{:S(2)}) collective-permute-start(f32[64,128]{1,0:T(8,128)S(1)} %slice.12), channel_id=1, source_target_pairs={{0,1},{1,0},{2,3},{3,2},{4,5},{5,4},{6,7},{7,6},{8,9},{9,8},{10,11... | collective-permute-start | bytes 98312 | tf_op jit(solution)/shard_map/ppermute | solution.py:333
  38.3 29.8 %all-to-all-start.1 = ((bf16[4,1536,128]{2,1,0:T(8,128)(2,1)}), bf16[4,1536,128]{2,1,0:T(8,128)(2,1)}, u32[]{:S(2)}, u32[]{:S(2)}) async-start(bf16[4,1536,128]{2,1,0:T(8,128)(2,1)} %broadcast_in_dim.10), calls=%async_computation.1 | async-start | bytes 3145728 | tf_op jit(solution)/shard_map/all_to_all | solution.py:408
  43.1 4.3 %collective-permute-start.5 = (f32[64,128]{1,0:T(8,128)S(1)}, f32[64,128]{1,0:T(8,128)S(1)}, u32[]{:S(2)}, u32[]{:S(2)}) collective-permute-start(f32[64,128]{1,0:T(8,128)S(1)} %pad_maximum_fusion.2), channel_id=1, source_target_pairs={{0,32},{8,40},{16,48},{24,56},{32,0},{40,8},{48,16},{56,24},{64,96... | collective-permute-start | bytes 98312 | tf_op jit(solution)/shard_map/ppermute | solution.py:333
  46.1 4.0 %collective-permute-start.6 = (f32[64,128]{1,0:T(8,128)S(1)}, f32[64,128]{1,0:T(8,128)S(1)}, u32[]{:S(2)}, u32[]{:S(2)}) collective-permute-start(f32[64,128]{1,0:T(8,128)S(1)} %pad_maximum_fusion.2), channel_id=1, source_target_pairs={{0,48},{8,56},{16,32},{24,40},{32,16},{40,24},{48,0},{56,8},{64,11... | collective-permute-start | bytes 98312 | tf_op jit(solution)/shard_map/ppermute | solution.py:333
  46.9 3.2 %collective-permute-start.4 = (f32[64,128]{1,0:T(8,128)S(1)}, f32[64,128]{1,0:T(8,128)S(1)}, u32[]{:S(2)}, u32[]{:S(2)}) collective-permute-start(f32[64,128]{1,0:T(8,128)S(1)} %pad_maximum_fusion.2), channel_id=1, source_target_pairs={{0,16},{8,24},{16,0},{24,8},{32,48},{40,56},{48,32},{56,40},{64,80... | collective-permute-start | bytes 98312 | tf_op jit(solution)/shard_map/ppermute | solution.py:333
  50.1 5.3 %collective-permute-start.7 = (f32[64,128]{1,0:T(8,128)S(1)}, f32[64,128]{1,0:T(8,128)S(1)}, u32[]{:S(2)}, u32[]{:S(2)}) collective-permute-start(f32[64,128]{1,0:T(8,128)S(1)} %add_add_fusion), channel_id=1, source_target_pairs={{0,8},{8,0},{16,24},{24,16},{32,40},{40,32},{48,56},{56,48},{64,72... | collective-permute-start | bytes 98312 | tf_op jit(solution)/shard_map/ppermute | solution.py:333
  55.4 12.6 %copy-start.1 = (bf16[1,1,16,128,512]{4,3,2,1,0:T(8,128)(2,1)S(1)}, bf16[1,1,16,128,512]{4,3,2,1,0:T(8,128)(2,1)}, u32[]{:S(2)}) copy-start(bf16[1,1,16,128,512]{4,3,2,1,0:T(8,128)(2,1)} %tile_hbm.1) | copy-start | bytes 6291460
  55.5 5.1 %collective-permute-start.10 = (f32[96,128]{1,0:T(8,128)S(1)}, f32[96,128]{1,0:T(8,128)S(1)}, u32[]{:S(2)}, u32[]{:S(2)}) collective-permute-start(f32[96,128]{1,0:T(8,128)S(1)} %pad_maximum_fusion.1.a_ref), channel_id=1, source_target_pairs={{0,68},{1,69},{2,70},{3,71},{4,64},{5,65},{6,66},{7,67},{8,76},{9,... | collective-permute-start | bytes 147464 | tf_op jit(solution)/shard_map/ppermute | solution.py:343
  58.8 4.4 %collective-permute-start.9 = (f32[96,128]{1,0:T(8,128)S(1)}, f32[96,128]{1,0:T(8,128)S(1)}, u32[]{:S(2)}, u32[]{:S(2)}) collective-permute-start(f32[96,128]{1,0:T(8,128)S(1)} %pad_maximum_fusion.1.a_ref), channel_id=1, source_target_pairs={{0,64},{1,65},{2,66},{3,67},{4,68},{5,69},{6,70},{7,71},{8,72},{9,... | collective-permute-start | bytes 147464 | tf_op jit(solution)/shard_map/ppermute | solution.py:343
  58.9 4.3 %collective-permute-start.8 = (f32[96,128]{1,0:T(8,128)S(1)}, f32[96,128]{1,0:T(8,128)S(1)}, u32[]{:S(2)}, u32[]{:S(2)}) collective-permute-start(f32[96,128]{1,0:T(8,128)S(1)} %pad_maximum_fusion.1.a_ref), channel_id=1, source_target_pairs={{0,4},{1,5},{2,6},{3,7},{4,0},{5,1},{6,2},{7,3},{8,12},{9,13},{10,... | collective-permute-start | bytes 147464 | tf_op jit(solution)/shard_map/ppermute | solution.py:343
  72.8 3.5 %collective-permute-start.11 = (bf16[8,64,512]{2,1,0:T(8,128)(2,1)S(1)}, bf16[8,64,512]{2,1,0:T(8,128)(2,1)S(1)}, u32[]{:S(2)}, u32[]{:S(2)}) collective-permute-start(bf16[8,64,512]{2,1,0:T(8,128)(2,1)S(1)} %get-tuple-element.26), channel_id=1, source_target_pairs={{0,8},{8,0},{16,24},{24,16},{32,40},{40,32},{48,56},{56,48},{64,72... | collective-permute-start | bytes 1572872 | tf_op jit(solution)/shard_map/ppermute | solution.py:333
  74.7 1.6 %collective-permute-start.12 = (f32[32,128]{1,0:T(8,128)S(1)}, f32[32,128]{1,0:T(8,128)S(1)}, u32[]{:S(2)}, u32[]{:S(2)}) collective-permute-start(f32[32,128]{1,0:T(8,128)S(1)} %get-tuple-element.27.gram_a), channel_id=1, source_target_pairs={{0,8},{8,0},{16,24},{24,16},{32,40},{40,32},{48,56},{56,48},{64,72... | collective-permute-start | bytes 49160 | tf_op jit(solution)/shard_map/ppermute | solution.py:333
  108.4 3.9 %collective-permute-start.13 = (bf16[8,64,512]{2,1,0:T(8,128)(2,1)S(1)}, bf16[8,64,512]{2,1,0:T(8,128)(2,1)S(1)}, u32[]{:S(2)}, u32[]{:S(2)}) collective-permute-start(bf16[8,64,512]{2,1,0:T(8,128)(2,1)S(1)} %all_to_all.21.from_ref), channel_id=1, source_target_pairs={{0,8},{8,0},{16,24},{24,16},{32,40},{40,32},{48,56},{56,48},{64,72... | collective-permute-start | bytes 1572872 | tf_op jit(solution)/shard_map/ppermute | solution.py:333

commit v15 on v14

--- a/solution.py
+++ b/solution.py
@@ -379,7 +379,7 @@
         [
             pltpu.SMEM(meta.shape, jnp.int32), pltpu.VMEM(tiles.shape, BF16),
             pltpu.VMEM(code_factor_t.shape, F32), pltpu.SemaphoreType.DMA(()),
-            pltpu.SemaphoreType.DMA((5,)),
+            pltpu.SemaphoreType.DMA((3,)),
         ],
         vmem=50,
     )

time: 115 us -> 115 us (level)
  no operation moved by 1% of the time
where the time goes in v15:
time: 115 us; the launch traced here: 114 us
  starting transfers between devices  31.3 us (27%)
  blocking collectives  29.7 us (26%)
  waiting for transfers between devices  25 us (22%)
  Pallas kernels  22.6 us (20%)
  other arithmetic  2.26 us (2%)
  between operations  1.58 us (1%)
  local copies, waits for them, and re-layouts  1.45 us (1%)
    all_to_all x2, blocking collectives, exchange(): return lax.all_to_all(x, 'pat', 0, 0, axis_index_groups=groups, tiled=True)  29.7 us
    pallas_call x9, Pallas kernels, call(): pl.pallas_call(kernel, out_shape=outs, in_specs=specs, out_specs=(spec,)...  22.6 us
    ppermute x11, starting transfers between devices, swap(): return lax.ppermute(x, axis, [(i, i ^ bit) for i in range(size)])  16.9 us
    all_to_all x1, waiting for transfers between devices, body(): got = lax.all_to_all(sent, 'code', 0, 0, tiled=True)  12.7 us
    ppermute x11, waiting for transfers between devices, swap(): return lax.ppermute(x, axis, [(i, i ^ bit) for i in range(size)])  8.54 us
    all_to_all x1, starting transfers between devices, body(): got = lax.all_to_all(sent, 'code', 0, 0, tiled=True)  5.63 us
    all_to_all x1, starting transfers between devices, body(): lax.all_to_all(message, 'code', 0, 0, axis_index_groups=layers, tiled=True)  4.81 us
    ppermute x3, starting transfers between devices, swap_z(): return lax.ppermute(x, ('pat', 'code'), pairs)  4.01 us
  transfers between devices with their start and end apart: 16, of which 10 were waited for; matrix products, arithmetic and copies ran while one was open for 0% of the time, Pallas kernels for 6%

profile of v15, /device:TPU:3, one launch (start us, length us, event | category | flops | bytes accessed | tf_op | source)
XLA Modules:
  0.0 113.9 jit_solution(11089679766369140109)
XLA Ops:
  1.3 0.1 pad.12.clone
  1.4 0.8 fusion.meta_hbm.meta_ref
  2.1 2.9 %shard_map.94 = f32[64,64,128]{2,1,0:T(8,128)S(1)} custom-call(s32[1,5,1,32]{3,2,1,0:T(1,128)S(1)} %fusion.meta_hbm.meta_ref, bf16[1,1,16,128,512]{4,3,2,1,0:T(8,128)(2,1)} %tile_hbm.1, f32[64,8192]{1,0:T(8,128)} %code_ref.1), custom_call_target="tpu_custom_call" | custom-call | flops 1000000000 | bytes 65536 | tf_op jit(solution)/shard_map/pallas_call | solution.py:319
  5.0 0.0 copy-start
  5.0 1.2 %convert_element_type.6 = f16[64,64,128]{2,1,0:T(8,128)(2,1)} convert(f32[64,64,128]{2,1,0:T(8,128)S(1)} %shard_map.94) | non-fusion elementwise | flops 524288 | bytes 3145728 | tf_op jit(solution)/shard_map/convert_element_type | solution.py:386
  6.2 5.6 %all-to-all-start = ((f16[8,512,128]{2,1,0:T(8,128)(2,1)}), f16[8,512,128]{2,1,0:T(8,128)(2,1)S(1)}, u32[]{:S(2)}, u32[]{:S(2)}) async-start(f16[8,512,128]{2,1,0:T(8,128)(2,1)} %bitcast.5), calls=%async_computation | async-start | bytes 2097152 | tf_op jit(solution)/shard_map/all_to_all | solution.py:387
  11.8 0.8 shard_map.95.gram_ref
  12.7 0.1 pad_add_fusion.1.at_ref.place_ref
  12.7 12.7 %all-to-all-done = f16[8,512,128]{2,1,0:T(8,128)(2,1)S(1)} async-done(((f16[8,512,128]{2,1,0:T(8,128)(2,1)}), f16[8,512,128]{2,1,0:T(8,128)(2,1)S(1)}, u32[]{:S(2)}, u32[]{:S(2)}) %all-to-all-start) | async-done | bytes 1048608 | tf_op jit(solution)/shard_map/all_to_all | solution.py:387
  25.4 0.1 convert_reduce_fusion
  25.6 3.8 %shard_map.96 = (f32[96,128]{1,0:T(8,128)S(1)}, bf16[768,128]{1,0:T(8,128)(2,1)S(1)}) custom-call(s32[2]{0:T(128)S(1)} %pad_add_fusion.1.at_ref.place_ref, f32[8,64,128]{2,1,0:T(8,128)S(1)} %bitcast.13, f32[64,64]{1,0:T(8,128)S(1)} %copy-done.2, f32[32,64]{1,0:T(8,128)S(1)} %copy-done.3, f32[32,128]{1,0:T(8,128)S(1)} %shard_map.95.gram_ref), custom_call_target="tpu_custom_call" | custom-call | flops 5000000000 | bytes 65536 | tf_op jit(solution)/shard_map/pallas_call | solution.py:319
  29.4 0.4 collective-permute-start
  29.8 1.5 %collective-permute-start.3 = (f32[64,128]{1,0:T(8,128)S(1)}, f32[64,128]{1,0:T(8,128)S(1)}, u32[]{:S(2)}, u32[]{:S(2)}) collective-permute-start(f32[64,128]{1,0:T(8,128)S(1)} %slice.12), channel_id=1, source_target_pairs={{0,3},{1,2},{2,1},{3,0},{4,7},{5,6},{6,5},{7,4},{8,11},{9,10},{10,... | collective-permute-start | bytes 98312 | tf_op jit(solution)/shard_map/ppermute | solution.py:333
  31.3 2.5 %collective-permute-start.2 = (f32[64,128]{1,0:T(8,128)S(1)}, f32[64,128]{1,0:T(8,128)S(1)}, u32[]{:S(2)}, u32[]{:S(2)}) collective-permute-start(f32[64,128]{1,0:T(8,128)S(1)} %slice.12), channel_id=1, source_target_pairs={{0,2},{1,3},{2,0},{3,1},{4,6},{5,7},{6,4},{7,5},{8,10},{9,11},{10,... | collective-permute-start | bytes 98312 | tf_op jit(solution)/shard_map/ppermute | solution.py:333
  33.8 0.0 collective-permute-start.1
  33.8 0.2 collective-permute-done
  34.1 1.6 %collective-permute-done.2 = f32[64,128]{1,0:T(8,128)S(1)} collective-permute-done((f32[64,128]{1,0:T(8,128)S(1)}, f32[64,128]{1,0:T(8,128)S(1)}, u32[]{:S(2)}, u32[]{:S(2)}) %collective-permute-start.2) | collective-permute-done | bytes 32800 | tf_op jit(solution)/shard_map/ppermute | solution.py:333
  35.7 1.2 %collective-permute-done.1 = f32[64,128]{1,0:T(8,128)S(1)} collective-permute-done((f32[64,128]{1,0:T(8,128)S(1)}, f32[64,128]{1,0:T(8,128)S(1)}, u32[]{:S(2)}, u32[]{:S(2)}) %collective-permute-start.1) | collective-permute-done | bytes 32800 | tf_op jit(solution)/shard_map/ppermute | solution.py:333
  36.9 1.3 %broadcast_in_dim.10 = bf16[4,1536,128]{2,1,0:T(8,128)(2,1)} broadcast(bf16[1536,128]{1,0:T(8,128)(2,1)S(1)} %pad_maximum_fusion), dimensions={1,2} | broadcast | bytes 1966080 | tf_op jit(solution)/shard_map/broadcast_in_dim | solution.py:403
  38.2 4.8 %all-to-all-start.1 = ((bf16[4,1536,128]{2,1,0:T(8,128)(2,1)}), bf16[4,1536,128]{2,1,0:T(8,128)(2,1)}, u32[]{:S(2)}, u32[]{:S(2)}) async-start(bf16[4,1536,128]{2,1,0:T(8,128)(2,1)} %broadcast_in_dim.10), calls=%async_computation.1 | async-start | bytes 3145728 | tf_op jit(solution)/shard_map/all_to_all | solution.py:408
  43.1 3.0 %collective-permute-start.5 = (f32[64,128]{1,0:T(8,128)S(1)}, f32[64,128]{1,0:T(8,128)S(1)}, u32[]{:S(2)}, u32[]{:S(2)}) collective-permute-start(f32[64,128]{1,0:T(8,128)S(1)} %pad_maximum_fusion.2), channel_id=1, source_target_pairs={{0,32},{8,40},{16,48},{24,56},{32,0},{40,8},{48,16},{56,24},{64,96... | collective-permute-start | bytes 98312 | tf_op jit(solution)/shard_map/ppermute | solution.py:333
  46.1 0.8 collective-permute-start.6
  46.8 0.0 collective-permute-start.4
  46.8 0.6 collective-permute-done.5
  47.4 2.6 %collective-permute-done.6 = f32[64,128]{1,0:T(8,128)S(1)} collective-permute-done((f32[64,128]{1,0:T(8,128)S(1)}, f32[64,128]{1,0:T(8,128)S(1)}, u32[]{:S(2)}, u32[]{:S(2)}) %collective-permute-start.6) | collective-permute-done | bytes 32800 | tf_op jit(solution)/shard_map/ppermute | solution.py:333
  50.0 4.4 %collective-permute-start.7 = (f32[64,128]{1,0:T(8,128)S(1)}, f32[64,128]{1,0:T(8,128)S(1)}, u32[]{:S(2)}, u32[]{:S(2)}) collective-permute-start(f32[64,128]{1,0:T(8,128)S(1)} %add_add_fusion), channel_id=1, source_target_pairs={{0,8},{8,0},{16,24},{24,16},{32,40},{40,32},{48,56},{56,48},{64,72... | collective-permute-start | bytes 98312 | tf_op jit(solution)/shard_map/ppermute | solution.py:333
  54.5 0.9 collective-permute-done.7
  55.4 0.0 copy-start.1
  55.4 3.3 %collective-permute-start.10 = (f32[96,128]{1,0:T(8,128)S(1)}, f32[96,128]{1,0:T(8,128)S(1)}, u32[]{:S(2)}, u32[]{:S(2)}) collective-permute-start(f32[96,128]{1,0:T(8,128)S(1)} %pad_maximum_fusion.1.a_ref), channel_id=1, source_target_pairs={{0,68},{1,69},{2,70},{3,71},{4,64},{5,65},{6,66},{7,67},{8,76},{9,... | collective-permute-start | bytes 147464 | tf_op jit(solution)/shard_map/ppermute | solution.py:343
  58.7 0.1 collective-permute-start.9
  58.9 0.5 collective-permute-start.8
  59.4 1.1 collective-permute-done.10.d_ref
  60.4 2.7 %collective-permute-done.9.c_ref = f32[96,128]{1,0:T(8,128)S(1)} collective-permute-done((f32[96,128]{1,0:T(8,128)S(1)}, f32[96,128]{1,0:T(8,128)S(1)}, u32[]{:S(2)}, u32[]{:S(2)}) %collective-permute-start.9) | collective-permute-done | bytes 49184 | tf_op jit(solution)/shard_map/ppermute | solution.py:343
  63.2 0.0 collective-permute-done.8.b_ref
  63.2 4.8 %shard_map.97 = (f32[64,64]{1,0:T(8,128)}, f32[64,64]{1,0:T(8,128)S(1)}, f32[64,64]{1,0:T(8,128)S(1)}, f32[64,64]{1,0:T(8,128)S(1)}) custom-call(f32[96,128]{1,0:T(8,128)S(1)} %pad_maximum_fusion.1.a_ref, f32[96,128]{1,0:T(8,128)S(1)} %collective-permute-done.8.b_ref, f32[96,128]{1,0:T(8,128)S(1)} %collective-permute-done.9.c_ref, ...), custom_call_target="tpu_custom_call" | custom-call | flops 5000000000 | bytes 65536 | tf_op jit(solution)/shard_map/pallas_call | solution.py:319
  68.0 0.0 all-to-all-done.1
  68.0 4.7 %shard_map.98 = (f32[8,64,512]{2,1,0:T(8,128)S(1)}, bf16[8,64,512]{2,1,0:T(8,128)(2,1)S(1)}, f32[32,128]{1,0:T(8,128)S(1)}, f32[4,64]{1,0:T(4,128)}) custom-call(s32[2]{0:T(128)S(1)} %pad_add_fusion.1.at_ref.place_ref, s32[1,5,1,32]{3,2,1,0:T(1,128)S(1)} %fusion.meta_hbm.meta_ref, bf16[8,768,128]{2,1,0:T(8,128)(2,1)} %bitcast.7.got_ref, ...), custom_call_target="tpu_custom_call" | custom-call | flops 5000000000 | bytes 65536 | tf_op jit(solution)/shard_map/pallas_call | solution.py:319
  72.7 1.9 %collective-permute-start.11 = (bf16[8,64,512]{2,1,0:T(8,128)(2,1)S(1)}, bf16[8,64,512]{2,1,0:T(8,128)(2,1)S(1)}, u32[]{:S(2)}, u32[]{:S(2)}) collective-permute-start(bf16[8,64,512]{2,1,0:T(8,128)(2,1)S(1)} %get-tuple-element.26), channel_id=1, source_target_pairs={{0,8},{8,0},{16,24},{24,16},{32,40},{40,32},{48,56},{56,48},{64,72... | collective-permute-start | bytes 1572872 | tf_op jit(solution)/shard_map/ppermute | solution.py:333
  74.6 0.1 collective-permute-start.12
  74.7 1.5 %collective-permute-done.12.gram_b = f32[32,128]{1,0:T(8,128)S(1)} collective-permute-done((f32[32,128]{1,0:T(8,128)S(1)}, f32[32,128]{1,0:T(8,128)S(1)}, u32[]{:S(2)}, u32[]{:S(2)}) %collective-permute-start.12) | collective-permute-done | bytes 16416 | tf_op jit(solution)/shard_map/ppermute | solution.py:333
  76.1 0.1 shard_map.99
  76.2 17.0 %all_to_all.20.got_ref = bf16[8,5,64,128]{3,2,1,0:T(8,128)(2,1)S(1)} all-to-all(bf16[8,5,64,128]{3,2,1,0:T(8,128)(2,1)S(1)} %shard_map.99), channel_id=1, replica_groups={{0,16,32,48,64,80,96,112},{8,24,40,56,72,88,104,120},{1,17,33,49,65,81,..., dimensions={0} | all-to-all | bytes 1310720 | tf_op jit(solution)/shard_map/all_to_all | solution.py:431
  93.3 2.4 %shard_map.100 = bf16[8,64,512]{2,1,0:T(8,128)(2,1)S(1)} custom-call(bf16[8,5,64,128]{3,2,1,0:T(8,128)(2,1)S(1)} %all_to_all.20.got_ref, f32[64,64]{1,0:T(8,128)S(1)} %get-tuple-element.28.mgram_ref), custom_call_target="tpu_custom_call" | custom-call | flops 1000000000 | bytes 65536 | tf_op jit(solution)/shard_map/pallas_call | solution.py:319
  95.6 12.6 %all_to_all.21.from_ref = bf16[8,64,512]{2,1,0:T(8,128)(2,1)S(1)} all-to-all(bf16[8,64,512]{2,1,0:T(8,128)(2,1)S(1)} %shard_map.100), channel_id=1, replica_groups={{0,16,32,48,64,80,96,112},{8,24,40,56,72,88,104,120},{1,17,33,49,65,81,..., dimensions={0} | all-to-all | bytes 1048576 | tf_op jit(solution)/shard_map/all_to_all | solution.py:431
  108.3 2.3 %collective-permute-start.13 = (bf16[8,64,512]{2,1,0:T(8,128)(2,1)S(1)}, bf16[8,64,512]{2,1,0:T(8,128)(2,1)S(1)}, u32[]{:S(2)}, u32[]{:S(2)}) collective-permute-start(bf16[8,64,512]{2,1,0:T(8,128)(2,1)S(1)} %all_to_all.21.from_ref), channel_id=1, source_target_pairs={{0,8},{8,0},{16,24},{24,16},{32,40},{40,32},{48,56},{56,48},{64,72... | collective-permute-start | bytes 1572872 | tf_op jit(solution)/shard_map/ppermute | solution.py:333
  110.6 1.6 %shard_map.101.refs_0_ = f32[64,8192]{1,0:T(8,128)} custom-call(s32[2]{0:T(128)S(1)} %pad_add_fusion.1.at_ref.place_ref, bf16[8,64,512]{2,1,0:T(8,128)(2,1)S(1)} %all_to_all.21.from_ref), custom_call_target="tpu_custom_call" | custom-call | flops 1000000000 | bytes 65536 | tf_op jit(solution)/shard_map/pallas_call | solution.py:319
  112.2 0.0 collective-permute-done.13.from_ref
  112.2 1.6 %shard_map.102 = f32[64,8192]{1,0:T(8,128)} custom-call(s32[2]{0:T(128)S(1)} %pad_add_fusion.1.at_ref.place_ref, bf16[8,64,512]{2,1,0:T(8,128)(2,1)S(1)} %collective-permute-done.13.from_ref, f32[64,8192]{1,0:T(8,128)} %shard_map.101.refs_0_), custom_call_target="tpu_custom_call", output_to_operand_aliasing={{}: (2, {})} | custom-call | flops 1000000000 | bytes 65536 | tf_op jit(solution)/shard_map/pallas_call | solution.py:319
  (18 shorter events, 0.1 us)
Async XLA Ops:
  5.0 6.9 %copy-start = (f32[64,8192]{1,0:T(8,128)S(1)}, f32[64,8192]{1,0:T(8,128)}, u32[]{:S(2)}) copy-start(f32[64,8192]{1,0:T(8,128)} %code_ref.1) | copy-start | bytes 6291460
  6.2 19.2 %all-to-all-start = ((f16[8,512,128]{2,1,0:T(8,128)(2,1)}), f16[8,512,128]{2,1,0:T(8,128)(2,1)S(1)}, u32[]{:S(2)}, u32[]{:S(2)}) async-start(f16[8,512,128]{2,1,0:T(8,128)(2,1)} %bitcast.5), calls=%async_computation | async-start | bytes 2097152 | tf_op jit(solution)/shard_map/all_to_all | solution.py:387
  11.8 13.8 %copy-start.2 = (f32[64,64]{1,0:T(8,128)S(1)}, f32[64,64]{1,0:T(8,128)}, u32[]{:S(2)}) copy-start(f32[64,64]{1,0:T(8,128)} %mix_ref.1) | copy-start | bytes 49156
  11.8 13.8 %copy-start.3 = (f32[32,64]{1,0:T(8,128)S(1)}, f32[32,64]{1,0:T(8,128)}, u32[]{:S(2)}) copy-start(f32[32,64]{1,0:T(8,128)} %weight_ref.1) | copy-start | bytes 24580
  29.4 4.6 %collective-permute-start = (bf16[768,128]{1,0:T(8,128)(2,1)S(1)}, bf16[768,128]{1,0:T(8,128)(2,1)S(1)}, u32[]{:S(2)}, u32[]{:S(2)}) collective-permute-start(bf16[768,128]{1,0:T(8,128)(2,1)S(1)} %get-tuple-element.17), channel_id=1, source_target_pairs={{0,4},{1,5},{2,6},{3,7},{4,0},{5,1},{6,2},{7,3},{8,12},{9,13},{10,... | collective-permute-start | bytes 589832 | tf_op jit(solution)/shard_map/ppermute | solution.py:333
  29.8 4.3 %collective-permute-start.3 = (f32[64,128]{1,0:T(8,128)S(1)}, f32[64,128]{1,0:T(8,128)S(1)}, u32[]{:S(2)}, u32[]{:S(2)}) collective-permute-start(f32[64,128]{1,0:T(8,128)S(1)} %slice.12), channel_id=1, source_target_pairs={{0,3},{1,2},{2,1},{3,0},{4,7},{5,6},{6,5},{7,4},{8,11},{9,10},{10,... | collective-permute-start | bytes 98312 | tf_op jit(solution)/shard_map/ppermute | solution.py:333
  31.3 4.4 %collective-permute-start.2 = (f32[64,128]{1,0:T(8,128)S(1)}, f32[64,128]{1,0:T(8,128)S(1)}, u32[]{:S(2)}, u32[]{:S(2)}) collective-permute-start(f32[64,128]{1,0:T(8,128)S(1)} %slice.12), channel_id=1, source_target_pairs={{0,2},{1,3},{2,0},{3,1},{4,6},{5,7},{6,4},{7,5},{8,10},{9,11},{10,... | collective-permute-start | bytes 98312 | tf_op jit(solution)/shard_map/ppermute | solution.py:333
  33.8 3.1 %collective-permute-start.1 = (f32[64,128]{1,0:T(8,128)S(1)}, f32[64,128]{1,0:T(8,128)S(1)}, u32[]{:S(2)}, u32[]{:S(2)}) collective-permute-start(f32[64,128]{1,0:T(8,128)S(1)} %slice.12), channel_id=1, source_target_pairs={{0,1},{1,0},{2,3},{3,2},{4,5},{5,4},{6,7},{7,6},{8,9},{9,8},{10,11... | collective-permute-start | bytes 98312 | tf_op jit(solution)/shard_map/ppermute | solution.py:333
  38.2 29.8 %all-to-all-start.1 = ((bf16[4,1536,128]{2,1,0:T(8,128)(2,1)}), bf16[4,1536,128]{2,1,0:T(8,128)(2,1)}, u32[]{:S(2)}, u32[]{:S(2)}) async-start(bf16[4,1536,128]{2,1,0:T(8,128)(2,1)} %broadcast_in_dim.10), calls=%async_computation.1 | async-start | bytes 3145728 | tf_op jit(solution)/shard_map/all_to_all | solution.py:408
  43.1 4.3 %collective-permute-start.5 = (f32[64,128]{1,0:T(8,128)S(1)}, f32[64,128]{1,0:T(8,128)S(1)}, u32[]{:S(2)}, u32[]{:S(2)}) collective-permute-start(f32[64,128]{1,0:T(8,128)S(1)} %pad_maximum_fusion.2), channel_id=1, source_target_pairs={{0,32},{8,40},{16,48},{24,56},{32,0},{40,8},{48,16},{56,24},{64,96... | collective-permute-start | bytes 98312 | tf_op jit(solution)/shard_map/ppermute | solution.py:333
  46.1 4.0 %collective-permute-start.6 = (f32[64,128]{1,0:T(8,128)S(1)}, f32[64,128]{1,0:T(8,128)S(1)}, u32[]{:S(2)}, u32[]{:S(2)}) collective-permute-start(f32[64,128]{1,0:T(8,128)S(1)} %pad_maximum_fusion.2), channel_id=1, source_target_pairs={{0,48},{8,56},{16,32},{24,40},{32,16},{40,24},{48,0},{56,8},{64,11... | collective-permute-start | bytes 98312 | tf_op jit(solution)/shard_map/ppermute | solution.py:333
  46.8 3.2 %collective-permute-start.4 = (f32[64,128]{1,0:T(8,128)S(1)}, f32[64,128]{1,0:T(8,128)S(1)}, u32[]{:S(2)}, u32[]{:S(2)}) collective-permute-start(f32[64,128]{1,0:T(8,128)S(1)} %pad_maximum_fusion.2), channel_id=1, source_target_pairs={{0,16},{8,24},{16,0},{24,8},{32,48},{40,56},{48,32},{56,40},{64,80... | collective-permute-start | bytes 98312 | tf_op jit(solution)/shard_map/ppermute | solution.py:333
  50.0 5.3 %collective-permute-start.7 = (f32[64,128]{1,0:T(8,128)S(1)}, f32[64,128]{1,0:T(8,128)S(1)}, u32[]{:S(2)}, u32[]{:S(2)}) collective-permute-start(f32[64,128]{1,0:T(8,128)S(1)} %add_add_fusion), channel_id=1, source_target_pairs={{0,8},{8,0},{16,24},{24,16},{32,40},{40,32},{48,56},{56,48},{64,72... | collective-permute-start | bytes 98312 | tf_op jit(solution)/shard_map/ppermute | solution.py:333
  55.4 12.6 %copy-start.1 = (bf16[1,1,16,128,512]{4,3,2,1,0:T(8,128)(2,1)S(1)}, bf16[1,1,16,128,512]{4,3,2,1,0:T(8,128)(2,1)}, u32[]{:S(2)}) copy-start(bf16[1,1,16,128,512]{4,3,2,1,0:T(8,128)(2,1)} %tile_hbm.1) | copy-start | bytes 6291460
  55.4 5.1 %collective-permute-start.10 = (f32[96,128]{1,0:T(8,128)S(1)}, f32[96,128]{1,0:T(8,128)S(1)}, u32[]{:S(2)}, u32[]{:S(2)}) collective-permute-start(f32[96,128]{1,0:T(8,128)S(1)} %pad_maximum_fusion.1.a_ref), channel_id=1, source_target_pairs={{0,68},{1,69},{2,70},{3,71},{4,64},{5,65},{6,66},{7,67},{8,76},{9,... | collective-permute-start | bytes 147464 | tf_op jit(solution)/shard_map/ppermute | solution.py:343
  58.7 4.4 %collective-permute-start.9 = (f32[96,128]{1,0:T(8,128)S(1)}, f32[96,128]{1,0:T(8,128)S(1)}, u32[]{:S(2)}, u32[]{:S(2)}) collective-permute-start(f32[96,128]{1,0:T(8,128)S(1)} %pad_maximum_fusion.1.a_ref), channel_id=1, source_target_pairs={{0,64},{1,65},{2,66},{3,67},{4,68},{5,69},{6,70},{7,71},{8,72},{9,... | collective-permute-start | bytes 147464 | tf_op jit(solution)/shard_map/ppermute | solution.py:343
  58.9 4.3 %collective-permute-start.8 = (f32[96,128]{1,0:T(8,128)S(1)}, f32[96,128]{1,0:T(8,128)S(1)}, u32[]{:S(2)}, u32[]{:S(2)}) collective-permute-start(f32[96,128]{1,0:T(8,128)S(1)} %pad_maximum_fusion.1.a_ref), channel_id=1, source_target_pairs={{0,4},{1,5},{2,6},{3,7},{4,0},{5,1},{6,2},{7,3},{8,12},{9,13},{10,... | collective-permute-start | bytes 147464 | tf_op jit(solution)/shard_map/ppermute | solution.py:343
  72.7 3.5 %collective-permute-start.11 = (bf16[8,64,512]{2,1,0:T(8,128)(2,1)S(1)}, bf16[8,64,512]{2,1,0:T(8,128)(2,1)S(1)}, u32[]{:S(2)}, u32[]{:S(2)}) collective-permute-start(bf16[8,64,512]{2,1,0:T(8,128)(2,1)S(1)} %get-tuple-element.26), channel_id=1, source_target_pairs={{0,8},{8,0},{16,24},{24,16},{32,40},{40,32},{48,56},{56,48},{64,72... | collective-permute-start | bytes 1572872 | tf_op jit(solution)/shard_map/ppermute | solution.py:333
  74.6 1.6 %collective-permute-start.12 = (f32[32,128]{1,0:T(8,128)S(1)}, f32[32,128]{1,0:T(8,128)S(1)}, u32[]{:S(2)}, u32[]{:S(2)}) collective-permute-start(f32[32,128]{1,0:T(8,128)S(1)} %get-tuple-element.27.gram_a), channel_id=1, source_target_pairs={{0,8},{8,0},{16,24},{24,16},{32,40},{40,32},{48,56},{56,48},{64,72... | collective-permute-start | bytes 49160 | tf_op jit(solution)/shard_map/ppermute | solution.py:333
  108.3 3.9 %collective-permute-start.13 = (bf16[8,64,512]{2,1,0:T(8,128)(2,1)S(1)}, bf16[8,64,512]{2,1,0:T(8,128)(2,1)S(1)}, u32[]{:S(2)}, u32[]{:S(2)}) collective-permute-start(bf16[8,64,512]{2,1,0:T(8,128)(2,1)S(1)} %all_to_all.21.from_ref), channel_id=1, source_target_pairs={{0,8},{8,0},{16,24},{24,16},{32,40},{40,32},{48,56},{56,48},{64,72... | collective-permute-start | bytes 1572872 | tf_op jit(solution)/shard_map/ppermute | solution.py:333
